TPU v7x, 32 devices: a whole 2x2x4 slice. The times are simulated.
32 devices in a mesh: dp: 4 (over z), proto: 8 (over y, x, core).
Axes of the slice: x: 2, y: 2, z: 4, core: 2. Of those that a mesh axis runs over, the one named last changes fastest.
Arguments:
- student_feat: bfloat16 [384, 256], P(('dp', 'proto'))
- teacher_feat: bfloat16 [384, 256], P(('dp', 'proto'))
- prototypes: bfloat16 [8192, 256], P('proto')
- teacher_prototypes: bfloat16 [8192, 256], P('proto')
- live_count: int32 [4], replicated, may hold values from 24 to 96, as said below
Outputs:
- student_grad: float32 [384, 256], P(('dp', 'proto'))
- proto_grad: float32 [8, 1024, 256], P('proto', 'dp')
Inputs may be any that keep to these rules, and one draw needn't show every extreme that they name: `live_count`: some group is full (96 live rows) in every draw; live rows are the first ones of each group.
All inputs are finite; a program needn't handle non-finite values.
Results may differ from a plain program's by a relative error of at most 0.0026.
Values may be sent and summed in bfloat16 or wider, within the bound.
No kernel may reach another device: no remote copies, remote signals or barrier semaphores. Data moves between devices by JAX's collectives and lax.ppermute only.
A program may use at most 64 MiB of HBM per device.

v0:
```python
import jax
import jax.numpy as jnp
from jax import lax
from jax.sharding import PartitionSpec as P

ITERS = 3


student_temp = 0.1
teacher_temp = 0.07
eps_norm = 1e-06


def unit_rows(values):
    widened = values.astype(jnp.float32)
    length = jnp.sqrt(jnp.sum(widened * widened, axis=1, keepdims=True) + eps_norm)
    return (widened / length, length)


def sample_totals(values):
    return lax.psum(values, "proto")


def proto_totals(values):
    return lax.psum(values, "dp")


def on_device(student_feat, teacher_feat, prototypes, teacher_prototypes, live_count):
    student_unit, student_length = unit_rows(student_feat)
    teacher_unit, teacher_length = unit_rows(teacher_feat)
    proto_unit, proto_length = unit_rows(prototypes)
    teacher_proto, teacher_proto_length = unit_rows(teacher_prototypes)
    proto_bf = proto_unit.astype(jnp.bfloat16)
    teacher_proto_bf = teacher_proto.astype(jnp.bfloat16)
    student_rows, teacher_rows = (
        lax.all_gather(student_unit.astype(jnp.bfloat16), "proto", axis=0, tiled=True),
        lax.all_gather(teacher_unit.astype(jnp.bfloat16), "proto", axis=0, tiled=True),
    )
    group_size = student_rows.shape[0]
    live_rows = live_count[lax.axis_index("dp")]
    live_mask = jnp.arange(group_size, dtype=jnp.int32) < live_rows
    live_column = live_mask[:, None]
    contract_last = (((1,), (1,)), ((), ()))
    logits = (
        lax.dot_general(student_rows, proto_bf, contract_last, preferred_element_type=jnp.float32)
        / student_temp
    )
    teacher_scores = (
        lax.dot_general(
            teacher_rows, teacher_proto_bf, contract_last, preferred_element_type=jnp.float32
        )
        / teacher_temp
    )
    weights = jnp.where(live_column, jnp.exp(teacher_scores), 0.0)
    partition = sample_totals(jnp.sum(jnp.exp(logits), axis=1))
    targets = weights
    for iteration in range(ITERS):
        targets = targets / proto_totals(jnp.sum(targets, axis=0))[None, :]
        row_sums = sample_totals(jnp.sum(targets, axis=1))
        targets = targets / jnp.where(live_mask, row_sums, 1.0)[:, None]
    student_probs = jnp.exp(logits - jnp.log(partition)[:, None])
    grad_logits = jnp.where(live_column, (student_probs - targets) / student_temp, 0.0).astype(
        jnp.bfloat16
    )
    grad_block = grad_logits
    pulled = lax.psum_scatter(
        jnp.dot(grad_block, proto_bf, preferred_element_type=jnp.float32),
        "proto",
        scatter_dimension=0,
        tiled=True,
    )
    student_grad = (
        pulled - student_unit * jnp.sum(student_unit * pulled, axis=1, keepdims=True)
    ) / student_length
    own_protos = prototypes.shape[0] // lax.axis_size("dp")
    contract_first = (((0,), (0,)), ((), ()))
    grad_block = grad_logits
    pushed = lax.psum_scatter(
        lax.dot_general(
            grad_block, student_rows, contract_first, preferred_element_type=jnp.float32
        ),
        "dp",
        scatter_dimension=0,
        tiled=True,
    )
    first_proto = lax.axis_index("dp") * own_protos
    own_units = lax.dynamic_slice_in_dim(proto_unit, first_proto, own_protos, 0)
    own_lengths = lax.dynamic_slice_in_dim(proto_length, first_proto, own_protos, 0)
    proto_grad = (
        pushed - own_units * jnp.sum(own_units * pushed, axis=1, keepdims=True)
    ) / own_lengths
    return (student_grad, proto_grad[None])


def solution(mesh):
    return jax.shard_map(
        on_device,
        mesh=mesh,
        in_specs=(
            P(("dp", "proto"), None),
            P(("dp", "proto"), None),
            P("proto", None),
            P("proto", None),
            P(),
        ),
        out_specs=(P(("dp", "proto"), None), P("proto", "dp", None)),
        check_vma=False,
    )
```

profile of v0, /device:TPU:0, one launch (start us, length us, event | category | flops | bytes accessed | tf_op | source)
XLA Modules:
  0.0 136.4 jit_solution(17654613464338097512)
XLA Ops:
  7.2 1.3 dynamic_slice.7
  8.5 0.6 iota_compare_fusion
  9.3 0.8 fusion.23
  10.1 1.3 fusion.4
  11.8 0.6 copy-done.3
  12.5 10.7 %all-gather = bf16[8,12,256]{2,1,0:T(8,128)(2,1)S(1)} all-gather(bf16[1,12,256]{2,1,0:T(8,128)(2,1)S(1)} %convert_bitcast_fusion), channel_id=1, replica_groups=mesh['dp'=4,'proto'=8] {'proto'}, dimensions={0}, use_global_device_ids=true | all-gather | bytes 55296 | tf_op jit(solution)/shard_map/all_gather | solution.py:36
  23.1 9.2 %all-gather.1 = bf16[8,12,256]{2,1,0:T(8,128)(2,1)S(1)} all-gather(bf16[1,12,256]{2,1,0:T(8,128)(2,1)S(1)} %fusion.26), channel_id=1, replica_groups=mesh['dp'=4,'proto'=8] {'proto'}, dimensions={0}, use_global_device_ids=true | all-gather | bytes 55296 | tf_op jit(solution)/shard_map/all_gather | solution.py:37
  32.8 12.0 %psum.50 = f32[1024]{0:T(1024)S(1)} all-reduce(f32[1024]{0:T(1024)S(1)} %get-tuple-element.4), channel_id=1, replica_groups=mesh['dp'=4,'proto'=8] {'dp'}, use_global_device_ids=true, to_apply=%region_7.8 | all-reduce | flops 1024 | bytes 8192 | tf_op jit(solution)/shard_map/psum | solution.py:25
  44.9 11.8 %psum.51 = f32[96]{0:T(128)S(1)} all-reduce(f32[96]{0:T(128)S(1)} %divide_reduce_fusion), channel_id=1, replica_groups=mesh['dp'=4,'proto'=8] {'proto'}, use_global_device_ids=true, to_apply=%region_9.10 | all-reduce | flops 96 | bytes 768 | tf_op jit(solution)/shard_map/psum | solution.py:21
  56.7 0.6 broadcast_select_fusion.2
  57.5 8.4 %psum.52 = f32[1024]{0:T(1024)S(1)} all-reduce(f32[1024]{0:T(1024)S(1)} %fusion.16), channel_id=1, replica_groups=mesh['dp'=4,'proto'=8] {'dp'}, use_global_device_ids=true, to_apply=%region_11.12 | all-reduce | flops 1024 | bytes 8192 | tf_op jit(solution)/shard_map/psum | solution.py:25
  66.1 11.8 %psum.53 = f32[96]{0:T(128)S(1)} all-reduce(f32[96]{0:T(128)S(1)} %fusion.17), channel_id=1, replica_groups=mesh['dp'=4,'proto'=8] {'proto'}, use_global_device_ids=true, to_apply=%region_13.14 | all-reduce | flops 96 | bytes 768 | tf_op jit(solution)/shard_map/psum | solution.py:21
  77.9 0.6 broadcast_select_fusion.1
  78.7 10.4 %psum.54 = f32[1024]{0:T(1024)S(1)} all-reduce(f32[1024]{0:T(1024)S(1)} %fusion.18), channel_id=1, replica_groups=mesh['dp'=4,'proto'=8] {'dp'}, use_global_device_ids=true, to_apply=%region_15.16 | all-reduce | flops 1024 | bytes 8192 | tf_op jit(solution)/shard_map/psum | solution.py:25
  89.8 11.8 %all-reduce.2 = (f32[96]{0:T(128)S(1)}, f32[96]{0:T(128)S(1)}) all-reduce(f32[96]{0:T(128)S(1)} %fusion.19, f32[96]{0:T(128)S(1)} %get-tuple-element.6), channel_id=1, replica_groups=mesh['dp'=4,'proto'=8] {'proto'}, use_global_device_ids=true, to_apply=%region_17.18 | all-reduce | flops 192 | bytes 1536 | tf_op jit(solution)/shard_map/psum | solution.py:21
  101.6 0.6 broadcast_select_fusion
  102.6 1.3 fusion.28
  104.3 14.6 %fusion = f32[16,256]{1,0:T(8,128)S(1)} fusion(f32[96,256]{1,0:T(8,128)S(1)} %fusion.20), kind=kCustom, calls=%all-reduce-scatter | all-reduce-scatter fusion | flops 32769 | bytes 115200
  118.8 1.3 collective-permute-start
  120.1 1.9 %collective-permute-start.1 = (f32[12,256]{1,0:T(8,128)S(1)}, f32[12,256]{1,0:T(8,128)S(1)}, u32[]{:S(2)}, u32[]{:S(2)}) collective-permute-start(f32[12,256]{1,0:T(8,128)S(1)} %slice), channel_id=1, source_target_pairs={{0,2},{1,3},{2,4},{3,5},{4,6},{5,7},{8,10},{9,11},{10,12},{11,13},... | collective-permute-start | bytes 36872
  124.7 0.7 subtract_divide_fusion
  125.4 2.2 %reduce-scatter.4.cloned.1.call-done = f32[256,256]{1,0:T(8,128)} async-done(((f32[1024,256]{1,0:T(8,128)}), f32[256,256]{1,0:T(8,128)}) %reduce-scatter.4.cloned.1.call-update) | async-done | bytes 262160 | tf_op jit(solution)/shard_map/reduce_scatter | solution.py:78
  127.6 1.1 multiply_reduce_fusion
  128.7 0.8 divide_bitcast_fusion
  (41 shorter events, 4.9 us)
Async XLA Ops:
  7.2 2.0 %copy-start.4 = (bf16[12,256]{1,0:T(8,128)(2,1)S(1)}, bf16[12,256]{1,0:T(8,128)(2,1)}, u32[]{:S(2)}) copy-start(bf16[12,256]{1,0:T(8,128)(2,1)} %param.6) | copy-start | bytes 18436
  7.2 4.3 %copy-start = (bf16[1024,256]{1,0:T(8,128)(2,1)S(1)}, bf16[1024,256]{1,0:T(8,128)(2,1)}, u32[]{:S(2)}) copy-start(bf16[1024,256]{1,0:T(8,128)(2,1)} %param.7) | copy-start | bytes 1572868
  7.2 120.4 %reduce-scatter.4.cloned.1.call-start = ((), (), s32[]{:S(2)}) async-start(), calls=%async_computation.1 | async-start | bytes 1310720 | tf_op jit(solution)/shard_map/reduce_scatter | solution.py:78
  11.4 21.0 %copy-start.2 = (bf16[1024,256]{1,0:T(8,128)(2,1)S(1)}, bf16[1024,256]{1,0:T(8,128)(2,1)}, u32[]{:S(2)}) copy-start(bf16[1024,256]{1,0:T(8,128)(2,1)} %param.8) | copy-start | bytes 1572868
  11.7 0.7 copy-start.3
  118.8 5.4 %collective-permute-start = (f32[16,256]{1,0:T(8,128)S(1)}, f32[16,256]{1,0:T(8,128)S(1)}, u32[]{:S(2)}, u32[]{:S(2)}) collective-permute-start(f32[16,256]{1,0:T(8,128)S(1)} %fusion), channel_id=1, source_target_pairs={{0,1},{1,2},{2,3},{3,4},{4,5},{5,6},{6,7},{8,9},{9,10},{10,11},{11... | collective-permute-start | bytes 49160
  120.1 4.1 %collective-permute-start.1 = (f32[12,256]{1,0:T(8,128)S(1)}, f32[12,256]{1,0:T(8,128)S(1)}, u32[]{:S(2)}, u32[]{:S(2)}) collective-permute-start(f32[12,256]{1,0:T(8,128)S(1)} %slice), channel_id=1, source_target_pairs={{0,2},{1,3},{2,4},{3,5},{4,6},{5,7},{8,10},{9,11},{10,12},{11,13},... | collective-permute-start | bytes 36872
  122.3 0.7 copy-start.5
  127.6 1.1 copy-start.1
Sparse Core Ops, SparseCore 0:
  104.0 23.4 reduce-scatter.3
where the time goes:
time: 137 us; the launch traced here: 136 us
  blocking collectives  101 us (74%)
  between operations  14.9 us (11%)
  other arithmetic  9.41 us (7%)
  local copies, waits for them, and re-layouts  3.45 us (3%)
  starting transfers between devices  3.26 us (2%)
  matrix products  2.56 us (2%)
  waiting for transfers between devices  2.2 us (2%)
    psum x3, blocking collectives, sample_totals(): return lax.psum(values, 'proto')  35.4 us
    psum x3, blocking collectives, proto_totals(): return lax.psum(values, 'dp')  30.7 us
    unnamed x1, blocking collectives  14.6 us
    all_gather x1, blocking collectives, on_device(): lax.all_gather(student_unit.astype(jnp.bfloat16), 'proto', axis=0, tiled=...  10.7 us
    all_gather x1, blocking collectives, on_device(): lax.all_gather(teacher_unit.astype(jnp.bfloat16), 'proto', axis=0, tiled=...  9.21 us
    unnamed x2, starting transfers between devices  3.22 us
  transfers between devices with their start and end apart: 3, of which 1 were waited for; matrix products, arithmetic and copies ran while one was open for 12% of the time, Pallas kernels for 0%

commit v1 on v0

--- a/solution.py
+++ b/solution.py
@@ -1,14 +1,22 @@
+import functools
+
 import jax
 import jax.numpy as jnp
 from jax import lax
+from jax.experimental import pallas as pl
+from jax.experimental.pallas import tpu as pltpu
 from jax.sharding import PartitionSpec as P
 
 ITERS = 3
-
 
 student_temp = 0.1
 teacher_temp = 0.07
 eps_norm = 1e-06
+
+SLOTS = 16
+LANES = 128
+CHUNK = 256
+BLOCK_BYTES = 8 * 2**20
 
 
 def unit_rows(values):
@@ -17,6 +25,275 @@
     return (widened / length, length)
 
 
+def live_lanes(live_ref, lanes, group_lanes, rows):
+    lane = lax.broadcasted_iota(jnp.int32, (1, lanes), 1)
+    group = lane // group_lanes
+    slot = lane % SLOTS
+    row = (lane % group_lanes) // SLOTS * rows + slot
+    count = jnp.zeros((1, lanes), jnp.int32)
+    for g in range(lanes // group_lanes):
+        count = jnp.where(group == g, live_ref[g], count)
+    return (slot < rows) & (row < count)
+
+
+def pack_lanes(values):
+    pieces = [values[:, k : k + LANES] for k in range(0, values.shape[1], LANES)]
+    return jnp.concatenate(pieces + [jnp.zeros((8 - len(pieces), LANES), jnp.float32)], axis=0)
+
+
+def unpack_lanes(tile, lanes):
+    return jnp.concatenate([tile[k : k + 1, :] for k in range(lanes // LANES)], axis=1)
+
+
+def rows_kernel(student_ref, teacher_ref, out_ref, scratch):
+    rows = student_ref.shape[0]
+    for k, ref in enumerate((student_ref, teacher_ref)):
+        unit, _ = unit_rows(ref[...])
+        scratch[...] = jnp.zeros_like(scratch)
+        scratch[:rows, :] = unit
+        out_ref[k * SLOTS : (k + 1) * SLOTS, :] = scratch[...].astype(jnp.bfloat16)
+
+
+def scores_of(proto_ref, start, rows_all):
+    unit, _ = unit_rows(proto_ref[start : start + CHUNK, :])
+    unit = unit.astype(jnp.bfloat16)
+    return unit, lax.dot_general(
+        unit, rows_all, (((1,), (1,)), ((), ())), preferred_element_type=jnp.float32
+    )
+
+
+def weights_kernel(group_lanes, rows, live_ref, gathered_ref, proto_ref, weights_ref, sums_ref):
+    lanes = weights_ref.shape[1]
+    live = live_lanes(live_ref, lanes, group_lanes, rows)
+    rows_all = gathered_ref[:, SLOTS:, :].reshape(lanes, gathered_ref.shape[2])
+    sums = jnp.zeros((1, lanes), jnp.float32)
+    for start in range(0, proto_ref.shape[0], CHUNK):
+        _, scores = scores_of(proto_ref, start, rows_all)
+        weights = jnp.where(live, jnp.exp(scores / teacher_temp), 0.0)
+        weights_ref[start : start + CHUNK, :] = weights
+        inverse = 1.0 / jnp.sum(weights, axis=1, keepdims=True)
+        sums = sums + jnp.sum(weights * inverse, axis=0, keepdims=True)
+    sums_ref[...] = pack_lanes(sums)
+
+
+def scale_rows_of(tile, live):
+    total = unpack_lanes(tile, live.shape[1])
+    return jnp.where(live, 1.0 / jnp.where(live, total, 1.0), 0.0)
+
+
+def step_kernel(group_lanes, rows, live_ref, parts_ref, weights_ref, sums_ref):
+    lanes = weights_ref.shape[1]
+    live = live_lanes(live_ref, lanes, group_lanes, rows)
+    scale = scale_rows_of(parts_ref[...], live)
+    sums = jnp.zeros((1, lanes), jnp.float32)
+    for start in range(0, weights_ref.shape[0], CHUNK):
+        weights = weights_ref[start : start + CHUNK, :]
+        inverse = 1.0 / jnp.sum(weights * scale, axis=1, keepdims=True)
+        sums = sums + jnp.sum(weights * inverse, axis=0, keepdims=True)
+    sums_ref[...] = pack_lanes(sums)
+
+
+def split_dot(wide, narrow):
+    high = wide.astype(jnp.bfloat16)
+    low = (wide - high.astype(jnp.float32)).astype(jnp.bfloat16)
+    contract_first = (((0,), (0,)), ((), ()))
+    return lax.dot_general(
+        high, narrow, contract_first, preferred_element_type=jnp.float32
+    ) + lax.dot_general(low, narrow, contract_first, preferred_element_type=jnp.float32)
+
+
+def last_kernel(
+    group_lanes,
+    rows,
+    place_ref,
+    live_ref,
+    parts_ref,
+    weights_ref,
+    gathered_ref,
+    proto_ref,
+    out_ref,
+    targets_ref,
+    exps_ref,
+    scaled_ref,
+    units_ref,
+    all_exps_ref,
+):
+    protos, lanes = weights_ref.shape
+    width = proto_ref.shape[1]
+    peers = out_ref.shape[0]
+    live = live_lanes(live_ref, lanes, group_lanes, rows)
+    scale = scale_rows_of(parts_ref[...], live)
+    rows_all = gathered_ref[:, :SLOTS, :].reshape(lanes, width)
+    sums = jnp.zeros((1, lanes), jnp.float32)
+    partition = jnp.zeros((1, lanes), jnp.float32)
+    for start in range(0, protos, CHUNK):
+        weights = weights_ref[start : start + CHUNK, :]
+        inverse = 1.0 / jnp.sum(weights * scale, axis=1, keepdims=True)
+        scaled = weights * inverse
+        scaled_ref[start : start + CHUNK, :] = scaled
+        sums = sums + jnp.sum(scaled, axis=0, keepdims=True)
+        unit, scores = scores_of(proto_ref, start, rows_all)
+        units_ref[start : start + CHUNK, :] = unit
+        exps = jnp.exp(scores / student_temp)
+        all_exps_ref[start : start + CHUNK, :] = exps
+        partition = partition + jnp.sum(exps, axis=0, keepdims=True)
+    dp = place_ref[0]
+    own = targets_ref.shape[0]
+    first = pl.multiple_of(dp * own, own)
+    targets_ref[...] = scaled_ref[pl.ds(first, own), :]
+    exps_ref[...] = all_exps_ref[pl.ds(first, own), :]
+    group = pl.ds(pl.multiple_of(dp * group_lanes, group_lanes), group_lanes)
+    units = units_ref[...]
+    exp_pull = split_dot(all_exps_ref[:, group], units)
+    target_pull = split_dot(scaled_ref[:, group], units)
+    out_ref[:, :SLOTS, :] = exp_pull.reshape(peers, SLOTS, width)
+    out_ref[:, SLOTS : 2 * SLOTS, :] = target_pull.reshape(peers, SLOTS, width)
+    tile = jnp.concatenate([pack_lanes(sums), pack_lanes(partition)], axis=1)
+    out_ref[:, 2 * SLOTS :, :] = jnp.broadcast_to(tile[None], (peers, 8, width))
+
+
+def grads_kernel(
+    group_lanes,
+    rows,
+    place_ref,
+    live_ref,
+    got_ref,
+    targets_ref,
+    exps_ref,
+    gathered_ref,
+    feat_ref,
+    proto_ref,
+    student_out_ref,
+    proto_out_ref,
+    lane_scratch,
+    row_scratch,
+):
+    own, lanes = targets_ref.shape
+    width = feat_ref.shape[1]
+    live = live_lanes(live_ref, lanes, group_lanes, rows)
+    tile = jnp.sum(got_ref[:, 2 * SLOTS :, :], axis=0)
+    total = unpack_lanes(tile[:, :LANES], lanes)
+    target_scale = jnp.where(live, 1.0 / jnp.where(live, total, 1.0), 0.0)
+    exp_scale = jnp.where(live, 1.0 / unpack_lanes(tile[:, LANES:], lanes), 0.0)
+
+    rows_all = gathered_ref[:, :SLOTS, :].reshape(lanes, width)
+    grad = (exps_ref[...] * exp_scale - targets_ref[...] * target_scale) / student_temp
+    pushed = jnp.dot(grad.astype(jnp.bfloat16), rows_all, preferred_element_type=jnp.float32)
+    dp = place_ref[0]
+    unit, length = unit_rows(proto_ref[pl.ds(pl.multiple_of(dp * own, own), own), :])
+    proto_out_ref[0] = (pushed - unit * jnp.sum(unit * pushed, axis=1, keepdims=True)) / length
+
+    lane_scratch[0:1, :] = target_scale
+    lane_scratch[1:2, :] = exp_scale
+    group = pl.ds(pl.multiple_of(dp * group_lanes, group_lanes), group_lanes)
+    slot = lax.broadcasted_iota(jnp.int32, (SLOTS, group_lanes), 0) + place_ref[1] * SLOTS
+    here = lax.broadcasted_iota(jnp.int32, (SLOTS, group_lanes), 1) == slot
+    columns = [
+        jnp.sum(jnp.where(here, lane_scratch[k : k + 1, group], 0.0), axis=1, keepdims=True)
+        for k in range(2)
+    ]
+    exp_pull = jnp.sum(got_ref[:, :SLOTS, :], axis=0)
+    target_pull = jnp.sum(got_ref[:, SLOTS : 2 * SLOTS, :], axis=0)
+    row_scratch[...] = (exp_pull * columns[1] - target_pull * columns[0]) / student_temp
+    pulled = row_scratch[:rows, :]
+    unit, length = unit_rows(feat_ref[...])
+    student_out_ref[...] = (
+        pulled - unit * jnp.sum(unit * pulled, axis=1, keepdims=True)
+    ) / length
+
+
+def call(kernel, out_shape, operands, smem=0, scratch=()):
+    vmem = pl.BlockSpec(memory_space=pltpu.VMEM)
+    return pl.pallas_call(
+        kernel,
+        out_shape=out_shape,
+        in_specs=[pl.BlockSpec(memory_space=pltpu.SMEM)] * smem + [vmem] * (len(operands) - smem),
+        out_specs=jax.tree.map(lambda _: vmem, out_shape),
+        scratch_shapes=scratch,
+        compiler_params=pltpu.CompilerParams(vmem_limit_bytes=48 * 2**20),
+    )(*operands)
+
+
+def gather_by_exchange(values, axis):
+    copies = jnp.broadcast_to(values[None], (lax.axis_size(axis),) + values.shape)
+    return lax.all_to_all(copies, axis, split_axis=0, concat_axis=0, tiled=True)
+
+
+def pairs(distance):
+    return [(k, k ^ distance) for k in range(lax.axis_size("proto"))]
+
+
+def pairwise_total(values):
+    distance = 1
+    while distance < lax.axis_size("proto"):
+        values = values + lax.ppermute(values, "proto", pairs(distance))
+        distance *= 2
+    return values
+
+
+def direct_total(values):
+    others = [lax.ppermute(values, "proto", pairs(d)) for d in range(1, lax.axis_size("proto"))]
+    return functools.reduce(jnp.add, others, values)
+
+
+def on_device_all_rows(student_feat, teacher_feat, prototypes, teacher_prototypes, live_count):
+    n_dp, n_proto = lax.axis_size("dp"), lax.axis_size("proto")
+    rows, width = student_feat.shape
+    protos = prototypes.shape[0]
+    own = protos // n_dp
+    group_lanes = n_proto * SLOTS
+    lanes = n_dp * group_lanes
+    f32 = functools.partial(jax.ShapeDtypeStruct, dtype=jnp.float32)
+    sizes = (group_lanes, rows)
+    place = jnp.stack([lax.axis_index("dp"), lax.axis_index("proto")]).astype(jnp.int32)
+
+    unit = call(
+        rows_kernel,
+        jax.ShapeDtypeStruct((2 * SLOTS, width), jnp.bfloat16),
+        (student_feat, teacher_feat),
+        scratch=[pltpu.VMEM((SLOTS, width), jnp.float32)],
+    )
+    gathered = jnp.swapaxes(gather_by_exchange(gather_by_exchange(unit, "dp"), "proto"), 0, 1)
+    gathered = gathered.reshape(n_dp * n_proto, 2 * SLOTS, width)
+    weights, sums = call(
+        functools.partial(weights_kernel, *sizes),
+        (f32((protos, lanes)), f32((8, LANES))),
+        (live_count, gathered, teacher_prototypes),
+        smem=1,
+    )
+    parts = pairwise_total(sums)
+    for _ in range(ITERS - 2):
+        sums = call(
+            functools.partial(step_kernel, *sizes),
+            f32((8, LANES)),
+            (live_count, parts, weights),
+            smem=1,
+        )
+        parts = direct_total(sums)
+    sent, targets, exps = call(
+        functools.partial(last_kernel, *sizes),
+        (f32((n_proto, 2 * SLOTS + 8, width)), f32((own, lanes)), f32((own, lanes))),
+        (place, live_count, parts, weights, gathered, prototypes),
+        smem=2,
+        scratch=[
+            pltpu.VMEM((protos, lanes), jnp.float32),
+            pltpu.VMEM((protos, width), jnp.bfloat16),
+            pltpu.VMEM((protos, lanes), jnp.float32),
+        ],
+    )
+    got = lax.all_to_all(sent, "proto", split_axis=0, concat_axis=0, tiled=True)
+    return call(
+        functools.partial(grads_kernel, *sizes),
+        (f32((rows, width)), f32((1, own, width))),
+        (place, live_count, got, targets, exps, gathered, student_feat, prototypes),
+        smem=2,
+        scratch=[
+            pltpu.VMEM((8, lanes), jnp.float32),
+            pltpu.VMEM((SLOTS, width), jnp.float32),
+        ],
+    )
+
+
 def sample_totals(values):
     return lax.psum(values, "proto")
 
@@ -25,7 +302,7 @@
     return lax.psum(values, "dp")
 
 
-def on_device(student_feat, teacher_feat, prototypes, teacher_prototypes, live_count):
+def on_device_group_rows(student_feat, teacher_feat, prototypes, teacher_prototypes, live_count):
     student_unit, student_length = unit_rows(student_feat)
     teacher_unit, teacher_length = unit_rows(teacher_feat)
     proto_unit, proto_length = unit_rows(prototypes)
@@ -59,10 +336,9 @@
         row_sums = sample_totals(jnp.sum(targets, axis=1))
         targets = targets / jnp.where(live_mask, row_sums, 1.0)[:, None]
     student_probs = jnp.exp(logits - jnp.log(partition)[:, None])
-    grad_logits = jnp.where(live_column, (student_probs - targets) / student_temp, 0.0).astype(
+    grad_block = jnp.where(live_column, (student_probs - targets) / student_temp, 0.0).astype(
         jnp.bfloat16
     )
-    grad_block = grad_logits
     pulled = lax.psum_scatter(
         jnp.dot(grad_block, proto_bf, preferred_element_type=jnp.float32),
         "proto",
@@ -74,7 +350,6 @@
     ) / student_length
     own_protos = prototypes.shape[0] // lax.axis_size("dp")
     contract_first = (((0,), (0,)), ((), ()))
-    grad_block = grad_logits
     pushed = lax.psum_scatter(
         lax.dot_general(
             grad_block, student_rows, contract_first, preferred_element_type=jnp.float32
@@ -90,6 +365,25 @@
         pushed - own_units * jnp.sum(own_units * pushed, axis=1, keepdims=True)
     ) / own_lengths
     return (student_grad, proto_grad[None])
+
+
+def on_device(student_feat, teacher_feat, prototypes, teacher_prototypes, live_count):
+    n_dp, n_proto = lax.axis_size("dp"), lax.axis_size("proto")
+    rows, width = student_feat.shape
+    protos = prototypes.shape[0]
+    lanes = n_dp * n_proto * SLOTS
+    fits = (
+        rows <= SLOTS
+        and n_proto & (n_proto - 1) == 0
+        and n_proto * SLOTS % LANES == 0
+        and lanes <= 8 * LANES
+        and width == 2 * LANES
+        and protos % CHUNK == 0
+        and protos % (n_dp * 16) == 0
+        and protos * lanes * 4 <= BLOCK_BYTES
+    )
+    plan = on_device_all_rows if fits else on_device_group_rows
+    return plan(student_feat, teacher_feat, prototypes, teacher_prototypes, live_count)
 
 
 def solution(mesh):

time: 137 us -> 60.6 us (0.44)
  blocking collectives: 101 us -> 35.1 us
  between operations: 14.9 us -> 0.74 us
  other arithmetic: 9.41 us -> 0.09 us
  waiting for transfers between devices: 2.2 us -> 8.94 us
  Pallas kernels: 0 us -> 6.28 us
  starting transfers between devices: 3.26 us -> 7.51 us
  matrix products: 2.56 us -> 0 us
  local copies, waits for them, and re-layouts: 3.45 us -> 1.56 us
    psum x6 -> x0, blocking collectives: 66.1 us -> none  [the longest x3 35.4 us: sample_totals(): return lax.psum(values, 'proto')]
    all_to_all x0 -> x3, blocking collectives: none -> 35.1 us  [the longest x2 25.1 us: gather_by_exchange(): return lax.all_to_all(copies, axis, split_axis=0, concat_axis=0, tiled=True)]
    all_gather x2 -> x0, blocking collectives: 19.9 us -> none  [the longest x1 10.7 us: on_device(): lax.all_gather(student_unit.astype(jnp.bfloat16), 'proto', axis=0, tiled=...]
    unnamed x1 -> x0, blocking collectives: 14.6 us -> none
    ppermute x0 -> x10, waiting for transfers between devices: none -> 8.94 us  [the longest x3 7.24 us: pairwise_total(): values = values + lax.ppermute(values, 'proto', pairs(distance))]
    ppermute x0 -> x10, starting transfers between devices: none -> 7.51 us  [the longest x7 6.31 us: direct_total(): lax.ppermute(values, 'proto', pairs(d))]
    pallas_call x0 -> x5, Pallas kernels: none -> 6.28 us  [call(): pl.pallas_call(kernel, out_shape=out_shape, in_specs=[pl.BlockSpec(memory...]
    reduce_sum x11 -> x0, other arithmetic: 4.61 us -> none  [the longest x4 2.4 us: unit_rows(): jnp.sum(widened * widened, axis=1, keepdims=True) + eps_norm]
  transfers between devices with their start and end apart: 3 -> 10, of which waited for: 1 -> 6; matrix products, arithmetic and copies ran while one was open for 12% -> 0% of each run, Pallas kernels for 0% -> 0%
where the time goes in v1:
time: 60.6 us; the launch traced here: 60.3 us
  blocking collectives  35.1 us (58%)
  waiting for transfers between devices  8.94 us (15%)
  starting transfers between devices  7.51 us (12%)
  Pallas kernels  6.28 us (10%)
  local copies, waits for them, and re-layouts  1.56 us (3%)
  between operations  0.74 us (1%)
    all_to_all x2, blocking collectives, gather_by_exchange(): return lax.all_to_all(copies, axis, split_axis=0, concat_axis=0, tiled=True)  25.1 us
    all_to_all x1, blocking collectives, on_device_all_rows(): got = lax.all_to_all(sent, 'proto', split_axis=0, concat_axis=0, tiled=True)  10 us
    ppermute x3, waiting for transfers between devices, pairwise_total(): values = values + lax.ppermute(values, 'proto', pairs(distance))  7.24 us
    ppermute x7, starting transfers between devices, direct_total(): lax.ppermute(values, 'proto', pairs(d))  6.31 us
    pallas_call x5, Pallas kernels, call(): pl.pallas_call(kernel, out_shape=out_shape, in_specs=[pl.BlockSpec(memory...  6.28 us
    ppermute x7, waiting for transfers between devices, direct_total(): lax.ppermute(values, 'proto', pairs(d))  1.7 us
    unnamed x12, local copies, waits for them, and re-layouts  1.46 us
  transfers between devices with their start and end apart: 10, of which 6 were waited for; matrix products, arithmetic and copies ran while one was open for 0% of the time, Pallas kernels for 0%

profile of v1, /device:TPU:0, one launch (start us, length us, event | category | flops | bytes accessed | tf_op | source)
XLA Modules:
  0.0 60.3 jit_solution(4778373513499226150)
XLA Ops:
  0.7 0.7 %copy-done.2 = bf16[12,256]{1,0:T(8,128)(2,1)S(1)} copy-done((bf16[12,256]{1,0:T(8,128)(2,1)S(1)}, bf16[12,256]{1,0:T(8,128)(2,1)}, u32[]{:S(2)}) %copy-start.2) | copy-done | bytes 6168
  1.4 0.7 %copy-done.5 = bf16[12,256]{1,0:T(8,128)(2,1)S(1)} copy-done((bf16[12,256]{1,0:T(8,128)(2,1)S(1)}, bf16[12,256]{1,0:T(8,128)(2,1)}, u32[]{:S(2)}) %copy-start.5) | copy-done | bytes 6168
  2.1 0.1 shard_map.68
  2.2 11.9 %all_to_all.15 = bf16[4,32,256]{2,1,0:T(8,128)(2,1)S(1)} all-to-all(bf16[4,32,256]{2,1,0:T(8,128)(2,1)S(1)} %broadcast_in_dim.4), channel_id=1, replica_groups=mesh['dp'=4,'proto'=8] {'dp'}, dimensions={0} | all-to-all | bytes 131072 | tf_op jit(solution)/shard_map/all_to_all | solution.py:219
  14.1 13.3 %all_to_all.16 = bf16[8,4,32,256]{3,2,1,0:T(8,128)(2,1)S(1)} all-to-all(bf16[8,4,32,256]{3,2,1,0:T(8,128)(2,1)S(1)} %broadcast_in_dim.5), channel_id=1, replica_groups=mesh['dp'=4,'proto'=8] {'proto'}, dimensions={0} | all-to-all | bytes 1048576 | tf_op jit(solution)/shard_map/all_to_all | solution.py:219
  27.5 1.5 %shard_map.69 = (f32[1024,512]{1,0:T(8,128)S(1)}, f32[8,128]{1,0:T(8,128)S(1)}) custom-call(s32[4]{0:T(128)S(1)} %copy-done.4, bf16[32,32,256]{2,1,0:T(8,128)(2,1)S(1)} %bitcast.4, bf16[1024,256]{1,0:T(8,128)(2,1)S(1)} %copy-done.1), custom_call_target="tpu_custom_call" | custom-call | tf_op jit(solution)/shard_map/pallas_call | solution.py:207
  29.0 1.2 %collective-permute-done = f32[8,128]{1,0:T(8,128)S(1)} collective-permute-done((f32[8,128]{1,0:T(8,128)S(1)}, f32[8,128]{1,0:T(8,128)S(1)}, u32[]{:S(2)}, u32[]{:S(2)}) %collective-permute-start) | collective-permute-done | bytes 4128 | tf_op jit(solution)/shard_map/ppermute | solution.py:229
  30.2 0.6 collective-permute-start.1
  30.7 3.0 %collective-permute-done.1 = f32[8,128]{1,0:T(8,128)S(1)} collective-permute-done((f32[8,128]{1,0:T(8,128)S(1)}, f32[8,128]{1,0:T(8,128)S(1)}, u32[]{:S(2)}, u32[]{:S(2)}) %collective-permute-start.1) | collective-permute-done | bytes 4128 | tf_op jit(solution)/shard_map/ppermute | solution.py:229
  33.8 0.6 collective-permute-start.2
  34.4 3.0 %collective-permute-done.2 = f32[8,128]{1,0:T(8,128)S(1)} collective-permute-done((f32[8,128]{1,0:T(8,128)S(1)}, f32[8,128]{1,0:T(8,128)S(1)}, u32[]{:S(2)}, u32[]{:S(2)}) %collective-permute-start.2) | collective-permute-done | bytes 4128 | tf_op jit(solution)/shard_map/ppermute | solution.py:229
  37.4 0.9 %shard_map.70 = f32[8,128]{1,0:T(8,128)S(1)} custom-call(s32[4]{0:T(128)S(1)} %copy-done.4, f32[8,128]{1,0:T(8,128)S(1)} %add.32.parts_ref, f32[1024,512]{1,0:T(8,128)S(1)} %get-tuple-element.8.weights_ref), custom_call_target="tpu_custom_call" | custom-call | tf_op jit(solution)/shard_map/pallas_call | solution.py:207
  38.4 0.6 %collective-permute-start.8 = (f32[8,128]{1,0:T(8,128)S(1)}, f32[8,128]{1,0:T(8,128)S(1)}, u32[]{:S(2)}, u32[]{:S(2)}) collective-permute-start(f32[8,128]{1,0:T(8,128)S(1)} %shard_map.70), channel_id=1, source_target_pairs={{0,6},{1,7},{2,4},{3,5},{4,2},{5,3},{6,0},{7,1},{8,14},{9,15},{10,... | collective-permute-start | bytes 12296 | tf_op jit(solution)/shard_map/ppermute | solution.py:235
  39.0 2.3 %collective-permute-start.7 = (f32[8,128]{1,0:T(8,128)S(1)}, f32[8,128]{1,0:T(8,128)S(1)}, u32[]{:S(2)}, u32[]{:S(2)}) collective-permute-start(f32[8,128]{1,0:T(8,128)S(1)} %shard_map.70), channel_id=1, source_target_pairs={{0,5},{1,4},{2,7},{3,6},{4,1},{5,0},{6,3},{7,2},{8,13},{9,12},{10,... | collective-permute-start | bytes 12296 | tf_op jit(solution)/shard_map/ppermute | solution.py:235
  41.3 1.5 %collective-permute-start.6 = (f32[8,128]{1,0:T(8,128)S(1)}, f32[8,128]{1,0:T(8,128)S(1)}, u32[]{:S(2)}, u32[]{:S(2)}) collective-permute-start(f32[8,128]{1,0:T(8,128)S(1)} %shard_map.70), channel_id=1, source_target_pairs={{0,4},{1,5},{2,6},{3,7},{4,0},{5,1},{6,2},{7,3},{8,12},{9,13},{10,... | collective-permute-start | bytes 12296 | tf_op jit(solution)/shard_map/ppermute | solution.py:235
  42.7 0.6 collective-permute-start.4
  43.3 1.3 %collective-permute-start.3 = (f32[8,128]{1,0:T(8,128)S(1)}, f32[8,128]{1,0:T(8,128)S(1)}, u32[]{:S(2)}, u32[]{:S(2)}) collective-permute-start(f32[8,128]{1,0:T(8,128)S(1)} %shard_map.70), channel_id=1, source_target_pairs={{0,1},{1,0},{2,3},{3,2},{4,5},{5,4},{6,7},{7,6},{8,9},{9,8},{10,11... | collective-permute-start | bytes 12296 | tf_op jit(solution)/shard_map/ppermute | solution.py:235
  44.6 0.1 pad_add_fusion.place_ref
  44.7 0.2 collective-permute-done.6
  44.9 0.9 %collective-permute-done.5 = f32[8,128]{1,0:T(8,128)S(1)} collective-permute-done((f32[8,128]{1,0:T(8,128)S(1)}, f32[8,128]{1,0:T(8,128)S(1)}, u32[]{:S(2)}, u32[]{:S(2)}) %collective-permute-start.5) | collective-permute-done | bytes 4128 | tf_op jit(solution)/shard_map/ppermute | solution.py:235
  45.8 0.6 %collective-permute-done.4 = f32[8,128]{1,0:T(8,128)S(1)} collective-permute-done((f32[8,128]{1,0:T(8,128)S(1)}, f32[8,128]{1,0:T(8,128)S(1)}, u32[]{:S(2)}, u32[]{:S(2)}) %collective-permute-start.4) | collective-permute-done | bytes 4128 | tf_op jit(solution)/shard_map/ppermute | solution.py:235
  46.4 2.2 %shard_map.71 = (f32[8,40,256]{2,1,0:T(8,128)S(1)}, f32[256,512]{1,0:T(8,128)S(1)}, f32[256,512]{1,0:T(8,128)S(1)}) custom-call(s32[2]{0:T(128)S(1)} %pad_add_fusion.place_ref, s32[4]{0:T(128)S(1)} %copy-done.4, f32[8,128]{1,0:T(8,128)S(1)} %add_add_fusion.parts_ref, f32[1024,512]{1,0:T(8,128)S(1)} %get-tuple-element.8.weights_ref, ...), custom_call_target="tpu_custom_call" | custom-call | tf_op jit(solution)/shard_map/pallas_call | solution.py:207
  48.6 10.0 %all_to_all.17.got_ref = f32[8,40,256]{2,1,0:T(8,128)S(1)} all-to-all(f32[8,40,256]{2,1,0:T(8,128)S(1)} %get-tuple-element.9), channel_id=1, replica_groups=mesh['dp'=4,'proto'=8] {'proto'}, dimensions={0} | all-to-all | bytes 655360 | tf_op jit(solution)/shard_map/all_to_all | solution.py:284
  58.7 1.6 %shard_map.72 = (f32[12,256]{1,0:T(8,128)}, f32[1,256,256]{2,1,0:T(8,128)}) custom-call(s32[2]{0:T(128)S(1)} %pad_add_fusion.place_ref, s32[4]{0:T(128)S(1)} %copy-done.4, f32[8,40,256]{2,1,0:T(8,128)S(1)} %all_to_all.17.got_ref, f32[256,512]{1,0:T(8,128)S(1)} %get-tuple-element.10.targets_ref, f32[256,512]{1,0:T(8,128)S(1)} %get-tuple-element.11.exps_ref, ...), custom_call_target="tpu_custom_call" | custom-call | tf_op jit(solution)/shard_map/pallas_call | solution.py:207
  (24 shorter events, 0.3 us)
Async XLA Ops:
  0.6 26.8 %copy-start.1 = (bf16[1024,256]{1,0:T(8,128)(2,1)S(1)}, bf16[1024,256]{1,0:T(8,128)(2,1)}, u32[]{:S(2)}) copy-start(bf16[1024,256]{1,0:T(8,128)(2,1)} %proto_ref.3) | copy-start | bytes 1572868
  0.6 0.8 %copy-start.2 = (bf16[12,256]{1,0:T(8,128)(2,1)S(1)}, bf16[12,256]{1,0:T(8,128)(2,1)}, u32[]{:S(2)}) copy-start(bf16[12,256]{1,0:T(8,128)(2,1)} %feat_ref.1) | copy-start | bytes 18436
  1.4 0.7 %copy-start.5 = (bf16[12,256]{1,0:T(8,128)(2,1)S(1)}, bf16[12,256]{1,0:T(8,128)(2,1)}, u32[]{:S(2)}) copy-start(bf16[12,256]{1,0:T(8,128)(2,1)} %teacher_ref.1) | copy-start | bytes 18436
  2.1 25.4 %copy-start.4 = (s32[4]{0:T(128)S(1)}, s32[4]{0:T(128)}, u32[]{:S(2)}) copy-start(s32[4]{0:T(128)} %live_ref.7) | copy-start | bytes 52
  27.4 19.0 %copy-start = (bf16[1024,256]{1,0:T(8,128)(2,1)S(1)}, bf16[1024,256]{1,0:T(8,128)(2,1)}, u32[]{:S(2)}) copy-start(bf16[1024,256]{1,0:T(8,128)(2,1)} %proto_ref.5) | copy-start | bytes 1572868
  28.9 1.2 %collective-permute-start = (f32[8,128]{1,0:T(8,128)S(1)}, f32[8,128]{1,0:T(8,128)S(1)}, u32[]{:S(2)}, u32[]{:S(2)}) collective-permute-start(f32[8,128]{1,0:T(8,128)S(1)} %get-tuple-element.7), channel_id=1, source_target_pairs={{0,1},{1,0},{2,3},{3,2},{4,5},{5,4},{6,7},{7,6},{8,9},{9,8},{10,11... | collective-permute-start | bytes 12296 | tf_op jit(solution)/shard_map/ppermute | solution.py:229
  30.2 3.6 %collective-permute-start.1 = (f32[8,128]{1,0:T(8,128)S(1)}, f32[8,128]{1,0:T(8,128)S(1)}, u32[]{:S(2)}, u32[]{:S(2)}) collective-permute-start(f32[8,128]{1,0:T(8,128)S(1)} %add.30), channel_id=1, source_target_pairs={{0,2},{1,3},{2,0},{3,1},{4,6},{5,7},{6,4},{7,5},{8,10},{9,11},{10,... | collective-permute-start | bytes 12296 | tf_op jit(solution)/shard_map/ppermute | solution.py:229
  33.8 3.6 %collective-permute-start.2 = (f32[8,128]{1,0:T(8,128)S(1)}, f32[8,128]{1,0:T(8,128)S(1)}, u32[]{:S(2)}, u32[]{:S(2)}) collective-permute-start(f32[8,128]{1,0:T(8,128)S(1)} %add.31), channel_id=1, source_target_pairs={{0,4},{1,5},{2,6},{3,7},{4,0},{5,1},{6,2},{7,3},{8,12},{9,13},{10,... | collective-permute-start | bytes 12296 | tf_op jit(solution)/shard_map/ppermute | solution.py:229
  38.3 20.4 %copy-start.3 = (bf16[12,256]{1,0:T(8,128)(2,1)S(1)}, bf16[12,256]{1,0:T(8,128)(2,1)}, u32[]{:S(2)}) copy-start(bf16[12,256]{1,0:T(8,128)(2,1)} %feat_ref.1) | copy-start | bytes 18436
  38.3 4.5 %collective-permute-start.9 = (f32[8,128]{1,0:T(8,128)S(1)}, f32[8,128]{1,0:T(8,128)S(1)}, u32[]{:S(2)}, u32[]{:S(2)}) collective-permute-start(f32[8,128]{1,0:T(8,128)S(1)} %shard_map.70), channel_id=1, source_target_pairs={{0,7},{1,6},{2,5},{3,4},{4,3},{5,2},{6,1},{7,0},{8,15},{9,14},{10,... | collective-permute-start | bytes 12296 | tf_op jit(solution)/shard_map/ppermute | solution.py:235
  38.4 5.0 %collective-permute-start.8 = (f32[8,128]{1,0:T(8,128)S(1)}, f32[8,128]{1,0:T(8,128)S(1)}, u32[]{:S(2)}, u32[]{:S(2)}) collective-permute-start(f32[8,128]{1,0:T(8,128)S(1)} %shard_map.70), channel_id=1, source_target_pairs={{0,6},{1,7},{2,4},{3,5},{4,2},{5,3},{6,0},{7,1},{8,14},{9,15},{10,... | collective-permute-start | bytes 12296 | tf_op jit(solution)/shard_map/ppermute | solution.py:235
  39.0 5.7 %collective-permute-start.7 = (f32[8,128]{1,0:T(8,128)S(1)}, f32[8,128]{1,0:T(8,128)S(1)}, u32[]{:S(2)}, u32[]{:S(2)}) collective-permute-start(f32[8,128]{1,0:T(8,128)S(1)} %shard_map.70), channel_id=1, source_target_pairs={{0,5},{1,4},{2,7},{3,6},{4,1},{5,0},{6,3},{7,2},{8,13},{9,12},{10,... | collective-permute-start | bytes 12296 | tf_op jit(solution)/shard_map/ppermute | solution.py:235
  41.3 3.6 %collective-permute-start.6 = (f32[8,128]{1,0:T(8,128)S(1)}, f32[8,128]{1,0:T(8,128)S(1)}, u32[]{:S(2)}, u32[]{:S(2)}) collective-permute-start(f32[8,128]{1,0:T(8,128)S(1)} %shard_map.70), channel_id=1, source_target_pairs={{0,4},{1,5},{2,6},{3,7},{4,0},{5,1},{6,2},{7,3},{8,12},{9,13},{10,... | collective-permute-start | bytes 12296 | tf_op jit(solution)/shard_map/ppermute | solution.py:235
  42.7 3.0 %collective-permute-start.5 = (f32[8,128]{1,0:T(8,128)S(1)}, f32[8,128]{1,0:T(8,128)S(1)}, u32[]{:S(2)}, u32[]{:S(2)}) collective-permute-start(f32[8,128]{1,0:T(8,128)S(1)} %shard_map.70), channel_id=1, source_target_pairs={{0,3},{1,2},{2,1},{3,0},{4,7},{5,6},{6,5},{7,4},{8,11},{9,10},{10,... | collective-permute-start | bytes 12296 | tf_op jit(solution)/shard_map/ppermute | solution.py:235
  42.7 3.6 %collective-permute-start.4 = (f32[8,128]{1,0:T(8,128)S(1)}, f32[8,128]{1,0:T(8,128)S(1)}, u32[]{:S(2)}, u32[]{:S(2)}) collective-permute-start(f32[8,128]{1,0:T(8,128)S(1)} %shard_map.70), channel_id=1, source_target_pairs={{0,2},{1,3},{2,0},{3,1},{4,6},{5,7},{6,4},{7,5},{8,10},{9,11},{10,... | collective-permute-start | bytes 12296 | tf_op jit(solution)/shard_map/ppermute | solution.py:235
  43.3 3.0 %collective-permute-start.3 = (f32[8,128]{1,0:T(8,128)S(1)}, f32[8,128]{1,0:T(8,128)S(1)}, u32[]{:S(2)}, u32[]{:S(2)}) collective-permute-start(f32[8,128]{1,0:T(8,128)S(1)} %shard_map.70), channel_id=1, source_target_pairs={{0,1},{1,0},{2,3},{3,2},{4,5},{5,4},{6,7},{7,6},{8,9},{9,8},{10,11... | collective-permute-start | bytes 12296 | tf_op jit(solution)/shard_map/ppermute | solution.py:235

commit v2 on v0

--- a/solution.py
+++ b/solution.py
@@ -1,14 +1,20 @@
+import functools
+
 import jax
 import jax.numpy as jnp
 from jax import lax
+from jax.experimental import pallas as pl
+from jax.experimental.pallas import tpu as pltpu
 from jax.sharding import PartitionSpec as P
 
 ITERS = 3
-
 
 student_temp = 0.1
 teacher_temp = 0.07
 eps_norm = 1e-06
+
+LANES = 128
+BLOCK_BYTES = 8 * 2**20
 
 
 def unit_rows(values):
@@ -17,6 +23,377 @@
     return (widened / length, length)
 
 
+CORE, X, Y = 1, 2, 4
+
+
+def quick_unit(values):
+    widened = values.astype(jnp.float32)
+    squares = jnp.sum(widened * widened, axis=1, keepdims=True) + eps_norm
+    scale = lax.rsqrt(squares)
+    return widened * scale, scale
+
+
+def live_lanes(place_ref, lanes, n_dp, rows):
+    lane = lax.broadcasted_iota(jnp.int32, (1, lanes), 1)
+    live = jnp.zeros((1, lanes), jnp.float32)
+    start = 0
+    for t in range(n_dp):
+        count = place_ref[2 + (place_ref[0] ^ t)]
+        for c in range(2):
+            for x in range(2):
+                for y in range(2):
+                    proto = ((place_ref[1] ^ c) & CORE) + X * x + Y * y
+                    end = start + jnp.clip(count - proto * rows, 0, rows)
+                    live = jnp.where((lane >= start) & (lane < end), 1.0, live)
+                    start += rows
+    return live
+
+
+def pack_lanes(values):
+    pieces = [values[:, k : k + LANES] for k in range(0, values.shape[1], LANES)]
+    return jnp.concatenate(pieces + [jnp.zeros((8 - len(pieces), LANES), jnp.float32)], axis=0)
+
+
+def unpack_lanes(tile, lanes):
+    return jnp.concatenate([tile[k : k + 1, :] for k in range(lanes // LANES)], axis=1)
+
+
+def as_column(values):
+    return jnp.broadcast_to(values, (LANES, values.shape[1])).T
+
+
+def as_tile(partial):
+    return pack_lanes(jnp.sum(partial.T, axis=0, keepdims=True))
+
+
+def inverse_rows(tile, rows):
+    total = unpack_lanes(tile, rows)
+    live = total > 0.0
+    return jnp.where(live, 1.0 / jnp.where(live, total, 1.0), 0.0)
+
+
+def units_kernel(student_ref, teacher_ref, student_out_ref, teacher_out_ref):
+    for ref, out_ref in ((teacher_ref, teacher_out_ref), (student_ref, student_out_ref)):
+        unit, _ = quick_unit(ref[...])
+        out_ref[...] = unit.astype(jnp.bfloat16)
+
+
+def place_rows(place_ref, near_ref, far_ref, which, rows, scratch):
+    mine_x = (place_ref[1] >> 1) & 1
+    mine_y = (place_ref[1] >> 2) & 1
+    start = 0
+    for t in range(near_ref.shape[1]):
+        for ref in (near_ref, far_ref):
+            for x in range(2):
+                for y in range(2):
+                    block = ref[mine_y ^ y, t, mine_x ^ x].astype(jnp.float32)
+                    scratch[start : start + rows, :] = block[which * rows : (which + 1) * rows]
+                    start += rows
+    unit, _ = quick_unit(scratch[...])
+    return unit.astype(jnp.bfloat16)
+
+
+def scores_of(rows_all, units):
+    return lax.dot_general(
+        rows_all, units, (((1,), (1,)), ((), ())), preferred_element_type=jnp.float32
+    )
+
+
+def twice(column):
+    return jnp.concatenate([column, column], axis=1)
+
+
+def weighted_rows(weights_ref, scale_ref, part_ref):
+    tiles = weights_ref.shape[1] // LANES
+    scales = [scale_ref[:, k * LANES : (k + 1) * LANES] for k in range(tiles)]
+
+    def body(i, _):
+        at = pl.ds(pl.multiple_of(i * 8, 8), 8)
+        sums = [None] * 4
+        for k in range(tiles):
+            term = weights_ref[at, k * LANES : (k + 1) * LANES] * scales[k]
+            sums[k % 4] = term if sums[k % 4] is None else sums[k % 4] + term
+        part_ref[at, :] = (sums[0] + sums[1]) + (sums[2] + sums[3])
+        return 0
+
+    lax.fori_loop(0, weights_ref.shape[0] // 8, body, 0, unroll=4)
+
+
+def column_scales(weights_ref, row_ref, scale_ref):
+    tiles = weights_ref.shape[1] // LANES
+
+    def body(i, sums):
+        at = pl.ds(pl.multiple_of(i * 8, 8), 8)
+        row = row_ref[at, :]
+        return [
+            total + weights_ref[at, k * LANES : (k + 1) * LANES] * row
+            for k, total in enumerate(sums)
+        ]
+
+    zeros = [jnp.zeros((8, LANES), jnp.float32)] * tiles
+    sums = lax.fori_loop(0, weights_ref.shape[0] // 8, body, zeros, unroll=4)
+    for k, total in enumerate(sums):
+        inverse = 1.0 / jnp.sum(total, axis=0, keepdims=True)
+        scale_ref[:, k * LANES : (k + 1) * LANES] = jnp.broadcast_to(inverse, (8, LANES))
+
+
+def weights_kernel(chunk, place_ref, near_ref, far_ref, *refs):
+    *unit_refs, weights_ref, sums_ref, scratch, scale_ref, part_ref = refs
+    all_rows = weights_ref.shape[0]
+    protos = unit_refs[0].shape[0]
+    rows = near_ref.shape[3] // 2
+    rows_all = place_rows(place_ref, near_ref, far_ref, 0, rows, scratch)
+    live = twice(as_column(live_lanes(place_ref, all_rows, near_ref.shape[1], rows)))
+    for k, unit_ref in enumerate(unit_refs):
+        for start in range(0, protos, chunk):
+            scores = scores_of(rows_all, unit_ref[start : start + chunk, :])
+            weights = jnp.exp(scores * (1 / teacher_temp)) * live
+            at = k * protos + start
+            weights_ref[:, at : at + chunk] = weights
+            inverse = 1.0 / jnp.sum(weights, axis=0, keepdims=True)
+            scale_ref[:, at : at + chunk] = jnp.broadcast_to(inverse, (8, chunk))
+    weighted_rows(weights_ref, scale_ref, part_ref)
+    sums_ref[...] = as_tile(part_ref[...])
+
+
+def step_kernel(mine_ref, other_ref, weights_ref, sums_ref, row_ref, scale_ref, part_ref):
+    all_rows = weights_ref.shape[0]
+    row_ref[...] = as_column(inverse_rows(mine_ref[...] + other_ref[...], all_rows))
+    column_scales(weights_ref, row_ref, scale_ref)
+    weighted_rows(weights_ref, scale_ref, part_ref)
+    sums_ref[...] = as_tile(part_ref[...])
+
+
+def split(values):
+    high = values.astype(jnp.bfloat16)
+    low = (values - high.astype(jnp.float32)).astype(jnp.bfloat16)
+    return jnp.concatenate([high, low], axis=0)
+
+
+def exps_kernel(chunk, place_ref, near_ref, far_ref, *refs):
+    *unit_refs, rows_ref, exps_ref, pull_ref, sums_ref, scratch, own_ref = refs
+    all_rows = exps_ref.shape[0]
+    protos = unit_refs[0].shape[0]
+    first = pull_ref.shape[0]
+    rows_ref[...] = place_rows(place_ref, near_ref, far_ref, 1, near_ref.shape[3] // 2, scratch)
+    rows_all = rows_ref[...]
+    part = jnp.zeros((all_rows, LANES), jnp.float32)
+    pull = jnp.zeros((2 * first, pull_ref.shape[1]), jnp.float32)
+    for k, unit_ref in enumerate(unit_refs):
+        for start in range(0, protos, chunk):
+            units = unit_ref[start : start + chunk, :]
+            exps = jnp.exp(scores_of(rows_all, units) * (1 / student_temp))
+            if k == 0:
+                own_ref[:, start : start + chunk] = exps
+            for at in range(0, chunk, LANES):
+                part = part + exps[:, at : at + LANES]
+            pull = pull + jnp.dot(split(exps[:first]), units, preferred_element_type=jnp.float32)
+    own = exps_ref.shape[1]
+    exps_ref[...] = own_ref[:, pl.ds(pl.multiple_of(place_ref[0] * own, own), own)]
+    pull_ref[...] = pull[:first] + pull[first:]
+    sums_ref[...] = as_tile(part)
+
+
+def last_kernel(chunk, sum_x, place_ref, mine_ref, other_ref, weights_ref, *refs):
+    *unit_refs, exp_pull_ref, exp_sums_ref, targets_ref, keep_ref, send_ref = refs[:-3]
+    row_ref, scale_ref, part_ref = refs[-3:]
+    all_rows = weights_ref.shape[0]
+    first = exp_pull_ref.shape[0]
+    protos = unit_refs[0].shape[0]
+    row_ref[...] = as_column(inverse_rows(mine_ref[...] + other_ref[...], all_rows))
+    column_scales(weights_ref, row_ref, scale_ref)
+    weighted_rows(weights_ref, scale_ref, part_ref)
+    sums = as_tile(part_ref[...])
+    pull = jnp.zeros((2 * first, exp_pull_ref.shape[1]), jnp.float32)
+    for k, unit_ref in enumerate(unit_refs):
+        for start in range(0, protos, chunk):
+            at = k * protos + start
+            scaled = weights_ref[:first, at : at + chunk] * scale_ref[:1, at : at + chunk]
+            pull = pull + jnp.dot(
+                split(scaled), unit_ref[start : start + chunk, :], preferred_element_type=jnp.float32
+            )
+    own = pl.ds(pl.multiple_of(place_ref[0] * chunk, chunk), chunk)
+    targets_ref[...] = weights_ref[:, own] * scale_ref[:1, own]
+    half = first // 2
+    upper = (place_ref[1] & X) > 0
+    for k, pull in enumerate((pull[:first] + pull[first:], exp_pull_ref[...])):
+        at = slice(k * half, (k + 1) * half)
+        keep_ref[at, :] = jnp.where(upper, pull[half:], pull[:half])
+        send_ref[at, :] = jnp.where(upper, pull[:half], pull[half:])
+    for ref in (keep_ref, send_ref):
+        ref[first:, :LANES] = exp_sums_ref[...]
+        ref[first:, LANES:] = sums
+    if not sum_x:
+        send_ref[first:, LANES:] = jnp.zeros_like(sums)
+
+
+def grads_kernel(
+    place_ref,
+    mine_ref,
+    other_ref,
+    targets_ref,
+    exps_ref,
+    rows_ref,
+    feat_ref,
+    proto_ref,
+    student_out_ref,
+    proto_out_ref,
+):
+    all_rows, own = targets_ref.shape
+    rows = feat_ref.shape[0]
+    total = mine_ref[...] + other_ref[...]
+    first = total.shape[0] - 8
+    target_scale = inverse_rows(total[first:, LANES:], all_rows) * (1 / student_temp)
+    exp_scale = (1 / student_temp) / unpack_lanes(total[first:, :LANES], all_rows)
+    exp_scale = as_column(jnp.where(target_scale > 0.0, exp_scale, 0.0))
+    target_scale = as_column(target_scale)
+
+    grad = exps_ref[...] * twice(exp_scale) - targets_ref[...] * twice(target_scale)
+    pushed = lax.dot_general(
+        grad.astype(jnp.bfloat16),
+        rows_ref[...],
+        (((0,), (0,)), ((), ())),
+        preferred_element_type=jnp.float32,
+    )
+    unit, scale = quick_unit(proto_ref[pl.ds(pl.multiple_of(place_ref[0] * own, own), own), :])
+    along = jnp.sum(unit * pushed, axis=1, keepdims=True)
+    proto_out_ref[0] = (pushed - unit * along) * scale
+
+    upper_x, upper_y = (place_ref[1] & X) > 0, (place_ref[1] & Y) > 0
+
+    def own_rows(values):
+        return jnp.where(upper_y, values[rows : 2 * rows], values[:rows])
+
+    def own_scale(column):
+        return own_rows(jnp.where(upper_x, column[2 * rows : 4 * rows], column[: 2 * rows]))
+
+    half = first // 2
+    pulled = own_rows(total[half:first]) * twice(own_scale(exp_scale))
+    pulled = pulled - own_rows(total[:half]) * twice(own_scale(target_scale))
+    unit, scale = quick_unit(feat_ref[...])
+    student_out_ref[...] = (
+        pulled - unit * jnp.sum(unit * pulled, axis=1, keepdims=True)
+    ) * scale
+
+
+def call(kernel, out_shape, operands, smem=0, scratch=(), work=0):
+    vmem = pl.BlockSpec(memory_space=pltpu.VMEM)
+    return pl.pallas_call(
+        kernel,
+        out_shape=out_shape,
+        in_specs=[pl.BlockSpec(memory_space=pltpu.SMEM)] * smem + [vmem] * (len(operands) - smem),
+        out_specs=jax.tree.map(lambda _: vmem, out_shape),
+        scratch_shapes=scratch,
+        compiler_params=pltpu.CompilerParams(vmem_limit_bytes=48 * 2**20),
+        cost_estimate=pl.CostEstimate(
+            flops=512 * work, bytes_accessed=4 * work, transcendentals=work
+        ),
+    )(*operands)
+
+
+def swap(values, axis, distance):
+    others = [(k, k ^ distance) for k in range(lax.axis_size(axis))]
+    return lax.ppermute(values, axis, others)
+
+
+def gather_rows(values):
+    held = jnp.stack([values, swap(values, "proto", X)])
+    held = jnp.stack([held] + [swap(held, "dp", t) for t in range(1, lax.axis_size("dp"))])
+    held = jnp.stack([held, swap(held, "proto", Y)])
+    return held, swap(held, "proto", CORE)
+
+
+def share_units(units):
+    return units, swap(units, "proto", CORE)
+
+
+def row_totals(values):
+    values = values + swap(values, "proto", X)
+    return values, swap(values, "proto", Y)
+
+
+def on_device_all_rows(student_feat, teacher_feat, prototypes, teacher_prototypes, live_count):
+    n_dp, n_proto = lax.axis_size("dp"), lax.axis_size("proto")
+    rows, width = student_feat.shape
+    protos = prototypes.shape[0]
+    own = protos // n_dp
+    all_rows = n_dp * n_proto * rows
+    first = 4 * rows
+    f32 = functools.partial(jax.ShapeDtypeStruct, dtype=jnp.float32)
+    bf16 = functools.partial(jax.ShapeDtypeStruct, dtype=jnp.bfloat16)
+    place = jnp.stack([lax.axis_index("dp"), lax.axis_index("proto")]).astype(jnp.int32)
+    place = jnp.concatenate([place, live_count])
+    tile = f32((8, LANES))
+    message = f32((first + 8, width))
+    row_scratch = pltpu.VMEM((all_rows, width), jnp.float32)
+    column = pltpu.VMEM((all_rows, LANES), jnp.float32)
+
+    near, far = gather_rows(jnp.concatenate([teacher_feat, student_feat], axis=0))
+    student_units, teacher_units = call(
+        units_kernel,
+        (bf16((protos, width)), bf16((protos, width))),
+        (prototypes, teacher_prototypes),
+        work=protos * width // 8,
+    )
+    teacher_units = share_units(teacher_units)
+    student_units = share_units(student_units)
+    held = len(teacher_units) * protos
+    scale_row = pltpu.VMEM((8, held), jnp.float32)
+
+    weights, sums = call(
+        functools.partial(weights_kernel, own),
+        (f32((all_rows, held)), tile),
+        (place, near, far, *teacher_units),
+        smem=1,
+        scratch=[row_scratch, scale_row, column],
+        work=held * all_rows,
+    )
+    near, far, sums = lax.optimization_barrier((near, far, sums))
+    parts = row_totals(sums)
+    student_rows, exps, exp_pull, exp_sums = call(
+        functools.partial(exps_kernel, own),
+        (bf16((all_rows, width)), f32((all_rows, own)), f32((first, width)), tile),
+        (place, near, far, *student_units),
+        smem=1,
+        scratch=[row_scratch, pltpu.VMEM((all_rows, protos), jnp.float32)],
+        work=len(student_units) * protos * all_rows,
+    )
+    for _ in range(ITERS - 2):
+        sums = call(
+            step_kernel,
+            tile,
+            (*parts, weights),
+            scratch=[column, scale_row, column],
+            work=held * all_rows // 2,
+        )
+        parts = row_totals(sums)
+    targets, keep, send = call(
+        functools.partial(last_kernel, own, True),
+        (f32((all_rows, own)), message, message),
+        (place, *parts, weights, *student_units, exp_pull, exp_sums),
+        smem=1,
+        scratch=[column, scale_row, column],
+        work=held * all_rows // 2,
+    )
+    total = keep + swap(send, "proto", X)
+    return call(
+        grads_kernel,
+        (f32((rows, width)), f32((1, own, width))),
+        (
+            place,
+            total,
+            swap(total, "proto", Y),
+            targets,
+            exps,
+            student_rows,
+            student_feat,
+            prototypes,
+        ),
+        smem=1,
+        work=own * all_rows,
+    )
+
+
 def sample_totals(values):
     return lax.psum(values, "proto")
 
@@ -25,7 +402,7 @@
     return lax.psum(values, "dp")
 
 
-def on_device(student_feat, teacher_feat, prototypes, teacher_prototypes, live_count):
+def on_device_group_rows(student_feat, teacher_feat, prototypes, teacher_prototypes, live_count):
     student_unit, student_length = unit_rows(student_feat)
     teacher_unit, teacher_length = unit_rows(teacher_feat)
     proto_unit, proto_length = unit_rows(prototypes)
@@ -59,10 +436,9 @@
         row_sums = sample_totals(jnp.sum(targets, axis=1))
         targets = targets / jnp.where(live_mask, row_sums, 1.0)[:, None]
     student_probs = jnp.exp(logits - jnp.log(partition)[:, None])
-    grad_logits = jnp.where(live_column, (student_probs - targets) / student_temp, 0.0).astype(
+    grad_block = jnp.where(live_column, (student_probs - targets) / student_temp, 0.0).astype(
         jnp.bfloat16
     )
-    grad_block = grad_logits
     pulled = lax.psum_scatter(
         jnp.dot(grad_block, proto_bf, preferred_element_type=jnp.float32),
         "proto",
@@ -74,7 +450,6 @@
     ) / student_length
     own_protos = prototypes.shape[0] // lax.axis_size("dp")
     contract_first = (((0,), (0,)), ((), ()))
-    grad_block = grad_logits
     pushed = lax.psum_scatter(
         lax.dot_general(
             grad_block, student_rows, contract_first, preferred_element_type=jnp.float32
@@ -90,6 +465,25 @@
         pushed - own_units * jnp.sum(own_units * pushed, axis=1, keepdims=True)
     ) / own_lengths
     return (student_grad, proto_grad[None])
+
+
+def on_device(student_feat, teacher_feat, prototypes, teacher_prototypes, live_count):
+    n_dp, n_proto = lax.axis_size("dp"), lax.axis_size("proto")
+    rows, width = student_feat.shape
+    protos = prototypes.shape[0]
+    lanes = n_dp * n_proto * rows
+    fits = (
+        n_proto == 2 * Y
+        and n_dp & (n_dp - 1) == 0
+        and rows % 4 == 0
+        and lanes % LANES == 0
+        and lanes <= 8 * LANES
+        and width == 2 * LANES
+        and protos == n_dp * 2 * LANES
+        and 4 * protos * lanes * 4 <= BLOCK_BYTES
+    )
+    plan = on_device_all_rows if fits else on_device_group_rows
+    return plan(student_feat, teacher_feat, prototypes, teacher_prototypes, live_count)
 
 
 def solution(mesh):

time: 137 us -> 52.1 us (0.38)
  blocking collectives: 101 us -> 0 us
  waiting for transfers between devices: 2.2 us -> 19.4 us
  starting transfers between devices: 3.26 us -> 19.2 us
  between operations: 14.9 us -> 0.71 us
  Pallas kernels: 0 us -> 8 us
  other arithmetic: 9.41 us -> 2.24 us
  matrix products: 2.56 us -> 0 us
    psum x6 -> x0, blocking collectives: 66.1 us -> none  [the longest x3 35.4 us: sample_totals(): return lax.psum(values, 'proto')]
    all_gather x2 -> x0, blocking collectives: 19.9 us -> none  [the longest x1 10.7 us: on_device(): lax.all_gather(student_unit.astype(jnp.bfloat16), 'proto', axis=0, tiled=...]
    ppermute x0 -> x14, waiting for transfers between devices: none -> 19.4 us  [swap(): return lax.ppermute(values, axis, others)]
    ppermute x0 -> x14, starting transfers between devices: none -> 19.2 us  [swap(): return lax.ppermute(values, axis, others)]
    unnamed x1 -> x0, blocking collectives: 14.6 us -> none
    pallas_call x0 -> x6, Pallas kernels: none -> 8 us  [call(): pl.pallas_call(kernel, out_shape=out_shape, in_specs=[pl.BlockSpec(memory...]
    reduce_sum x11 -> x0, other arithmetic: 4.61 us -> none  [the longest x4 2.4 us: unit_rows(): jnp.sum(widened * widened, axis=1, keepdims=True) + eps_norm]
    unnamed x2 -> x0, starting transfers between devices: 3.22 us -> none
  transfers between devices with their start and end apart: 3 -> 14, of which waited for: 1 -> 10; matrix products, arithmetic and copies ran while one was open for 12% -> 3% of each run, Pallas kernels for 0% -> 9%
where the time goes in v2:
time: 52.1 us; the launch traced here: 51.7 us
  waiting for transfers between devices  19.4 us (37%)
  starting transfers between devices  19.2 us (37%)
  Pallas kernels  8 us (15%)
  other arithmetic  2.24 us (4%)
  local copies, waits for them, and re-layouts  2.1 us (4%)
  between operations  0.71 us (1%)
    ppermute x14, waiting for transfers between devices, swap(): return lax.ppermute(values, axis, others)  19.4 us
    ppermute x14, starting transfers between devices, swap(): return lax.ppermute(values, axis, others)  19.2 us
    pallas_call x6, Pallas kernels, call(): pl.pallas_call(kernel, out_shape=out_shape, in_specs=[pl.BlockSpec(memory...  8 us
    unnamed x8, local copies, waits for them, and re-layouts  2.1 us
  transfers between devices with their start and end apart: 14, of which 10 were waited for; matrix products, arithmetic and copies ran while one was open for 3% of the time, Pallas kernels for 9%

profile of v2, /device:TPU:0, one launch (start us, length us, event | category | flops | bytes accessed | tf_op | source)
XLA Modules:
  0.0 51.7 jit_solution(8497809898395678004)
XLA Ops:
  1.4 3.0 %collective-permute-start = (bf16[24,256]{1,0:T(8,128)(2,1)S(1)}, bf16[24,256]{1,0:T(8,128)(2,1)S(1)}, u32[]{:S(2)}, u32[]{:S(2)}) collective-permute-start(bf16[24,256]{1,0:T(8,128)(2,1)S(1)} %pad_maximum_fusion.3), channel_id=1, source_target_pairs={{0,2},{1,3},{2,0},{3,1},{4,6},{5,7},{6,4},{7,5},{8,10},{9,11},{10,... | collective-permute-start | bytes 36872 | tf_op jit(solution)/shard_map/ppermute | solution.py:296
  5.1 1.0 %collective-permute-done = bf16[24,256]{1,0:T(8,128)(2,1)S(1)} collective-permute-done((bf16[24,256]{1,0:T(8,128)(2,1)S(1)}, bf16[24,256]{1,0:T(8,128)(2,1)S(1)}, u32[]{:S(2)}, u32[]{:S(2)}) %collective-permute-start) | collective-permute-done | bytes 12320 | tf_op jit(solution)/shard_map/ppermute | solution.py:296
  6.0 2.1 %collective-permute-start.1 = (bf16[2,24,256]{2,1,0:T(8,128)(2,1)S(1)}, bf16[2,24,256]{2,1,0:T(8,128)(2,1)S(1)}, u32[]{:S(2)}, u32[]{:S(2)}) collective-permute-start(bf16[2,24,256]{2,1,0:T(8,128)(2,1)S(1)} %get-tuple-element.33), channel_id=1, source_target_pairs={{0,8},{8,0},{16,24},{24,16},{1,9},{9,1},{17,25},{25,17},{2,10},{10... | collective-permute-start | bytes 73736 | tf_op jit(solution)/shard_map/ppermute | solution.py:296
  8.1 2.6 %collective-permute-start.2 = (bf16[2,24,256]{2,1,0:T(8,128)(2,1)S(1)}, bf16[2,24,256]{2,1,0:T(8,128)(2,1)S(1)}, u32[]{:S(2)}, u32[]{:S(2)}) collective-permute-start(bf16[2,24,256]{2,1,0:T(8,128)(2,1)S(1)} %get-tuple-element.33), channel_id=1, source_target_pairs={{0,16},{8,24},{16,0},{24,8},{1,17},{9,25},{17,1},{25,9},{2,18},{10... | collective-permute-start | bytes 73736 | tf_op jit(solution)/shard_map/ppermute | solution.py:296
  10.7 1.0 %copy-done = bf16[1024,256]{1,0:T(8,128)(2,1)S(1)} copy-done((bf16[1024,256]{1,0:T(8,128)(2,1)S(1)}, bf16[1024,256]{1,0:T(8,128)(2,1)}, u32[]{:S(2)}) %copy-start) | copy-done | bytes 524312
  11.8 1.0 %copy-done.2 = bf16[1024,256]{1,0:T(8,128)(2,1)S(1)} copy-done((bf16[1024,256]{1,0:T(8,128)(2,1)S(1)}, bf16[1024,256]{1,0:T(8,128)(2,1)}, u32[]{:S(2)}) %copy-start.2) | copy-done | bytes 524312
  13.8 2.6 %collective-permute-done.3 = bf16[2,24,256]{2,1,0:T(8,128)(2,1)S(1)} collective-permute-done((bf16[2,24,256]{2,1,0:T(8,128)(2,1)S(1)}, bf16[2,24,256]{2,1,0:T(8,128)(2,1)S(1)}, u32[]{:S(2)}, u32[]{:S(2)}) %collective-permute-start.3) | collective-permute-done | bytes 24608 | tf_op jit(solution)/shard_map/ppermute | solution.py:296
  16.4 1.6 %collective-permute-start.4 = (bf16[4,2,24,256]{3,2,1,0:T(8,128)(2,1)S(1)}, bf16[4,2,24,256]{3,2,1,0:T(8,128)(2,1)S(1)}, u32[]{:S(2)}, u32[]{:S(2)}) collective-permute-start(bf16[4,2,24,256]{3,2,1,0:T(8,128)(2,1)S(1)} %get-tuple-element.31), channel_id=1, source_target_pairs={{0,4},{1,5},{2,6},{3,7},{4,0},{5,1},{6,2},{7,3},{8,12},{9,13},{10,... | collective-permute-start | bytes 294920 | tf_op jit(solution)/shard_map/ppermute | solution.py:296
  18.0 3.1 %collective-permute-done.4 = bf16[4,2,24,256]{3,2,1,0:T(8,128)(2,1)S(1)} collective-permute-done((bf16[4,2,24,256]{3,2,1,0:T(8,128)(2,1)S(1)}, bf16[4,2,24,256]{3,2,1,0:T(8,128)(2,1)S(1)}, u32[]{:S(2)}, u32[]{:S(2)}) %collective-permute-start.4) | collective-permute-done | bytes 98336 | tf_op jit(solution)/shard_map/ppermute | solution.py:296
  22.6 1.8 %shard_map.69 = (f32[384,2048]{1,0:T(8,128)S(1)}, f32[8,128]{1,0:T(8,128)S(1)}) custom-call(s32[6]{0:T(128)S(1)} %pad_add_fusion.place_ref, bf16[2,4,2,24,256]{4,3,2,1,0:T(8,128)(2,1)S(1)} %pad_maximum_fusion.near_ref, bf16[2,4,2,24,256]{4,3,2,1,0:T(8,128)(2,1)S(1)} %collective-permute-done.5.far_ref, bf16[1024,256]{1,0:T(8,128)(2,1)S(1)} %get-tuple-element.16.refs_0_, ...), custom_call_target="tpu_custom_call" | custom-call | flops 402653184 | bytes 3145728 | tf_op jit(solution)/shard_map/pallas_call | solution.py:281
  24.4 1.6 %collective-permute-start.7 = (f32[8,128]{1,0:T(8,128)S(1)}, f32[8,128]{1,0:T(8,128)S(1)}, u32[]{:S(2)}, u32[]{:S(2)}) collective-permute-start(f32[8,128]{1,0:T(8,128)S(1)} %get-tuple-element.18), channel_id=1, source_target_pairs={{0,2},{1,3},{2,0},{3,1},{4,6},{5,7},{6,4},{7,5},{8,10},{9,11},{10,... | collective-permute-start | bytes 12296 | tf_op jit(solution)/shard_map/ppermute | solution.py:296
  25.9 2.1 %collective-permute-done.7 = f32[8,128]{1,0:T(8,128)S(1)} collective-permute-done((f32[8,128]{1,0:T(8,128)S(1)}, f32[8,128]{1,0:T(8,128)S(1)}, u32[]{:S(2)}, u32[]{:S(2)}) %collective-permute-start.7) | collective-permute-done | bytes 4128 | tf_op jit(solution)/shard_map/ppermute | solution.py:296
  28.1 1.5 %collective-permute-start.8 = (f32[8,128]{1,0:T(8,128)S(1)}, f32[8,128]{1,0:T(8,128)S(1)}, u32[]{:S(2)}, u32[]{:S(2)}) collective-permute-start(f32[8,128]{1,0:T(8,128)S(1)} %add.9.mine_ref), channel_id=1, source_target_pairs={{0,4},{1,5},{2,6},{3,7},{4,0},{5,1},{6,2},{7,3},{8,12},{9,13},{10,... | collective-permute-start | bytes 12296 | tf_op jit(solution)/shard_map/ppermute | solution.py:296
  29.6 2.1 %collective-permute-done.8.other_ref = f32[8,128]{1,0:T(8,128)S(1)} collective-permute-done((f32[8,128]{1,0:T(8,128)S(1)}, f32[8,128]{1,0:T(8,128)S(1)}, u32[]{:S(2)}, u32[]{:S(2)}) %collective-permute-start.8) | collective-permute-done | bytes 4128 | tf_op jit(solution)/shard_map/ppermute | solution.py:296
  32.5 1.6 %collective-permute-start.9 = (f32[8,128]{1,0:T(8,128)S(1)}, f32[8,128]{1,0:T(8,128)S(1)}, u32[]{:S(2)}, u32[]{:S(2)}) collective-permute-start(f32[8,128]{1,0:T(8,128)S(1)} %shard_map.70), channel_id=1, source_target_pairs={{0,2},{1,3},{2,0},{3,1},{4,6},{5,7},{6,4},{7,5},{8,10},{9,11},{10,... | collective-permute-start | bytes 12296 | tf_op jit(solution)/shard_map/ppermute | solution.py:296
  34.1 2.1 %collective-permute-done.9 = f32[8,128]{1,0:T(8,128)S(1)} collective-permute-done((f32[8,128]{1,0:T(8,128)S(1)}, f32[8,128]{1,0:T(8,128)S(1)}, u32[]{:S(2)}, u32[]{:S(2)}) %collective-permute-start.9) | collective-permute-done | bytes 4128 | tf_op jit(solution)/shard_map/ppermute | solution.py:296
  36.2 1.5 %collective-permute-start.10 = (f32[8,128]{1,0:T(8,128)S(1)}, f32[8,128]{1,0:T(8,128)S(1)}, u32[]{:S(2)}, u32[]{:S(2)}) collective-permute-start(f32[8,128]{1,0:T(8,128)S(1)} %add.10.mine_ref), channel_id=1, source_target_pairs={{0,4},{1,5},{2,6},{3,7},{4,0},{5,1},{6,2},{7,3},{8,12},{9,13},{10,... | collective-permute-start | bytes 12296 | tf_op jit(solution)/shard_map/ppermute | solution.py:296
  37.7 1.6 %shard_map.71 = (bf16[384,256]{1,0:T(8,128)(2,1)S(1)}, f32[384,256]{1,0:T(8,128)S(1)}, f32[48,256]{1,0:T(8,128)S(1)}, f32[8,128]{1,0:T(8,128)S(1)}) custom-call(s32[6]{0:T(128)S(1)} %pad_add_fusion.place_ref, bf16[2,4,2,24,256]{4,3,2,1,0:T(8,128)(2,1)S(1)} %pad_maximum_fusion.near_ref, bf16[2,4,2,24,256]{4,3,2,1,0:T(8,128)(2,1)S(1)} %collective-permute-done.5.far_ref, ...), custom_call_target="tpu_custom_call" | custom-call | flops 402653184 | bytes 3145728 | tf_op jit(solution)/shard_map/pallas_call | solution.py:281
  39.8 1.6 %shard_map.72 = (f32[384,256]{1,0:T(8,128)S(1)}, f32[56,256]{1,0:T(8,128)S(1)}, f32[56,256]{1,0:T(8,128)S(1)}) custom-call(s32[6]{0:T(128)S(1)} %pad_add_fusion.place_ref, f32[8,128]{1,0:T(8,128)S(1)} %add.10.mine_ref, f32[8,128]{1,0:T(8,128)S(1)} %collective-permute-done.10.other_ref, f32[384,2048]{1,0:T(8,128)S(1)} %get-tuple-element.19.weights_ref, ...), custom_call_target="tpu_custom_call" | custom-call | flops 201326592 | bytes 1572864 | tf_op jit(solution)/shard_map/pallas_call | solution.py:281
  41.4 1.6 %collective-permute-start.12 = (f32[56,256]{1,0:T(8,128)S(1)}, f32[56,256]{1,0:T(8,128)S(1)}, u32[]{:S(2)}, u32[]{:S(2)}) collective-permute-start(f32[56,256]{1,0:T(8,128)S(1)} %get-tuple-element.26), channel_id=1, source_target_pairs={{0,2},{1,3},{2,0},{3,1},{4,6},{5,7},{6,4},{7,5},{8,10},{9,11},{10,... | collective-permute-start | bytes 172040 | tf_op jit(solution)/shard_map/ppermute | solution.py:296
  43.0 2.7 %collective-permute-done.12 = f32[56,256]{1,0:T(8,128)S(1)} collective-permute-done((f32[56,256]{1,0:T(8,128)S(1)}, f32[56,256]{1,0:T(8,128)S(1)}, u32[]{:S(2)}, u32[]{:S(2)}) %collective-permute-start.12) | collective-permute-done | bytes 57376 | tf_op jit(solution)/shard_map/ppermute | solution.py:296
  45.7 1.6 %collective-permute-start.13 = (f32[56,256]{1,0:T(8,128)S(1)}, f32[56,256]{1,0:T(8,128)S(1)}, u32[]{:S(2)}, u32[]{:S(2)}) collective-permute-start(f32[56,256]{1,0:T(8,128)S(1)} %add.11.mine_ref), channel_id=1, source_target_pairs={{0,4},{1,5},{2,6},{3,7},{4,0},{5,1},{6,2},{7,3},{8,12},{9,13},{10,... | collective-permute-start | bytes 172040 | tf_op jit(solution)/shard_map/ppermute | solution.py:296
  47.2 2.7 %collective-permute-done.13.other_ref = f32[56,256]{1,0:T(8,128)S(1)} collective-permute-done((f32[56,256]{1,0:T(8,128)S(1)}, f32[56,256]{1,0:T(8,128)S(1)}, u32[]{:S(2)}, u32[]{:S(2)}) %collective-permute-start.13) | collective-permute-done | bytes 57376 | tf_op jit(solution)/shard_map/ppermute | solution.py:296
  49.9 1.8 %shard_map.73 = (f32[12,256]{1,0:T(8,128)}, f32[1,256,256]{2,1,0:T(8,128)}) custom-call(s32[6]{0:T(128)S(1)} %pad_add_fusion.place_ref, f32[56,256]{1,0:T(8,128)S(1)} %add.11.mine_ref, f32[56,256]{1,0:T(8,128)S(1)} %collective-permute-done.13.other_ref, f32[384,256]{1,0:T(8,128)S(1)} %get-tuple-element.27.targets_ref, ...), custom_call_target="tpu_custom_call" | custom-call | flops 50331648 | bytes 393216 | tf_op jit(solution)/shard_map/pallas_call | solution.py:281
  (27 shorter events, 5.3 us)
Async XLA Ops:
  1.4 4.7 %collective-permute-start = (bf16[24,256]{1,0:T(8,128)(2,1)S(1)}, bf16[24,256]{1,0:T(8,128)(2,1)S(1)}, u32[]{:S(2)}, u32[]{:S(2)}) collective-permute-start(bf16[24,256]{1,0:T(8,128)(2,1)S(1)} %pad_maximum_fusion.3), channel_id=1, source_target_pairs={{0,2},{1,3},{2,0},{3,1},{4,6},{5,7},{6,4},{7,5},{8,10},{9,11},{10,... | collective-permute-start | bytes 36872 | tf_op jit(solution)/shard_map/ppermute | solution.py:296
  6.0 7.7 %collective-permute-start.1 = (bf16[2,24,256]{2,1,0:T(8,128)(2,1)S(1)}, bf16[2,24,256]{2,1,0:T(8,128)(2,1)S(1)}, u32[]{:S(2)}, u32[]{:S(2)}) collective-permute-start(bf16[2,24,256]{2,1,0:T(8,128)(2,1)S(1)} %get-tuple-element.33), channel_id=1, source_target_pairs={{0,8},{8,0},{16,24},{24,16},{1,9},{9,1},{17,25},{25,17},{2,10},{10... | collective-permute-start | bytes 73736 | tf_op jit(solution)/shard_map/ppermute | solution.py:296
  8.1 5.6 %collective-permute-start.2 = (bf16[2,24,256]{2,1,0:T(8,128)(2,1)S(1)}, bf16[2,24,256]{2,1,0:T(8,128)(2,1)S(1)}, u32[]{:S(2)}, u32[]{:S(2)}) collective-permute-start(bf16[2,24,256]{2,1,0:T(8,128)(2,1)S(1)} %get-tuple-element.33), channel_id=1, source_target_pairs={{0,16},{8,24},{16,0},{24,8},{1,17},{9,25},{17,1},{25,9},{2,18},{10... | collective-permute-start | bytes 73736 | tf_op jit(solution)/shard_map/ppermute | solution.py:296
  10.7 5.6 %collective-permute-start.3 = (bf16[2,24,256]{2,1,0:T(8,128)(2,1)S(1)}, bf16[2,24,256]{2,1,0:T(8,128)(2,1)S(1)}, u32[]{:S(2)}, u32[]{:S(2)}) collective-permute-start(bf16[2,24,256]{2,1,0:T(8,128)(2,1)S(1)} %get-tuple-element.33), channel_id=1, source_target_pairs={{0,24},{8,16},{16,8},{24,0},{1,25},{9,17},{17,9},{25,1},{2,26},{10... | collective-permute-start | bytes 73736 | tf_op jit(solution)/shard_map/ppermute | solution.py:296
  10.7 1.0 %copy-start = (bf16[1024,256]{1,0:T(8,128)(2,1)S(1)}, bf16[1024,256]{1,0:T(8,128)(2,1)}, u32[]{:S(2)}) copy-start(bf16[1024,256]{1,0:T(8,128)(2,1)} %proto_ref.1) | copy-start | bytes 1572868
  11.8 1.0 %copy-start.2 = (bf16[1024,256]{1,0:T(8,128)(2,1)S(1)}, bf16[1024,256]{1,0:T(8,128)(2,1)}, u32[]{:S(2)}) copy-start(bf16[1024,256]{1,0:T(8,128)(2,1)} %teacher_ref.1) | copy-start | bytes 1572868
  13.2 9.4 %collective-permute-start.6 = (bf16[1024,256]{1,0:T(8,128)(2,1)S(1)}, bf16[1024,256]{1,0:T(8,128)(2,1)S(1)}, u32[]{:S(2)}, u32[]{:S(2)}) collective-permute-start(bf16[1024,256]{1,0:T(8,128)(2,1)S(1)} %get-tuple-element.16.refs_0_), channel_id=1, source_target_pairs={{0,1},{1,0},{2,3},{3,2},{4,5},{5,4},{6,7},{7,6},{8,9},{9,8},{10,11... | collective-permute-start | bytes 1572872 | tf_op jit(solution)/shard_map/ppermute | solution.py:296
  13.3 24.5 %collective-permute-start.11 = (bf16[1024,256]{1,0:T(8,128)(2,1)S(1)}, bf16[1024,256]{1,0:T(8,128)(2,1)S(1)}, u32[]{:S(2)}, u32[]{:S(2)}) collective-permute-start(bf16[1024,256]{1,0:T(8,128)(2,1)S(1)} %get-tuple-element.20.refs_0_), channel_id=1, source_target_pairs={{0,1},{1,0},{2,3},{3,2},{4,5},{5,4},{6,7},{7,6},{8,9},{9,8},{10,11... | collective-permute-start | bytes 1572872 | tf_op jit(solution)/shard_map/ppermute | solution.py:296
  16.4 4.7 %collective-permute-start.4 = (bf16[4,2,24,256]{3,2,1,0:T(8,128)(2,1)S(1)}, bf16[4,2,24,256]{3,2,1,0:T(8,128)(2,1)S(1)}, u32[]{:S(2)}, u32[]{:S(2)}) collective-permute-start(bf16[4,2,24,256]{3,2,1,0:T(8,128)(2,1)S(1)} %get-tuple-element.31), channel_id=1, source_target_pairs={{0,4},{1,5},{2,6},{3,7},{4,0},{5,1},{6,2},{7,3},{8,12},{9,13},{10,... | collective-permute-start | bytes 294920 | tf_op jit(solution)/shard_map/ppermute | solution.py:296
  21.1 1.5 %collective-permute-start.5 = (bf16[2,4,2,24,256]{4,3,2,1,0:T(8,128)(2,1)S(1)}, bf16[2,4,2,24,256]{4,3,2,1,0:T(8,128)(2,1)S(1)}, u32[]{:S(2)}, u32[]{:S(2)}) collective-permute-start(bf16[2,4,2,24,256]{4,3,2,1,0:T(8,128)(2,1)S(1)} %pad_maximum_fusion.near_ref), channel_id=1, source_target_pairs={{0,1},{1,0},{2,3},{3,2},{4,5},{5,4},{6,7},{7,6},{8,9},{9,8},{10,11... | collective-permute-start | bytes 589832 | tf_op jit(solution)/shard_map/ppermute | solution.py:296
  24.4 3.7 %collective-permute-start.7 = (f32[8,128]{1,0:T(8,128)S(1)}, f32[8,128]{1,0:T(8,128)S(1)}, u32[]{:S(2)}, u32[]{:S(2)}) collective-permute-start(f32[8,128]{1,0:T(8,128)S(1)} %get-tuple-element.18), channel_id=1, source_target_pairs={{0,2},{1,3},{2,0},{3,1},{4,6},{5,7},{6,4},{7,5},{8,10},{9,11},{10,... | collective-permute-start | bytes 12296 | tf_op jit(solution)/shard_map/ppermute | solution.py:296
  28.1 3.6 %collective-permute-start.8 = (f32[8,128]{1,0:T(8,128)S(1)}, f32[8,128]{1,0:T(8,128)S(1)}, u32[]{:S(2)}, u32[]{:S(2)}) collective-permute-start(f32[8,128]{1,0:T(8,128)S(1)} %add.9.mine_ref), channel_id=1, source_target_pairs={{0,4},{1,5},{2,6},{3,7},{4,0},{5,1},{6,2},{7,3},{8,12},{9,13},{10,... | collective-permute-start | bytes 12296 | tf_op jit(solution)/shard_map/ppermute | solution.py:296
  32.5 17.4 %copy-start.1 = (bf16[1024,256]{1,0:T(8,128)(2,1)S(1)}, bf16[1024,256]{1,0:T(8,128)(2,1)}, u32[]{:S(2)}) copy-start(bf16[1024,256]{1,0:T(8,128)(2,1)} %proto_ref.1) | copy-start | bytes 1572868
  32.5 17.4 %copy-start.3 = (bf16[12,256]{1,0:T(8,128)(2,1)S(1)}, bf16[12,256]{1,0:T(8,128)(2,1)}, u32[]{:S(2)}) copy-start(bf16[12,256]{1,0:T(8,128)(2,1)} %feat_ref.1) | copy-start | bytes 18436
  32.5 3.7 %collective-permute-start.9 = (f32[8,128]{1,0:T(8,128)S(1)}, f32[8,128]{1,0:T(8,128)S(1)}, u32[]{:S(2)}, u32[]{:S(2)}) collective-permute-start(f32[8,128]{1,0:T(8,128)S(1)} %shard_map.70), channel_id=1, source_target_pairs={{0,2},{1,3},{2,0},{3,1},{4,6},{5,7},{6,4},{7,5},{8,10},{9,11},{10,... | collective-permute-start | bytes 12296 | tf_op jit(solution)/shard_map/ppermute | solution.py:296
  36.2 3.6 %collective-permute-start.10 = (f32[8,128]{1,0:T(8,128)S(1)}, f32[8,128]{1,0:T(8,128)S(1)}, u32[]{:S(2)}, u32[]{:S(2)}) collective-permute-start(f32[8,128]{1,0:T(8,128)S(1)} %add.10.mine_ref), channel_id=1, source_target_pairs={{0,4},{1,5},{2,6},{3,7},{4,0},{5,1},{6,2},{7,3},{8,12},{9,13},{10,... | collective-permute-start | bytes 12296 | tf_op jit(solution)/shard_map/ppermute | solution.py:296
  41.4 4.2 %collective-permute-start.12 = (f32[56,256]{1,0:T(8,128)S(1)}, f32[56,256]{1,0:T(8,128)S(1)}, u32[]{:S(2)}, u32[]{:S(2)}) collective-permute-start(f32[56,256]{1,0:T(8,128)S(1)} %get-tuple-element.26), channel_id=1, source_target_pairs={{0,2},{1,3},{2,0},{3,1},{4,6},{5,7},{6,4},{7,5},{8,10},{9,11},{10,... | collective-permute-start | bytes 172040 | tf_op jit(solution)/shard_map/ppermute | solution.py:296
  45.7 4.2 %collective-permute-start.13 = (f32[56,256]{1,0:T(8,128)S(1)}, f32[56,256]{1,0:T(8,128)S(1)}, u32[]{:S(2)}, u32[]{:S(2)}) collective-permute-start(f32[56,256]{1,0:T(8,128)S(1)} %add.11.mine_ref), channel_id=1, source_target_pairs={{0,4},{1,5},{2,6},{3,7},{4,0},{5,1},{6,2},{7,3},{8,12},{9,13},{10,... | collective-permute-start | bytes 172040 | tf_op jit(solution)/shard_map/ppermute | solution.py:296

commit v3 on v2

--- a/solution.py
+++ b/solution.py
@@ -24,6 +24,11 @@
 
 
 CORE, X, Y = 1, 2, 4
+X_CROSS, Y_CROSS = X | CORE, Y | CORE
+
+
+def block_of(proto):
+    return (proto & CORE) * 4 + (proto & X) + ((proto >> 2) & 1)
 
 
 def quick_unit(values):
@@ -42,7 +47,7 @@
         for c in range(2):
             for x in range(2):
                 for y in range(2):
-                    proto = ((place_ref[1] ^ c) & CORE) + X * x + Y * y
+                    proto = CORE * c + X * x + Y * y
                     end = start + jnp.clip(count - proto * rows, 0, rows)
                     live = jnp.where((lane >= start) & (lane < end), 1.0, live)
                     start += rows
@@ -72,23 +77,32 @@
     return jnp.where(live, 1.0 / jnp.where(live, total, 1.0), 0.0)
 
 
-def units_kernel(student_ref, teacher_ref, student_out_ref, teacher_out_ref):
-    for ref, out_ref in ((teacher_ref, teacher_out_ref), (student_ref, student_out_ref)):
-        unit, _ = quick_unit(ref[...])
+def units_kernel(place_ref, student_ref, teacher_ref, student_out_ref, teacher_out_ref, *scratch):
+    del place_ref
+    *held, sems = scratch
+    copies = []
+    for k, ref in enumerate((teacher_ref, student_ref)):
+        copies.append(pltpu.make_async_copy(ref, held[k], sems.at[k]))
+        copies[k].start()
+    for k, out_ref in enumerate((teacher_out_ref, student_out_ref)):
+        copies[k].wait()
+        unit, _ = quick_unit(held[k][...])
         out_ref[...] = unit.astype(jnp.bfloat16)
 
 
 def place_rows(place_ref, near_ref, far_ref, which, rows, scratch):
-    mine_x = (place_ref[1] >> 1) & 1
-    mine_y = (place_ref[1] >> 2) & 1
-    start = 0
+    mine_core, mine_x, mine_y = (place_ref[1] & 1, (place_ref[1] >> 1) & 1, (place_ref[1] >> 2) & 1)
+    cut = slice(which * rows, (which + 1) * rows)
     for t in range(near_ref.shape[1]):
-        for ref in (near_ref, far_ref):
-            for x in range(2):
-                for y in range(2):
-                    block = ref[mine_y ^ y, t, mine_x ^ x].astype(jnp.float32)
-                    scratch[start : start + rows, :] = block[which * rows : (which + 1) * rows]
-                    start += rows
+        for x in range(2):
+            for y in range(2):
+                rel_x, rel_y = mine_x ^ x, mine_y ^ y
+                near = near_ref[rel_y, t, rel_x].astype(jnp.float32)[cut]
+                far = far_ref[rel_y, t, rel_x].astype(jnp.float32)[cut]
+                near_core = mine_core ^ rel_x ^ rel_y ^ (1 if t else 0)
+                for c in range(2):
+                    start = (t * 8 + block_of(CORE * c + X * x + Y * y)) * rows
+                    scratch[start : start + rows, :] = jnp.where(near_core == c, near, far)
     unit, _ = quick_unit(scratch[...])
     return unit.astype(jnp.bfloat16)
 
@@ -194,9 +208,9 @@
     sums_ref[...] = as_tile(part)
 
 
-def last_kernel(chunk, sum_x, place_ref, mine_ref, other_ref, weights_ref, *refs):
-    *unit_refs, exp_pull_ref, exp_sums_ref, targets_ref, keep_ref, send_ref = refs[:-3]
-    row_ref, scale_ref, part_ref = refs[-3:]
+def last_kernel(chunk, rows, place_ref, mine_ref, other_ref, weights_ref, *refs):
+    *unit_refs, exp_pull_ref, exp_sums_ref, targets_ref, keep_ref, send_ref = refs[:-4]
+    row_ref, scale_ref, part_ref, blocks_ref = refs[-4:]
     all_rows = weights_ref.shape[0]
     first = exp_pull_ref.shape[0]
     protos = unit_refs[0].shape[0]
@@ -214,17 +228,18 @@
             )
     own = pl.ds(pl.multiple_of(place_ref[0] * chunk, chunk), chunk)
     targets_ref[...] = weights_ref[:, own] * scale_ref[:1, own]
-    half = first // 2
-    upper = (place_ref[1] & X) > 0
-    for k, pull in enumerate((pull[:first] + pull[first:], exp_pull_ref[...])):
-        at = slice(k * half, (k + 1) * half)
-        keep_ref[at, :] = jnp.where(upper, pull[half:], pull[:half])
-        send_ref[at, :] = jnp.where(upper, pull[:half], pull[half:])
-    for ref in (keep_ref, send_ref):
-        ref[first:, :LANES] = exp_sums_ref[...]
-        ref[first:, LANES:] = sums
-    if not sum_x:
-        send_ref[first:, LANES:] = jnp.zeros_like(sums)
+    pulls = (pull[:first] + pull[first:], exp_pull_ref[...])
+    for k, pull in enumerate(pulls):
+        for block in range(first // rows):
+            blocks_ref[k, block, :rows, :] = pull[block * rows : (block + 1) * rows]
+    mine = place_ref[1]
+    for ref, proto in ((keep_ref, mine), (send_ref, mine ^ X_CROSS)):
+        for j, owner in enumerate((proto, proto ^ Y_CROSS)):
+            for k in range(2):
+                start = (2 * j + k) * rows
+                ref[start : start + rows, :] = blocks_ref[k, block_of(owner), :rows, :]
+        ref[4 * rows :, :LANES] = exp_sums_ref[...]
+        ref[4 * rows :, LANES:] = sums
 
 
 def grads_kernel(
@@ -241,10 +256,9 @@
 ):
     all_rows, own = targets_ref.shape
     rows = feat_ref.shape[0]
-    total = mine_ref[...] + other_ref[...]
-    first = total.shape[0] - 8
-    target_scale = inverse_rows(total[first:, LANES:], all_rows) * (1 / student_temp)
-    exp_scale = (1 / student_temp) / unpack_lanes(total[first:, :LANES], all_rows)
+    sums = mine_ref[4 * rows :, :] + other_ref[2 * rows :, :]
+    target_scale = inverse_rows(sums[:, LANES:], all_rows) * (1 / student_temp)
+    exp_scale = (1 / student_temp) / unpack_lanes(sums[:, :LANES], all_rows)
     exp_scale = as_column(jnp.where(target_scale > 0.0, exp_scale, 0.0))
     target_scale = as_column(target_scale)
 
@@ -259,29 +273,31 @@
     along = jnp.sum(unit * pushed, axis=1, keepdims=True)
     proto_out_ref[0] = (pushed - unit * along) * scale
 
-    upper_x, upper_y = (place_ref[1] & X) > 0, (place_ref[1] & Y) > 0
-
-    def own_rows(values):
-        return jnp.where(upper_y, values[rows : 2 * rows], values[:rows])
-
     def own_scale(column):
-        return own_rows(jnp.where(upper_x, column[2 * rows : 4 * rows], column[: 2 * rows]))
-
-    half = first // 2
-    pulled = own_rows(total[half:first]) * twice(own_scale(exp_scale))
-    pulled = pulled - own_rows(total[:half]) * twice(own_scale(target_scale))
+        block = block_of(place_ref[1])
+        scale = column[:rows]
+        for k in range(1, 8):
+            scale = jnp.where(block == k, column[k * rows : (k + 1) * rows], scale)
+        return twice(scale)
+
+    target_pull, exp_pull = [
+        mine_ref[k * rows : (k + 1) * rows, :] + other_ref[k * rows : (k + 1) * rows, :]
+        for k in range(2)
+    ]
+    pulled = exp_pull * own_scale(exp_scale) - target_pull * own_scale(target_scale)
     unit, scale = quick_unit(feat_ref[...])
     student_out_ref[...] = (
         pulled - unit * jnp.sum(unit * pulled, axis=1, keepdims=True)
     ) * scale
 
 
-def call(kernel, out_shape, operands, smem=0, scratch=(), work=0):
+def call(kernel, out_shape, operands, smem=0, scratch=(), work=0, space=pltpu.VMEM):
     vmem = pl.BlockSpec(memory_space=pltpu.VMEM)
+    rest = pl.BlockSpec(memory_space=space)
     return pl.pallas_call(
         kernel,
         out_shape=out_shape,
-        in_specs=[pl.BlockSpec(memory_space=pltpu.SMEM)] * smem + [vmem] * (len(operands) - smem),
+        in_specs=[pl.BlockSpec(memory_space=pltpu.SMEM)] * smem + [rest] * (len(operands) - smem),
         out_specs=jax.tree.map(lambda _: vmem, out_shape),
         scratch_shapes=scratch,
         compiler_params=pltpu.CompilerParams(vmem_limit_bytes=48 * 2**20),
@@ -296,20 +312,27 @@
     return lax.ppermute(values, axis, others)
 
 
-def gather_rows(values):
-    held = jnp.stack([values, swap(values, "proto", X)])
-    held = jnp.stack([held] + [swap(held, "dp", t) for t in range(1, lax.axis_size("dp"))])
-    held = jnp.stack([held, swap(held, "proto", Y)])
-    return held, swap(held, "proto", CORE)
-
-
-def share_units(units):
-    return units, swap(units, "proto", CORE)
+def swap_dp(values, t):
+    n_dp, n_proto = lax.axis_size("dp"), lax.axis_size("proto")
+    others = [
+        (d * n_proto + p, (d ^ t) * n_proto + (p ^ CORE)) for d in range(n_dp) for p in range(n_proto)
+    ]
+    return lax.ppermute(values, ("dp", "proto"), others)
+
+
+def gather_rows(values, units):
+    held = jnp.stack([values, swap(values, "proto", X_CROSS)])
+    held, *operands = lax.optimization_barrier((held, *units[1]))
+    units = units[0](*operands)
+    held = jnp.stack([held] + [swap_dp(held, t) for t in range(1, lax.axis_size("dp"))])
+    held = jnp.stack([held, swap(held, "proto", Y_CROSS)])
+    held, *units = lax.optimization_barrier((held, *units))
+    return held, swap(held, "proto", CORE), *((unit, swap(unit, "proto", CORE)) for unit in units)
 
 
 def row_totals(values):
-    values = values + swap(values, "proto", X)
-    return values, swap(values, "proto", Y)
+    values = values + swap(values, "proto", X_CROSS)
+    return values, swap(values, "proto", Y_CROSS)
 
 
 def on_device_all_rows(student_feat, teacher_feat, prototypes, teacher_prototypes, live_count):
@@ -318,25 +341,29 @@
     protos = prototypes.shape[0]
     own = protos // n_dp
     all_rows = n_dp * n_proto * rows
-    first = 4 * rows
+    first = n_proto * rows
     f32 = functools.partial(jax.ShapeDtypeStruct, dtype=jnp.float32)
     bf16 = functools.partial(jax.ShapeDtypeStruct, dtype=jnp.bfloat16)
     place = jnp.stack([lax.axis_index("dp"), lax.axis_index("proto")]).astype(jnp.int32)
     place = jnp.concatenate([place, live_count])
     tile = f32((8, LANES))
-    message = f32((first + 8, width))
+    message = f32((4 * rows + 8, width))
     row_scratch = pltpu.VMEM((all_rows, width), jnp.float32)
     column = pltpu.VMEM((all_rows, LANES), jnp.float32)
 
-    near, far = gather_rows(jnp.concatenate([teacher_feat, student_feat], axis=0))
-    student_units, teacher_units = call(
+    units = functools.partial(
+        call,
         units_kernel,
         (bf16((protos, width)), bf16((protos, width))),
-        (prototypes, teacher_prototypes),
+        smem=1,
+        scratch=[pltpu.VMEM((protos, width), jnp.bfloat16)] * 2 + [pltpu.SemaphoreType.DMA((2,))],
         work=protos * width // 8,
-    )
-    teacher_units = share_units(teacher_units)
-    student_units = share_units(student_units)
+        space=pltpu.HBM,
+    )
+    near, far, student_units, teacher_units = gather_rows(
+        jnp.concatenate([teacher_feat, student_feat], axis=0),
+        (lambda *operands: units(operands), (place, prototypes, teacher_prototypes)),
+    )
     held = len(teacher_units) * protos
     scale_row = pltpu.VMEM((8, held), jnp.float32)
 
@@ -368,21 +395,21 @@
         )
         parts = row_totals(sums)
     targets, keep, send = call(
-        functools.partial(last_kernel, own, True),
+        functools.partial(last_kernel, own, rows),
         (f32((all_rows, own)), message, message),
         (place, *parts, weights, *student_units, exp_pull, exp_sums),
         smem=1,
-        scratch=[column, scale_row, column],
+        scratch=[column, scale_row, column, pltpu.VMEM((2, n_proto, 16, width), jnp.float32)],
         work=held * all_rows // 2,
     )
-    total = keep + swap(send, "proto", X)
+    total = keep + swap(send, "proto", X_CROSS)
     return call(
         grads_kernel,
         (f32((rows, width)), f32((1, own, width))),
         (
             place,
             total,
-            swap(total, "proto", Y),
+            swap(total[2 * rows :], "proto", Y_CROSS),
             targets,
             exps,
             student_rows,
@@ -476,6 +503,7 @@
         n_proto == 2 * Y
         and n_dp & (n_dp - 1) == 0
         and rows % 4 == 0
+        and rows <= 16
         and lanes % LANES == 0
         and lanes <= 8 * LANES
         and width == 2 * LANES

time: 52.1 us -> 49.1 us (0.942)
  starting transfers between devices: 19.2 us -> 17.2 us
  waiting for transfers between devices: 19.4 us -> 17.7 us
  Pallas kernels: 8 us -> 8.79 us
    ppermute x14 -> x11, starting transfers between devices: 19.2 us -> 12.4 us  [swap(): return lax.ppermute(values, axis, others)]
    ppermute x14 -> x11, waiting for transfers between devices: 19.4 us -> 12.6 us  [swap(): return lax.ppermute(values, axis, others)]
    ppermute x0 -> x3, waiting for transfers between devices: none -> 5.05 us  [swap_dp(): return lax.ppermute(values, ('dp', 'proto'), others)]
    ppermute x0 -> x3, starting transfers between devices: none -> 4.74 us  [swap_dp(): return lax.ppermute(values, ('dp', 'proto'), others)]
    pallas_call x6, Pallas kernels: 8 us -> 8.79 us  [call(): pl.pallas_call(kernel, out_shape=out_shape, in_specs=[pl.BlockSpec(memory...]
  transfers between devices with their start and end apart: 14 -> 14, of which waited for: 10 -> 10; matrix products, arithmetic and copies ran while one was open for 3% -> 3% of each run, Pallas kernels for 9% -> 11%
where the time goes in v3:
time: 49.1 us; the launch traced here: 48.7 us
  waiting for transfers between devices  17.7 us (36%)
  starting transfers between devices  17.2 us (35%)
  Pallas kernels  8.79 us (18%)
  other arithmetic  2.23 us (5%)
  local copies, waits for them, and re-layouts  2.1 us (4%)
  between operations  0.71 us (1%)
    ppermute x11, waiting for transfers between devices, swap(): return lax.ppermute(values, axis, others)  12.6 us
    ppermute x11, starting transfers between devices, swap(): return lax.ppermute(values, axis, others)  12.4 us
    pallas_call x6, Pallas kernels, call(): pl.pallas_call(kernel, out_shape=out_shape, in_specs=[pl.BlockSpec(memory...  8.79 us
    ppermute x3, waiting for transfers between devices, swap_dp(): return lax.ppermute(values, ('dp', 'proto'), others)  5.05 us
    ppermute x3, starting transfers between devices, swap_dp(): return lax.ppermute(values, ('dp', 'proto'), others)  4.74 us
    unnamed x8, local copies, waits for them, and re-layouts  2.09 us
  transfers between devices with their start and end apart: 14, of which 10 were waited for; matrix products, arithmetic and copies ran while one was open for 3% of the time, Pallas kernels for 11%

profile of v3, /device:TPU:0, one launch (start us, length us, event | category | flops | bytes accessed | tf_op | source)
XLA Modules:
  0.0 48.7 jit_solution(13467685989217562987)
XLA Ops:
  1.4 2.4 %collective-permute-start = (bf16[24,256]{1,0:T(8,128)(2,1)S(1)}, bf16[24,256]{1,0:T(8,128)(2,1)S(1)}, u32[]{:S(2)}, u32[]{:S(2)}) collective-permute-start(bf16[24,256]{1,0:T(8,128)(2,1)S(1)} %pad_maximum_fusion.3), channel_id=1, source_target_pairs={{0,3},{1,2},{2,1},{3,0},{4,7},{5,6},{6,5},{7,4},{8,11},{9,10},{10,... | collective-permute-start | bytes 36872 | tf_op jit(solution)/shard_map/ppermute | solution.py:312
  5.2 2.1 %collective-permute-start.1 = (bf16[2,24,256]{2,1,0:T(8,128)(2,1)S(1)}, bf16[2,24,256]{2,1,0:T(8,128)(2,1)S(1)}, u32[]{:S(2)}, u32[]{:S(2)}) collective-permute-start(bf16[2,24,256]{2,1,0:T(8,128)(2,1)S(1)} %pad_maximum_fusion.2), channel_id=1, source_target_pairs={{0,9},{1,8},{2,11},{3,10},{4,13},{5,12},{6,15},{7,14},{8,1},{9,0},... | collective-permute-start | bytes 73736 | tf_op jit(solution)/shard_map/ppermute | solution.py:320
  7.4 2.6 %collective-permute-start.2 = (bf16[2,24,256]{2,1,0:T(8,128)(2,1)S(1)}, bf16[2,24,256]{2,1,0:T(8,128)(2,1)S(1)}, u32[]{:S(2)}, u32[]{:S(2)}) collective-permute-start(bf16[2,24,256]{2,1,0:T(8,128)(2,1)S(1)} %pad_maximum_fusion.2), channel_id=1, source_target_pairs={{0,17},{1,16},{2,19},{3,18},{4,21},{5,20},{6,23},{7,22},{8,25},{9,... | collective-permute-start | bytes 73736 | tf_op jit(solution)/shard_map/ppermute | solution.py:320
  10.0 1.7 %collective-permute-done.2 = bf16[2,24,256]{2,1,0:T(8,128)(2,1)S(1)} collective-permute-done((bf16[2,24,256]{2,1,0:T(8,128)(2,1)S(1)}, bf16[2,24,256]{2,1,0:T(8,128)(2,1)S(1)}, u32[]{:S(2)}, u32[]{:S(2)}) %collective-permute-start.2) | collective-permute-done | bytes 24608 | tf_op jit(solution)/shard_map/ppermute | solution.py:320
  11.7 3.3 %collective-permute-done.3 = bf16[2,24,256]{2,1,0:T(8,128)(2,1)S(1)} collective-permute-done((bf16[2,24,256]{2,1,0:T(8,128)(2,1)S(1)}, bf16[2,24,256]{2,1,0:T(8,128)(2,1)S(1)}, u32[]{:S(2)}, u32[]{:S(2)}) %collective-permute-start.3) | collective-permute-done | bytes 24608 | tf_op jit(solution)/shard_map/ppermute | solution.py:320
  15.1 1.3 %collective-permute-start.4 = (bf16[4,2,24,256]{3,2,1,0:T(8,128)(2,1)S(1)}, bf16[4,2,24,256]{3,2,1,0:T(8,128)(2,1)S(1)}, u32[]{:S(2)}, u32[]{:S(2)}) collective-permute-start(bf16[4,2,24,256]{3,2,1,0:T(8,128)(2,1)S(1)} %get-tuple-element.45), channel_id=1, source_target_pairs={{0,5},{1,4},{2,7},{3,6},{4,1},{5,0},{6,3},{7,2},{8,13},{9,12},{10,... | collective-permute-start | bytes 294920 | tf_op jit(solution)/shard_map/ppermute | solution.py:312
  16.4 1.0 %copy-done = bf16[1024,256]{1,0:T(8,128)(2,1)S(1)} copy-done((bf16[1024,256]{1,0:T(8,128)(2,1)S(1)}, bf16[1024,256]{1,0:T(8,128)(2,1)}, u32[]{:S(2)}) %copy-start) | copy-done | bytes 524312
  18.4 1.1 %shard_map.68 = (bf16[1024,256]{1,0:T(8,128)(2,1)S(1)}, bf16[1024,256]{1,0:T(8,128)(2,1)S(1)}) custom-call(s32[6]{0:T(128)S(1)} %pad_add_fusion.place_ref, bf16[1024,256]{1,0:T(8,128)(2,1)S(1)} %copy-done, bf16[1024,256]{1,0:T(8,128)(2,1)S(1)} %copy-done.2), custom_call_target="tpu_custom_call" | custom-call | flops 16777216 | bytes 131072 | tf_op jit(solution)/shard_map/pallas_call | solution.py:297
  20.6 2.3 %collective-permute-done.5.far_ref = bf16[2,4,2,24,256]{4,3,2,1,0:T(8,128)(2,1)S(1)} collective-permute-done((bf16[2,4,2,24,256]{4,3,2,1,0:T(8,128)(2,1)S(1)}, bf16[2,4,2,24,256]{4,3,2,1,0:T(8,128)(2,1)S(1)}, u32[]{:S(2)}, u32[]{:S(2)}) %collective-permute-start.5) | collective-permute-done | bytes 196640 | tf_op jit(solution)/shard_map/ppermute | solution.py:312
  23.0 1.8 %shard_map.69 = (f32[384,2048]{1,0:T(8,128)S(1)}, f32[8,128]{1,0:T(8,128)S(1)}) custom-call(s32[6]{0:T(128)S(1)} %pad_add_fusion.place_ref, bf16[2,4,2,24,256]{4,3,2,1,0:T(8,128)(2,1)S(1)} %pad_maximum_fusion.near_ref, bf16[2,4,2,24,256]{4,3,2,1,0:T(8,128)(2,1)S(1)} %collective-permute-done.5.far_ref, bf16[1024,256]{1,0:T(8,128)(2,1)S(1)} %get-tuple-element.30.refs_0_, ...), custom_call_target="tpu_custom_call" | custom-call | flops 402653184 | bytes 3145728 | tf_op jit(solution)/shard_map/pallas_call | solution.py:297
  24.8 1.3 %collective-permute-start.7 = (f32[8,128]{1,0:T(8,128)S(1)}, f32[8,128]{1,0:T(8,128)S(1)}, u32[]{:S(2)}, u32[]{:S(2)}) collective-permute-start(f32[8,128]{1,0:T(8,128)S(1)} %get-tuple-element.32), channel_id=1, source_target_pairs={{0,3},{1,2},{2,1},{3,0},{4,7},{5,6},{6,5},{7,4},{8,11},{9,10},{10,... | collective-permute-start | bytes 12296 | tf_op jit(solution)/shard_map/ppermute | solution.py:312
  26.1 1.8 %collective-permute-done.7 = f32[8,128]{1,0:T(8,128)S(1)} collective-permute-done((f32[8,128]{1,0:T(8,128)S(1)}, f32[8,128]{1,0:T(8,128)S(1)}, u32[]{:S(2)}, u32[]{:S(2)}) %collective-permute-start.7) | collective-permute-done | bytes 4128 | tf_op jit(solution)/shard_map/ppermute | solution.py:312
  27.9 1.3 %collective-permute-start.8 = (f32[8,128]{1,0:T(8,128)S(1)}, f32[8,128]{1,0:T(8,128)S(1)}, u32[]{:S(2)}, u32[]{:S(2)}) collective-permute-start(f32[8,128]{1,0:T(8,128)S(1)} %add.9.mine_ref), channel_id=1, source_target_pairs={{0,5},{1,4},{2,7},{3,6},{4,1},{5,0},{6,3},{7,2},{8,13},{9,12},{10,... | collective-permute-start | bytes 12296 | tf_op jit(solution)/shard_map/ppermute | solution.py:312
  29.1 1.8 %collective-permute-done.8.other_ref = f32[8,128]{1,0:T(8,128)S(1)} collective-permute-done((f32[8,128]{1,0:T(8,128)S(1)}, f32[8,128]{1,0:T(8,128)S(1)}, u32[]{:S(2)}, u32[]{:S(2)}) %collective-permute-start.8) | collective-permute-done | bytes 4128 | tf_op jit(solution)/shard_map/ppermute | solution.py:312
  31.8 1.3 %collective-permute-start.9 = (f32[8,128]{1,0:T(8,128)S(1)}, f32[8,128]{1,0:T(8,128)S(1)}, u32[]{:S(2)}, u32[]{:S(2)}) collective-permute-start(f32[8,128]{1,0:T(8,128)S(1)} %shard_map.70), channel_id=1, source_target_pairs={{0,3},{1,2},{2,1},{3,0},{4,7},{5,6},{6,5},{7,4},{8,11},{9,10},{10,... | collective-permute-start | bytes 12296 | tf_op jit(solution)/shard_map/ppermute | solution.py:312
  33.1 1.8 %collective-permute-done.9 = f32[8,128]{1,0:T(8,128)S(1)} collective-permute-done((f32[8,128]{1,0:T(8,128)S(1)}, f32[8,128]{1,0:T(8,128)S(1)}, u32[]{:S(2)}, u32[]{:S(2)}) %collective-permute-start.9) | collective-permute-done | bytes 4128 | tf_op jit(solution)/shard_map/ppermute | solution.py:312
  34.9 1.3 %collective-permute-start.10 = (f32[8,128]{1,0:T(8,128)S(1)}, f32[8,128]{1,0:T(8,128)S(1)}, u32[]{:S(2)}, u32[]{:S(2)}) collective-permute-start(f32[8,128]{1,0:T(8,128)S(1)} %add.10.mine_ref), channel_id=1, source_target_pairs={{0,5},{1,4},{2,7},{3,6},{4,1},{5,0},{6,3},{7,2},{8,13},{9,12},{10,... | collective-permute-start | bytes 12296 | tf_op jit(solution)/shard_map/ppermute | solution.py:312
  36.1 1.6 %shard_map.71 = (bf16[384,256]{1,0:T(8,128)(2,1)S(1)}, f32[384,256]{1,0:T(8,128)S(1)}, f32[96,256]{1,0:T(8,128)S(1)}, f32[8,128]{1,0:T(8,128)S(1)}) custom-call(s32[6]{0:T(128)S(1)} %pad_add_fusion.place_ref, bf16[2,4,2,24,256]{4,3,2,1,0:T(8,128)(2,1)S(1)} %pad_maximum_fusion.near_ref, bf16[2,4,2,24,256]{4,3,2,1,0:T(8,128)(2,1)S(1)} %collective-permute-done.5.far_ref, ...), custom_call_target="tpu_custom_call" | custom-call | flops 402653184 | bytes 3145728 | tf_op jit(solution)/shard_map/pallas_call | solution.py:297
  37.9 1.6 %shard_map.72 = (f32[384,256]{1,0:T(8,128)S(1)}, f32[56,256]{1,0:T(8,128)S(1)}, f32[56,256]{1,0:T(8,128)S(1)}) custom-call(s32[6]{0:T(128)S(1)} %pad_add_fusion.place_ref, f32[8,128]{1,0:T(8,128)S(1)} %add.10.mine_ref, f32[8,128]{1,0:T(8,128)S(1)} %collective-permute-done.10.other_ref, f32[384,2048]{1,0:T(8,128)S(1)} %get-tuple-element.33.weights_ref, ...), custom_call_target="tpu_custom_call" | custom-call | flops 201326592 | bytes 1572864 | tf_op jit(solution)/shard_map/pallas_call | solution.py:297
  39.6 1.5 %collective-permute-start.12 = (f32[56,256]{1,0:T(8,128)S(1)}, f32[56,256]{1,0:T(8,128)S(1)}, u32[]{:S(2)}, u32[]{:S(2)}) collective-permute-start(f32[56,256]{1,0:T(8,128)S(1)} %get-tuple-element.40), channel_id=1, source_target_pairs={{0,3},{1,2},{2,1},{3,0},{4,7},{5,6},{6,5},{7,4},{8,11},{9,10},{10,... | collective-permute-start | bytes 172040 | tf_op jit(solution)/shard_map/ppermute | solution.py:312
  41.0 2.5 %collective-permute-done.12 = f32[56,256]{1,0:T(8,128)S(1)} collective-permute-done((f32[56,256]{1,0:T(8,128)S(1)}, f32[56,256]{1,0:T(8,128)S(1)}, u32[]{:S(2)}, u32[]{:S(2)}) %collective-permute-start.12) | collective-permute-done | bytes 57376 | tf_op jit(solution)/shard_map/ppermute | solution.py:312
  43.5 1.4 %collective-permute-start.13 = (f32[32,256]{1,0:T(8,128)S(1)}, f32[32,256]{1,0:T(8,128)S(1)}, u32[]{:S(2)}, u32[]{:S(2)}) collective-permute-start(f32[32,256]{1,0:T(8,128)S(1)} %slice.4), channel_id=1, source_target_pairs={{0,5},{1,4},{2,7},{3,6},{4,1},{5,0},{6,3},{7,2},{8,13},{9,12},{10,... | collective-permute-start | bytes 98312 | tf_op jit(solution)/shard_map/ppermute | solution.py:312
  44.9 2.0 %collective-permute-done.13.other_ref = f32[32,256]{1,0:T(8,128)S(1)} collective-permute-done((f32[32,256]{1,0:T(8,128)S(1)}, f32[32,256]{1,0:T(8,128)S(1)}, u32[]{:S(2)}, u32[]{:S(2)}) %collective-permute-start.13) | collective-permute-done | bytes 32800 | tf_op jit(solution)/shard_map/ppermute | solution.py:312
  46.9 1.8 %shard_map.73 = (f32[12,256]{1,0:T(8,128)}, f32[1,256,256]{2,1,0:T(8,128)}) custom-call(s32[6]{0:T(128)S(1)} %pad_add_fusion.place_ref, f32[56,256]{1,0:T(8,128)S(1)} %add.11.mine_ref, f32[32,256]{1,0:T(8,128)S(1)} %collective-permute-done.13.other_ref, f32[384,256]{1,0:T(8,128)S(1)} %get-tuple-element.41.targets_ref, ...), custom_call_target="tpu_custom_call" | custom-call | flops 50331648 | bytes 393216 | tf_op jit(solution)/shard_map/pallas_call | solution.py:297
  (28 shorter events, 5.4 us)
Async XLA Ops:
  1.4 3.9 %collective-permute-start = (bf16[24,256]{1,0:T(8,128)(2,1)S(1)}, bf16[24,256]{1,0:T(8,128)(2,1)S(1)}, u32[]{:S(2)}, u32[]{:S(2)}) collective-permute-start(bf16[24,256]{1,0:T(8,128)(2,1)S(1)} %pad_maximum_fusion.3), channel_id=1, source_target_pairs={{0,3},{1,2},{2,1},{3,0},{4,7},{5,6},{6,5},{7,4},{8,11},{9,10},{10,... | collective-permute-start | bytes 36872 | tf_op jit(solution)/shard_map/ppermute | solution.py:312
  5.2 4.7 %collective-permute-start.1 = (bf16[2,24,256]{2,1,0:T(8,128)(2,1)S(1)}, bf16[2,24,256]{2,1,0:T(8,128)(2,1)S(1)}, u32[]{:S(2)}, u32[]{:S(2)}) collective-permute-start(bf16[2,24,256]{2,1,0:T(8,128)(2,1)S(1)} %pad_maximum_fusion.2), channel_id=1, source_target_pairs={{0,9},{1,8},{2,11},{3,10},{4,13},{5,12},{6,15},{7,14},{8,1},{9,0},... | collective-permute-start | bytes 73736 | tf_op jit(solution)/shard_map/ppermute | solution.py:320
  7.4 4.3 %collective-permute-start.2 = (bf16[2,24,256]{2,1,0:T(8,128)(2,1)S(1)}, bf16[2,24,256]{2,1,0:T(8,128)(2,1)S(1)}, u32[]{:S(2)}, u32[]{:S(2)}) collective-permute-start(bf16[2,24,256]{2,1,0:T(8,128)(2,1)S(1)} %pad_maximum_fusion.2), channel_id=1, source_target_pairs={{0,17},{1,16},{2,19},{3,18},{4,21},{5,20},{6,23},{7,22},{8,25},{9,... | collective-permute-start | bytes 73736 | tf_op jit(solution)/shard_map/ppermute | solution.py:320
  10.0 5.0 %collective-permute-start.3 = (bf16[2,24,256]{2,1,0:T(8,128)(2,1)S(1)}, bf16[2,24,256]{2,1,0:T(8,128)(2,1)S(1)}, u32[]{:S(2)}, u32[]{:S(2)}) collective-permute-start(bf16[2,24,256]{2,1,0:T(8,128)(2,1)S(1)} %pad_maximum_fusion.2), channel_id=1, source_target_pairs={{0,25},{1,24},{2,27},{3,26},{4,29},{5,28},{6,31},{7,30},{8,17},{9,... | collective-permute-start | bytes 73736 | tf_op jit(solution)/shard_map/ppermute | solution.py:320
  15.1 4.9 %collective-permute-start.4 = (bf16[4,2,24,256]{3,2,1,0:T(8,128)(2,1)S(1)}, bf16[4,2,24,256]{3,2,1,0:T(8,128)(2,1)S(1)}, u32[]{:S(2)}, u32[]{:S(2)}) collective-permute-start(bf16[4,2,24,256]{3,2,1,0:T(8,128)(2,1)S(1)} %get-tuple-element.45), channel_id=1, source_target_pairs={{0,5},{1,4},{2,7},{3,6},{4,1},{5,0},{6,3},{7,2},{8,13},{9,12},{10,... | collective-permute-start | bytes 294920 | tf_op jit(solution)/shard_map/ppermute | solution.py:312
  16.4 1.0 %copy-start = (bf16[1024,256]{1,0:T(8,128)(2,1)S(1)}, bf16[1024,256]{1,0:T(8,128)(2,1)}, u32[]{:S(2)}) copy-start(bf16[1024,256]{1,0:T(8,128)(2,1)} %proto_ref.1) | copy-start | bytes 1572868
  17.4 1.0 %copy-start.2 = (bf16[1024,256]{1,0:T(8,128)(2,1)S(1)}, bf16[1024,256]{1,0:T(8,128)(2,1)}, u32[]{:S(2)}) copy-start(bf16[1024,256]{1,0:T(8,128)(2,1)} %teacher_ref) | copy-start | bytes 1572868
  19.9 3.0 %collective-permute-start.6 = (bf16[1024,256]{1,0:T(8,128)(2,1)S(1)}, bf16[1024,256]{1,0:T(8,128)(2,1)S(1)}, u32[]{:S(2)}, u32[]{:S(2)}) collective-permute-start(bf16[1024,256]{1,0:T(8,128)(2,1)S(1)} %get-tuple-element.30.refs_0_), channel_id=1, source_target_pairs={{0,1},{1,0},{2,3},{3,2},{4,5},{5,4},{6,7},{7,6},{8,9},{9,8},{10,11... | collective-permute-start | bytes 1572872 | tf_op jit(solution)/shard_map/ppermute | solution.py:312
  20.1 16.0 %collective-permute-start.11 = (bf16[1024,256]{1,0:T(8,128)(2,1)S(1)}, bf16[1024,256]{1,0:T(8,128)(2,1)S(1)}, u32[]{:S(2)}, u32[]{:S(2)}) collective-permute-start(bf16[1024,256]{1,0:T(8,128)(2,1)S(1)} %get-tuple-element.34.refs_0_), channel_id=1, source_target_pairs={{0,1},{1,0},{2,3},{3,2},{4,5},{5,4},{6,7},{7,6},{8,9},{9,8},{10,11... | collective-permute-start | bytes 1572872 | tf_op jit(solution)/shard_map/ppermute | solution.py:312
  20.5 2.4 %collective-permute-start.5 = (bf16[2,4,2,24,256]{4,3,2,1,0:T(8,128)(2,1)S(1)}, bf16[2,4,2,24,256]{4,3,2,1,0:T(8,128)(2,1)S(1)}, u32[]{:S(2)}, u32[]{:S(2)}) collective-permute-start(bf16[2,4,2,24,256]{4,3,2,1,0:T(8,128)(2,1)S(1)} %pad_maximum_fusion.near_ref), channel_id=1, source_target_pairs={{0,1},{1,0},{2,3},{3,2},{4,5},{5,4},{6,7},{7,6},{8,9},{9,8},{10,11... | collective-permute-start | bytes 589832 | tf_op jit(solution)/shard_map/ppermute | solution.py:312
  24.8 3.1 %collective-permute-start.7 = (f32[8,128]{1,0:T(8,128)S(1)}, f32[8,128]{1,0:T(8,128)S(1)}, u32[]{:S(2)}, u32[]{:S(2)}) collective-permute-start(f32[8,128]{1,0:T(8,128)S(1)} %get-tuple-element.32), channel_id=1, source_target_pairs={{0,3},{1,2},{2,1},{3,0},{4,7},{5,6},{6,5},{7,4},{8,11},{9,10},{10,... | collective-permute-start | bytes 12296 | tf_op jit(solution)/shard_map/ppermute | solution.py:312
  27.9 3.0 %collective-permute-start.8 = (f32[8,128]{1,0:T(8,128)S(1)}, f32[8,128]{1,0:T(8,128)S(1)}, u32[]{:S(2)}, u32[]{:S(2)}) collective-permute-start(f32[8,128]{1,0:T(8,128)S(1)} %add.9.mine_ref), channel_id=1, source_target_pairs={{0,5},{1,4},{2,7},{3,6},{4,1},{5,0},{6,3},{7,2},{8,13},{9,12},{10,... | collective-permute-start | bytes 12296 | tf_op jit(solution)/shard_map/ppermute | solution.py:312
  31.8 15.2 %copy-start.1 = (bf16[1024,256]{1,0:T(8,128)(2,1)S(1)}, bf16[1024,256]{1,0:T(8,128)(2,1)}, u32[]{:S(2)}) copy-start(bf16[1024,256]{1,0:T(8,128)(2,1)} %proto_ref.1) | copy-start | bytes 1572868
  31.8 15.1 %copy-start.3 = (bf16[12,256]{1,0:T(8,128)(2,1)S(1)}, bf16[12,256]{1,0:T(8,128)(2,1)}, u32[]{:S(2)}) copy-start(bf16[12,256]{1,0:T(8,128)(2,1)} %feat_ref.1) | copy-start | bytes 18436
  31.8 3.1 %collective-permute-start.9 = (f32[8,128]{1,0:T(8,128)S(1)}, f32[8,128]{1,0:T(8,128)S(1)}, u32[]{:S(2)}, u32[]{:S(2)}) collective-permute-start(f32[8,128]{1,0:T(8,128)S(1)} %shard_map.70), channel_id=1, source_target_pairs={{0,3},{1,2},{2,1},{3,0},{4,7},{5,6},{6,5},{7,4},{8,11},{9,10},{10,... | collective-permute-start | bytes 12296 | tf_op jit(solution)/shard_map/ppermute | solution.py:312
  34.9 3.0 %collective-permute-start.10 = (f32[8,128]{1,0:T(8,128)S(1)}, f32[8,128]{1,0:T(8,128)S(1)}, u32[]{:S(2)}, u32[]{:S(2)}) collective-permute-start(f32[8,128]{1,0:T(8,128)S(1)} %add.10.mine_ref), channel_id=1, source_target_pairs={{0,5},{1,4},{2,7},{3,6},{4,1},{5,0},{6,3},{7,2},{8,13},{9,12},{10,... | collective-permute-start | bytes 12296 | tf_op jit(solution)/shard_map/ppermute | solution.py:312
  39.6 3.9 %collective-permute-start.12 = (f32[56,256]{1,0:T(8,128)S(1)}, f32[56,256]{1,0:T(8,128)S(1)}, u32[]{:S(2)}, u32[]{:S(2)}) collective-permute-start(f32[56,256]{1,0:T(8,128)S(1)} %get-tuple-element.40), channel_id=1, source_target_pairs={{0,3},{1,2},{2,1},{3,0},{4,7},{5,6},{6,5},{7,4},{8,11},{9,10},{10,... | collective-permute-start | bytes 172040 | tf_op jit(solution)/shard_map/ppermute | solution.py:312
  43.5 3.4 %collective-permute-start.13 = (f32[32,256]{1,0:T(8,128)S(1)}, f32[32,256]{1,0:T(8,128)S(1)}, u32[]{:S(2)}, u32[]{:S(2)}) collective-permute-start(f32[32,256]{1,0:T(8,128)S(1)} %slice.4), channel_id=1, source_target_pairs={{0,5},{1,4},{2,7},{3,6},{4,1},{5,0},{6,3},{7,2},{8,13},{9,12},{10,... | collective-permute-start | bytes 98312 | tf_op jit(solution)/shard_map/ppermute | solution.py:312

commit v4 on v0

--- a/solution.py
+++ b/solution.py
@@ -1,14 +1,20 @@
+import functools
+
 import jax
 import jax.numpy as jnp
 from jax import lax
+from jax.experimental import pallas as pl
+from jax.experimental.pallas import tpu as pltpu
 from jax.sharding import PartitionSpec as P
 
 ITERS = 3
-
 
 student_temp = 0.1
 teacher_temp = 0.07
 eps_norm = 1e-06
+
+LANES = 128
+BLOCK_BYTES = 8 * 2**20
 
 
 def unit_rows(values):
@@ -17,6 +23,455 @@
     return (widened / length, length)
 
 
+CORE, X, Y = 1, 2, 4
+X_CROSS, Y_CROSS = X | CORE, Y | CORE
+
+
+def block_of(proto):
+    return (proto & X) + ((proto >> 2) & 1)
+
+
+def quick_unit(values):
+    widened = values.astype(jnp.float32)
+    squares = jnp.sum(widened * widened, axis=1, keepdims=True) + eps_norm
+    scale = lax.rsqrt(squares)
+    return widened * scale, scale
+
+
+def dp_order(n_dp):
+    return [0, *reversed(range(1, n_dp))]
+
+
+def live_lanes(place_ref, half, lanes, n_dp, rows):
+    mine = place_ref[1]
+    parity = (mine ^ (mine >> 1) ^ (mine >> 2)) & 1
+    lane = lax.broadcasted_iota(jnp.int32, (1, lanes), 1)
+    live = jnp.zeros((1, lanes), jnp.float32)
+    start = 0
+    for t in dp_order(n_dp):
+        count = place_ref[2 + (place_ref[0] ^ t)]
+        for x in range(2):
+            for y in range(2):
+                core = parity ^ x ^ y ^ half ^ (1 if t else 0)
+                proto = core + X * x + Y * y
+                end = start + jnp.clip(count - proto * rows, 0, rows)
+                live = jnp.where((lane >= start) & (lane < end), 1.0, live)
+                start += rows
+    return live
+
+
+def pack_lanes(values):
+    pieces = [values[:, k : k + LANES] for k in range(0, values.shape[1], LANES)]
+    return jnp.concatenate(pieces + [jnp.zeros((8 - len(pieces), LANES), jnp.float32)], axis=0)
+
+
+def unpack_lanes(tile, lanes):
+    return jnp.concatenate([tile[k : k + 1, :] for k in range(lanes // LANES)], axis=1)
+
+
+def as_column(values):
+    return jnp.broadcast_to(values, (LANES, values.shape[1])).T
+
+
+def as_tile(partial):
+    return pack_lanes(jnp.sum(partial.T, axis=0, keepdims=True))
+
+
+def inverse_rows(tile, rows):
+    total = unpack_lanes(tile, rows)
+    live = total > 0.0
+    return jnp.where(live, 1.0 / jnp.where(live, total, 1.0), 0.0)
+
+
+def place_rows(place_ref, ref, which, rows, scratch):
+    mine_x, mine_y = (place_ref[1] >> 1) & 1, (place_ref[1] >> 2) & 1
+    start = 0
+    for t in range(ref.shape[1]):
+        for x in range(2):
+            for y in range(2):
+                block = ref[mine_y ^ y, t, mine_x ^ x].astype(jnp.float32)
+                scratch[start : start + rows, :] = block[which * rows : (which + 1) * rows]
+                start += rows
+    unit, _ = quick_unit(scratch[...])
+    return unit.astype(jnp.bfloat16)
+
+
+def scores_of(rows_all, units):
+    return lax.dot_general(
+        rows_all, units, (((1,), (1,)), ((), ())), preferred_element_type=jnp.float32
+    )
+
+
+def twice(column):
+    return jnp.concatenate([column, column], axis=1)
+
+
+def weighted_rows(panels, left, scale_ref, part_ref, add=False):
+    tiles = panels[0].shape[1] // LANES
+    scales = [scale_ref[:, left + k * LANES : left + (k + 1) * LANES] for k in range(tiles)]
+    top = 0
+    for ref in panels:
+
+        def body(i, _, ref=ref, top=top):
+            at = pl.ds(pl.multiple_of(i * 8, 8), 8)
+            to = pl.ds(pl.multiple_of(i * 8 + top, 8), 8)
+            sums = [None] * 4
+            for k in range(tiles):
+                term = ref[at, k * LANES : (k + 1) * LANES] * scales[k]
+                sums[k % 4] = term if sums[k % 4] is None else sums[k % 4] + term
+            total = (sums[0] + sums[1]) + (sums[2] + sums[3])
+            part_ref[to, :] = part_ref[to, :] + total if add else total
+            return 0
+
+        lax.fori_loop(0, ref.shape[0] // 8, body, 0, unroll=4)
+        top += ref.shape[0]
+
+
+def column_scales(panels, left, row_ref, scale_ref):
+    tiles = panels[0].shape[1] // LANES
+    sums = [jnp.zeros((8, LANES), jnp.float32)] * tiles
+    top = 0
+    for ref in panels:
+
+        def body(i, sums, ref=ref, top=top):
+            at = pl.ds(pl.multiple_of(i * 8, 8), 8)
+            row = row_ref[pl.ds(pl.multiple_of(i * 8 + top, 8), 8), :]
+            return [
+                total + ref[at, k * LANES : (k + 1) * LANES] * row for k, total in enumerate(sums)
+            ]
+
+        sums = lax.fori_loop(0, ref.shape[0] // 8, body, sums, unroll=4)
+        top += ref.shape[0]
+    for k, total in enumerate(sums):
+        inverse = 1.0 / jnp.sum(total, axis=0, keepdims=True)
+        at = slice(left + k * LANES, left + (k + 1) * LANES)
+        scale_ref[:, at] = jnp.broadcast_to(inverse, (8, LANES))
+
+
+def weights_of(rows, units, live):
+    weights = jnp.exp(scores_of(rows, units) * (1 / teacher_temp)) * live
+    return weights, fold(weights)
+
+
+def fold(values):
+    return jnp.sum(values.reshape(values.shape[0] // 8, 8, values.shape[1]), axis=0)
+
+
+def units_kernel(proto_ref, units_ref):
+    units_ref[...] = quick_unit(proto_ref[...])[0].astype(jnp.bfloat16)
+
+
+def near_kernel(chunk, place_ref, near_ref, *refs):
+    *unit_refs, weights_ref, sums_ref, rows_ref, scratch = refs
+    half = rows_ref.shape[0]
+    rows = near_ref.shape[3] // 2
+    protos = unit_refs[0].shape[0]
+    rows_near = place_rows(place_ref, near_ref, 0, rows, scratch)
+    rows_ref[...] = rows_near
+    live = twice(as_column(live_lanes(place_ref, 0, half, near_ref.shape[1], rows)))
+    for k, unit_ref in enumerate(unit_refs):
+        for start in range(0, protos, chunk):
+            at = slice(k * protos + start, k * protos + start + chunk)
+            weights_ref[:, at], sums_ref[:, at] = weights_of(
+                rows_near, unit_ref[start : start + chunk, :], live
+            )
+
+
+def far_kernel(chunk, place_ref, far_ref, near_rows_ref, near_weights_ref, near_sums_ref, *refs):
+    *unit_refs, weights_ref, rows_ref, live_ref, sums_ref, scratch, scale_ref, part_ref = refs
+    half = near_rows_ref.shape[0]
+    rows = far_ref.shape[3] // 2
+    protos = unit_refs[0].shape[0]
+    rows_far = place_rows(place_ref, far_ref, 0, rows, scratch)
+    rows_ref[:half, :] = near_rows_ref[...]
+    rows_ref[half:, :] = rows_far
+    live = as_column(live_lanes(place_ref, 1, half, far_ref.shape[1], rows))
+    live_ref[half:, :] = live
+    for k, unit_ref in enumerate(unit_refs):
+        for start in range(0, protos, chunk):
+            at = slice(k * protos + start, k * protos + start + chunk)
+            weights, sums = weights_of(rows_far, unit_ref[start : start + chunk, :], twice(live))
+            weights_ref[:, at] = weights
+            inverse = 1.0 / jnp.sum(near_sums_ref[:, at] + sums, axis=0, keepdims=True)
+            scale_ref[:, at] = jnp.broadcast_to(inverse, (8, chunk))
+    weighted_rows([near_weights_ref, weights_ref], 0, scale_ref, part_ref)
+    sums_ref[...] = as_tile(part_ref[...])
+    live_ref[:half, :] = as_column(live_lanes(place_ref, 0, half, far_ref.shape[1], rows))
+
+
+def across_kernel(chunk, rows_ref, live_ref, *refs):
+    *proto_refs, weights_ref = refs
+    protos = proto_refs[0].shape[0]
+    rows_all = rows_ref[...]
+    live = twice(live_ref[...])
+    for k, proto_ref in enumerate(proto_refs):
+        for start in range(0, protos, chunk):
+            units = quick_unit(proto_ref[start : start + chunk, :])[0].astype(jnp.bfloat16)
+            at = slice(k * protos + start, k * protos + start + chunk)
+            weights_ref[:, at], _ = weights_of(rows_all, units, live)
+
+
+def sweep(sums, near_ref, far_ref, across_ref, row_ref, scale_ref, part_ref):
+    held = near_ref.shape[1]
+    row_ref[...] = as_column(inverse_rows(sums, row_ref.shape[0]))
+    own = [near_ref, far_ref]
+    column_scales(own, 0, row_ref, scale_ref)
+    column_scales([across_ref], held, row_ref, scale_ref)
+    weighted_rows(own, 0, scale_ref, part_ref)
+    weighted_rows([across_ref], held, scale_ref, part_ref, add=True)
+    return as_tile(part_ref[...])
+
+
+def step_kernel(mine_ref, other_ref, near_ref, far_ref, across_ref, sums_ref, *scratch):
+    sums_ref[...] = sweep(mine_ref[...] + other_ref[...], near_ref, far_ref, across_ref, *scratch)
+
+
+def split(values):
+    high = values.astype(jnp.bfloat16)
+    low = (values - high.astype(jnp.float32)).astype(jnp.bfloat16)
+    return jnp.concatenate([high, low], axis=0)
+
+
+def exps_kernel(chunk, place_ref, near_ref, far_ref, *refs):
+    *proto_refs, rows_ref, units_ref, pull_ref, sums_ref, scratch, exps_ref = refs
+    all_rows, half = rows_ref.shape[0], rows_ref.shape[0] // 2
+    protos = proto_refs[0].shape[0]
+    first = pull_ref.shape[0]
+    for k, ref in enumerate((near_ref, far_ref)):
+        rows_half = place_rows(place_ref, ref, 1, ref.shape[3] // 2, scratch)
+        rows_ref[k * half : (k + 1) * half, :] = rows_half
+    rows_all = rows_ref[...]
+    part = jnp.zeros((all_rows, LANES), jnp.float32)
+    pull = jnp.zeros((2 * first, pull_ref.shape[1]), jnp.float32)
+    for k, proto_ref in enumerate(proto_refs):
+        for start in range(0, protos, chunk):
+            units = quick_unit(proto_ref[start : start + chunk, :])[0].astype(jnp.bfloat16)
+            units_ref[k * protos + start : k * protos + start + chunk, :] = units
+            exps_ref[...] = jnp.exp(scores_of(rows_all, units) * (1 / student_temp))
+            for at in range(0, chunk, LANES):
+                part = part + exps_ref[:, at : at + LANES]
+            exps = split(exps_ref[:first, :])
+            pull = pull + jnp.dot(exps, units, preferred_element_type=jnp.float32)
+    pull_ref[...] = pull[:first] + pull[first:]
+    sums_ref[...] = as_tile(part)
+
+
+def last_kernel(chunk, rows, place_ref, mine_ref, other_ref, near_ref, far_ref, across_ref, *refs):
+    units_ref, exp_pull_ref, exp_sums_ref, keep_ref, send_ref, *scratch, blocks_ref = refs
+    scale_ref = scratch[1]
+    first = exp_pull_ref.shape[0]
+    sums = sweep(mine_ref[...] + other_ref[...], near_ref, far_ref, across_ref, *scratch)
+    pull = jnp.zeros((2 * first, exp_pull_ref.shape[1]), jnp.float32)
+    for start in range(0, units_ref.shape[0], chunk):
+        at = slice(start, start + chunk)
+        scaled = split(near_ref[:first, at] * scale_ref[:1, at])
+        pull = pull + jnp.dot(scaled, units_ref[at, :], preferred_element_type=jnp.float32)
+    pulls = (pull[:first] + pull[first:], exp_pull_ref[...])
+    for k, pull in enumerate(pulls):
+        for block in range(4):
+            blocks_ref[k, block, :rows, :] = pull[block * rows : (block + 1) * rows]
+    mine = place_ref[1]
+    for ref, proto in ((keep_ref, mine), (send_ref, mine ^ X)):
+        for j, owner in enumerate((proto, proto ^ Y)):
+            for k in range(2):
+                start = (2 * j + k) * rows
+                ref[start : start + rows, :] = blocks_ref[k, block_of(owner), :rows, :]
+        ref[4 * rows :, :LANES] = exp_sums_ref[...]
+    keep_ref[4 * rows :, LANES:] = sums
+    send_ref[4 * rows :, LANES:] = jnp.zeros_like(sums)
+
+
+def own_kernel(place_ref, mine_ref, other_ref, teacher_rows_ref, student_rows_ref, *refs):
+    teacher_proto_ref, proto_ref, targets_ref, exps_ref, unit_ref, scale_ref = refs
+    own, all_rows = targets_ref.shape
+    row_scale = inverse_rows(mine_ref[...] + other_ref[...], all_rows)
+    live = jnp.where(row_scale > 0.0, 1.0, 0.0)
+    first = pl.ds(pl.multiple_of(place_ref[0] * own, own), own)
+    units = quick_unit(teacher_proto_ref[first, :])[0].astype(jnp.bfloat16)
+    weights = jnp.exp(scores_of(units, teacher_rows_ref[...]) * (1 / teacher_temp)) * live
+    inverse = 1.0 / jnp.sum(weights * row_scale, axis=1, keepdims=True)
+    targets_ref[...] = weights * (inverse * (1 / student_temp))
+    unit, scale = quick_unit(proto_ref[first, :])
+    unit_ref[...] = unit
+    scale_ref[...] = jnp.broadcast_to(scale, scale_ref.shape)
+    units = unit.astype(jnp.bfloat16)
+    exps = jnp.exp(scores_of(units, student_rows_ref[...]) * (1 / student_temp))
+    exps_ref[...] = exps * (1 / student_temp)
+
+
+def grads_kernel(place_ref, mine_ref, other_ref, targets_ref, exps_ref, unit_ref, *refs):
+    scale_ref, rows_ref, feat_ref, student_out_ref, proto_out_ref = refs
+    all_rows = targets_ref.shape[1]
+    rows = feat_ref.shape[0]
+    sums = mine_ref[4 * rows :, :] + other_ref[2 * rows :, :]
+    target_scale = inverse_rows(sums[:, LANES:], all_rows)
+    exp_scale = jnp.where(target_scale > 0.0, 1.0 / unpack_lanes(sums[:, :LANES], all_rows), 0.0)
+
+    grad = exps_ref[...] * exp_scale - targets_ref[...] * target_scale
+    pushed = jnp.dot(grad.astype(jnp.bfloat16), rows_ref[...], preferred_element_type=jnp.float32)
+    unit = unit_ref[...]
+    along = jnp.sum(unit * pushed, axis=1, keepdims=True)
+    proto_out_ref[0] = (pushed - unit * along) * twice(scale_ref[...])
+
+    row = lax.broadcasted_iota(jnp.int32, (rows, LANES), 0) + block_of(place_ref[1]) * rows
+    here = lax.broadcasted_iota(jnp.int32, (rows, LANES), 1) == row
+    target_column, exp_column = [
+        jnp.sum(jnp.where(here, scale[:, :LANES], 0.0), axis=1, keepdims=True) * (1 / student_temp)
+        for scale in (target_scale, exp_scale)
+    ]
+    target_pull, exp_pull = [
+        mine_ref[k * rows : (k + 1) * rows, :] + other_ref[k * rows : (k + 1) * rows, :]
+        for k in range(2)
+    ]
+    pulled = exp_pull * exp_column - target_pull * target_column
+    unit, scale = quick_unit(feat_ref[...])
+    student_out_ref[...] = (
+        pulled - unit * jnp.sum(unit * pulled, axis=1, keepdims=True)
+    ) * scale
+
+
+def call(kernel, out_shape, operands, smem=0, scratch=(), work=0):
+    vmem = pl.BlockSpec(memory_space=pltpu.VMEM)
+    return pl.pallas_call(
+        kernel,
+        out_shape=out_shape,
+        in_specs=[pl.BlockSpec(memory_space=pltpu.SMEM)] * smem + [vmem] * (len(operands) - smem),
+        out_specs=jax.tree.map(lambda _: vmem, out_shape),
+        scratch_shapes=scratch,
+        compiler_params=pltpu.CompilerParams(vmem_limit_bytes=24 * 2**20),
+        cost_estimate=pl.CostEstimate(
+            flops=512 * work, bytes_accessed=4 * work, transcendentals=work
+        ),
+    )(*operands)
+
+
+def swap(values, axis, distance):
+    others = [(k, k ^ distance) for k in range(lax.axis_size(axis))]
+    return lax.ppermute(values, axis, others)
+
+
+def swap_dp(values, t):
+    n_dp, n_proto = lax.axis_size("dp"), lax.axis_size("proto")
+    others = [
+        (d * n_proto + p, (d ^ t) * n_proto + (p ^ CORE)) for d in range(n_dp) for p in range(n_proto)
+    ]
+    return lax.ppermute(values, ("dp", "proto"), others)
+
+
+def on_device_all_rows(student_feat, teacher_feat, prototypes, teacher_prototypes, live_count):
+    n_dp, n_proto = lax.axis_size("dp"), lax.axis_size("proto")
+    rows, width = student_feat.shape
+    protos = prototypes.shape[0]
+    own = protos // n_dp
+    all_rows = n_dp * n_proto * rows
+    half = all_rows // 2
+    first = 4 * rows
+    held = 2 * protos
+    f32 = functools.partial(jax.ShapeDtypeStruct, dtype=jnp.float32)
+    bf16 = functools.partial(jax.ShapeDtypeStruct, dtype=jnp.bfloat16)
+    place = jnp.stack([lax.axis_index("dp"), lax.axis_index("proto")]).astype(jnp.int32)
+    place = jnp.concatenate([place, live_count])
+    tile = f32((8, LANES))
+    message = f32((4 * rows + 8, width))
+    row_scratch = pltpu.VMEM((half, width), jnp.float32)
+    column = pltpu.VMEM((all_rows, LANES), jnp.float32)
+    scale_row = pltpu.VMEM((8, held), jnp.float32)
+    sweep_scratch = [column, pltpu.VMEM((8, 2 * held), jnp.float32), column]
+
+    both = lax.optimization_barrier(jnp.concatenate([teacher_feat, student_feat], axis=0))
+    across_x = swap(both, "proto", X_CROSS)
+    across_x, own_protos, place = lax.optimization_barrier((across_x, teacher_prototypes, place))
+    across_protos = swap(own_protos, "proto", X_CROSS)
+    student_protos = (prototypes, swap(prototypes, "proto", CORE))
+    near = jnp.stack([both, across_x])
+    teacher_units = call(units_kernel, bf16((protos, width)), (own_protos,), work=protos * width)
+    teacher_units = (teacher_units, swap(teacher_units, "proto", CORE))
+    near = jnp.stack([near] + [swap_dp(near, t) for t in dp_order(n_dp)[1:]])
+    near = jnp.stack([near, swap(near, "proto", Y_CROSS)])
+    far = swap(near, "proto", CORE)
+
+    near_weights, near_sums, near_rows = call(
+        functools.partial(near_kernel, own),
+        (f32((half, held)), f32((8, held)), bf16((half, width))),
+        (place, near, *teacher_units),
+        smem=1,
+        scratch=[row_scratch],
+        work=held * half,
+    )
+    far_weights, teacher_rows, live, sums = call(
+        functools.partial(far_kernel, own),
+        (f32((half, held)), bf16((all_rows, width)), f32((all_rows, LANES)), tile),
+        (place, far, near_rows, near_weights, near_sums, *teacher_units),
+        smem=1,
+        scratch=[row_scratch, scale_row, column],
+        work=held * half,
+    )
+    sums = sums + swap(sums, "proto", Y_CROSS)
+    sums, across_protos = lax.optimization_barrier((sums, across_protos))
+    parts = (sums, swap(sums, "proto", X_CROSS))
+    across_weights = call(
+        functools.partial(across_kernel, own),
+        f32((all_rows, held)),
+        (teacher_rows, live, across_protos, swap(across_protos, "proto", CORE)),
+        work=held * all_rows,
+    )
+    weights = (near_weights, far_weights, across_weights)
+    for _ in range(ITERS - 2):
+        sums = call(
+            step_kernel,
+            tile,
+            (*parts, *weights),
+            scratch=sweep_scratch,
+            work=held * all_rows,
+        )
+        sums, near, far, *student_protos = lax.optimization_barrier(
+            (sums, near, far, *student_protos)
+        )
+        parts = (sums, swap(sums, "proto", Y_CROSS))
+    student_rows, student_units, exp_pull, exp_sums = call(
+        functools.partial(exps_kernel, own),
+        (bf16((all_rows, width)), bf16((held, width)), f32((first, width)), tile),
+        (place, near, far, *student_protos),
+        smem=1,
+        scratch=[row_scratch, pltpu.VMEM((all_rows, own), jnp.float32)],
+        work=held * all_rows,
+    )
+    keep, send = call(
+        functools.partial(last_kernel, own, rows),
+        (message, message),
+        (place, *parts, *weights, student_units, exp_pull, exp_sums),
+        smem=1,
+        scratch=[*sweep_scratch, pltpu.VMEM((2, 4, 16, width), jnp.float32)],
+        work=held * all_rows,
+    )
+    *parts, send = lax.optimization_barrier((*parts, send))
+    targets, exps, own_units, own_scales = call(
+        own_kernel,
+        (f32((own, all_rows)), f32((own, all_rows)), f32((own, width)), f32((own, LANES))),
+        (place, *parts, teacher_rows, student_rows, teacher_prototypes, prototypes),
+        smem=1,
+        work=own * all_rows,
+    )
+    total = keep + swap(send, "proto", X_CROSS)
+    return call(
+        grads_kernel,
+        (f32((rows, width)), f32((1, own, width))),
+        (
+            place,
+            total,
+            swap(total[2 * rows :], "proto", Y_CROSS),
+            targets,
+            exps,
+            own_units,
+            own_scales,
+            student_rows,
+            student_feat,
+        ),
+        smem=1,
+        work=own * all_rows,
+    )
+
+
 def sample_totals(values):
     return lax.psum(values, "proto")
 
@@ -25,7 +480,7 @@
     return lax.psum(values, "dp")
 
 
-def on_device(student_feat, teacher_feat, prototypes, teacher_prototypes, live_count):
+def on_device_group_rows(student_feat, teacher_feat, prototypes, teacher_prototypes, live_count):
     student_unit, student_length = unit_rows(student_feat)
     teacher_unit, teacher_length = unit_rows(teacher_feat)
     proto_unit, proto_length = unit_rows(prototypes)
@@ -59,10 +514,9 @@
         row_sums = sample_totals(jnp.sum(targets, axis=1))
         targets = targets / jnp.where(live_mask, row_sums, 1.0)[:, None]
     student_probs = jnp.exp(logits - jnp.log(partition)[:, None])
-    grad_logits = jnp.where(live_column, (student_probs - targets) / student_temp, 0.0).astype(
+    grad_block = jnp.where(live_column, (student_probs - targets) / student_temp, 0.0).astype(
         jnp.bfloat16
     )
-    grad_block = grad_logits
     pulled = lax.psum_scatter(
         jnp.dot(grad_block, proto_bf, preferred_element_type=jnp.float32),
         "proto",
@@ -74,7 +528,6 @@
     ) / student_length
     own_protos = prototypes.shape[0] // lax.axis_size("dp")
     contract_first = (((0,), (0,)), ((), ()))
-    grad_block = grad_logits
     pushed = lax.psum_scatter(
         lax.dot_general(
             grad_block, student_rows, contract_first, preferred_element_type=jnp.float32
@@ -90,6 +543,26 @@
         pushed - own_units * jnp.sum(own_units * pushed, axis=1, keepdims=True)
     ) / own_lengths
     return (student_grad, proto_grad[None])
+
+
+def on_device(student_feat, teacher_feat, prototypes, teacher_prototypes, live_count):
+    n_dp, n_proto = lax.axis_size("dp"), lax.axis_size("proto")
+    rows, width = student_feat.shape
+    protos = prototypes.shape[0]
+    lanes = n_dp * n_proto * rows
+    fits = (
+        n_proto == 2 * Y
+        and n_dp & (n_dp - 1) == 0
+        and rows % 4 == 0
+        and rows <= 16
+        and lanes % LANES == 0
+        and lanes <= 8 * LANES
+        and width == 2 * LANES
+        and protos == n_dp * 2 * LANES
+        and 4 * protos * lanes * 4 <= BLOCK_BYTES
+    )
+    plan = on_device_all_rows if fits else on_device_group_rows
+    return plan(student_feat, teacher_feat, prototypes, teacher_prototypes, live_count)
 
 
 def solution(mesh):

time: 137 us -> 45.1 us (0.33)
  blocking collectives: 101 us -> 0 us
  starting transfers between devices: 3.26 us -> 19.7 us
  between operations: 14.9 us -> 0.75 us
  Pallas kernels: 0 us -> 13.2 us
  other arithmetic: 9.41 us -> 1.51 us
  waiting for transfers between devices: 2.2 us -> 9.67 us
  local copies, waits for them, and re-layouts: 3.45 us -> 0.02 us
  matrix products: 2.56 us -> 0 us
    psum x6 -> x0, blocking collectives: 66.1 us -> none  [the longest x3 35.4 us: sample_totals(): return lax.psum(values, 'proto')]
    all_gather x2 -> x0, blocking collectives: 19.9 us -> none  [the longest x1 10.7 us: on_device(): lax.all_gather(student_unit.astype(jnp.bfloat16), 'proto', axis=0, tiled=...]
    ppermute x0 -> x15, starting transfers between devices: none -> 19.7 us  [the longest x12 14.8 us: swap(): return lax.ppermute(values, axis, others)]
    unnamed x1 -> x0, blocking collectives: 14.6 us -> none
    pallas_call x0 -> x9, Pallas kernels: none -> 13.2 us  [call(): pl.pallas_call(kernel, out_shape=out_shape, in_specs=[pl.BlockSpec(memory...]
    ppermute x0 -> x15, waiting for transfers between devices: none -> 9.67 us  [the longest x12 9.12 us: swap(): return lax.ppermute(values, axis, others)]
    reduce_sum x11 -> x0, other arithmetic: 4.61 us -> none  [the longest x4 2.4 us: unit_rows(): jnp.sum(widened * widened, axis=1, keepdims=True) + eps_norm]
    unnamed x2 -> x0, starting transfers between devices: 3.22 us -> none
  transfers between devices with their start and end apart: 3 -> 15, of which waited for: 1 -> 8; matrix products, arithmetic and copies ran while one was open for 12% -> 2% of each run, Pallas kernels for 0% -> 21%
where the time goes in v4:
time: 45.1 us; the launch traced here: 44.9 us
  starting transfers between devices  19.7 us (44%)
  Pallas kernels  13.2 us (29%)
  waiting for transfers between devices  9.67 us (21%)
  other arithmetic  1.51 us (3%)
  between operations  0.75 us (2%)
    ppermute x12, starting transfers between devices, swap(): return lax.ppermute(values, axis, others)  14.8 us
    pallas_call x9, Pallas kernels, call(): pl.pallas_call(kernel, out_shape=out_shape, in_specs=[pl.BlockSpec(memory...  13.2 us
    ppermute x12, waiting for transfers between devices, swap(): return lax.ppermute(values, axis, others)  9.12 us
    ppermute x3, starting transfers between devices, swap_dp(): return lax.ppermute(values, ('dp', 'proto'), others)  4.86 us
  transfers between devices with their start and end apart: 15, of which 8 were waited for; matrix products, arithmetic and copies ran while one was open for 2% of the time, Pallas kernels for 21%

profile of v4, /device:TPU:0, one launch (start us, length us, event | category | flops | bytes accessed | tf_op | source)
XLA Modules:
  0.0 44.9 jit_solution(17874442150603376175)
XLA Ops:
  0.6 0.7 %pad_maximum_fusion.3 = bf16[24,256]{1,0:T(8,128)(2,1)S(1)} fusion(bf16[12,256]{1,0:T(8,128)(2,1)} %refs_2_.1, bf16[12,256]{1,0:T(8,128)(2,1)} %param.6), kind=kLoop, calls=%fused_computation.3 | loop fusion | flops 24576 | bytes 24576 | tf_op jit(solution)/shard_map/concatenate | solution.py:381
  1.4 2.4 %collective-permute-start = (bf16[24,256]{1,0:T(8,128)(2,1)S(1)}, bf16[24,256]{1,0:T(8,128)(2,1)S(1)}, u32[]{:S(2)}, u32[]{:S(2)}) collective-permute-start(bf16[24,256]{1,0:T(8,128)(2,1)S(1)} %pad_maximum_fusion.3), channel_id=1, source_target_pairs={{0,3},{1,2},{2,1},{3,0},{4,7},{5,6},{6,5},{7,4},{8,11},{9,10},{10,... | collective-permute-start | bytes 36872 | tf_op jit(solution)/shard_map/ppermute | solution.py:350
  3.8 0.7 %pad_add_fusion.place_ref = s32[6]{0:T(128)S(1)} fusion(s32[4]{0:T(128)} %param.9, s32[1]{0:T(128)} %bitcast.1, s32[1]{0:T(128)} %bitcast), kind=kLoop, calls=%fused_computation.4 | loop fusion | flops 12 | bytes 48 | tf_op jit(solution)/shard_map/concatenate | solution.py:373
  5.2 4.2 %collective-permute-start.1 = (bf16[2,24,256]{2,1,0:T(8,128)(2,1)S(1)}, bf16[2,24,256]{2,1,0:T(8,128)(2,1)S(1)}, u32[]{:S(2)}, u32[]{:S(2)}) collective-permute-start(bf16[2,24,256]{2,1,0:T(8,128)(2,1)S(1)} %get-tuple-element.65), channel_id=1, source_target_pairs={{0,25},{1,24},{2,27},{3,26},{4,29},{5,28},{6,31},{7,30},{8,17},{9,... | collective-permute-start | bytes 73736 | tf_op jit(solution)/shard_map/ppermute | solution.py:358
  10.1 1.3 %shard_map.68.refs_0_ = bf16[1024,256]{1,0:T(8,128)(2,1)S(1)} custom-call(bf16[1024,256]{1,0:T(8,128)(2,1)} %refs_0_.2), custom_call_target="tpu_custom_call" | custom-call | flops 134217728 | bytes 1048576 | tf_op jit(solution)/shard_map/pallas_call | solution.py:335
  11.5 1.5 %collective-permute-start.8 = (bf16[1024,256]{1,0:T(8,128)(2,1)}, bf16[1024,256]{1,0:T(8,128)(2,1)S(1)}, u32[]{:S(2)}, u32[]{:S(2)}) collective-permute-start(bf16[1024,256]{1,0:T(8,128)(2,1)} %refs_0_.2), channel_id=1, source_target_pairs={{0,3},{1,2},{2,1},{3,0},{4,7},{5,6},{6,5},{7,4},{8,11},{9,10},{10,... | collective-permute-start | bytes 1572872 | tf_op jit(solution)/shard_map/ppermute | solution.py:350
  13.6 1.6 %collective-permute-start.4 = (bf16[4,2,24,256]{3,2,1,0:T(8,128)(2,1)S(1)}, bf16[4,2,24,256]{3,2,1,0:T(8,128)(2,1)S(1)}, u32[]{:S(2)}, u32[]{:S(2)}) collective-permute-start(bf16[4,2,24,256]{3,2,1,0:T(8,128)(2,1)S(1)} %get-tuple-element.63), channel_id=1, source_target_pairs={{0,5},{1,4},{2,7},{3,6},{4,1},{5,0},{6,3},{7,2},{8,13},{9,12},{10,... | collective-permute-start | bytes 294920 | tf_op jit(solution)/shard_map/ppermute | solution.py:350
  15.2 3.0 %collective-permute-done.4 = bf16[4,2,24,256]{3,2,1,0:T(8,128)(2,1)S(1)} collective-permute-done((bf16[4,2,24,256]{3,2,1,0:T(8,128)(2,1)S(1)}, bf16[4,2,24,256]{3,2,1,0:T(8,128)(2,1)S(1)}, u32[]{:S(2)}, u32[]{:S(2)}) %collective-permute-start.4) | collective-permute-done | bytes 98336 | tf_op jit(solution)/shard_map/ppermute | solution.py:350
  18.2 0.8 %collective-permute-start.5 = (bf16[2,4,2,24,256]{4,3,2,1,0:T(8,128)(2,1)S(1)}, bf16[2,4,2,24,256]{4,3,2,1,0:T(8,128)(2,1)S(1)}, u32[]{:S(2)}, u32[]{:S(2)}) collective-permute-start(bf16[2,4,2,24,256]{4,3,2,1,0:T(8,128)(2,1)S(1)} %pad_maximum_fusion.near_ref), channel_id=1, source_target_pairs={{0,1},{1,0},{2,3},{3,2},{4,5},{5,4},{6,7},{7,6},{8,9},{9,8},{10,11... | collective-permute-start | bytes 589832 | tf_op jit(solution)/shard_map/ppermute | solution.py:350
  18.9 1.1 %shard_map.69 = (f32[192,2048]{1,0:T(8,128)S(1)}, f32[8,2048]{1,0:T(8,128)S(1)}, bf16[192,256]{1,0:T(8,128)(2,1)S(1)}) custom-call(s32[6]{0:T(128)S(1)} %pad_add_fusion.place_ref, bf16[2,4,2,24,256]{4,3,2,1,0:T(8,128)(2,1)S(1)} %pad_maximum_fusion.near_ref, bf16[1024,256]{1,0:T(8,128)(2,1)S(1)} %shard_map.68.refs_0_, ...), custom_call_target="tpu_custom_call" | custom-call | flops 201326592 | bytes 1572864 | tf_op jit(solution)/shard_map/pallas_call | solution.py:335
  20.1 1.6 %shard_map.70 = (f32[192,2048]{1,0:T(8,128)S(1)}, bf16[384,256]{1,0:T(8,128)(2,1)S(1)}, f32[384,128]{1,0:T(8,128)S(1)}, f32[8,128]{1,0:T(8,128)S(1)}) custom-call(s32[6]{0:T(128)S(1)} %pad_add_fusion.place_ref, bf16[2,4,2,24,256]{4,3,2,1,0:T(8,128)(2,1)S(1)} %collective-permute-done.5.far_ref, bf16[192,256]{1,0:T(8,128)(2,1)S(1)} %get-tuple-element.35.near_rows_ref, ...), custom_call_target="tpu_custom_call" | custom-call | flops 201326592 | bytes 1572864 | tf_op jit(solution)/shard_map/pallas_call | solution.py:335
  21.6 1.5 %collective-permute-start.7 = (f32[8,128]{1,0:T(8,128)S(1)}, f32[8,128]{1,0:T(8,128)S(1)}, u32[]{:S(2)}, u32[]{:S(2)}) collective-permute-start(f32[8,128]{1,0:T(8,128)S(1)} %get-tuple-element.38), channel_id=1, source_target_pairs={{0,5},{1,4},{2,7},{3,6},{4,1},{5,0},{6,3},{7,2},{8,13},{9,12},{10,... | collective-permute-start | bytes 12296 | tf_op jit(solution)/shard_map/ppermute | solution.py:350
  23.1 1.6 %collective-permute-done.7 = f32[8,128]{1,0:T(8,128)S(1)} collective-permute-done((f32[8,128]{1,0:T(8,128)S(1)}, f32[8,128]{1,0:T(8,128)S(1)}, u32[]{:S(2)}, u32[]{:S(2)}) %collective-permute-start.7) | collective-permute-done | bytes 4128 | tf_op jit(solution)/shard_map/ppermute | solution.py:350
  25.8 1.7 %collective-permute-start.9 = (f32[8,128]{1,0:T(8,128)S(1)}, f32[8,128]{1,0:T(8,128)S(1)}, u32[]{:S(2)}, u32[]{:S(2)}) collective-permute-start(f32[8,128]{1,0:T(8,128)S(1)} %add.6.mine_ref), channel_id=1, source_target_pairs={{0,3},{1,2},{2,1},{3,0},{4,7},{5,6},{6,5},{7,4},{8,11},{9,10},{10,... | collective-permute-start | bytes 12296 | tf_op jit(solution)/shard_map/ppermute | solution.py:350
  27.5 0.9 %shard_map.71.across_ref = f32[384,2048]{1,0:T(8,128)S(1)} custom-call(bf16[384,256]{1,0:T(8,128)(2,1)S(1)} %get-tuple-element.41.rows_ref.teacher_rows_ref, f32[384,128]{1,0:T(8,128)S(1)} %get-tuple-element.42.live_ref, bf16[1024,256]{1,0:T(8,128)(2,1)S(1)} %collective-permute-done.8.refs_0_, bf16[1024,256]{1,0:T(8,128)(2,1)S(1)} %collective-permute-done.10.refs_1_), custom_call_target="tpu_custom_call" | custom-call | flops 402653184 | bytes 3145728 | tf_op jit(solution)/shard_map/pallas_call | solution.py:335
  28.9 1.5 %shard_map.72.mine_ref = f32[8,128]{1,0:T(8,128)S(1)} custom-call(f32[8,128]{1,0:T(8,128)S(1)} %add.6.mine_ref, f32[8,128]{1,0:T(8,128)S(1)} %collective-permute-done.9.other_ref, f32[192,2048]{1,0:T(8,128)S(1)} %get-tuple-element.36.near_weights_ref.near_ref, f32[192,2048]{1,0:T(8,128)S(1)} %get-tuple-element.40.far_ref, f32[384,2048]{1,0:T(8,128)S(1)} %shard_map.71.across_ref), custom_call_target="tpu_custom_call" | custom-call | flops 402653184 | bytes 3145728 | tf_op jit(solution)/shard_map/pallas_call | solution.py:335
  30.4 1.7 %collective-permute-start.12 = (f32[8,128]{1,0:T(8,128)S(1)}, f32[8,128]{1,0:T(8,128)S(1)}, u32[]{:S(2)}, u32[]{:S(2)}) collective-permute-start(f32[8,128]{1,0:T(8,128)S(1)} %shard_map.72.mine_ref), channel_id=1, source_target_pairs={{0,5},{1,4},{2,7},{3,6},{4,1},{5,0},{6,3},{7,2},{8,13},{9,12},{10,... | collective-permute-start | bytes 12296 | tf_op jit(solution)/shard_map/ppermute | solution.py:350
  32.1 1.8 %shard_map.73 = (bf16[384,256]{1,0:T(8,128)(2,1)S(1)}, bf16[2048,256]{1,0:T(8,128)(2,1)S(1)}, f32[48,256]{1,0:T(8,128)S(1)}, f32[8,128]{1,0:T(8,128)S(1)}) custom-call(s32[6]{0:T(128)S(1)} %pad_add_fusion.place_ref, bf16[2,4,2,24,256]{4,3,2,1,0:T(8,128)(2,1)S(1)} %pad_maximum_fusion.near_ref, bf16[2,4,2,24,256]{4,3,2,1,0:T(8,128)(2,1)S(1)} %collective-permute-done.5.far_ref, ...), custom_call_target="tpu_custom_call" | custom-call | flops 402653184 | bytes 3145728 | tf_op jit(solution)/shard_map/pallas_call | solution.py:335
  33.9 2.2 %shard_map.74 = (f32[56,256]{1,0:T(8,128)S(1)}, f32[56,256]{1,0:T(8,128)S(1)}) custom-call(s32[6]{0:T(128)S(1)} %pad_add_fusion.place_ref, f32[8,128]{1,0:T(8,128)S(1)} %shard_map.72.mine_ref, f32[8,128]{1,0:T(8,128)S(1)} %collective-permute-done.12.other_ref, f32[192,2048]{1,0:T(8,128)S(1)} %get-tuple-element.36.near_weights_ref.near_ref, ...), custom_call_target="tpu_custom_call" | custom-call | flops 402653184 | bytes 3145728 | tf_op jit(solution)/shard_map/pallas_call | solution.py:335
  36.1 1.5 %collective-permute-start.13 = (f32[56,256]{1,0:T(8,128)S(1)}, f32[56,256]{1,0:T(8,128)S(1)}, u32[]{:S(2)}, u32[]{:S(2)}) collective-permute-start(f32[56,256]{1,0:T(8,128)S(1)} %get-tuple-element.54), channel_id=1, source_target_pairs={{0,3},{1,2},{2,1},{3,0},{4,7},{5,6},{6,5},{7,4},{8,11},{9,10},{10,... | collective-permute-start | bytes 172040 | tf_op jit(solution)/shard_map/ppermute | solution.py:350
  37.6 2.3 %collective-permute-done.13 = f32[56,256]{1,0:T(8,128)S(1)} collective-permute-done((f32[56,256]{1,0:T(8,128)S(1)}, f32[56,256]{1,0:T(8,128)S(1)}, u32[]{:S(2)}, u32[]{:S(2)}) %collective-permute-start.13) | collective-permute-done | bytes 57376 | tf_op jit(solution)/shard_map/ppermute | solution.py:350
  39.9 1.4 %collective-permute-start.14 = (f32[32,256]{1,0:T(8,128)S(1)}, f32[32,256]{1,0:T(8,128)S(1)}, u32[]{:S(2)}, u32[]{:S(2)}) collective-permute-start(f32[32,256]{1,0:T(8,128)S(1)} %slice.4), channel_id=1, source_target_pairs={{0,5},{1,4},{2,7},{3,6},{4,1},{5,0},{6,3},{7,2},{8,13},{9,12},{10,... | collective-permute-start | bytes 98312 | tf_op jit(solution)/shard_map/ppermute | solution.py:350
  41.3 1.5 %shard_map.75 = (f32[256,384]{1,0:T(8,128)S(1)}, f32[256,384]{1,0:T(8,128)S(1)}, f32[256,256]{1,0:T(8,128)S(1)}, f32[256,128]{1,0:T(8,128)S(1)}) custom-call(s32[6]{0:T(128)S(1)} %pad_add_fusion.place_ref, f32[8,128]{1,0:T(8,128)S(1)} %shard_map.72.mine_ref, f32[8,128]{1,0:T(8,128)S(1)} %collective-permute-done.12.other_ref, ...), custom_call_target="tpu_custom_call" | custom-call | flops 50331648 | bytes 393216 | tf_op jit(solution)/shard_map/pallas_call | solution.py:335
  43.3 1.6 %shard_map.76 = (f32[12,256]{1,0:T(8,128)}, f32[1,256,256]{2,1,0:T(8,128)}) custom-call(s32[6]{0:T(128)S(1)} %pad_add_fusion.place_ref, f32[56,256]{1,0:T(8,128)S(1)} %add.7.mine_ref, f32[32,256]{1,0:T(8,128)S(1)} %collective-permute-done.14.other_ref, f32[256,384]{1,0:T(8,128)S(1)} %get-tuple-element.58.targets_ref, ...), custom_call_target="tpu_custom_call" | custom-call | flops 50331648 | bytes 393216 | tf_op jit(solution)/shard_map/pallas_call | solution.py:335
  (27 shorter events, 4.2 us)
Async XLA Ops:
  1.4 3.8 %collective-permute-start = (bf16[24,256]{1,0:T(8,128)(2,1)S(1)}, bf16[24,256]{1,0:T(8,128)(2,1)S(1)}, u32[]{:S(2)}, u32[]{:S(2)}) collective-permute-start(bf16[24,256]{1,0:T(8,128)(2,1)S(1)} %pad_maximum_fusion.3), channel_id=1, source_target_pairs={{0,3},{1,2},{2,1},{3,0},{4,7},{5,6},{6,5},{7,4},{8,11},{9,10},{10,... | collective-permute-start | bytes 36872 | tf_op jit(solution)/shard_map/ppermute | solution.py:350
  5.2 7.8 %collective-permute-start.1 = (bf16[2,24,256]{2,1,0:T(8,128)(2,1)S(1)}, bf16[2,24,256]{2,1,0:T(8,128)(2,1)S(1)}, u32[]{:S(2)}, u32[]{:S(2)}) collective-permute-start(bf16[2,24,256]{2,1,0:T(8,128)(2,1)S(1)} %get-tuple-element.65), channel_id=1, source_target_pairs={{0,25},{1,24},{2,27},{3,26},{4,29},{5,28},{6,31},{7,30},{8,17},{9,... | collective-permute-start | bytes 73736 | tf_op jit(solution)/shard_map/ppermute | solution.py:358
  9.4 4.2 %collective-permute-start.2 = (bf16[2,24,256]{2,1,0:T(8,128)(2,1)S(1)}, bf16[2,24,256]{2,1,0:T(8,128)(2,1)S(1)}, u32[]{:S(2)}, u32[]{:S(2)}) collective-permute-start(bf16[2,24,256]{2,1,0:T(8,128)(2,1)S(1)} %get-tuple-element.65), channel_id=1, source_target_pairs={{0,17},{1,16},{2,19},{3,18},{4,21},{5,20},{6,23},{7,22},{8,25},{9,... | collective-permute-start | bytes 73736 | tf_op jit(solution)/shard_map/ppermute | solution.py:358
  9.4 4.2 %collective-permute-start.3 = (bf16[2,24,256]{2,1,0:T(8,128)(2,1)S(1)}, bf16[2,24,256]{2,1,0:T(8,128)(2,1)S(1)}, u32[]{:S(2)}, u32[]{:S(2)}) collective-permute-start(bf16[2,24,256]{2,1,0:T(8,128)(2,1)S(1)} %get-tuple-element.65), channel_id=1, source_target_pairs={{0,9},{1,8},{2,11},{3,10},{4,13},{5,12},{6,15},{7,14},{8,1},{9,0},... | collective-permute-start | bytes 73736 | tf_op jit(solution)/shard_map/ppermute | solution.py:358
  11.3 7.6 %collective-permute-start.6 = (bf16[1024,256]{1,0:T(8,128)(2,1)S(1)}, bf16[1024,256]{1,0:T(8,128)(2,1)S(1)}, u32[]{:S(2)}, u32[]{:S(2)}) collective-permute-start(bf16[1024,256]{1,0:T(8,128)(2,1)S(1)} %shard_map.68.refs_0_), channel_id=1, source_target_pairs={{0,1},{1,0},{2,3},{3,2},{4,5},{5,4},{6,7},{7,6},{8,9},{9,8},{10,11... | collective-permute-start | bytes 1572872 | tf_op jit(solution)/shard_map/ppermute | solution.py:350
  11.5 13.9 %collective-permute-start.8 = (bf16[1024,256]{1,0:T(8,128)(2,1)}, bf16[1024,256]{1,0:T(8,128)(2,1)S(1)}, u32[]{:S(2)}, u32[]{:S(2)}) collective-permute-start(bf16[1024,256]{1,0:T(8,128)(2,1)} %refs_0_.2), channel_id=1, source_target_pairs={{0,3},{1,2},{2,1},{3,0},{4,7},{5,6},{6,5},{7,4},{8,11},{9,10},{10,... | collective-permute-start | bytes 1572872 | tf_op jit(solution)/shard_map/ppermute | solution.py:350
  13.6 4.6 %collective-permute-start.4 = (bf16[4,2,24,256]{3,2,1,0:T(8,128)(2,1)S(1)}, bf16[4,2,24,256]{3,2,1,0:T(8,128)(2,1)S(1)}, u32[]{:S(2)}, u32[]{:S(2)}) collective-permute-start(bf16[4,2,24,256]{3,2,1,0:T(8,128)(2,1)S(1)} %get-tuple-element.63), channel_id=1, source_target_pairs={{0,5},{1,4},{2,7},{3,6},{4,1},{5,0},{6,3},{7,2},{8,13},{9,12},{10,... | collective-permute-start | bytes 294920 | tf_op jit(solution)/shard_map/ppermute | solution.py:350
  18.2 1.9 %collective-permute-start.5 = (bf16[2,4,2,24,256]{4,3,2,1,0:T(8,128)(2,1)S(1)}, bf16[2,4,2,24,256]{4,3,2,1,0:T(8,128)(2,1)S(1)}, u32[]{:S(2)}, u32[]{:S(2)}) collective-permute-start(bf16[2,4,2,24,256]{4,3,2,1,0:T(8,128)(2,1)S(1)} %pad_maximum_fusion.near_ref), channel_id=1, source_target_pairs={{0,1},{1,0},{2,3},{3,2},{4,5},{5,4},{6,7},{7,6},{8,9},{9,8},{10,11... | collective-permute-start | bytes 589832 | tf_op jit(solution)/shard_map/ppermute | solution.py:350
  20.0 5.7 %copy-start = (bf16[1024,256]{1,0:T(8,128)(2,1)S(1)}, bf16[1024,256]{1,0:T(8,128)(2,1)}, u32[]{:S(2)}) copy-start(bf16[1024,256]{1,0:T(8,128)(2,1)} %refs_1_.1) | copy-start | bytes 1572868
  21.6 3.1 %collective-permute-start.7 = (f32[8,128]{1,0:T(8,128)S(1)}, f32[8,128]{1,0:T(8,128)S(1)}, u32[]{:S(2)}, u32[]{:S(2)}) collective-permute-start(f32[8,128]{1,0:T(8,128)S(1)} %get-tuple-element.38), channel_id=1, source_target_pairs={{0,5},{1,4},{2,7},{3,6},{4,1},{5,0},{6,3},{7,2},{8,13},{9,12},{10,... | collective-permute-start | bytes 12296 | tf_op jit(solution)/shard_map/ppermute | solution.py:350
  25.3 2.2 %collective-permute-start.10 = (bf16[1024,256]{1,0:T(8,128)(2,1)S(1)}, bf16[1024,256]{1,0:T(8,128)(2,1)S(1)}, u32[]{:S(2)}, u32[]{:S(2)}) collective-permute-start(bf16[1024,256]{1,0:T(8,128)(2,1)S(1)} %collective-permute-done.8.refs_0_), channel_id=1, source_target_pairs={{0,1},{1,0},{2,3},{3,2},{4,5},{5,4},{6,7},{7,6},{8,9},{9,8},{10,11... | collective-permute-start | bytes 1572872 | tf_op jit(solution)/shard_map/ppermute | solution.py:350
  25.7 4.6 %collective-permute-start.11 = (bf16[1024,256]{1,0:T(8,128)(2,1)S(1)}, bf16[1024,256]{1,0:T(8,128)(2,1)S(1)}, u32[]{:S(2)}, u32[]{:S(2)}) collective-permute-start(bf16[1024,256]{1,0:T(8,128)(2,1)S(1)} %copy-done), channel_id=1, source_target_pairs={{0,1},{1,0},{2,3},{3,2},{4,5},{5,4},{6,7},{7,6},{8,9},{9,8},{10,11... | collective-permute-start | bytes 1572872 | tf_op jit(solution)/shard_map/ppermute | solution.py:350
  25.8 3.1 %collective-permute-start.9 = (f32[8,128]{1,0:T(8,128)S(1)}, f32[8,128]{1,0:T(8,128)S(1)}, u32[]{:S(2)}, u32[]{:S(2)}) collective-permute-start(f32[8,128]{1,0:T(8,128)S(1)} %add.6.mine_ref), channel_id=1, source_target_pairs={{0,3},{1,2},{2,1},{3,0},{4,7},{5,6},{6,5},{7,4},{8,11},{9,10},{10,... | collective-permute-start | bytes 12296 | tf_op jit(solution)/shard_map/ppermute | solution.py:350
  30.4 3.5 %collective-permute-start.12 = (f32[8,128]{1,0:T(8,128)S(1)}, f32[8,128]{1,0:T(8,128)S(1)}, u32[]{:S(2)}, u32[]{:S(2)}) collective-permute-start(f32[8,128]{1,0:T(8,128)S(1)} %shard_map.72.mine_ref), channel_id=1, source_target_pairs={{0,5},{1,4},{2,7},{3,6},{4,1},{5,0},{6,3},{7,2},{8,13},{9,12},{10,... | collective-permute-start | bytes 12296 | tf_op jit(solution)/shard_map/ppermute | solution.py:350
  36.0 7.3 %copy-start.1 = (bf16[12,256]{1,0:T(8,128)(2,1)S(1)}, bf16[12,256]{1,0:T(8,128)(2,1)}, u32[]{:S(2)}) copy-start(bf16[12,256]{1,0:T(8,128)(2,1)} %refs_2_.1) | copy-start | bytes 18436
  36.1 3.8 %collective-permute-start.13 = (f32[56,256]{1,0:T(8,128)S(1)}, f32[56,256]{1,0:T(8,128)S(1)}, u32[]{:S(2)}, u32[]{:S(2)}) collective-permute-start(f32[56,256]{1,0:T(8,128)S(1)} %get-tuple-element.54), channel_id=1, source_target_pairs={{0,3},{1,2},{2,1},{3,0},{4,7},{5,6},{6,5},{7,4},{8,11},{9,10},{10,... | collective-permute-start | bytes 172040 | tf_op jit(solution)/shard_map/ppermute | solution.py:350
  39.9 3.4 %collective-permute-start.14 = (f32[32,256]{1,0:T(8,128)S(1)}, f32[32,256]{1,0:T(8,128)S(1)}, u32[]{:S(2)}, u32[]{:S(2)}) collective-permute-start(f32[32,256]{1,0:T(8,128)S(1)} %slice.4), channel_id=1, source_target_pairs={{0,5},{1,4},{2,7},{3,6},{4,1},{5,0},{6,3},{7,2},{8,13},{9,12},{10,... | collective-permute-start | bytes 98312 | tf_op jit(solution)/shard_map/ppermute | solution.py:350

commit v5 on v4

--- a/solution.py
+++ b/solution.py
@@ -123,7 +123,7 @@
             part_ref[to, :] = part_ref[to, :] + total if add else total
             return 0
 
-        lax.fori_loop(0, ref.shape[0] // 8, body, 0, unroll=4)
+        lax.fori_loop(0, ref.shape[0] // 8, body, 0, unroll=8)
         top += ref.shape[0]
 
 
@@ -140,7 +140,7 @@
                 total + ref[at, k * LANES : (k + 1) * LANES] * row for k, total in enumerate(sums)
             ]
 
-        sums = lax.fori_loop(0, ref.shape[0] // 8, body, sums, unroll=4)
+        sums = lax.fori_loop(0, ref.shape[0] // 8, body, sums, unroll=8)
         top += ref.shape[0]
     for k, total in enumerate(sums):
         inverse = 1.0 / jnp.sum(total, axis=0, keepdims=True)
@@ -162,13 +162,15 @@
 
 
 def near_kernel(chunk, place_ref, near_ref, *refs):
-    *unit_refs, weights_ref, sums_ref, rows_ref, scratch = refs
+    *unit_refs, weights_ref, sums_ref, rows_ref, live_ref, scratch = refs
     half = rows_ref.shape[0]
     rows = near_ref.shape[3] // 2
     protos = unit_refs[0].shape[0]
     rows_near = place_rows(place_ref, near_ref, 0, rows, scratch)
     rows_ref[...] = rows_near
-    live = twice(as_column(live_lanes(place_ref, 0, half, near_ref.shape[1], rows)))
+    live = as_column(live_lanes(place_ref, 0, half, near_ref.shape[1], rows))
+    live_ref[...] = live
+    live = twice(live)
     for k, unit_ref in enumerate(unit_refs):
         for start in range(0, protos, chunk):
             at = slice(k * protos + start, k * protos + start + chunk)
@@ -183,10 +185,9 @@
     rows = far_ref.shape[3] // 2
     protos = unit_refs[0].shape[0]
     rows_far = place_rows(place_ref, far_ref, 0, rows, scratch)
-    rows_ref[:half, :] = near_rows_ref[...]
-    rows_ref[half:, :] = rows_far
+    rows_ref[...] = rows_far
     live = as_column(live_lanes(place_ref, 1, half, far_ref.shape[1], rows))
-    live_ref[half:, :] = live
+    live_ref[...] = live
     for k, unit_ref in enumerate(unit_refs):
         for start in range(0, protos, chunk):
             at = slice(k * protos + start, k * protos + start + chunk)
@@ -196,14 +197,13 @@
             scale_ref[:, at] = jnp.broadcast_to(inverse, (8, chunk))
     weighted_rows([near_weights_ref, weights_ref], 0, scale_ref, part_ref)
     sums_ref[...] = as_tile(part_ref[...])
-    live_ref[:half, :] = as_column(live_lanes(place_ref, 0, half, far_ref.shape[1], rows))
-
-
-def across_kernel(chunk, rows_ref, live_ref, *refs):
+
+
+def across_kernel(chunk, near_rows_ref, far_rows_ref, near_live_ref, far_live_ref, *refs):
     *proto_refs, weights_ref = refs
     protos = proto_refs[0].shape[0]
-    rows_all = rows_ref[...]
-    live = twice(live_ref[...])
+    rows_all = jnp.concatenate([near_rows_ref[...], far_rows_ref[...]], axis=0)
+    live = twice(jnp.concatenate([near_live_ref[...], far_live_ref[...]], axis=0))
     for k, proto_ref in enumerate(proto_refs):
         for start in range(0, protos, chunk):
             units = quick_unit(proto_ref[start : start + chunk, :])[0].astype(jnp.bfloat16)
@@ -211,19 +211,23 @@
             weights_ref[:, at], _ = weights_of(rows_all, units, live)
 
 
-def sweep(sums, near_ref, far_ref, across_ref, row_ref, scale_ref, part_ref):
-    held = near_ref.shape[1]
+def scale_columns(sums, near_ref, far_ref, across_ref, row_ref, scale_ref):
     row_ref[...] = as_column(inverse_rows(sums, row_ref.shape[0]))
-    own = [near_ref, far_ref]
-    column_scales(own, 0, row_ref, scale_ref)
-    column_scales([across_ref], held, row_ref, scale_ref)
-    weighted_rows(own, 0, scale_ref, part_ref)
-    weighted_rows([across_ref], held, scale_ref, part_ref, add=True)
+    column_scales([near_ref, far_ref], 0, row_ref, scale_ref)
+    column_scales([across_ref], near_ref.shape[1], row_ref, scale_ref)
+
+
+def next_sums(near_ref, far_ref, across_ref, scale_ref, part_ref):
+    weighted_rows([near_ref, far_ref], 0, scale_ref, part_ref)
+    weighted_rows([across_ref], near_ref.shape[1], scale_ref, part_ref, add=True)
     return as_tile(part_ref[...])
 
 
 def step_kernel(mine_ref, other_ref, near_ref, far_ref, across_ref, sums_ref, *scratch):
-    sums_ref[...] = sweep(mine_ref[...] + other_ref[...], near_ref, far_ref, across_ref, *scratch)
+    row_ref, scale_ref, part_ref = scratch
+    sums = mine_ref[...] + other_ref[...]
+    scale_columns(sums, near_ref, far_ref, across_ref, row_ref, scale_ref)
+    sums_ref[...] = next_sums(near_ref, far_ref, across_ref, scale_ref, part_ref)
 
 
 def split(values):
@@ -257,10 +261,10 @@
 
 
 def last_kernel(chunk, rows, place_ref, mine_ref, other_ref, near_ref, far_ref, across_ref, *refs):
-    units_ref, exp_pull_ref, exp_sums_ref, keep_ref, send_ref, *scratch, blocks_ref = refs
-    scale_ref = scratch[1]
+    units_ref, exp_pull_ref, exp_sums_ref, scale_ref, keep_ref, send_ref, row_ref, blocks_ref = refs
     first = exp_pull_ref.shape[0]
-    sums = sweep(mine_ref[...] + other_ref[...], near_ref, far_ref, across_ref, *scratch)
+    sums = mine_ref[...] + other_ref[...]
+    scale_columns(sums, near_ref, far_ref, across_ref, row_ref, scale_ref)
     pull = jnp.zeros((2 * first, exp_pull_ref.shape[1]), jnp.float32)
     for start in range(0, units_ref.shape[0], chunk):
         at = slice(start, start + chunk)
@@ -277,18 +281,24 @@
                 start = (2 * j + k) * rows
                 ref[start : start + rows, :] = blocks_ref[k, block_of(owner), :rows, :]
         ref[4 * rows :, :LANES] = exp_sums_ref[...]
-    keep_ref[4 * rows :, LANES:] = sums
-    send_ref[4 * rows :, LANES:] = jnp.zeros_like(sums)
-
-
-def own_kernel(place_ref, mine_ref, other_ref, teacher_rows_ref, student_rows_ref, *refs):
-    teacher_proto_ref, proto_ref, targets_ref, exps_ref, unit_ref, scale_ref = refs
+        ref[4 * rows :, LANES:] = jnp.zeros_like(exp_sums_ref)
+
+
+def last_sums_kernel(near_ref, far_ref, across_ref, scale_ref, sums_ref, part_ref):
+    sums_ref[:, :LANES] = jnp.zeros_like(sums_ref[:, :LANES])
+    sums_ref[:, LANES:] = next_sums(near_ref, far_ref, across_ref, scale_ref, part_ref)
+
+
+def own_kernel(place_ref, mine_ref, other_ref, near_rows_ref, far_rows_ref, *refs):
+    student_rows_ref, teacher_proto_ref, proto_ref, *refs = refs
+    targets_ref, exps_ref, unit_ref, scale_ref = refs
+    teacher_rows = jnp.concatenate([near_rows_ref[...], far_rows_ref[...]], axis=0)
     own, all_rows = targets_ref.shape
     row_scale = inverse_rows(mine_ref[...] + other_ref[...], all_rows)
     live = jnp.where(row_scale > 0.0, 1.0, 0.0)
     first = pl.ds(pl.multiple_of(place_ref[0] * own, own), own)
     units = quick_unit(teacher_proto_ref[first, :])[0].astype(jnp.bfloat16)
-    weights = jnp.exp(scores_of(units, teacher_rows_ref[...]) * (1 / teacher_temp)) * live
+    weights = jnp.exp(scores_of(units, teacher_rows) * (1 / teacher_temp)) * live
     inverse = 1.0 / jnp.sum(weights * row_scale, axis=1, keepdims=True)
     targets_ref[...] = weights * (inverse * (1 / student_temp))
     unit, scale = quick_unit(proto_ref[first, :])
@@ -299,11 +309,11 @@
     exps_ref[...] = exps * (1 / student_temp)
 
 
-def grads_kernel(place_ref, mine_ref, other_ref, targets_ref, exps_ref, unit_ref, *refs):
-    scale_ref, rows_ref, feat_ref, student_out_ref, proto_out_ref = refs
+def grads_kernel(place_ref, mine_ref, sums_ref, other_ref, targets_ref, exps_ref, *refs):
+    unit_ref, scale_ref, rows_ref, feat_ref, student_out_ref, proto_out_ref = refs
     all_rows = targets_ref.shape[1]
     rows = feat_ref.shape[0]
-    sums = mine_ref[4 * rows :, :] + other_ref[2 * rows :, :]
+    sums = sums_ref[...] + other_ref[2 * rows :, :]
     target_scale = inverse_rows(sums[:, LANES:], all_rows)
     exp_scale = jnp.where(target_scale > 0.0, 1.0 / unpack_lanes(sums[:, :LANES], all_rows), 0.0)
 
@@ -390,17 +400,17 @@
     near = jnp.stack([near, swap(near, "proto", Y_CROSS)])
     far = swap(near, "proto", CORE)
 
-    near_weights, near_sums, near_rows = call(
+    near_weights, near_sums, near_rows, near_live = call(
         functools.partial(near_kernel, own),
-        (f32((half, held)), f32((8, held)), bf16((half, width))),
+        (f32((half, held)), f32((8, held)), bf16((half, width)), f32((half, LANES))),
         (place, near, *teacher_units),
         smem=1,
         scratch=[row_scratch],
         work=held * half,
     )
-    far_weights, teacher_rows, live, sums = call(
+    far_weights, far_rows, far_live, sums = call(
         functools.partial(far_kernel, own),
-        (f32((half, held)), bf16((all_rows, width)), f32((all_rows, LANES)), tile),
+        (f32((half, held)), bf16((half, width)), f32((half, LANES)), tile),
         (place, far, near_rows, near_weights, near_sums, *teacher_units),
         smem=1,
         scratch=[row_scratch, scale_row, column],
@@ -412,7 +422,7 @@
     across_weights = call(
         functools.partial(across_kernel, own),
         f32((all_rows, held)),
-        (teacher_rows, live, across_protos, swap(across_protos, "proto", CORE)),
+        (near_rows, far_rows, near_live, far_live, across_protos, swap(across_protos, "proto", CORE)),
         work=held * all_rows,
     )
     weights = (near_weights, far_weights, across_weights)
@@ -436,30 +446,39 @@
         scratch=[row_scratch, pltpu.VMEM((all_rows, own), jnp.float32)],
         work=held * all_rows,
     )
-    keep, send = call(
+    scales, keep, send = call(
         functools.partial(last_kernel, own, rows),
-        (message, message),
+        (f32((8, 2 * held)), message, message),
         (place, *parts, *weights, student_units, exp_pull, exp_sums),
         smem=1,
-        scratch=[*sweep_scratch, pltpu.VMEM((2, 4, 16, width), jnp.float32)],
+        scratch=[column, pltpu.VMEM((2, 4, 16, width), jnp.float32)],
+        work=held * all_rows,
+    )
+    last_sums = call(
+        last_sums_kernel,
+        f32((8, width)),
+        (*weights, scales),
+        scratch=[column],
         work=held * all_rows,
     )
     *parts, send = lax.optimization_barrier((*parts, send))
     targets, exps, own_units, own_scales = call(
         own_kernel,
         (f32((own, all_rows)), f32((own, all_rows)), f32((own, width)), f32((own, LANES))),
-        (place, *parts, teacher_rows, student_rows, teacher_prototypes, prototypes),
+        (place, *parts, near_rows, far_rows, student_rows, teacher_prototypes, prototypes),
         smem=1,
         work=own * all_rows,
     )
     total = keep + swap(send, "proto", X_CROSS)
+    last_sums = total[4 * rows :] + last_sums
     return call(
         grads_kernel,
         (f32((rows, width)), f32((1, own, width))),
         (
             place,
             total,
-            swap(total[2 * rows :], "proto", Y_CROSS),
+            last_sums,
+            swap(jnp.concatenate([total[2 * rows : 4 * rows], last_sums]), "proto", Y_CROSS),
             targets,
             exps,
             own_units,

time: 45.1 us -> 44.3 us (0.982)
  waiting for transfers between devices: 9.67 us -> 9.08 us
    ppermute x12, waiting for transfers between devices: 9.12 us -> 8.54 us  [swap(): return lax.ppermute(values, axis, others)]
    pallas_call x9 -> x10, Pallas kernels: 13.2 us -> 13 us  [call(): pl.pallas_call(kernel, out_shape=out_shape, in_specs=[pl.BlockSpec(memory...]
  transfers between devices with their start and end apart: 15 -> 15, of which waited for: 8 -> 8; matrix products, arithmetic and copies ran while one was open for 2% -> 2% of each run, Pallas kernels for 21% -> 23%
where the time goes in v5:
time: 44.3 us; the launch traced here: 44 us
  starting transfers between devices  19.7 us (44%)
  Pallas kernels  13 us (29%)
  waiting for transfers between devices  9.08 us (20%)
  other arithmetic  1.52 us (3%)
  between operations  0.76 us (2%)
    ppermute x12, starting transfers between devices, swap(): return lax.ppermute(values, axis, others)  14.8 us
    pallas_call x10, Pallas kernels, call(): pl.pallas_call(kernel, out_shape=out_shape, in_specs=[pl.BlockSpec(memory...  13 us
    ppermute x12, waiting for transfers between devices, swap(): return lax.ppermute(values, axis, others)  8.54 us
    ppermute x3, starting transfers between devices, swap_dp(): return lax.ppermute(values, ('dp', 'proto'), others)  4.86 us
  transfers between devices with their start and end apart: 15, of which 8 were waited for; matrix products, arithmetic and copies ran while one was open for 2% of the time, Pallas kernels for 23%

profile of v5, /device:TPU:0, one launch (start us, length us, event | category | flops | bytes accessed | tf_op | source)
XLA Modules:
  0.0 44.0 jit_solution(12159474816606542769)
XLA Ops:
  0.6 0.7 %pad_maximum_fusion.4 = bf16[24,256]{1,0:T(8,128)(2,1)S(1)} fusion(bf16[12,256]{1,0:T(8,128)(2,1)} %refs_3_.1, bf16[12,256]{1,0:T(8,128)(2,1)} %param.6), kind=kLoop, calls=%fused_computation.4 | loop fusion | flops 24576 | bytes 24576 | tf_op jit(solution)/shard_map/concatenate | solution.py:391
  1.4 2.4 %collective-permute-start = (bf16[24,256]{1,0:T(8,128)(2,1)S(1)}, bf16[24,256]{1,0:T(8,128)(2,1)S(1)}, u32[]{:S(2)}, u32[]{:S(2)}) collective-permute-start(bf16[24,256]{1,0:T(8,128)(2,1)S(1)} %pad_maximum_fusion.4), channel_id=1, source_target_pairs={{0,3},{1,2},{2,1},{3,0},{4,7},{5,6},{6,5},{7,4},{8,11},{9,10},{10,... | collective-permute-start | bytes 36872 | tf_op jit(solution)/shard_map/ppermute | solution.py:360
  3.8 0.7 %pad_add_fusion.place_ref = s32[6]{0:T(128)S(1)} fusion(s32[4]{0:T(128)} %param.9, s32[1]{0:T(128)} %bitcast.1, s32[1]{0:T(128)} %bitcast), kind=kLoop, calls=%fused_computation.6 | loop fusion | flops 12 | bytes 48 | tf_op jit(solution)/shard_map/concatenate | solution.py:383
  5.2 4.2 %collective-permute-start.1 = (bf16[2,24,256]{2,1,0:T(8,128)(2,1)S(1)}, bf16[2,24,256]{2,1,0:T(8,128)(2,1)S(1)}, u32[]{:S(2)}, u32[]{:S(2)}) collective-permute-start(bf16[2,24,256]{2,1,0:T(8,128)(2,1)S(1)} %get-tuple-element.69), channel_id=1, source_target_pairs={{0,25},{1,24},{2,27},{3,26},{4,29},{5,28},{6,31},{7,30},{8,17},{9,... | collective-permute-start | bytes 73736 | tf_op jit(solution)/shard_map/ppermute | solution.py:368
  10.1 1.3 %shard_map.68.refs_0_ = bf16[1024,256]{1,0:T(8,128)(2,1)S(1)} custom-call(bf16[1024,256]{1,0:T(8,128)(2,1)} %refs_1_.1), custom_call_target="tpu_custom_call" | custom-call | flops 134217728 | bytes 1048576 | tf_op jit(solution)/shard_map/pallas_call | solution.py:345
  11.5 1.5 %collective-permute-start.8 = (bf16[1024,256]{1,0:T(8,128)(2,1)}, bf16[1024,256]{1,0:T(8,128)(2,1)S(1)}, u32[]{:S(2)}, u32[]{:S(2)}) collective-permute-start(bf16[1024,256]{1,0:T(8,128)(2,1)} %refs_1_.1), channel_id=1, source_target_pairs={{0,3},{1,2},{2,1},{3,0},{4,7},{5,6},{6,5},{7,4},{8,11},{9,10},{10,... | collective-permute-start | bytes 1572872 | tf_op jit(solution)/shard_map/ppermute | solution.py:360
  13.6 1.6 %collective-permute-start.4 = (bf16[4,2,24,256]{3,2,1,0:T(8,128)(2,1)S(1)}, bf16[4,2,24,256]{3,2,1,0:T(8,128)(2,1)S(1)}, u32[]{:S(2)}, u32[]{:S(2)}) collective-permute-start(bf16[4,2,24,256]{3,2,1,0:T(8,128)(2,1)S(1)} %get-tuple-element.67), channel_id=1, source_target_pairs={{0,5},{1,4},{2,7},{3,6},{4,1},{5,0},{6,3},{7,2},{8,13},{9,12},{10,... | collective-permute-start | bytes 294920 | tf_op jit(solution)/shard_map/ppermute | solution.py:360
  15.2 3.0 %collective-permute-done.4 = bf16[4,2,24,256]{3,2,1,0:T(8,128)(2,1)S(1)} collective-permute-done((bf16[4,2,24,256]{3,2,1,0:T(8,128)(2,1)S(1)}, bf16[4,2,24,256]{3,2,1,0:T(8,128)(2,1)S(1)}, u32[]{:S(2)}, u32[]{:S(2)}) %collective-permute-start.4) | collective-permute-done | bytes 98336 | tf_op jit(solution)/shard_map/ppermute | solution.py:360
  18.2 0.8 %collective-permute-start.5 = (bf16[2,4,2,24,256]{4,3,2,1,0:T(8,128)(2,1)S(1)}, bf16[2,4,2,24,256]{4,3,2,1,0:T(8,128)(2,1)S(1)}, u32[]{:S(2)}, u32[]{:S(2)}) collective-permute-start(bf16[2,4,2,24,256]{4,3,2,1,0:T(8,128)(2,1)S(1)} %pad_maximum_fusion.near_ref), channel_id=1, source_target_pairs={{0,1},{1,0},{2,3},{3,2},{4,5},{5,4},{6,7},{7,6},{8,9},{9,8},{10,11... | collective-permute-start | bytes 589832 | tf_op jit(solution)/shard_map/ppermute | solution.py:360
  18.9 1.1 %shard_map.69 = (f32[192,2048]{1,0:T(8,128)S(1)}, f32[8,2048]{1,0:T(8,128)S(1)}, bf16[192,256]{1,0:T(8,128)(2,1)S(1)}, f32[192,128]{1,0:T(8,128)S(1)}) custom-call(s32[6]{0:T(128)S(1)} %pad_add_fusion.place_ref, bf16[2,4,2,24,256]{4,3,2,1,0:T(8,128)(2,1)S(1)} %pad_maximum_fusion.near_ref, bf16[1024,256]{1,0:T(8,128)(2,1)S(1)} %shard_map.68.refs_0_, ...), custom_call_target="tpu_custom_call" | custom-call | flops 201326592 | bytes 1572864 | tf_op jit(solution)/shard_map/pallas_call | solution.py:345
  20.1 1.5 %shard_map.70 = (f32[192,2048]{1,0:T(8,128)S(1)}, bf16[192,256]{1,0:T(8,128)(2,1)S(1)}, f32[192,128]{1,0:T(8,128)S(1)}, f32[8,128]{1,0:T(8,128)S(1)}) custom-call(s32[6]{0:T(128)S(1)} %pad_add_fusion.place_ref, bf16[2,4,2,24,256]{4,3,2,1,0:T(8,128)(2,1)S(1)} %collective-permute-done.5.far_ref, bf16[192,256]{1,0:T(8,128)(2,1)S(1)} %get-tuple-element.37.near_rows_ref, ...), custom_call_target="tpu_custom_call" | custom-call | flops 201326592 | bytes 1572864 | tf_op jit(solution)/shard_map/pallas_call | solution.py:345
  21.6 1.5 %collective-permute-start.7 = (f32[8,128]{1,0:T(8,128)S(1)}, f32[8,128]{1,0:T(8,128)S(1)}, u32[]{:S(2)}, u32[]{:S(2)}) collective-permute-start(f32[8,128]{1,0:T(8,128)S(1)} %get-tuple-element.40), channel_id=1, source_target_pairs={{0,5},{1,4},{2,7},{3,6},{4,1},{5,0},{6,3},{7,2},{8,13},{9,12},{10,... | collective-permute-start | bytes 12296 | tf_op jit(solution)/shard_map/ppermute | solution.py:360
  23.1 1.6 %collective-permute-done.7 = f32[8,128]{1,0:T(8,128)S(1)} collective-permute-done((f32[8,128]{1,0:T(8,128)S(1)}, f32[8,128]{1,0:T(8,128)S(1)}, u32[]{:S(2)}, u32[]{:S(2)}) %collective-permute-start.7) | collective-permute-done | bytes 4128 | tf_op jit(solution)/shard_map/ppermute | solution.py:360
  25.8 1.7 %collective-permute-start.9 = (f32[8,128]{1,0:T(8,128)S(1)}, f32[8,128]{1,0:T(8,128)S(1)}, u32[]{:S(2)}, u32[]{:S(2)}) collective-permute-start(f32[8,128]{1,0:T(8,128)S(1)} %add.9.mine_ref), channel_id=1, source_target_pairs={{0,3},{1,2},{2,1},{3,0},{4,7},{5,6},{6,5},{7,4},{8,11},{9,10},{10,... | collective-permute-start | bytes 12296 | tf_op jit(solution)/shard_map/ppermute | solution.py:360
  27.5 0.9 %shard_map.71.across_ref = f32[384,2048]{1,0:T(8,128)S(1)} custom-call(bf16[192,256]{1,0:T(8,128)(2,1)S(1)} %get-tuple-element.37.near_rows_ref, bf16[192,256]{1,0:T(8,128)(2,1)S(1)} %get-tuple-element.43.far_rows_ref, f32[192,128]{1,0:T(8,128)S(1)} %get-tuple-element.44.near_live_ref, f32[192,128]{1,0:T(8,128)S(1)} %get-tuple-element.45.far_live_ref, ...), custom_call_target="tpu_custom_call" | custom-call | flops 402653184 | bytes 3145728 | tf_op jit(solution)/shard_map/pallas_call | solution.py:345
  28.9 1.3 %shard_map.72.mine_ref = f32[8,128]{1,0:T(8,128)S(1)} custom-call(f32[8,128]{1,0:T(8,128)S(1)} %add.9.mine_ref, f32[8,128]{1,0:T(8,128)S(1)} %collective-permute-done.9.other_ref, f32[192,2048]{1,0:T(8,128)S(1)} %get-tuple-element.38.near_weights_ref.near_ref, f32[192,2048]{1,0:T(8,128)S(1)} %get-tuple-element.42.far_ref, f32[384,2048]{1,0:T(8,128)S(1)} %shard_map.71.across_ref), custom_call_target="tpu_custom_call" | custom-call | flops 402653184 | bytes 3145728 | tf_op jit(solution)/shard_map/pallas_call | solution.py:345
  30.2 1.7 %collective-permute-start.12 = (f32[8,128]{1,0:T(8,128)S(1)}, f32[8,128]{1,0:T(8,128)S(1)}, u32[]{:S(2)}, u32[]{:S(2)}) collective-permute-start(f32[8,128]{1,0:T(8,128)S(1)} %shard_map.72.mine_ref), channel_id=1, source_target_pairs={{0,5},{1,4},{2,7},{3,6},{4,1},{5,0},{6,3},{7,2},{8,13},{9,12},{10,... | collective-permute-start | bytes 12296 | tf_op jit(solution)/shard_map/ppermute | solution.py:360
  31.9 1.8 %shard_map.73 = (bf16[384,256]{1,0:T(8,128)(2,1)S(1)}, bf16[2048,256]{1,0:T(8,128)(2,1)S(1)}, f32[48,256]{1,0:T(8,128)S(1)}, f32[8,128]{1,0:T(8,128)S(1)}) custom-call(s32[6]{0:T(128)S(1)} %pad_add_fusion.place_ref, bf16[2,4,2,24,256]{4,3,2,1,0:T(8,128)(2,1)S(1)} %pad_maximum_fusion.near_ref, bf16[2,4,2,24,256]{4,3,2,1,0:T(8,128)(2,1)S(1)} %collective-permute-done.5.far_ref, ...), custom_call_target="tpu_custom_call" | custom-call | flops 402653184 | bytes 3145728 | tf_op jit(solution)/shard_map/pallas_call | solution.py:345
  33.7 1.5 %shard_map.74 = (f32[8,4096]{1,0:T(8,128)S(1)}, f32[56,256]{1,0:T(8,128)S(1)}, f32[56,256]{1,0:T(8,128)S(1)}) custom-call(s32[6]{0:T(128)S(1)} %pad_add_fusion.place_ref, f32[8,128]{1,0:T(8,128)S(1)} %shard_map.72.mine_ref, f32[8,128]{1,0:T(8,128)S(1)} %collective-permute-done.12.other_ref, f32[192,2048]{1,0:T(8,128)S(1)} %get-tuple-element.38.near_weights_ref.near_ref, ...), custom_call_target="tpu_custom_call" | custom-call | flops 402653184 | bytes 3145728 | tf_op jit(solution)/shard_map/pallas_call | solution.py:345
  35.2 1.5 %collective-permute-start.13 = (f32[56,256]{1,0:T(8,128)S(1)}, f32[56,256]{1,0:T(8,128)S(1)}, u32[]{:S(2)}, u32[]{:S(2)}) collective-permute-start(f32[56,256]{1,0:T(8,128)S(1)} %get-tuple-element.57), channel_id=1, source_target_pairs={{0,3},{1,2},{2,1},{3,0},{4,7},{5,6},{6,5},{7,4},{8,11},{9,10},{10,... | collective-permute-start | bytes 172040 | tf_op jit(solution)/shard_map/ppermute | solution.py:360
  37.4 1.7 %collective-permute-done.13 = f32[56,256]{1,0:T(8,128)S(1)} collective-permute-done((f32[56,256]{1,0:T(8,128)S(1)}, f32[56,256]{1,0:T(8,128)S(1)}, u32[]{:S(2)}, u32[]{:S(2)}) %collective-permute-start.13) | collective-permute-done | bytes 57376 | tf_op jit(solution)/shard_map/ppermute | solution.py:360
  39.1 1.4 %collective-permute-start.14 = (f32[32,256]{1,0:T(8,128)S(1)}, f32[32,256]{1,0:T(8,128)S(1)}, u32[]{:S(2)}, u32[]{:S(2)}) collective-permute-start(f32[32,256]{1,0:T(8,128)S(1)} %pad_maximum_fusion.2), channel_id=1, source_target_pairs={{0,5},{1,4},{2,7},{3,6},{4,1},{5,0},{6,3},{7,2},{8,13},{9,12},{10,... | collective-permute-start | bytes 98312 | tf_op jit(solution)/shard_map/ppermute | solution.py:360
  40.5 1.5 %shard_map.76 = (f32[256,384]{1,0:T(8,128)S(1)}, f32[256,384]{1,0:T(8,128)S(1)}, f32[256,256]{1,0:T(8,128)S(1)}, f32[256,128]{1,0:T(8,128)S(1)}) custom-call(s32[6]{0:T(128)S(1)} %pad_add_fusion.place_ref, f32[8,128]{1,0:T(8,128)S(1)} %shard_map.72.mine_ref, f32[8,128]{1,0:T(8,128)S(1)} %collective-permute-done.12.other_ref, ...), custom_call_target="tpu_custom_call" | custom-call | flops 50331648 | bytes 393216 | tf_op jit(solution)/shard_map/pallas_call | solution.py:345
  42.5 1.6 %shard_map.77 = (f32[12,256]{1,0:T(8,128)}, f32[1,256,256]{2,1,0:T(8,128)}) custom-call(s32[6]{0:T(128)S(1)} %pad_add_fusion.place_ref, f32[56,256]{1,0:T(8,128)S(1)} %add.10.mine_ref, f32[8,256]{1,0:T(8,128)S(1)} %slice_add_fusion.sums_ref, f32[32,256]{1,0:T(8,128)S(1)} %collective-permute-done.14.other_ref, f32[256,384]{1,0:T(8,128)S(1)} %get-tuple-element.62.targets_ref, ...), custom_call_target="tpu_custom_call" | custom-call | flops 50331648 | bytes 393216 | tf_op jit(solution)/shard_map/pallas_call | solution.py:345
  (30 shorter events, 4.9 us)
Async XLA Ops:
  1.4 3.8 %collective-permute-start = (bf16[24,256]{1,0:T(8,128)(2,1)S(1)}, bf16[24,256]{1,0:T(8,128)(2,1)S(1)}, u32[]{:S(2)}, u32[]{:S(2)}) collective-permute-start(bf16[24,256]{1,0:T(8,128)(2,1)S(1)} %pad_maximum_fusion.4), channel_id=1, source_target_pairs={{0,3},{1,2},{2,1},{3,0},{4,7},{5,6},{6,5},{7,4},{8,11},{9,10},{10,... | collective-permute-start | bytes 36872 | tf_op jit(solution)/shard_map/ppermute | solution.py:360
  5.2 7.8 %collective-permute-start.1 = (bf16[2,24,256]{2,1,0:T(8,128)(2,1)S(1)}, bf16[2,24,256]{2,1,0:T(8,128)(2,1)S(1)}, u32[]{:S(2)}, u32[]{:S(2)}) collective-permute-start(bf16[2,24,256]{2,1,0:T(8,128)(2,1)S(1)} %get-tuple-element.69), channel_id=1, source_target_pairs={{0,25},{1,24},{2,27},{3,26},{4,29},{5,28},{6,31},{7,30},{8,17},{9,... | collective-permute-start | bytes 73736 | tf_op jit(solution)/shard_map/ppermute | solution.py:368
  9.4 4.2 %collective-permute-start.2 = (bf16[2,24,256]{2,1,0:T(8,128)(2,1)S(1)}, bf16[2,24,256]{2,1,0:T(8,128)(2,1)S(1)}, u32[]{:S(2)}, u32[]{:S(2)}) collective-permute-start(bf16[2,24,256]{2,1,0:T(8,128)(2,1)S(1)} %get-tuple-element.69), channel_id=1, source_target_pairs={{0,17},{1,16},{2,19},{3,18},{4,21},{5,20},{6,23},{7,22},{8,25},{9,... | collective-permute-start | bytes 73736 | tf_op jit(solution)/shard_map/ppermute | solution.py:368
  9.4 4.2 %collective-permute-start.3 = (bf16[2,24,256]{2,1,0:T(8,128)(2,1)S(1)}, bf16[2,24,256]{2,1,0:T(8,128)(2,1)S(1)}, u32[]{:S(2)}, u32[]{:S(2)}) collective-permute-start(bf16[2,24,256]{2,1,0:T(8,128)(2,1)S(1)} %get-tuple-element.69), channel_id=1, source_target_pairs={{0,9},{1,8},{2,11},{3,10},{4,13},{5,12},{6,15},{7,14},{8,1},{9,0},... | collective-permute-start | bytes 73736 | tf_op jit(solution)/shard_map/ppermute | solution.py:368
  11.3 7.6 %collective-permute-start.6 = (bf16[1024,256]{1,0:T(8,128)(2,1)S(1)}, bf16[1024,256]{1,0:T(8,128)(2,1)S(1)}, u32[]{:S(2)}, u32[]{:S(2)}) collective-permute-start(bf16[1024,256]{1,0:T(8,128)(2,1)S(1)} %shard_map.68.refs_0_), channel_id=1, source_target_pairs={{0,1},{1,0},{2,3},{3,2},{4,5},{5,4},{6,7},{7,6},{8,9},{9,8},{10,11... | collective-permute-start | bytes 1572872 | tf_op jit(solution)/shard_map/ppermute | solution.py:360
  11.5 13.9 %collective-permute-start.8 = (bf16[1024,256]{1,0:T(8,128)(2,1)}, bf16[1024,256]{1,0:T(8,128)(2,1)S(1)}, u32[]{:S(2)}, u32[]{:S(2)}) collective-permute-start(bf16[1024,256]{1,0:T(8,128)(2,1)} %refs_1_.1), channel_id=1, source_target_pairs={{0,3},{1,2},{2,1},{3,0},{4,7},{5,6},{6,5},{7,4},{8,11},{9,10},{10,... | collective-permute-start | bytes 1572872 | tf_op jit(solution)/shard_map/ppermute | solution.py:360
  13.6 4.6 %collective-permute-start.4 = (bf16[4,2,24,256]{3,2,1,0:T(8,128)(2,1)S(1)}, bf16[4,2,24,256]{3,2,1,0:T(8,128)(2,1)S(1)}, u32[]{:S(2)}, u32[]{:S(2)}) collective-permute-start(bf16[4,2,24,256]{3,2,1,0:T(8,128)(2,1)S(1)} %get-tuple-element.67), channel_id=1, source_target_pairs={{0,5},{1,4},{2,7},{3,6},{4,1},{5,0},{6,3},{7,2},{8,13},{9,12},{10,... | collective-permute-start | bytes 294920 | tf_op jit(solution)/shard_map/ppermute | solution.py:360
  18.2 1.9 %collective-permute-start.5 = (bf16[2,4,2,24,256]{4,3,2,1,0:T(8,128)(2,1)S(1)}, bf16[2,4,2,24,256]{4,3,2,1,0:T(8,128)(2,1)S(1)}, u32[]{:S(2)}, u32[]{:S(2)}) collective-permute-start(bf16[2,4,2,24,256]{4,3,2,1,0:T(8,128)(2,1)S(1)} %pad_maximum_fusion.near_ref), channel_id=1, source_target_pairs={{0,1},{1,0},{2,3},{3,2},{4,5},{5,4},{6,7},{7,6},{8,9},{9,8},{10,11... | collective-permute-start | bytes 589832 | tf_op jit(solution)/shard_map/ppermute | solution.py:360
  20.0 5.7 %copy-start = (bf16[1024,256]{1,0:T(8,128)(2,1)S(1)}, bf16[1024,256]{1,0:T(8,128)(2,1)}, u32[]{:S(2)}) copy-start(bf16[1024,256]{1,0:T(8,128)(2,1)} %refs_2_.1) | copy-start | bytes 1572868
  21.6 3.1 %collective-permute-start.7 = (f32[8,128]{1,0:T(8,128)S(1)}, f32[8,128]{1,0:T(8,128)S(1)}, u32[]{:S(2)}, u32[]{:S(2)}) collective-permute-start(f32[8,128]{1,0:T(8,128)S(1)} %get-tuple-element.40), channel_id=1, source_target_pairs={{0,5},{1,4},{2,7},{3,6},{4,1},{5,0},{6,3},{7,2},{8,13},{9,12},{10,... | collective-permute-start | bytes 12296 | tf_op jit(solution)/shard_map/ppermute | solution.py:360
  25.3 2.2 %collective-permute-start.10 = (bf16[1024,256]{1,0:T(8,128)(2,1)S(1)}, bf16[1024,256]{1,0:T(8,128)(2,1)S(1)}, u32[]{:S(2)}, u32[]{:S(2)}) collective-permute-start(bf16[1024,256]{1,0:T(8,128)(2,1)S(1)} %collective-permute-done.8.refs_0_), channel_id=1, source_target_pairs={{0,1},{1,0},{2,3},{3,2},{4,5},{5,4},{6,7},{7,6},{8,9},{9,8},{10,11... | collective-permute-start | bytes 1572872 | tf_op jit(solution)/shard_map/ppermute | solution.py:360
  25.7 4.5 %collective-permute-start.11 = (bf16[1024,256]{1,0:T(8,128)(2,1)S(1)}, bf16[1024,256]{1,0:T(8,128)(2,1)S(1)}, u32[]{:S(2)}, u32[]{:S(2)}) collective-permute-start(bf16[1024,256]{1,0:T(8,128)(2,1)S(1)} %copy-done), channel_id=1, source_target_pairs={{0,1},{1,0},{2,3},{3,2},{4,5},{5,4},{6,7},{7,6},{8,9},{9,8},{10,11... | collective-permute-start | bytes 1572872 | tf_op jit(solution)/shard_map/ppermute | solution.py:360
  25.8 3.1 %collective-permute-start.9 = (f32[8,128]{1,0:T(8,128)S(1)}, f32[8,128]{1,0:T(8,128)S(1)}, u32[]{:S(2)}, u32[]{:S(2)}) collective-permute-start(f32[8,128]{1,0:T(8,128)S(1)} %add.9.mine_ref), channel_id=1, source_target_pairs={{0,3},{1,2},{2,1},{3,0},{4,7},{5,6},{6,5},{7,4},{8,11},{9,10},{10,... | collective-permute-start | bytes 12296 | tf_op jit(solution)/shard_map/ppermute | solution.py:360
  30.2 3.5 %collective-permute-start.12 = (f32[8,128]{1,0:T(8,128)S(1)}, f32[8,128]{1,0:T(8,128)S(1)}, u32[]{:S(2)}, u32[]{:S(2)}) collective-permute-start(f32[8,128]{1,0:T(8,128)S(1)} %shard_map.72.mine_ref), channel_id=1, source_target_pairs={{0,5},{1,4},{2,7},{3,6},{4,1},{5,0},{6,3},{7,2},{8,13},{9,12},{10,... | collective-permute-start | bytes 12296 | tf_op jit(solution)/shard_map/ppermute | solution.py:360
  35.2 3.8 %collective-permute-start.13 = (f32[56,256]{1,0:T(8,128)S(1)}, f32[56,256]{1,0:T(8,128)S(1)}, u32[]{:S(2)}, u32[]{:S(2)}) collective-permute-start(f32[56,256]{1,0:T(8,128)S(1)} %get-tuple-element.57), channel_id=1, source_target_pairs={{0,3},{1,2},{2,1},{3,0},{4,7},{5,6},{6,5},{7,4},{8,11},{9,10},{10,... | collective-permute-start | bytes 172040 | tf_op jit(solution)/shard_map/ppermute | solution.py:360
  37.4 5.1 %copy-start.1 = (bf16[12,256]{1,0:T(8,128)(2,1)S(1)}, bf16[12,256]{1,0:T(8,128)(2,1)}, u32[]{:S(2)}) copy-start(bf16[12,256]{1,0:T(8,128)(2,1)} %refs_3_.1) | copy-start | bytes 18436
  39.1 3.4 %collective-permute-start.14 = (f32[32,256]{1,0:T(8,128)S(1)}, f32[32,256]{1,0:T(8,128)S(1)}, u32[]{:S(2)}, u32[]{:S(2)}) collective-permute-start(f32[32,256]{1,0:T(8,128)S(1)} %pad_maximum_fusion.2), channel_id=1, source_target_pairs={{0,5},{1,4},{2,7},{3,6},{4,1},{5,0},{6,3},{7,2},{8,13},{9,12},{10,... | collective-permute-start | bytes 98312 | tf_op jit(solution)/shard_map/ppermute | solution.py:360

commit v6 on v5

--- a/solution.py
+++ b/solution.py
@@ -199,8 +199,9 @@
     sums_ref[...] = as_tile(part_ref[...])
 
 
-def across_kernel(chunk, near_rows_ref, far_rows_ref, near_live_ref, far_live_ref, *refs):
-    *proto_refs, weights_ref = refs
+def across_kernel(chunk, place_ref, near_ref, far_ref, *refs):
+    near_rows_ref, far_rows_ref, near_live_ref, far_live_ref, *refs = refs
+    *proto_refs, weights_ref, student_ref, scratch = refs
     protos = proto_refs[0].shape[0]
     rows_all = jnp.concatenate([near_rows_ref[...], far_rows_ref[...]], axis=0)
     live = twice(jnp.concatenate([near_live_ref[...], far_live_ref[...]], axis=0))
@@ -209,6 +210,10 @@
             units = quick_unit(proto_ref[start : start + chunk, :])[0].astype(jnp.bfloat16)
             at = slice(k * protos + start, k * protos + start + chunk)
             weights_ref[:, at], _ = weights_of(rows_all, units, live)
+    half = student_ref.shape[0] // 2
+    for k, ref in enumerate((near_ref, far_ref)):
+        rows_half = place_rows(place_ref, ref, 1, ref.shape[3] // 2, scratch)
+        student_ref[k * half : (k + 1) * half, :] = rows_half
 
 
 def scale_columns(sums, near_ref, far_ref, across_ref, row_ref, scale_ref):
@@ -236,14 +241,11 @@
     return jnp.concatenate([high, low], axis=0)
 
 
-def exps_kernel(chunk, place_ref, near_ref, far_ref, *refs):
-    *proto_refs, rows_ref, units_ref, pull_ref, sums_ref, scratch, exps_ref = refs
-    all_rows, half = rows_ref.shape[0], rows_ref.shape[0] // 2
+def exps_kernel(chunk, rows_ref, *refs):
+    *proto_refs, units_ref, pull_ref, sums_ref, exps_ref = refs
+    all_rows = rows_ref.shape[0]
     protos = proto_refs[0].shape[0]
     first = pull_ref.shape[0]
-    for k, ref in enumerate((near_ref, far_ref)):
-        rows_half = place_rows(place_ref, ref, 1, ref.shape[3] // 2, scratch)
-        rows_ref[k * half : (k + 1) * half, :] = rows_half
     rows_all = rows_ref[...]
     part = jnp.zeros((all_rows, LANES), jnp.float32)
     pull = jnp.zeros((2 * first, pull_ref.shape[1]), jnp.float32)
@@ -419,10 +421,22 @@
     sums = sums + swap(sums, "proto", Y_CROSS)
     sums, across_protos = lax.optimization_barrier((sums, across_protos))
     parts = (sums, swap(sums, "proto", X_CROSS))
-    across_weights = call(
+    across_weights, student_rows = call(
         functools.partial(across_kernel, own),
-        f32((all_rows, held)),
-        (near_rows, far_rows, near_live, far_live, across_protos, swap(across_protos, "proto", CORE)),
+        (f32((all_rows, held)), bf16((all_rows, width))),
+        (
+            place,
+            near,
+            far,
+            near_rows,
+            far_rows,
+            near_live,
+            far_live,
+            across_protos,
+            swap(across_protos, "proto", CORE),
+        ),
+        smem=1,
+        scratch=[row_scratch],
         work=held * all_rows,
     )
     weights = (near_weights, far_weights, across_weights)
@@ -434,16 +448,15 @@
             scratch=sweep_scratch,
             work=held * all_rows,
         )
-        sums, near, far, *student_protos = lax.optimization_barrier(
-            (sums, near, far, *student_protos)
+        sums, student_rows, *student_protos = lax.optimization_barrier(
+            (sums, student_rows, *student_protos)
         )
         parts = (sums, swap(sums, "proto", Y_CROSS))
-    student_rows, student_units, exp_pull, exp_sums = call(
+    student_units, exp_pull, exp_sums = call(
         functools.partial(exps_kernel, own),
-        (bf16((all_rows, width)), bf16((held, width)), f32((first, width)), tile),
-        (place, near, far, *student_protos),
-        smem=1,
-        scratch=[row_scratch, pltpu.VMEM((all_rows, own), jnp.float32)],
+        (bf16((held, width)), f32((first, width)), tile),
+        (student_rows, *student_protos),
+        scratch=[pltpu.VMEM((all_rows, own), jnp.float32)],
         work=held * all_rows,
     )
     scales, keep, send = call(

time: 44.3 us -> 44.1 us (level)
  no operation moved by 1% of the time
where the time goes in v6:
time: 44.1 us; the launch traced here: 43.8 us
  starting transfers between devices  19.7 us (45%)
  Pallas kernels  13.1 us (30%)
  waiting for transfers between devices  8.78 us (20%)
  other arithmetic  1.52 us (3%)
  between operations  0.76 us (2%)
    ppermute x12, starting transfers between devices, swap(): return lax.ppermute(values, axis, others)  14.8 us
    pallas_call x10, Pallas kernels, call(): pl.pallas_call(kernel, out_shape=out_shape, in_specs=[pl.BlockSpec(memory...  13.1 us
    ppermute x12, waiting for transfers between devices, swap(): return lax.ppermute(values, axis, others)  8.24 us
    ppermute x3, starting transfers between devices, swap_dp(): return lax.ppermute(values, ('dp', 'proto'), others)  4.86 us
  transfers between devices with their start and end apart: 15, of which 8 were waited for; matrix products, arithmetic and copies ran while one was open for 2% of the time, Pallas kernels for 23%

profile of v6, /device:TPU:0, one launch (start us, length us, event | category | flops | bytes accessed | tf_op | source)
XLA Modules:
  0.0 43.8 jit_solution(2612275735896785269)
XLA Ops:
  0.6 0.7 %pad_maximum_fusion.4 = bf16[24,256]{1,0:T(8,128)(2,1)S(1)} fusion(bf16[12,256]{1,0:T(8,128)(2,1)} %refs_3_.1, bf16[12,256]{1,0:T(8,128)(2,1)} %param.6), kind=kLoop, calls=%fused_computation.4 | loop fusion | flops 24576 | bytes 24576 | tf_op jit(solution)/shard_map/concatenate | solution.py:393
  1.4 2.4 %collective-permute-start = (bf16[24,256]{1,0:T(8,128)(2,1)S(1)}, bf16[24,256]{1,0:T(8,128)(2,1)S(1)}, u32[]{:S(2)}, u32[]{:S(2)}) collective-permute-start(bf16[24,256]{1,0:T(8,128)(2,1)S(1)} %pad_maximum_fusion.4), channel_id=1, source_target_pairs={{0,3},{1,2},{2,1},{3,0},{4,7},{5,6},{6,5},{7,4},{8,11},{9,10},{10,... | collective-permute-start | bytes 36872 | tf_op jit(solution)/shard_map/ppermute | solution.py:362
  3.8 0.7 %pad_add_fusion.place_ref = s32[6]{0:T(128)S(1)} fusion(s32[4]{0:T(128)} %param.9, s32[1]{0:T(128)} %bitcast.1, s32[1]{0:T(128)} %bitcast), kind=kLoop, calls=%fused_computation.6 | loop fusion | flops 12 | bytes 48 | tf_op jit(solution)/shard_map/concatenate | solution.py:385
  5.2 4.2 %collective-permute-start.1 = (bf16[2,24,256]{2,1,0:T(8,128)(2,1)S(1)}, bf16[2,24,256]{2,1,0:T(8,128)(2,1)S(1)}, u32[]{:S(2)}, u32[]{:S(2)}) collective-permute-start(bf16[2,24,256]{2,1,0:T(8,128)(2,1)S(1)} %get-tuple-element.69), channel_id=1, source_target_pairs={{0,25},{1,24},{2,27},{3,26},{4,29},{5,28},{6,31},{7,30},{8,17},{9,... | collective-permute-start | bytes 73736 | tf_op jit(solution)/shard_map/ppermute | solution.py:370
  10.1 1.3 %shard_map.68.refs_0_ = bf16[1024,256]{1,0:T(8,128)(2,1)S(1)} custom-call(bf16[1024,256]{1,0:T(8,128)(2,1)} %refs_1_.1), custom_call_target="tpu_custom_call" | custom-call | flops 134217728 | bytes 1048576 | tf_op jit(solution)/shard_map/pallas_call | solution.py:347
  11.5 1.5 %collective-permute-start.8 = (bf16[1024,256]{1,0:T(8,128)(2,1)}, bf16[1024,256]{1,0:T(8,128)(2,1)S(1)}, u32[]{:S(2)}, u32[]{:S(2)}) collective-permute-start(bf16[1024,256]{1,0:T(8,128)(2,1)} %refs_1_.1), channel_id=1, source_target_pairs={{0,3},{1,2},{2,1},{3,0},{4,7},{5,6},{6,5},{7,4},{8,11},{9,10},{10,... | collective-permute-start | bytes 1572872 | tf_op jit(solution)/shard_map/ppermute | solution.py:362
  13.6 1.6 %collective-permute-start.4 = (bf16[4,2,24,256]{3,2,1,0:T(8,128)(2,1)S(1)}, bf16[4,2,24,256]{3,2,1,0:T(8,128)(2,1)S(1)}, u32[]{:S(2)}, u32[]{:S(2)}) collective-permute-start(bf16[4,2,24,256]{3,2,1,0:T(8,128)(2,1)S(1)} %get-tuple-element.67), channel_id=1, source_target_pairs={{0,5},{1,4},{2,7},{3,6},{4,1},{5,0},{6,3},{7,2},{8,13},{9,12},{10,... | collective-permute-start | bytes 294920 | tf_op jit(solution)/shard_map/ppermute | solution.py:362
  15.2 3.0 %collective-permute-done.4 = bf16[4,2,24,256]{3,2,1,0:T(8,128)(2,1)S(1)} collective-permute-done((bf16[4,2,24,256]{3,2,1,0:T(8,128)(2,1)S(1)}, bf16[4,2,24,256]{3,2,1,0:T(8,128)(2,1)S(1)}, u32[]{:S(2)}, u32[]{:S(2)}) %collective-permute-start.4) | collective-permute-done | bytes 98336 | tf_op jit(solution)/shard_map/ppermute | solution.py:362
  18.2 0.8 %collective-permute-start.5 = (bf16[2,4,2,24,256]{4,3,2,1,0:T(8,128)(2,1)S(1)}, bf16[2,4,2,24,256]{4,3,2,1,0:T(8,128)(2,1)S(1)}, u32[]{:S(2)}, u32[]{:S(2)}) collective-permute-start(bf16[2,4,2,24,256]{4,3,2,1,0:T(8,128)(2,1)S(1)} %pad_maximum_fusion.near_ref), channel_id=1, source_target_pairs={{0,1},{1,0},{2,3},{3,2},{4,5},{5,4},{6,7},{7,6},{8,9},{9,8},{10,11... | collective-permute-start | bytes 589832 | tf_op jit(solution)/shard_map/ppermute | solution.py:362
  18.9 1.1 %shard_map.69 = (f32[192,2048]{1,0:T(8,128)S(1)}, f32[8,2048]{1,0:T(8,128)S(1)}, bf16[192,256]{1,0:T(8,128)(2,1)S(1)}, f32[192,128]{1,0:T(8,128)S(1)}) custom-call(s32[6]{0:T(128)S(1)} %pad_add_fusion.place_ref, bf16[2,4,2,24,256]{4,3,2,1,0:T(8,128)(2,1)S(1)} %pad_maximum_fusion.near_ref, bf16[1024,256]{1,0:T(8,128)(2,1)S(1)} %shard_map.68.refs_0_, ...), custom_call_target="tpu_custom_call" | custom-call | flops 201326592 | bytes 1572864 | tf_op jit(solution)/shard_map/pallas_call | solution.py:347
  20.1 1.5 %shard_map.70 = (f32[192,2048]{1,0:T(8,128)S(1)}, bf16[192,256]{1,0:T(8,128)(2,1)S(1)}, f32[192,128]{1,0:T(8,128)S(1)}, f32[8,128]{1,0:T(8,128)S(1)}) custom-call(s32[6]{0:T(128)S(1)} %pad_add_fusion.place_ref, bf16[2,4,2,24,256]{4,3,2,1,0:T(8,128)(2,1)S(1)} %collective-permute-done.5.far_ref, bf16[192,256]{1,0:T(8,128)(2,1)S(1)} %get-tuple-element.37.near_rows_ref.refs_0_, ...), custom_call_target="tpu_custom_call" | custom-call | flops 201326592 | bytes 1572864 | tf_op jit(solution)/shard_map/pallas_call | solution.py:347
  21.6 1.5 %collective-permute-start.7 = (f32[8,128]{1,0:T(8,128)S(1)}, f32[8,128]{1,0:T(8,128)S(1)}, u32[]{:S(2)}, u32[]{:S(2)}) collective-permute-start(f32[8,128]{1,0:T(8,128)S(1)} %get-tuple-element.40), channel_id=1, source_target_pairs={{0,5},{1,4},{2,7},{3,6},{4,1},{5,0},{6,3},{7,2},{8,13},{9,12},{10,... | collective-permute-start | bytes 12296 | tf_op jit(solution)/shard_map/ppermute | solution.py:362
  23.1 1.6 %collective-permute-done.7 = f32[8,128]{1,0:T(8,128)S(1)} collective-permute-done((f32[8,128]{1,0:T(8,128)S(1)}, f32[8,128]{1,0:T(8,128)S(1)}, u32[]{:S(2)}, u32[]{:S(2)}) %collective-permute-start.7) | collective-permute-done | bytes 4128 | tf_op jit(solution)/shard_map/ppermute | solution.py:362
  25.8 1.7 %collective-permute-start.9 = (f32[8,128]{1,0:T(8,128)S(1)}, f32[8,128]{1,0:T(8,128)S(1)}, u32[]{:S(2)}, u32[]{:S(2)}) collective-permute-start(f32[8,128]{1,0:T(8,128)S(1)} %add.9.mine_ref), channel_id=1, source_target_pairs={{0,3},{1,2},{2,1},{3,0},{4,7},{5,6},{6,5},{7,4},{8,11},{9,10},{10,... | collective-permute-start | bytes 12296 | tf_op jit(solution)/shard_map/ppermute | solution.py:362
  27.5 1.6 %shard_map.71 = (f32[384,2048]{1,0:T(8,128)S(1)}, bf16[384,256]{1,0:T(8,128)(2,1)S(1)}) custom-call(s32[6]{0:T(128)S(1)} %pad_add_fusion.place_ref, bf16[2,4,2,24,256]{4,3,2,1,0:T(8,128)(2,1)S(1)} %pad_maximum_fusion.near_ref, bf16[2,4,2,24,256]{4,3,2,1,0:T(8,128)(2,1)S(1)} %collective-permute-done.5.far_ref, ...), custom_call_target="tpu_custom_call" | custom-call | flops 402653184 | bytes 3145728 | tf_op jit(solution)/shard_map/pallas_call | solution.py:347
  29.1 1.3 %shard_map.72.mine_ref = f32[8,128]{1,0:T(8,128)S(1)} custom-call(f32[8,128]{1,0:T(8,128)S(1)} %add.9.mine_ref, f32[8,128]{1,0:T(8,128)S(1)} %collective-permute-done.9.other_ref, f32[192,2048]{1,0:T(8,128)S(1)} %get-tuple-element.38.near_weights_ref.near_ref, f32[192,2048]{1,0:T(8,128)S(1)} %get-tuple-element.42.far_ref, ...), custom_call_target="tpu_custom_call" | custom-call | flops 402653184 | bytes 3145728 | tf_op jit(solution)/shard_map/pallas_call | solution.py:347
  30.4 1.5 %collective-permute-start.12 = (f32[8,128]{1,0:T(8,128)S(1)}, f32[8,128]{1,0:T(8,128)S(1)}, u32[]{:S(2)}, u32[]{:S(2)}) collective-permute-start(f32[8,128]{1,0:T(8,128)S(1)} %shard_map.72.mine_ref), channel_id=1, source_target_pairs={{0,5},{1,4},{2,7},{3,6},{4,1},{5,0},{6,3},{7,2},{8,13},{9,12},{10,... | collective-permute-start | bytes 12296 | tf_op jit(solution)/shard_map/ppermute | solution.py:362
  31.9 1.2 %shard_map.73 = (bf16[2048,256]{1,0:T(8,128)(2,1)S(1)}, f32[48,256]{1,0:T(8,128)S(1)}, f32[8,128]{1,0:T(8,128)S(1)}) custom-call(bf16[384,256]{1,0:T(8,128)(2,1)S(1)} %get-tuple-element.50.rows_ref.refs_0_.refs_2_, bf16[1024,256]{1,0:T(8,128)(2,1)S(1)} %copy-done, bf16[1024,256]{1,0:T(8,128)(2,1)S(1)} %collective-permute-done.11.refs_1_), custom_call_target="tpu_custom_call" | custom-call | flops 402653184 | bytes 3145728 | tf_op jit(solution)/shard_map/pallas_call | solution.py:347
  33.5 1.5 %shard_map.74 = (f32[8,4096]{1,0:T(8,128)S(1)}, f32[56,256]{1,0:T(8,128)S(1)}, f32[56,256]{1,0:T(8,128)S(1)}) custom-call(s32[6]{0:T(128)S(1)} %pad_add_fusion.place_ref, f32[8,128]{1,0:T(8,128)S(1)} %shard_map.72.mine_ref, f32[8,128]{1,0:T(8,128)S(1)} %collective-permute-done.12.other_ref, f32[192,2048]{1,0:T(8,128)S(1)} %get-tuple-element.38.near_weights_ref.near_ref, ...), custom_call_target="tpu_custom_call" | custom-call | flops 402653184 | bytes 3145728 | tf_op jit(solution)/shard_map/pallas_call | solution.py:347
  35.0 1.5 %collective-permute-start.13 = (f32[56,256]{1,0:T(8,128)S(1)}, f32[56,256]{1,0:T(8,128)S(1)}, u32[]{:S(2)}, u32[]{:S(2)}) collective-permute-start(f32[56,256]{1,0:T(8,128)S(1)} %get-tuple-element.58), channel_id=1, source_target_pairs={{0,3},{1,2},{2,1},{3,0},{4,7},{5,6},{6,5},{7,4},{8,11},{9,10},{10,... | collective-permute-start | bytes 172040 | tf_op jit(solution)/shard_map/ppermute | solution.py:362
  37.1 1.7 %collective-permute-done.13 = f32[56,256]{1,0:T(8,128)S(1)} collective-permute-done((f32[56,256]{1,0:T(8,128)S(1)}, f32[56,256]{1,0:T(8,128)S(1)}, u32[]{:S(2)}, u32[]{:S(2)}) %collective-permute-start.13) | collective-permute-done | bytes 57376 | tf_op jit(solution)/shard_map/ppermute | solution.py:362
  38.9 1.6 %collective-permute-start.14 = (f32[32,256]{1,0:T(8,128)S(1)}, f32[32,256]{1,0:T(8,128)S(1)}, u32[]{:S(2)}, u32[]{:S(2)}) collective-permute-start(f32[32,256]{1,0:T(8,128)S(1)} %pad_maximum_fusion.2), channel_id=1, source_target_pairs={{0,5},{1,4},{2,7},{3,6},{4,1},{5,0},{6,3},{7,2},{8,13},{9,12},{10,... | collective-permute-start | bytes 98312 | tf_op jit(solution)/shard_map/ppermute | solution.py:362
  40.5 1.5 %shard_map.76 = (f32[256,384]{1,0:T(8,128)S(1)}, f32[256,384]{1,0:T(8,128)S(1)}, f32[256,256]{1,0:T(8,128)S(1)}, f32[256,128]{1,0:T(8,128)S(1)}) custom-call(s32[6]{0:T(128)S(1)} %pad_add_fusion.place_ref, f32[8,128]{1,0:T(8,128)S(1)} %shard_map.72.mine_ref, f32[8,128]{1,0:T(8,128)S(1)} %collective-permute-done.12.other_ref, ...), custom_call_target="tpu_custom_call" | custom-call | flops 50331648 | bytes 393216 | tf_op jit(solution)/shard_map/pallas_call | solution.py:347
  42.3 1.6 %shard_map.77 = (f32[12,256]{1,0:T(8,128)}, f32[1,256,256]{2,1,0:T(8,128)}) custom-call(s32[6]{0:T(128)S(1)} %pad_add_fusion.place_ref, f32[56,256]{1,0:T(8,128)S(1)} %add.10.mine_ref, f32[8,256]{1,0:T(8,128)S(1)} %slice_add_fusion.sums_ref, f32[32,256]{1,0:T(8,128)S(1)} %collective-permute-done.14.other_ref, f32[256,384]{1,0:T(8,128)S(1)} %get-tuple-element.62.targets_ref, ...), custom_call_target="tpu_custom_call" | custom-call | flops 50331648 | bytes 393216 | tf_op jit(solution)/shard_map/pallas_call | solution.py:347
  (30 shorter events, 4.6 us)
Async XLA Ops:
  1.4 3.8 %collective-permute-start = (bf16[24,256]{1,0:T(8,128)(2,1)S(1)}, bf16[24,256]{1,0:T(8,128)(2,1)S(1)}, u32[]{:S(2)}, u32[]{:S(2)}) collective-permute-start(bf16[24,256]{1,0:T(8,128)(2,1)S(1)} %pad_maximum_fusion.4), channel_id=1, source_target_pairs={{0,3},{1,2},{2,1},{3,0},{4,7},{5,6},{6,5},{7,4},{8,11},{9,10},{10,... | collective-permute-start | bytes 36872 | tf_op jit(solution)/shard_map/ppermute | solution.py:362
  5.2 7.8 %collective-permute-start.1 = (bf16[2,24,256]{2,1,0:T(8,128)(2,1)S(1)}, bf16[2,24,256]{2,1,0:T(8,128)(2,1)S(1)}, u32[]{:S(2)}, u32[]{:S(2)}) collective-permute-start(bf16[2,24,256]{2,1,0:T(8,128)(2,1)S(1)} %get-tuple-element.69), channel_id=1, source_target_pairs={{0,25},{1,24},{2,27},{3,26},{4,29},{5,28},{6,31},{7,30},{8,17},{9,... | collective-permute-start | bytes 73736 | tf_op jit(solution)/shard_map/ppermute | solution.py:370
  9.4 4.2 %collective-permute-start.2 = (bf16[2,24,256]{2,1,0:T(8,128)(2,1)S(1)}, bf16[2,24,256]{2,1,0:T(8,128)(2,1)S(1)}, u32[]{:S(2)}, u32[]{:S(2)}) collective-permute-start(bf16[2,24,256]{2,1,0:T(8,128)(2,1)S(1)} %get-tuple-element.69), channel_id=1, source_target_pairs={{0,17},{1,16},{2,19},{3,18},{4,21},{5,20},{6,23},{7,22},{8,25},{9,... | collective-permute-start | bytes 73736 | tf_op jit(solution)/shard_map/ppermute | solution.py:370
  9.4 4.2 %collective-permute-start.3 = (bf16[2,24,256]{2,1,0:T(8,128)(2,1)S(1)}, bf16[2,24,256]{2,1,0:T(8,128)(2,1)S(1)}, u32[]{:S(2)}, u32[]{:S(2)}) collective-permute-start(bf16[2,24,256]{2,1,0:T(8,128)(2,1)S(1)} %get-tuple-element.69), channel_id=1, source_target_pairs={{0,9},{1,8},{2,11},{3,10},{4,13},{5,12},{6,15},{7,14},{8,1},{9,0},... | collective-permute-start | bytes 73736 | tf_op jit(solution)/shard_map/ppermute | solution.py:370
  11.3 7.6 %collective-permute-start.6 = (bf16[1024,256]{1,0:T(8,128)(2,1)S(1)}, bf16[1024,256]{1,0:T(8,128)(2,1)S(1)}, u32[]{:S(2)}, u32[]{:S(2)}) collective-permute-start(bf16[1024,256]{1,0:T(8,128)(2,1)S(1)} %shard_map.68.refs_0_), channel_id=1, source_target_pairs={{0,1},{1,0},{2,3},{3,2},{4,5},{5,4},{6,7},{7,6},{8,9},{9,8},{10,11... | collective-permute-start | bytes 1572872 | tf_op jit(solution)/shard_map/ppermute | solution.py:362
  11.5 13.9 %collective-permute-start.8 = (bf16[1024,256]{1,0:T(8,128)(2,1)}, bf16[1024,256]{1,0:T(8,128)(2,1)S(1)}, u32[]{:S(2)}, u32[]{:S(2)}) collective-permute-start(bf16[1024,256]{1,0:T(8,128)(2,1)} %refs_1_.1), channel_id=1, source_target_pairs={{0,3},{1,2},{2,1},{3,0},{4,7},{5,6},{6,5},{7,4},{8,11},{9,10},{10,... | collective-permute-start | bytes 1572872 | tf_op jit(solution)/shard_map/ppermute | solution.py:362
  13.6 4.6 %collective-permute-start.4 = (bf16[4,2,24,256]{3,2,1,0:T(8,128)(2,1)S(1)}, bf16[4,2,24,256]{3,2,1,0:T(8,128)(2,1)S(1)}, u32[]{:S(2)}, u32[]{:S(2)}) collective-permute-start(bf16[4,2,24,256]{3,2,1,0:T(8,128)(2,1)S(1)} %get-tuple-element.67), channel_id=1, source_target_pairs={{0,5},{1,4},{2,7},{3,6},{4,1},{5,0},{6,3},{7,2},{8,13},{9,12},{10,... | collective-permute-start | bytes 294920 | tf_op jit(solution)/shard_map/ppermute | solution.py:362
  18.2 1.9 %collective-permute-start.5 = (bf16[2,4,2,24,256]{4,3,2,1,0:T(8,128)(2,1)S(1)}, bf16[2,4,2,24,256]{4,3,2,1,0:T(8,128)(2,1)S(1)}, u32[]{:S(2)}, u32[]{:S(2)}) collective-permute-start(bf16[2,4,2,24,256]{4,3,2,1,0:T(8,128)(2,1)S(1)} %pad_maximum_fusion.near_ref), channel_id=1, source_target_pairs={{0,1},{1,0},{2,3},{3,2},{4,5},{5,4},{6,7},{7,6},{8,9},{9,8},{10,11... | collective-permute-start | bytes 589832 | tf_op jit(solution)/shard_map/ppermute | solution.py:362
  20.0 5.7 %copy-start = (bf16[1024,256]{1,0:T(8,128)(2,1)S(1)}, bf16[1024,256]{1,0:T(8,128)(2,1)}, u32[]{:S(2)}) copy-start(bf16[1024,256]{1,0:T(8,128)(2,1)} %refs_2_.1) | copy-start | bytes 1572868
  21.6 3.1 %collective-permute-start.7 = (f32[8,128]{1,0:T(8,128)S(1)}, f32[8,128]{1,0:T(8,128)S(1)}, u32[]{:S(2)}, u32[]{:S(2)}) collective-permute-start(f32[8,128]{1,0:T(8,128)S(1)} %get-tuple-element.40), channel_id=1, source_target_pairs={{0,5},{1,4},{2,7},{3,6},{4,1},{5,0},{6,3},{7,2},{8,13},{9,12},{10,... | collective-permute-start | bytes 12296 | tf_op jit(solution)/shard_map/ppermute | solution.py:362
  25.3 2.2 %collective-permute-start.10 = (bf16[1024,256]{1,0:T(8,128)(2,1)S(1)}, bf16[1024,256]{1,0:T(8,128)(2,1)S(1)}, u32[]{:S(2)}, u32[]{:S(2)}) collective-permute-start(bf16[1024,256]{1,0:T(8,128)(2,1)S(1)} %collective-permute-done.8.refs_4_), channel_id=1, source_target_pairs={{0,1},{1,0},{2,3},{3,2},{4,5},{5,4},{6,7},{7,6},{8,9},{9,8},{10,11... | collective-permute-start | bytes 1572872 | tf_op jit(solution)/shard_map/ppermute | solution.py:362
  25.7 4.7 %collective-permute-start.11 = (bf16[1024,256]{1,0:T(8,128)(2,1)S(1)}, bf16[1024,256]{1,0:T(8,128)(2,1)S(1)}, u32[]{:S(2)}, u32[]{:S(2)}) collective-permute-start(bf16[1024,256]{1,0:T(8,128)(2,1)S(1)} %copy-done), channel_id=1, source_target_pairs={{0,1},{1,0},{2,3},{3,2},{4,5},{5,4},{6,7},{7,6},{8,9},{9,8},{10,11... | collective-permute-start | bytes 1572872 | tf_op jit(solution)/shard_map/ppermute | solution.py:362
  25.8 3.2 %collective-permute-start.9 = (f32[8,128]{1,0:T(8,128)S(1)}, f32[8,128]{1,0:T(8,128)S(1)}, u32[]{:S(2)}, u32[]{:S(2)}) collective-permute-start(f32[8,128]{1,0:T(8,128)S(1)} %add.9.mine_ref), channel_id=1, source_target_pairs={{0,3},{1,2},{2,1},{3,0},{4,7},{5,6},{6,5},{7,4},{8,11},{9,10},{10,... | collective-permute-start | bytes 12296 | tf_op jit(solution)/shard_map/ppermute | solution.py:362
  30.4 3.1 %collective-permute-start.12 = (f32[8,128]{1,0:T(8,128)S(1)}, f32[8,128]{1,0:T(8,128)S(1)}, u32[]{:S(2)}, u32[]{:S(2)}) collective-permute-start(f32[8,128]{1,0:T(8,128)S(1)} %shard_map.72.mine_ref), channel_id=1, source_target_pairs={{0,5},{1,4},{2,7},{3,6},{4,1},{5,0},{6,3},{7,2},{8,13},{9,12},{10,... | collective-permute-start | bytes 12296 | tf_op jit(solution)/shard_map/ppermute | solution.py:362
  35.0 3.8 %collective-permute-start.13 = (f32[56,256]{1,0:T(8,128)S(1)}, f32[56,256]{1,0:T(8,128)S(1)}, u32[]{:S(2)}, u32[]{:S(2)}) collective-permute-start(f32[56,256]{1,0:T(8,128)S(1)} %get-tuple-element.58), channel_id=1, source_target_pairs={{0,3},{1,2},{2,1},{3,0},{4,7},{5,6},{6,5},{7,4},{8,11},{9,10},{10,... | collective-permute-start | bytes 172040 | tf_op jit(solution)/shard_map/ppermute | solution.py:362
  37.1 5.2 %copy-start.1 = (bf16[12,256]{1,0:T(8,128)(2,1)S(1)}, bf16[12,256]{1,0:T(8,128)(2,1)}, u32[]{:S(2)}) copy-start(bf16[12,256]{1,0:T(8,128)(2,1)} %refs_3_.1) | copy-start | bytes 18436
  38.9 3.4 %collective-permute-start.14 = (f32[32,256]{1,0:T(8,128)S(1)}, f32[32,256]{1,0:T(8,128)S(1)}, u32[]{:S(2)}, u32[]{:S(2)}) collective-permute-start(f32[32,256]{1,0:T(8,128)S(1)} %pad_maximum_fusion.2), channel_id=1, source_target_pairs={{0,5},{1,4},{2,7},{3,6},{4,1},{5,0},{6,3},{7,2},{8,13},{9,12},{10,... | collective-permute-start | bytes 98312 | tf_op jit(solution)/shard_map/ppermute | solution.py:362

commit v7 on v6

--- a/solution.py
+++ b/solution.py
@@ -157,41 +157,41 @@
     return jnp.sum(values.reshape(values.shape[0] // 8, 8, values.shape[1]), axis=0)
 
 
-def units_kernel(proto_ref, units_ref):
+def units_kernel(n_dp, rows, place_ref, proto_ref, units_ref, *live_refs):
     units_ref[...] = quick_unit(proto_ref[...])[0].astype(jnp.bfloat16)
-
-
-def near_kernel(chunk, place_ref, near_ref, *refs):
-    *unit_refs, weights_ref, sums_ref, rows_ref, live_ref, scratch = refs
-    half = rows_ref.shape[0]
+    for k, live_ref in enumerate(live_refs):
+        live_ref[...] = as_column(live_lanes(place_ref, k, live_ref.shape[0], n_dp, rows))
+
+
+def near_kernel(chunk, place_ref, near_ref, live_ref, own_units_ref, proto_ref, *refs):
+    weights_ref, sums_ref, rows_ref, units_ref, scratch = refs
     rows = near_ref.shape[3] // 2
-    protos = unit_refs[0].shape[0]
     rows_near = place_rows(place_ref, near_ref, 0, rows, scratch)
     rows_ref[...] = rows_near
-    live = as_column(live_lanes(place_ref, 0, half, near_ref.shape[1], rows))
-    live_ref[...] = live
-    live = twice(live)
+    live = twice(live_ref[...])
+    protos = own_units_ref.shape[0]
+    for start in range(0, 2 * protos, chunk):
+        at = slice(start, start + chunk)
+        if start < protos:
+            units = own_units_ref[at, :]
+        else:
+            here = slice(start - protos, start - protos + chunk)
+            units = quick_unit(proto_ref[here, :])[0].astype(jnp.bfloat16)
+            units_ref[here, :] = units
+        weights_ref[:, at], sums_ref[:, at] = weights_of(rows_near, units, live)
+
+
+def far_kernel(chunk, place_ref, far_ref, live_ref, near_weights_ref, near_sums_ref, *refs):
+    *unit_refs, weights_ref, rows_ref, sums_ref, scratch, scale_ref, part_ref = refs
+    rows = far_ref.shape[3] // 2
+    rows_far = place_rows(place_ref, far_ref, 0, rows, scratch)
+    rows_ref[...] = rows_far
+    live = twice(live_ref[...])
+    protos = unit_refs[0].shape[0]
     for k, unit_ref in enumerate(unit_refs):
         for start in range(0, protos, chunk):
             at = slice(k * protos + start, k * protos + start + chunk)
-            weights_ref[:, at], sums_ref[:, at] = weights_of(
-                rows_near, unit_ref[start : start + chunk, :], live
-            )
-
-
-def far_kernel(chunk, place_ref, far_ref, near_rows_ref, near_weights_ref, near_sums_ref, *refs):
-    *unit_refs, weights_ref, rows_ref, live_ref, sums_ref, scratch, scale_ref, part_ref = refs
-    half = near_rows_ref.shape[0]
-    rows = far_ref.shape[3] // 2
-    protos = unit_refs[0].shape[0]
-    rows_far = place_rows(place_ref, far_ref, 0, rows, scratch)
-    rows_ref[...] = rows_far
-    live = as_column(live_lanes(place_ref, 1, half, far_ref.shape[1], rows))
-    live_ref[...] = live
-    for k, unit_ref in enumerate(unit_refs):
-        for start in range(0, protos, chunk):
-            at = slice(k * protos + start, k * protos + start + chunk)
-            weights, sums = weights_of(rows_far, unit_ref[start : start + chunk, :], twice(live))
+            weights, sums = weights_of(rows_far, unit_ref[start : start + chunk, :], live)
             weights_ref[:, at] = weights
             inverse = 1.0 / jnp.sum(near_sums_ref[:, at] + sums, axis=0, keepdims=True)
             scale_ref[:, at] = jnp.broadcast_to(inverse, (8, chunk))
@@ -392,28 +392,42 @@
 
     both = lax.optimization_barrier(jnp.concatenate([teacher_feat, student_feat], axis=0))
     across_x = swap(both, "proto", X_CROSS)
-    across_x, own_protos, place = lax.optimization_barrier((across_x, teacher_prototypes, place))
-    across_protos = swap(own_protos, "proto", X_CROSS)
+    across_x, late_protos, place = lax.optimization_barrier((across_x, teacher_prototypes, place))
+    across_protos = swap(late_protos, "proto", X_CROSS)
     student_protos = (prototypes, swap(prototypes, "proto", CORE))
+    teacher_protos = swap(late_protos, "proto", CORE)
     near = jnp.stack([both, across_x])
-    teacher_units = call(units_kernel, bf16((protos, width)), (own_protos,), work=protos * width)
-    teacher_units = (teacher_units, swap(teacher_units, "proto", CORE))
     near = jnp.stack([near] + [swap_dp(near, t) for t in dp_order(n_dp)[1:]])
+    near, own_protos = lax.optimization_barrier((near, teacher_prototypes))
+    live = f32((half, LANES))
+    teacher_units, near_live, far_live = call(
+        functools.partial(units_kernel, n_dp, rows),
+        (bf16((protos, width)), live, live),
+        (place, own_protos),
+        smem=1,
+        work=protos * width,
+    )
     near = jnp.stack([near, swap(near, "proto", Y_CROSS)])
+    near, teacher_units = lax.optimization_barrier((near, teacher_units))
     far = swap(near, "proto", CORE)
 
-    near_weights, near_sums, near_rows, near_live = call(
+    near_weights, near_sums, near_rows, other_units = call(
         functools.partial(near_kernel, own),
-        (f32((half, held)), f32((8, held)), bf16((half, width)), f32((half, LANES))),
-        (place, near, *teacher_units),
+        (
+            f32((half, held)),
+            f32((8, held)),
+            bf16((half, width)),
+            bf16((protos, width)),
+        ),
+        (place, near, near_live, teacher_units, teacher_protos),
         smem=1,
         scratch=[row_scratch],
         work=held * half,
     )
-    far_weights, far_rows, far_live, sums = call(
+    far_weights, far_rows, sums = call(
         functools.partial(far_kernel, own),
-        (f32((half, held)), bf16((half, width)), f32((half, LANES)), tile),
-        (place, far, near_rows, near_weights, near_sums, *teacher_units),
+        (f32((half, held)), bf16((half, width)), tile),
+        (place, far, far_live, near_weights, near_sums, teacher_units, other_units),
         smem=1,
         scratch=[row_scratch, scale_row, column],
         work=held * half,

time: 44.1 us -> 43.5 us (0.986)
  starting transfers between devices: 19.7 us -> 18.6 us
  local copies, waits for them, and re-layouts: 0.02 us -> 1.06 us
  Pallas kernels: 13.1 us -> 12.2 us
    ppermute x3, waiting for transfers between devices: 0.54 us -> 1.87 us  [swap_dp(): return lax.ppermute(values, ('dp', 'proto'), others)]
    ppermute x12, waiting for transfers between devices: 8.24 us -> 7.12 us  [swap(): return lax.ppermute(values, axis, others)]
    ppermute x12, starting transfers between devices: 14.8 us -> 13.8 us  [swap(): return lax.ppermute(values, axis, others)]
    unnamed x4 -> x8, local copies, waits for them, and re-layouts: 0.01 us -> 1.06 us
    pallas_call x10, Pallas kernels: 13.1 us -> 12.2 us  [call(): pl.pallas_call(kernel, out_shape=out_shape, in_specs=[pl.BlockSpec(memory...]
  transfers between devices with their start and end apart: 15 -> 15, of which waited for: 8 -> 8; matrix products, arithmetic and copies ran while one was open for 2% -> 2% of each run, Pallas kernels for 23% -> 21%
where the time goes in v7:
time: 43.5 us; the launch traced here: 43.2 us
  starting transfers between devices  18.6 us (43%)
  Pallas kernels  12.2 us (28%)
  waiting for transfers between devices  9 us (21%)
  other arithmetic  1.51 us (3%)
  local copies, waits for them, and re-layouts  1.06 us (2%)
  between operations  0.75 us (2%)
    ppermute x12, starting transfers between devices, swap(): return lax.ppermute(values, axis, others)  13.8 us
    pallas_call x10, Pallas kernels, call(): pl.pallas_call(kernel, out_shape=out_shape, in_specs=[pl.BlockSpec(memory...  12.2 us
    ppermute x12, waiting for transfers between devices, swap(): return lax.ppermute(values, axis, others)  7.12 us
    ppermute x3, starting transfers between devices, swap_dp(): return lax.ppermute(values, ('dp', 'proto'), others)  4.86 us
    ppermute x3, waiting for transfers between devices, swap_dp(): return lax.ppermute(values, ('dp', 'proto'), others)  1.87 us
    unnamed x8, local copies, waits for them, and re-layouts  1.06 us
  transfers between devices with their start and end apart: 15, of which 8 were waited for; matrix products, arithmetic and copies ran while one was open for 2% of the time, Pallas kernels for 21%

profile of v7, /device:TPU:0, one launch (start us, length us, event | category | flops | bytes accessed | tf_op | source)
XLA Modules:
  0.0 43.2 jit_solution(1133230197971232840)
XLA Ops:
  1.4 2.4 %collective-permute-start = (bf16[24,256]{1,0:T(8,128)(2,1)S(1)}, bf16[24,256]{1,0:T(8,128)(2,1)S(1)}, u32[]{:S(2)}, u32[]{:S(2)}) collective-permute-start(bf16[24,256]{1,0:T(8,128)(2,1)S(1)} %pad_maximum_fusion.4), channel_id=1, source_target_pairs={{0,3},{1,2},{2,1},{3,0},{4,7},{5,6},{6,5},{7,4},{8,11},{9,10},{10,... | collective-permute-start | bytes 36872 | tf_op jit(solution)/shard_map/ppermute | solution.py:362
  5.2 4.2 %collective-permute-start.1 = (bf16[2,24,256]{2,1,0:T(8,128)(2,1)S(1)}, bf16[2,24,256]{2,1,0:T(8,128)(2,1)S(1)}, u32[]{:S(2)}, u32[]{:S(2)}) collective-permute-start(bf16[2,24,256]{2,1,0:T(8,128)(2,1)S(1)} %get-tuple-element.79), channel_id=1, source_target_pairs={{0,25},{1,24},{2,27},{3,26},{4,29},{5,28},{6,31},{7,30},{8,17},{9,... | collective-permute-start | bytes 73736 | tf_op jit(solution)/shard_map/ppermute | solution.py:370
  10.1 1.5 %collective-permute-start.8 = (bf16[1024,256]{1,0:T(8,128)(2,1)}, bf16[1024,256]{1,0:T(8,128)(2,1)S(1)}, u32[]{:S(2)}, u32[]{:S(2)}) collective-permute-start(bf16[1024,256]{1,0:T(8,128)(2,1)} %refs_1_.1), channel_id=1, source_target_pairs={{0,3},{1,2},{2,1},{3,0},{4,7},{5,6},{6,5},{7,4},{8,11},{9,10},{10,... | collective-permute-start | bytes 1572872 | tf_op jit(solution)/shard_map/ppermute | solution.py:362
  11.7 1.9 %collective-permute-done.2 = bf16[2,24,256]{2,1,0:T(8,128)(2,1)S(1)} collective-permute-done((bf16[2,24,256]{2,1,0:T(8,128)(2,1)S(1)}, bf16[2,24,256]{2,1,0:T(8,128)(2,1)S(1)}, u32[]{:S(2)}, u32[]{:S(2)}) %collective-permute-start.2) | collective-permute-done | bytes 24608 | tf_op jit(solution)/shard_map/ppermute | solution.py:370
  13.6 1.6 %collective-permute-start.4 = (bf16[4,2,24,256]{3,2,1,0:T(8,128)(2,1)S(1)}, bf16[4,2,24,256]{3,2,1,0:T(8,128)(2,1)S(1)}, u32[]{:S(2)}, u32[]{:S(2)}) collective-permute-start(bf16[4,2,24,256]{3,2,1,0:T(8,128)(2,1)S(1)} %pad_maximum_fusion.1), channel_id=1, source_target_pairs={{0,5},{1,4},{2,7},{3,6},{4,1},{5,0},{6,3},{7,2},{8,13},{9,12},{10,... | collective-permute-start | bytes 294920 | tf_op jit(solution)/shard_map/ppermute | solution.py:362
  15.2 1.0 %copy-done = bf16[1024,256]{1,0:T(8,128)(2,1)S(1)} copy-done((bf16[1024,256]{1,0:T(8,128)(2,1)S(1)}, bf16[1024,256]{1,0:T(8,128)(2,1)}, u32[]{:S(2)}) %copy-start) | copy-done | bytes 524312
  16.2 0.8 %shard_map.68 = (bf16[1024,256]{1,0:T(8,128)(2,1)S(1)}, f32[192,128]{1,0:T(8,128)S(1)}, f32[192,128]{1,0:T(8,128)S(1)}) custom-call(s32[6]{0:T(128)S(1)} %pad_add_fusion.place_ref, bf16[1024,256]{1,0:T(8,128)(2,1)S(1)} %copy-done), custom_call_target="tpu_custom_call" | custom-call | flops 134217728 | bytes 1048576 | tf_op jit(solution)/shard_map/pallas_call | solution.py:347
  17.0 1.1 %collective-permute-done.4 = bf16[4,2,24,256]{3,2,1,0:T(8,128)(2,1)S(1)} collective-permute-done((bf16[4,2,24,256]{3,2,1,0:T(8,128)(2,1)S(1)}, bf16[4,2,24,256]{3,2,1,0:T(8,128)(2,1)S(1)}, u32[]{:S(2)}, u32[]{:S(2)}) %collective-permute-start.4) | collective-permute-done | bytes 98336 | tf_op jit(solution)/shard_map/ppermute | solution.py:362
  18.9 1.2 %shard_map.69 = (f32[192,2048]{1,0:T(8,128)S(1)}, f32[8,2048]{1,0:T(8,128)S(1)}, bf16[192,256]{1,0:T(8,128)(2,1)S(1)}, bf16[1024,256]{1,0:T(8,128)(2,1)S(1)}) custom-call(s32[6]{0:T(128)S(1)} %pad_add_fusion.place_ref, bf16[2,4,2,24,256]{4,3,2,1,0:T(8,128)(2,1)S(1)} %pad_maximum_fusion.near_ref, f32[192,128]{1,0:T(8,128)S(1)} %get-tuple-element.47.live_ref.refs_2_, ...), custom_call_target="tpu_custom_call" | custom-call | flops 201326592 | bytes 1572864 | tf_op jit(solution)/shard_map/pallas_call | solution.py:347
  20.2 1.5 %shard_map.70 = (f32[192,2048]{1,0:T(8,128)S(1)}, bf16[192,256]{1,0:T(8,128)(2,1)S(1)}, f32[8,128]{1,0:T(8,128)S(1)}) custom-call(s32[6]{0:T(128)S(1)} %pad_add_fusion.place_ref, bf16[2,4,2,24,256]{4,3,2,1,0:T(8,128)(2,1)S(1)} %collective-permute-done.5.far_ref, f32[192,128]{1,0:T(8,128)S(1)} %get-tuple-element.46.live_ref.refs_3_, ...), custom_call_target="tpu_custom_call" | custom-call | flops 201326592 | bytes 1572864 | tf_op jit(solution)/shard_map/pallas_call | solution.py:347
  21.7 1.4 %collective-permute-start.7 = (f32[8,128]{1,0:T(8,128)S(1)}, f32[8,128]{1,0:T(8,128)S(1)}, u32[]{:S(2)}, u32[]{:S(2)}) collective-permute-start(f32[8,128]{1,0:T(8,128)S(1)} %get-tuple-element.53), channel_id=1, source_target_pairs={{0,5},{1,4},{2,7},{3,6},{4,1},{5,0},{6,3},{7,2},{8,13},{9,12},{10,... | collective-permute-start | bytes 12296 | tf_op jit(solution)/shard_map/ppermute | solution.py:362
  23.1 1.7 %collective-permute-done.7 = f32[8,128]{1,0:T(8,128)S(1)} collective-permute-done((f32[8,128]{1,0:T(8,128)S(1)}, f32[8,128]{1,0:T(8,128)S(1)}, u32[]{:S(2)}, u32[]{:S(2)}) %collective-permute-start.7) | collective-permute-done | bytes 4128 | tf_op jit(solution)/shard_map/ppermute | solution.py:362
  25.3 1.3 %collective-permute-start.9 = (f32[8,128]{1,0:T(8,128)S(1)}, f32[8,128]{1,0:T(8,128)S(1)}, u32[]{:S(2)}, u32[]{:S(2)}) collective-permute-start(f32[8,128]{1,0:T(8,128)S(1)} %add.9.mine_ref), channel_id=1, source_target_pairs={{0,3},{1,2},{2,1},{3,0},{4,7},{5,6},{6,5},{7,4},{8,11},{9,10},{10,... | collective-permute-start | bytes 12296 | tf_op jit(solution)/shard_map/ppermute | solution.py:362
  26.7 1.6 %shard_map.71 = (f32[384,2048]{1,0:T(8,128)S(1)}, bf16[384,256]{1,0:T(8,128)(2,1)S(1)}) custom-call(s32[6]{0:T(128)S(1)} %pad_add_fusion.place_ref, bf16[2,4,2,24,256]{4,3,2,1,0:T(8,128)(2,1)S(1)} %pad_maximum_fusion.near_ref, bf16[2,4,2,24,256]{4,3,2,1,0:T(8,128)(2,1)S(1)} %collective-permute-done.5.far_ref, ...), custom_call_target="tpu_custom_call" | custom-call | flops 402653184 | bytes 3145728 | tf_op jit(solution)/shard_map/pallas_call | solution.py:347
  28.3 1.3 %shard_map.72.mine_ref = f32[8,128]{1,0:T(8,128)S(1)} custom-call(f32[8,128]{1,0:T(8,128)S(1)} %add.9.mine_ref, f32[8,128]{1,0:T(8,128)S(1)} %collective-permute-done.9.other_ref, f32[192,2048]{1,0:T(8,128)S(1)} %get-tuple-element.50.near_weights_ref.near_ref, f32[192,2048]{1,0:T(8,128)S(1)} %get-tuple-element.55.far_ref, ...), custom_call_target="tpu_custom_call" | custom-call | flops 402653184 | bytes 3145728 | tf_op jit(solution)/shard_map/pallas_call | solution.py:347
  29.6 1.4 %collective-permute-start.12 = (f32[8,128]{1,0:T(8,128)S(1)}, f32[8,128]{1,0:T(8,128)S(1)}, u32[]{:S(2)}, u32[]{:S(2)}) collective-permute-start(f32[8,128]{1,0:T(8,128)S(1)} %shard_map.72.mine_ref), channel_id=1, source_target_pairs={{0,5},{1,4},{2,7},{3,6},{4,1},{5,0},{6,3},{7,2},{8,13},{9,12},{10,... | collective-permute-start | bytes 12296 | tf_op jit(solution)/shard_map/ppermute | solution.py:362
  31.0 1.2 %shard_map.73 = (bf16[2048,256]{1,0:T(8,128)(2,1)S(1)}, f32[48,256]{1,0:T(8,128)S(1)}, f32[8,128]{1,0:T(8,128)S(1)}) custom-call(bf16[384,256]{1,0:T(8,128)(2,1)S(1)} %get-tuple-element.62.rows_ref.refs_0_.refs_2_, bf16[1024,256]{1,0:T(8,128)(2,1)S(1)} %copy-done.2, bf16[1024,256]{1,0:T(8,128)(2,1)S(1)} %collective-permute-done.11.refs_1_), custom_call_target="tpu_custom_call" | custom-call | flops 402653184 | bytes 3145728 | tf_op jit(solution)/shard_map/pallas_call | solution.py:347
  32.7 1.5 %shard_map.74 = (f32[8,4096]{1,0:T(8,128)S(1)}, f32[56,256]{1,0:T(8,128)S(1)}, f32[56,256]{1,0:T(8,128)S(1)}) custom-call(s32[6]{0:T(128)S(1)} %pad_add_fusion.place_ref, f32[8,128]{1,0:T(8,128)S(1)} %shard_map.72.mine_ref, f32[8,128]{1,0:T(8,128)S(1)} %collective-permute-done.12.other_ref, f32[192,2048]{1,0:T(8,128)S(1)} %get-tuple-element.50.near_weights_ref.near_ref, ...), custom_call_target="tpu_custom_call" | custom-call | flops 402653184 | bytes 3145728 | tf_op jit(solution)/shard_map/pallas_call | solution.py:347
  34.2 1.4 %collective-permute-start.13 = (f32[56,256]{1,0:T(8,128)S(1)}, f32[56,256]{1,0:T(8,128)S(1)}, u32[]{:S(2)}, u32[]{:S(2)}) collective-permute-start(f32[56,256]{1,0:T(8,128)S(1)} %get-tuple-element.70), channel_id=1, source_target_pairs={{0,3},{1,2},{2,1},{3,0},{4,7},{5,6},{6,5},{7,4},{8,11},{9,10},{10,... | collective-permute-start | bytes 172040 | tf_op jit(solution)/shard_map/ppermute | solution.py:362
  36.2 1.9 %collective-permute-done.13 = f32[56,256]{1,0:T(8,128)S(1)} collective-permute-done((f32[56,256]{1,0:T(8,128)S(1)}, f32[56,256]{1,0:T(8,128)S(1)}, u32[]{:S(2)}, u32[]{:S(2)}) %collective-permute-start.13) | collective-permute-done | bytes 57376 | tf_op jit(solution)/shard_map/ppermute | solution.py:362
  38.2 1.3 %collective-permute-start.14 = (f32[32,256]{1,0:T(8,128)S(1)}, f32[32,256]{1,0:T(8,128)S(1)}, u32[]{:S(2)}, u32[]{:S(2)}) collective-permute-start(f32[32,256]{1,0:T(8,128)S(1)} %pad_maximum_fusion.2), channel_id=1, source_target_pairs={{0,5},{1,4},{2,7},{3,6},{4,1},{5,0},{6,3},{7,2},{8,13},{9,12},{10,... | collective-permute-start | bytes 98312 | tf_op jit(solution)/shard_map/ppermute | solution.py:362
  39.5 1.0 %shard_map.76 = (f32[256,384]{1,0:T(8,128)S(1)}, f32[256,384]{1,0:T(8,128)S(1)}, f32[256,256]{1,0:T(8,128)S(1)}, f32[256,128]{1,0:T(8,128)S(1)}) custom-call(s32[6]{0:T(128)S(1)} %pad_add_fusion.place_ref, f32[8,128]{1,0:T(8,128)S(1)} %shard_map.72.mine_ref, f32[8,128]{1,0:T(8,128)S(1)} %collective-permute-done.12.other_ref, ...), custom_call_target="tpu_custom_call" | custom-call | flops 50331648 | bytes 393216 | tf_op jit(solution)/shard_map/pallas_call | solution.py:347
  40.5 1.1 %collective-permute-done.14.other_ref = f32[32,256]{1,0:T(8,128)S(1)} collective-permute-done((f32[32,256]{1,0:T(8,128)S(1)}, f32[32,256]{1,0:T(8,128)S(1)}, u32[]{:S(2)}, u32[]{:S(2)}) %collective-permute-start.14) | collective-permute-done | bytes 32800 | tf_op jit(solution)/shard_map/ppermute | solution.py:362
  41.6 1.6 %shard_map.77 = (f32[12,256]{1,0:T(8,128)}, f32[1,256,256]{2,1,0:T(8,128)}) custom-call(s32[6]{0:T(128)S(1)} %pad_add_fusion.place_ref, f32[56,256]{1,0:T(8,128)S(1)} %add.10.mine_ref, f32[8,256]{1,0:T(8,128)S(1)} %slice_add_fusion.sums_ref, f32[32,256]{1,0:T(8,128)S(1)} %collective-permute-done.14.other_ref, f32[256,384]{1,0:T(8,128)S(1)} %get-tuple-element.74.targets_ref, ...), custom_call_target="tpu_custom_call" | custom-call | flops 50331648 | bytes 393216 | tf_op jit(solution)/shard_map/pallas_call | solution.py:347
  (34 shorter events, 5.4 us)
Async XLA Ops:
  1.4 3.8 %collective-permute-start = (bf16[24,256]{1,0:T(8,128)(2,1)S(1)}, bf16[24,256]{1,0:T(8,128)(2,1)S(1)}, u32[]{:S(2)}, u32[]{:S(2)}) collective-permute-start(bf16[24,256]{1,0:T(8,128)(2,1)S(1)} %pad_maximum_fusion.4), channel_id=1, source_target_pairs={{0,3},{1,2},{2,1},{3,0},{4,7},{5,6},{6,5},{7,4},{8,11},{9,10},{10,... | collective-permute-start | bytes 36872 | tf_op jit(solution)/shard_map/ppermute | solution.py:362
  5.2 6.5 %collective-permute-start.1 = (bf16[2,24,256]{2,1,0:T(8,128)(2,1)S(1)}, bf16[2,24,256]{2,1,0:T(8,128)(2,1)S(1)}, u32[]{:S(2)}, u32[]{:S(2)}) collective-permute-start(bf16[2,24,256]{2,1,0:T(8,128)(2,1)S(1)} %get-tuple-element.79), channel_id=1, source_target_pairs={{0,25},{1,24},{2,27},{3,26},{4,29},{5,28},{6,31},{7,30},{8,17},{9,... | collective-permute-start | bytes 73736 | tf_op jit(solution)/shard_map/ppermute | solution.py:370
  9.4 4.2 %collective-permute-start.2 = (bf16[2,24,256]{2,1,0:T(8,128)(2,1)S(1)}, bf16[2,24,256]{2,1,0:T(8,128)(2,1)S(1)}, u32[]{:S(2)}, u32[]{:S(2)}) collective-permute-start(bf16[2,24,256]{2,1,0:T(8,128)(2,1)S(1)} %get-tuple-element.79), channel_id=1, source_target_pairs={{0,17},{1,16},{2,19},{3,18},{4,21},{5,20},{6,23},{7,22},{8,25},{9,... | collective-permute-start | bytes 73736 | tf_op jit(solution)/shard_map/ppermute | solution.py:370
  9.4 4.2 %collective-permute-start.3 = (bf16[2,24,256]{2,1,0:T(8,128)(2,1)S(1)}, bf16[2,24,256]{2,1,0:T(8,128)(2,1)S(1)}, u32[]{:S(2)}, u32[]{:S(2)}) collective-permute-start(bf16[2,24,256]{2,1,0:T(8,128)(2,1)S(1)} %get-tuple-element.79), channel_id=1, source_target_pairs={{0,9},{1,8},{2,11},{3,10},{4,13},{5,12},{6,15},{7,14},{8,1},{9,0},... | collective-permute-start | bytes 73736 | tf_op jit(solution)/shard_map/ppermute | solution.py:370
  10.1 8.9 %collective-permute-start.6 = (bf16[1024,256]{1,0:T(8,128)(2,1)}, bf16[1024,256]{1,0:T(8,128)(2,1)S(1)}, u32[]{:S(2)}, u32[]{:S(2)}) collective-permute-start(bf16[1024,256]{1,0:T(8,128)(2,1)} %refs_1_.1), channel_id=1, source_target_pairs={{0,1},{1,0},{2,3},{3,2},{4,5},{5,4},{6,7},{7,6},{8,9},{9,8},{10,11... | collective-permute-start | bytes 1572872 | tf_op jit(solution)/shard_map/ppermute | solution.py:362
  10.1 14.6 %collective-permute-start.8 = (bf16[1024,256]{1,0:T(8,128)(2,1)}, bf16[1024,256]{1,0:T(8,128)(2,1)S(1)}, u32[]{:S(2)}, u32[]{:S(2)}) collective-permute-start(bf16[1024,256]{1,0:T(8,128)(2,1)} %refs_1_.1), channel_id=1, source_target_pairs={{0,3},{1,2},{2,1},{3,0},{4,7},{5,6},{6,5},{7,4},{8,11},{9,10},{10,... | collective-permute-start | bytes 1572872 | tf_op jit(solution)/shard_map/ppermute | solution.py:362
  13.6 4.6 %collective-permute-start.4 = (bf16[4,2,24,256]{3,2,1,0:T(8,128)(2,1)S(1)}, bf16[4,2,24,256]{3,2,1,0:T(8,128)(2,1)S(1)}, u32[]{:S(2)}, u32[]{:S(2)}) collective-permute-start(bf16[4,2,24,256]{3,2,1,0:T(8,128)(2,1)S(1)} %pad_maximum_fusion.1), channel_id=1, source_target_pairs={{0,5},{1,4},{2,7},{3,6},{4,1},{5,0},{6,3},{7,2},{8,13},{9,12},{10,... | collective-permute-start | bytes 294920 | tf_op jit(solution)/shard_map/ppermute | solution.py:362
  15.2 1.0 %copy-start = (bf16[1024,256]{1,0:T(8,128)(2,1)S(1)}, bf16[1024,256]{1,0:T(8,128)(2,1)}, u32[]{:S(2)}) copy-start(bf16[1024,256]{1,0:T(8,128)(2,1)} %refs_1_.1) | copy-start | bytes 1572868
  18.2 2.0 %collective-permute-start.5 = (bf16[2,4,2,24,256]{4,3,2,1,0:T(8,128)(2,1)S(1)}, bf16[2,4,2,24,256]{4,3,2,1,0:T(8,128)(2,1)S(1)}, u32[]{:S(2)}, u32[]{:S(2)}) collective-permute-start(bf16[2,4,2,24,256]{4,3,2,1,0:T(8,128)(2,1)S(1)} %pad_maximum_fusion.near_ref), channel_id=1, source_target_pairs={{0,1},{1,0},{2,3},{3,2},{4,5},{5,4},{6,7},{7,6},{8,9},{9,8},{10,11... | collective-permute-start | bytes 589832 | tf_op jit(solution)/shard_map/ppermute | solution.py:362
  20.1 4.8 %copy-start.2 = (bf16[1024,256]{1,0:T(8,128)(2,1)S(1)}, bf16[1024,256]{1,0:T(8,128)(2,1)}, u32[]{:S(2)}) copy-start(bf16[1024,256]{1,0:T(8,128)(2,1)} %refs_2_.1) | copy-start | bytes 1572868
  21.7 3.1 %collective-permute-start.7 = (f32[8,128]{1,0:T(8,128)S(1)}, f32[8,128]{1,0:T(8,128)S(1)}, u32[]{:S(2)}, u32[]{:S(2)}) collective-permute-start(f32[8,128]{1,0:T(8,128)S(1)} %get-tuple-element.53), channel_id=1, source_target_pairs={{0,5},{1,4},{2,7},{3,6},{4,1},{5,0},{6,3},{7,2},{8,13},{9,12},{10,... | collective-permute-start | bytes 12296 | tf_op jit(solution)/shard_map/ppermute | solution.py:362
  24.8 1.9 %collective-permute-start.10 = (bf16[1024,256]{1,0:T(8,128)(2,1)S(1)}, bf16[1024,256]{1,0:T(8,128)(2,1)S(1)}, u32[]{:S(2)}, u32[]{:S(2)}) collective-permute-start(bf16[1024,256]{1,0:T(8,128)(2,1)S(1)} %collective-permute-done.8.refs_4_), channel_id=1, source_target_pairs={{0,1},{1,0},{2,3},{3,2},{4,5},{5,4},{6,7},{7,6},{8,9},{9,8},{10,11... | collective-permute-start | bytes 1572872 | tf_op jit(solution)/shard_map/ppermute | solution.py:362
  25.0 4.6 %collective-permute-start.11 = (bf16[1024,256]{1,0:T(8,128)(2,1)S(1)}, bf16[1024,256]{1,0:T(8,128)(2,1)S(1)}, u32[]{:S(2)}, u32[]{:S(2)}) collective-permute-start(bf16[1024,256]{1,0:T(8,128)(2,1)S(1)} %copy-done.2), channel_id=1, source_target_pairs={{0,1},{1,0},{2,3},{3,2},{4,5},{5,4},{6,7},{7,6},{8,9},{9,8},{10,11... | collective-permute-start | bytes 1572872 | tf_op jit(solution)/shard_map/ppermute | solution.py:362
  25.3 3.0 %collective-permute-start.9 = (f32[8,128]{1,0:T(8,128)S(1)}, f32[8,128]{1,0:T(8,128)S(1)}, u32[]{:S(2)}, u32[]{:S(2)}) collective-permute-start(f32[8,128]{1,0:T(8,128)S(1)} %add.9.mine_ref), channel_id=1, source_target_pairs={{0,3},{1,2},{2,1},{3,0},{4,7},{5,6},{6,5},{7,4},{8,11},{9,10},{10,... | collective-permute-start | bytes 12296 | tf_op jit(solution)/shard_map/ppermute | solution.py:362
  29.6 3.1 %collective-permute-start.12 = (f32[8,128]{1,0:T(8,128)S(1)}, f32[8,128]{1,0:T(8,128)S(1)}, u32[]{:S(2)}, u32[]{:S(2)}) collective-permute-start(f32[8,128]{1,0:T(8,128)S(1)} %shard_map.72.mine_ref), channel_id=1, source_target_pairs={{0,5},{1,4},{2,7},{3,6},{4,1},{5,0},{6,3},{7,2},{8,13},{9,12},{10,... | collective-permute-start | bytes 12296 | tf_op jit(solution)/shard_map/ppermute | solution.py:362
  34.2 4.0 %collective-permute-start.13 = (f32[56,256]{1,0:T(8,128)S(1)}, f32[56,256]{1,0:T(8,128)S(1)}, u32[]{:S(2)}, u32[]{:S(2)}) collective-permute-start(f32[56,256]{1,0:T(8,128)S(1)} %get-tuple-element.70), channel_id=1, source_target_pairs={{0,3},{1,2},{2,1},{3,0},{4,7},{5,6},{6,5},{7,4},{8,11},{9,10},{10,... | collective-permute-start | bytes 172040 | tf_op jit(solution)/shard_map/ppermute | solution.py:362
  35.6 3.9 %copy-start.1 = (bf16[1024,256]{1,0:T(8,128)(2,1)S(1)}, bf16[1024,256]{1,0:T(8,128)(2,1)}, u32[]{:S(2)}) copy-start(bf16[1024,256]{1,0:T(8,128)(2,1)} %refs_1_.1) | copy-start | bytes 1572868
  36.2 5.4 %copy-start.3 = (bf16[12,256]{1,0:T(8,128)(2,1)S(1)}, bf16[12,256]{1,0:T(8,128)(2,1)}, u32[]{:S(2)}) copy-start(bf16[12,256]{1,0:T(8,128)(2,1)} %refs_3_.1) | copy-start | bytes 18436
  38.2 3.4 %collective-permute-start.14 = (f32[32,256]{1,0:T(8,128)S(1)}, f32[32,256]{1,0:T(8,128)S(1)}, u32[]{:S(2)}, u32[]{:S(2)}) collective-permute-start(f32[32,256]{1,0:T(8,128)S(1)} %pad_maximum_fusion.2), channel_id=1, source_target_pairs={{0,5},{1,4},{2,7},{3,6},{4,1},{5,0},{6,3},{7,2},{8,13},{9,12},{10,... | collective-permute-start | bytes 98312 | tf_op jit(solution)/shard_map/ppermute | solution.py:362

commit v8 on v7

--- a/solution.py
+++ b/solution.py
@@ -106,6 +106,10 @@
     return jnp.concatenate([column, column], axis=1)
 
 
+def spread(column, lanes):
+    return jnp.concatenate([column] * (lanes // LANES), axis=1)
+
+
 def weighted_rows(panels, left, scale_ref, part_ref, add=False):
     tiles = panels[0].shape[1] // LANES
     scales = [scale_ref[:, left + k * LANES : left + (k + 1) * LANES] for k in range(tiles)]
@@ -168,7 +172,7 @@
     rows = near_ref.shape[3] // 2
     rows_near = place_rows(place_ref, near_ref, 0, rows, scratch)
     rows_ref[...] = rows_near
-    live = twice(live_ref[...])
+    live = spread(live_ref[...], chunk)
     protos = own_units_ref.shape[0]
     for start in range(0, 2 * protos, chunk):
         at = slice(start, start + chunk)
@@ -186,7 +190,7 @@
     rows = far_ref.shape[3] // 2
     rows_far = place_rows(place_ref, far_ref, 0, rows, scratch)
     rows_ref[...] = rows_far
-    live = twice(live_ref[...])
+    live = spread(live_ref[...], chunk)
     protos = unit_refs[0].shape[0]
     for k, unit_ref in enumerate(unit_refs):
         for start in range(0, protos, chunk):
@@ -204,7 +208,7 @@
     *proto_refs, weights_ref, student_ref, scratch = refs
     protos = proto_refs[0].shape[0]
     rows_all = jnp.concatenate([near_rows_ref[...], far_rows_ref[...]], axis=0)
-    live = twice(jnp.concatenate([near_live_ref[...], far_live_ref[...]], axis=0))
+    live = spread(jnp.concatenate([near_live_ref[...], far_live_ref[...]], axis=0), chunk)
     for k, proto_ref in enumerate(proto_refs):
         for start in range(0, protos, chunk):
             units = quick_unit(proto_ref[start : start + chunk, :])[0].astype(jnp.bfloat16)
@@ -375,6 +379,7 @@
     rows, width = student_feat.shape
     protos = prototypes.shape[0]
     own = protos // n_dp
+    piece = 2 * own
     all_rows = n_dp * n_proto * rows
     half = all_rows // 2
     first = 4 * rows
@@ -412,7 +417,7 @@
     far = swap(near, "proto", CORE)
 
     near_weights, near_sums, near_rows, other_units = call(
-        functools.partial(near_kernel, own),
+        functools.partial(near_kernel, piece),
         (
             f32((half, held)),
             f32((8, held)),
@@ -425,7 +430,7 @@
         work=held * half,
     )
     far_weights, far_rows, sums = call(
-        functools.partial(far_kernel, own),
+        functools.partial(far_kernel, piece),
         (f32((half, held)), bf16((half, width)), tile),
         (place, far, far_live, near_weights, near_sums, teacher_units, other_units),
         smem=1,
@@ -436,7 +441,7 @@
     sums, across_protos = lax.optimization_barrier((sums, across_protos))
     parts = (sums, swap(sums, "proto", X_CROSS))
     across_weights, student_rows = call(
-        functools.partial(across_kernel, own),
+        functools.partial(across_kernel, piece),
         (f32((all_rows, held)), bf16((all_rows, width))),
         (
             place,
@@ -467,10 +472,10 @@
         )
         parts = (sums, swap(sums, "proto", Y_CROSS))
     student_units, exp_pull, exp_sums = call(
-        functools.partial(exps_kernel, own),
+        functools.partial(exps_kernel, piece),
         (bf16((held, width)), f32((first, width)), tile),
         (student_rows, *student_protos),
-        scratch=[pltpu.VMEM((all_rows, own), jnp.float32)],
+        scratch=[pltpu.VMEM((all_rows, piece), jnp.float32)],
         work=held * all_rows,
     )
     scales, keep, send = call(

time: 43.5 us -> 43.5 us (level)
  no operation moved by 1% of the time
where the time goes in v8:
time: 43.5 us; the launch traced here: 43.2 us
  starting transfers between devices  18.6 us (43%)
  Pallas kernels  12.1 us (28%)
  waiting for transfers between devices  9.16 us (21%)
  other arithmetic  1.51 us (3%)
  local copies, waits for them, and re-layouts  1.06 us (2%)
  between operations  0.76 us (2%)
    ppermute x12, starting transfers between devices, swap(): return lax.ppermute(values, axis, others)  13.8 us
    pallas_call x10, Pallas kernels, call(): pl.pallas_call(kernel, out_shape=out_shape, in_specs=[pl.BlockSpec(memory...  12.1 us
    ppermute x12, waiting for transfers between devices, swap(): return lax.ppermute(values, axis, others)  7.29 us
    ppermute x3, starting transfers between devices, swap_dp(): return lax.ppermute(values, ('dp', 'proto'), others)  4.86 us
    ppermute x3, waiting for transfers between devices, swap_dp(): return lax.ppermute(values, ('dp', 'proto'), others)  1.87 us
    unnamed x8, local copies, waits for them, and re-layouts  1.06 us
  transfers between devices with their start and end apart: 15, of which 8 were waited for; matrix products, arithmetic and copies ran while one was open for 2% of the time, Pallas kernels for 21%

profile of v8, /device:TPU:0, one launch (start us, length us, event | category | flops | bytes accessed | tf_op | source)
XLA Modules:
  0.0 43.2 jit_solution(13764168233420096283)
XLA Ops:
  1.4 2.4 %collective-permute-start = (bf16[24,256]{1,0:T(8,128)(2,1)S(1)}, bf16[24,256]{1,0:T(8,128)(2,1)S(1)}, u32[]{:S(2)}, u32[]{:S(2)}) collective-permute-start(bf16[24,256]{1,0:T(8,128)(2,1)S(1)} %pad_maximum_fusion.4), channel_id=1, source_target_pairs={{0,3},{1,2},{2,1},{3,0},{4,7},{5,6},{6,5},{7,4},{8,11},{9,10},{10,... | collective-permute-start | bytes 36872 | tf_op jit(solution)/shard_map/ppermute | solution.py:366
  5.2 4.2 %collective-permute-start.1 = (bf16[2,24,256]{2,1,0:T(8,128)(2,1)S(1)}, bf16[2,24,256]{2,1,0:T(8,128)(2,1)S(1)}, u32[]{:S(2)}, u32[]{:S(2)}) collective-permute-start(bf16[2,24,256]{2,1,0:T(8,128)(2,1)S(1)} %get-tuple-element.79), channel_id=1, source_target_pairs={{0,25},{1,24},{2,27},{3,26},{4,29},{5,28},{6,31},{7,30},{8,17},{9,... | collective-permute-start | bytes 73736 | tf_op jit(solution)/shard_map/ppermute | solution.py:374
  10.1 1.5 %collective-permute-start.8 = (bf16[1024,256]{1,0:T(8,128)(2,1)}, bf16[1024,256]{1,0:T(8,128)(2,1)S(1)}, u32[]{:S(2)}, u32[]{:S(2)}) collective-permute-start(bf16[1024,256]{1,0:T(8,128)(2,1)} %refs_1_.1), channel_id=1, source_target_pairs={{0,3},{1,2},{2,1},{3,0},{4,7},{5,6},{6,5},{7,4},{8,11},{9,10},{10,... | collective-permute-start | bytes 1572872 | tf_op jit(solution)/shard_map/ppermute | solution.py:366
  11.7 1.9 %collective-permute-done.2 = bf16[2,24,256]{2,1,0:T(8,128)(2,1)S(1)} collective-permute-done((bf16[2,24,256]{2,1,0:T(8,128)(2,1)S(1)}, bf16[2,24,256]{2,1,0:T(8,128)(2,1)S(1)}, u32[]{:S(2)}, u32[]{:S(2)}) %collective-permute-start.2) | collective-permute-done | bytes 24608 | tf_op jit(solution)/shard_map/ppermute | solution.py:374
  13.6 1.6 %collective-permute-start.4 = (bf16[4,2,24,256]{3,2,1,0:T(8,128)(2,1)S(1)}, bf16[4,2,24,256]{3,2,1,0:T(8,128)(2,1)S(1)}, u32[]{:S(2)}, u32[]{:S(2)}) collective-permute-start(bf16[4,2,24,256]{3,2,1,0:T(8,128)(2,1)S(1)} %pad_maximum_fusion.1), channel_id=1, source_target_pairs={{0,5},{1,4},{2,7},{3,6},{4,1},{5,0},{6,3},{7,2},{8,13},{9,12},{10,... | collective-permute-start | bytes 294920 | tf_op jit(solution)/shard_map/ppermute | solution.py:366
  15.2 1.0 %copy-done = bf16[1024,256]{1,0:T(8,128)(2,1)S(1)} copy-done((bf16[1024,256]{1,0:T(8,128)(2,1)S(1)}, bf16[1024,256]{1,0:T(8,128)(2,1)}, u32[]{:S(2)}) %copy-start) | copy-done | bytes 524312
  16.2 0.8 %shard_map.68 = (bf16[1024,256]{1,0:T(8,128)(2,1)S(1)}, f32[192,128]{1,0:T(8,128)S(1)}, f32[192,128]{1,0:T(8,128)S(1)}) custom-call(s32[6]{0:T(128)S(1)} %pad_add_fusion.place_ref, bf16[1024,256]{1,0:T(8,128)(2,1)S(1)} %copy-done), custom_call_target="tpu_custom_call" | custom-call | flops 134217728 | bytes 1048576 | tf_op jit(solution)/shard_map/pallas_call | solution.py:351
  17.0 1.1 %collective-permute-done.4 = bf16[4,2,24,256]{3,2,1,0:T(8,128)(2,1)S(1)} collective-permute-done((bf16[4,2,24,256]{3,2,1,0:T(8,128)(2,1)S(1)}, bf16[4,2,24,256]{3,2,1,0:T(8,128)(2,1)S(1)}, u32[]{:S(2)}, u32[]{:S(2)}) %collective-permute-start.4) | collective-permute-done | bytes 98336 | tf_op jit(solution)/shard_map/ppermute | solution.py:366
  18.9 1.2 %shard_map.69 = (f32[192,2048]{1,0:T(8,128)S(1)}, f32[8,2048]{1,0:T(8,128)S(1)}, bf16[192,256]{1,0:T(8,128)(2,1)S(1)}, bf16[1024,256]{1,0:T(8,128)(2,1)S(1)}) custom-call(s32[6]{0:T(128)S(1)} %pad_add_fusion.place_ref, bf16[2,4,2,24,256]{4,3,2,1,0:T(8,128)(2,1)S(1)} %pad_maximum_fusion.near_ref, f32[192,128]{1,0:T(8,128)S(1)} %get-tuple-element.47.live_ref.refs_2_, ...), custom_call_target="tpu_custom_call" | custom-call | flops 201326592 | bytes 1572864 | tf_op jit(solution)/shard_map/pallas_call | solution.py:351
  20.2 1.5 %shard_map.70 = (f32[192,2048]{1,0:T(8,128)S(1)}, bf16[192,256]{1,0:T(8,128)(2,1)S(1)}, f32[8,128]{1,0:T(8,128)S(1)}) custom-call(s32[6]{0:T(128)S(1)} %pad_add_fusion.place_ref, bf16[2,4,2,24,256]{4,3,2,1,0:T(8,128)(2,1)S(1)} %collective-permute-done.5.far_ref, f32[192,128]{1,0:T(8,128)S(1)} %get-tuple-element.46.live_ref.refs_3_, ...), custom_call_target="tpu_custom_call" | custom-call | flops 201326592 | bytes 1572864 | tf_op jit(solution)/shard_map/pallas_call | solution.py:351
  21.7 1.4 %collective-permute-start.7 = (f32[8,128]{1,0:T(8,128)S(1)}, f32[8,128]{1,0:T(8,128)S(1)}, u32[]{:S(2)}, u32[]{:S(2)}) collective-permute-start(f32[8,128]{1,0:T(8,128)S(1)} %get-tuple-element.53), channel_id=1, source_target_pairs={{0,5},{1,4},{2,7},{3,6},{4,1},{5,0},{6,3},{7,2},{8,13},{9,12},{10,... | collective-permute-start | bytes 12296 | tf_op jit(solution)/shard_map/ppermute | solution.py:366
  23.1 1.7 %collective-permute-done.7 = f32[8,128]{1,0:T(8,128)S(1)} collective-permute-done((f32[8,128]{1,0:T(8,128)S(1)}, f32[8,128]{1,0:T(8,128)S(1)}, u32[]{:S(2)}, u32[]{:S(2)}) %collective-permute-start.7) | collective-permute-done | bytes 4128 | tf_op jit(solution)/shard_map/ppermute | solution.py:366
  25.3 1.3 %collective-permute-start.9 = (f32[8,128]{1,0:T(8,128)S(1)}, f32[8,128]{1,0:T(8,128)S(1)}, u32[]{:S(2)}, u32[]{:S(2)}) collective-permute-start(f32[8,128]{1,0:T(8,128)S(1)} %add.9.mine_ref), channel_id=1, source_target_pairs={{0,3},{1,2},{2,1},{3,0},{4,7},{5,6},{6,5},{7,4},{8,11},{9,10},{10,... | collective-permute-start | bytes 12296 | tf_op jit(solution)/shard_map/ppermute | solution.py:366
  26.7 1.6 %shard_map.71 = (f32[384,2048]{1,0:T(8,128)S(1)}, bf16[384,256]{1,0:T(8,128)(2,1)S(1)}) custom-call(s32[6]{0:T(128)S(1)} %pad_add_fusion.place_ref, bf16[2,4,2,24,256]{4,3,2,1,0:T(8,128)(2,1)S(1)} %pad_maximum_fusion.near_ref, bf16[2,4,2,24,256]{4,3,2,1,0:T(8,128)(2,1)S(1)} %collective-permute-done.5.far_ref, ...), custom_call_target="tpu_custom_call" | custom-call | flops 402653184 | bytes 3145728 | tf_op jit(solution)/shard_map/pallas_call | solution.py:351
  28.3 1.3 %shard_map.72.mine_ref = f32[8,128]{1,0:T(8,128)S(1)} custom-call(f32[8,128]{1,0:T(8,128)S(1)} %add.9.mine_ref, f32[8,128]{1,0:T(8,128)S(1)} %collective-permute-done.9.other_ref, f32[192,2048]{1,0:T(8,128)S(1)} %get-tuple-element.50.near_weights_ref.near_ref, f32[192,2048]{1,0:T(8,128)S(1)} %get-tuple-element.55.far_ref, ...), custom_call_target="tpu_custom_call" | custom-call | flops 402653184 | bytes 3145728 | tf_op jit(solution)/shard_map/pallas_call | solution.py:351
  29.6 1.4 %collective-permute-start.12 = (f32[8,128]{1,0:T(8,128)S(1)}, f32[8,128]{1,0:T(8,128)S(1)}, u32[]{:S(2)}, u32[]{:S(2)}) collective-permute-start(f32[8,128]{1,0:T(8,128)S(1)} %shard_map.72.mine_ref), channel_id=1, source_target_pairs={{0,5},{1,4},{2,7},{3,6},{4,1},{5,0},{6,3},{7,2},{8,13},{9,12},{10,... | collective-permute-start | bytes 12296 | tf_op jit(solution)/shard_map/ppermute | solution.py:366
  31.0 1.1 %shard_map.73 = (bf16[2048,256]{1,0:T(8,128)(2,1)S(1)}, f32[48,256]{1,0:T(8,128)S(1)}, f32[8,128]{1,0:T(8,128)S(1)}) custom-call(bf16[384,256]{1,0:T(8,128)(2,1)S(1)} %get-tuple-element.62.rows_ref.refs_0_.refs_2_, bf16[1024,256]{1,0:T(8,128)(2,1)S(1)} %copy-done.2, bf16[1024,256]{1,0:T(8,128)(2,1)S(1)} %collective-permute-done.11.refs_1_), custom_call_target="tpu_custom_call" | custom-call | flops 402653184 | bytes 3145728 | tf_op jit(solution)/shard_map/pallas_call | solution.py:351
  32.7 1.5 %shard_map.74 = (f32[8,4096]{1,0:T(8,128)S(1)}, f32[56,256]{1,0:T(8,128)S(1)}, f32[56,256]{1,0:T(8,128)S(1)}) custom-call(s32[6]{0:T(128)S(1)} %pad_add_fusion.place_ref, f32[8,128]{1,0:T(8,128)S(1)} %shard_map.72.mine_ref, f32[8,128]{1,0:T(8,128)S(1)} %collective-permute-done.12.other_ref, f32[192,2048]{1,0:T(8,128)S(1)} %get-tuple-element.50.near_weights_ref.near_ref, ...), custom_call_target="tpu_custom_call" | custom-call | flops 402653184 | bytes 3145728 | tf_op jit(solution)/shard_map/pallas_call | solution.py:351
  34.2 1.4 %collective-permute-start.13 = (f32[56,256]{1,0:T(8,128)S(1)}, f32[56,256]{1,0:T(8,128)S(1)}, u32[]{:S(2)}, u32[]{:S(2)}) collective-permute-start(f32[56,256]{1,0:T(8,128)S(1)} %get-tuple-element.70), channel_id=1, source_target_pairs={{0,3},{1,2},{2,1},{3,0},{4,7},{5,6},{6,5},{7,4},{8,11},{9,10},{10,... | collective-permute-start | bytes 172040 | tf_op jit(solution)/shard_map/ppermute | solution.py:366
  36.2 1.9 %collective-permute-done.13 = f32[56,256]{1,0:T(8,128)S(1)} collective-permute-done((f32[56,256]{1,0:T(8,128)S(1)}, f32[56,256]{1,0:T(8,128)S(1)}, u32[]{:S(2)}, u32[]{:S(2)}) %collective-permute-start.13) | collective-permute-done | bytes 57376 | tf_op jit(solution)/shard_map/ppermute | solution.py:366
  38.2 1.3 %collective-permute-start.14 = (f32[32,256]{1,0:T(8,128)S(1)}, f32[32,256]{1,0:T(8,128)S(1)}, u32[]{:S(2)}, u32[]{:S(2)}) collective-permute-start(f32[32,256]{1,0:T(8,128)S(1)} %pad_maximum_fusion.2), channel_id=1, source_target_pairs={{0,5},{1,4},{2,7},{3,6},{4,1},{5,0},{6,3},{7,2},{8,13},{9,12},{10,... | collective-permute-start | bytes 98312 | tf_op jit(solution)/shard_map/ppermute | solution.py:366
  39.5 1.0 %shard_map.76 = (f32[256,384]{1,0:T(8,128)S(1)}, f32[256,384]{1,0:T(8,128)S(1)}, f32[256,256]{1,0:T(8,128)S(1)}, f32[256,128]{1,0:T(8,128)S(1)}) custom-call(s32[6]{0:T(128)S(1)} %pad_add_fusion.place_ref, f32[8,128]{1,0:T(8,128)S(1)} %shard_map.72.mine_ref, f32[8,128]{1,0:T(8,128)S(1)} %collective-permute-done.12.other_ref, ...), custom_call_target="tpu_custom_call" | custom-call | flops 50331648 | bytes 393216 | tf_op jit(solution)/shard_map/pallas_call | solution.py:351
  40.5 1.1 %collective-permute-done.14.other_ref = f32[32,256]{1,0:T(8,128)S(1)} collective-permute-done((f32[32,256]{1,0:T(8,128)S(1)}, f32[32,256]{1,0:T(8,128)S(1)}, u32[]{:S(2)}, u32[]{:S(2)}) %collective-permute-start.14) | collective-permute-done | bytes 32800 | tf_op jit(solution)/shard_map/ppermute | solution.py:366
  41.6 1.6 %shard_map.77 = (f32[12,256]{1,0:T(8,128)}, f32[1,256,256]{2,1,0:T(8,128)}) custom-call(s32[6]{0:T(128)S(1)} %pad_add_fusion.place_ref, f32[56,256]{1,0:T(8,128)S(1)} %add.10.mine_ref, f32[8,256]{1,0:T(8,128)S(1)} %slice_add_fusion.sums_ref, f32[32,256]{1,0:T(8,128)S(1)} %collective-permute-done.14.other_ref, f32[256,384]{1,0:T(8,128)S(1)} %get-tuple-element.74.targets_ref, ...), custom_call_target="tpu_custom_call" | custom-call | flops 50331648 | bytes 393216 | tf_op jit(solution)/shard_map/pallas_call | solution.py:351
  (34 shorter events, 5.6 us)
Async XLA Ops:
  1.4 3.8 %collective-permute-start = (bf16[24,256]{1,0:T(8,128)(2,1)S(1)}, bf16[24,256]{1,0:T(8,128)(2,1)S(1)}, u32[]{:S(2)}, u32[]{:S(2)}) collective-permute-start(bf16[24,256]{1,0:T(8,128)(2,1)S(1)} %pad_maximum_fusion.4), channel_id=1, source_target_pairs={{0,3},{1,2},{2,1},{3,0},{4,7},{5,6},{6,5},{7,4},{8,11},{9,10},{10,... | collective-permute-start | bytes 36872 | tf_op jit(solution)/shard_map/ppermute | solution.py:366
  5.2 6.5 %collective-permute-start.1 = (bf16[2,24,256]{2,1,0:T(8,128)(2,1)S(1)}, bf16[2,24,256]{2,1,0:T(8,128)(2,1)S(1)}, u32[]{:S(2)}, u32[]{:S(2)}) collective-permute-start(bf16[2,24,256]{2,1,0:T(8,128)(2,1)S(1)} %get-tuple-element.79), channel_id=1, source_target_pairs={{0,25},{1,24},{2,27},{3,26},{4,29},{5,28},{6,31},{7,30},{8,17},{9,... | collective-permute-start | bytes 73736 | tf_op jit(solution)/shard_map/ppermute | solution.py:374
  9.4 4.2 %collective-permute-start.2 = (bf16[2,24,256]{2,1,0:T(8,128)(2,1)S(1)}, bf16[2,24,256]{2,1,0:T(8,128)(2,1)S(1)}, u32[]{:S(2)}, u32[]{:S(2)}) collective-permute-start(bf16[2,24,256]{2,1,0:T(8,128)(2,1)S(1)} %get-tuple-element.79), channel_id=1, source_target_pairs={{0,17},{1,16},{2,19},{3,18},{4,21},{5,20},{6,23},{7,22},{8,25},{9,... | collective-permute-start | bytes 73736 | tf_op jit(solution)/shard_map/ppermute | solution.py:374
  9.4 4.2 %collective-permute-start.3 = (bf16[2,24,256]{2,1,0:T(8,128)(2,1)S(1)}, bf16[2,24,256]{2,1,0:T(8,128)(2,1)S(1)}, u32[]{:S(2)}, u32[]{:S(2)}) collective-permute-start(bf16[2,24,256]{2,1,0:T(8,128)(2,1)S(1)} %get-tuple-element.79), channel_id=1, source_target_pairs={{0,9},{1,8},{2,11},{3,10},{4,13},{5,12},{6,15},{7,14},{8,1},{9,0},... | collective-permute-start | bytes 73736 | tf_op jit(solution)/shard_map/ppermute | solution.py:374
  10.1 8.9 %collective-permute-start.6 = (bf16[1024,256]{1,0:T(8,128)(2,1)}, bf16[1024,256]{1,0:T(8,128)(2,1)S(1)}, u32[]{:S(2)}, u32[]{:S(2)}) collective-permute-start(bf16[1024,256]{1,0:T(8,128)(2,1)} %refs_1_.1), channel_id=1, source_target_pairs={{0,1},{1,0},{2,3},{3,2},{4,5},{5,4},{6,7},{7,6},{8,9},{9,8},{10,11... | collective-permute-start | bytes 1572872 | tf_op jit(solution)/shard_map/ppermute | solution.py:366
  10.1 14.6 %collective-permute-start.8 = (bf16[1024,256]{1,0:T(8,128)(2,1)}, bf16[1024,256]{1,0:T(8,128)(2,1)S(1)}, u32[]{:S(2)}, u32[]{:S(2)}) collective-permute-start(bf16[1024,256]{1,0:T(8,128)(2,1)} %refs_1_.1), channel_id=1, source_target_pairs={{0,3},{1,2},{2,1},{3,0},{4,7},{5,6},{6,5},{7,4},{8,11},{9,10},{10,... | collective-permute-start | bytes 1572872 | tf_op jit(solution)/shard_map/ppermute | solution.py:366
  13.6 4.6 %collective-permute-start.4 = (bf16[4,2,24,256]{3,2,1,0:T(8,128)(2,1)S(1)}, bf16[4,2,24,256]{3,2,1,0:T(8,128)(2,1)S(1)}, u32[]{:S(2)}, u32[]{:S(2)}) collective-permute-start(bf16[4,2,24,256]{3,2,1,0:T(8,128)(2,1)S(1)} %pad_maximum_fusion.1), channel_id=1, source_target_pairs={{0,5},{1,4},{2,7},{3,6},{4,1},{5,0},{6,3},{7,2},{8,13},{9,12},{10,... | collective-permute-start | bytes 294920 | tf_op jit(solution)/shard_map/ppermute | solution.py:366
  15.2 1.0 %copy-start = (bf16[1024,256]{1,0:T(8,128)(2,1)S(1)}, bf16[1024,256]{1,0:T(8,128)(2,1)}, u32[]{:S(2)}) copy-start(bf16[1024,256]{1,0:T(8,128)(2,1)} %refs_1_.1) | copy-start | bytes 1572868
  18.2 2.0 %collective-permute-start.5 = (bf16[2,4,2,24,256]{4,3,2,1,0:T(8,128)(2,1)S(1)}, bf16[2,4,2,24,256]{4,3,2,1,0:T(8,128)(2,1)S(1)}, u32[]{:S(2)}, u32[]{:S(2)}) collective-permute-start(bf16[2,4,2,24,256]{4,3,2,1,0:T(8,128)(2,1)S(1)} %pad_maximum_fusion.near_ref), channel_id=1, source_target_pairs={{0,1},{1,0},{2,3},{3,2},{4,5},{5,4},{6,7},{7,6},{8,9},{9,8},{10,11... | collective-permute-start | bytes 589832 | tf_op jit(solution)/shard_map/ppermute | solution.py:366
  20.1 4.8 %copy-start.2 = (bf16[1024,256]{1,0:T(8,128)(2,1)S(1)}, bf16[1024,256]{1,0:T(8,128)(2,1)}, u32[]{:S(2)}) copy-start(bf16[1024,256]{1,0:T(8,128)(2,1)} %refs_2_.1) | copy-start | bytes 1572868
  21.7 3.1 %collective-permute-start.7 = (f32[8,128]{1,0:T(8,128)S(1)}, f32[8,128]{1,0:T(8,128)S(1)}, u32[]{:S(2)}, u32[]{:S(2)}) collective-permute-start(f32[8,128]{1,0:T(8,128)S(1)} %get-tuple-element.53), channel_id=1, source_target_pairs={{0,5},{1,4},{2,7},{3,6},{4,1},{5,0},{6,3},{7,2},{8,13},{9,12},{10,... | collective-permute-start | bytes 12296 | tf_op jit(solution)/shard_map/ppermute | solution.py:366
  24.8 1.9 %collective-permute-start.10 = (bf16[1024,256]{1,0:T(8,128)(2,1)S(1)}, bf16[1024,256]{1,0:T(8,128)(2,1)S(1)}, u32[]{:S(2)}, u32[]{:S(2)}) collective-permute-start(bf16[1024,256]{1,0:T(8,128)(2,1)S(1)} %collective-permute-done.8.refs_4_), channel_id=1, source_target_pairs={{0,1},{1,0},{2,3},{3,2},{4,5},{5,4},{6,7},{7,6},{8,9},{9,8},{10,11... | collective-permute-start | bytes 1572872 | tf_op jit(solution)/shard_map/ppermute | solution.py:366
  25.0 4.6 %collective-permute-start.11 = (bf16[1024,256]{1,0:T(8,128)(2,1)S(1)}, bf16[1024,256]{1,0:T(8,128)(2,1)S(1)}, u32[]{:S(2)}, u32[]{:S(2)}) collective-permute-start(bf16[1024,256]{1,0:T(8,128)(2,1)S(1)} %copy-done.2), channel_id=1, source_target_pairs={{0,1},{1,0},{2,3},{3,2},{4,5},{5,4},{6,7},{7,6},{8,9},{9,8},{10,11... | collective-permute-start | bytes 1572872 | tf_op jit(solution)/shard_map/ppermute | solution.py:366
  25.3 3.0 %collective-permute-start.9 = (f32[8,128]{1,0:T(8,128)S(1)}, f32[8,128]{1,0:T(8,128)S(1)}, u32[]{:S(2)}, u32[]{:S(2)}) collective-permute-start(f32[8,128]{1,0:T(8,128)S(1)} %add.9.mine_ref), channel_id=1, source_target_pairs={{0,3},{1,2},{2,1},{3,0},{4,7},{5,6},{6,5},{7,4},{8,11},{9,10},{10,... | collective-permute-start | bytes 12296 | tf_op jit(solution)/shard_map/ppermute | solution.py:366
  29.6 3.1 %collective-permute-start.12 = (f32[8,128]{1,0:T(8,128)S(1)}, f32[8,128]{1,0:T(8,128)S(1)}, u32[]{:S(2)}, u32[]{:S(2)}) collective-permute-start(f32[8,128]{1,0:T(8,128)S(1)} %shard_map.72.mine_ref), channel_id=1, source_target_pairs={{0,5},{1,4},{2,7},{3,6},{4,1},{5,0},{6,3},{7,2},{8,13},{9,12},{10,... | collective-permute-start | bytes 12296 | tf_op jit(solution)/shard_map/ppermute | solution.py:366
  34.2 4.0 %collective-permute-start.13 = (f32[56,256]{1,0:T(8,128)S(1)}, f32[56,256]{1,0:T(8,128)S(1)}, u32[]{:S(2)}, u32[]{:S(2)}) collective-permute-start(f32[56,256]{1,0:T(8,128)S(1)} %get-tuple-element.70), channel_id=1, source_target_pairs={{0,3},{1,2},{2,1},{3,0},{4,7},{5,6},{6,5},{7,4},{8,11},{9,10},{10,... | collective-permute-start | bytes 172040 | tf_op jit(solution)/shard_map/ppermute | solution.py:366
  35.6 3.9 %copy-start.1 = (bf16[1024,256]{1,0:T(8,128)(2,1)S(1)}, bf16[1024,256]{1,0:T(8,128)(2,1)}, u32[]{:S(2)}) copy-start(bf16[1024,256]{1,0:T(8,128)(2,1)} %refs_1_.1) | copy-start | bytes 1572868
  36.2 5.4 %copy-start.3 = (bf16[12,256]{1,0:T(8,128)(2,1)S(1)}, bf16[12,256]{1,0:T(8,128)(2,1)}, u32[]{:S(2)}) copy-start(bf16[12,256]{1,0:T(8,128)(2,1)} %refs_3_.1) | copy-start | bytes 18436
  38.2 3.4 %collective-permute-start.14 = (f32[32,256]{1,0:T(8,128)S(1)}, f32[32,256]{1,0:T(8,128)S(1)}, u32[]{:S(2)}, u32[]{:S(2)}) collective-permute-start(f32[32,256]{1,0:T(8,128)S(1)} %pad_maximum_fusion.2), channel_id=1, source_target_pairs={{0,5},{1,4},{2,7},{3,6},{4,1},{5,0},{6,3},{7,2},{8,13},{9,12},{10,... | collective-permute-start | bytes 98312 | tf_op jit(solution)/shard_map/ppermute | solution.py:366

commit v9 on v8

--- a/solution.py
+++ b/solution.py
@@ -28,7 +28,7 @@
 
 
 def block_of(proto):
-    return (proto & X) + ((proto >> 2) & 1)
+    return 2 * ((proto >> 2) & 1) + ((proto >> 1) & 1)
 
 
 def quick_unit(values):
@@ -50,8 +50,8 @@
     start = 0
     for t in dp_order(n_dp):
         count = place_ref[2 + (place_ref[0] ^ t)]
-        for x in range(2):
-            for y in range(2):
+        for y in range(2):
+            for x in range(2):
                 core = parity ^ x ^ y ^ half ^ (1 if t else 0)
                 proto = core + X * x + Y * y
                 end = start + jnp.clip(count - proto * rows, 0, rows)
@@ -83,17 +83,27 @@
     return jnp.where(live, 1.0 / jnp.where(live, total, 1.0), 0.0)
 
 
-def place_rows(place_ref, ref, which, rows, scratch):
-    mine_x, mine_y = (place_ref[1] >> 1) & 1, (place_ref[1] >> 2) & 1
-    start = 0
-    for t in range(ref.shape[1]):
+def pair_kernel(place_ref, mine_ref, other_ref, out_ref, scratch):
+    rows = mine_ref.shape[0] // 2
+    swapped = (place_ref[1] & X) > 0
+    mine, other = [quick_unit(ref[...])[0] for ref in (mine_ref, other_ref)]
+    pair = (jnp.where(swapped, other, mine), jnp.where(swapped, mine, other))
+    for which in range(2):
         for x in range(2):
-            for y in range(2):
-                block = ref[mine_y ^ y, t, mine_x ^ x].astype(jnp.float32)
-                scratch[start : start + rows, :] = block[which * rows : (which + 1) * rows]
-                start += rows
-    unit, _ = quick_unit(scratch[...])
-    return unit.astype(jnp.bfloat16)
+            start = (2 * which + x) * rows
+            scratch[start : start + rows, :] = pair[x][which * rows : (which + 1) * rows]
+    out_ref[...] = scratch[...].astype(jnp.bfloat16)
+
+
+def place_rows(place_ref, ref, which):
+    mine_y = (place_ref[1] >> 2) & 1
+    pair = ref.shape[2] // 2
+    blocks = [
+        ref[mine_y ^ y, t].astype(jnp.float32)[which * pair : (which + 1) * pair]
+        for t in range(ref.shape[1])
+        for y in range(2)
+    ]
+    return jnp.concatenate(blocks, axis=0).astype(jnp.bfloat16)
 
 
 def scores_of(rows_all, units):
@@ -168,9 +178,8 @@
 
 
 def near_kernel(chunk, place_ref, near_ref, live_ref, own_units_ref, proto_ref, *refs):
-    weights_ref, sums_ref, rows_ref, units_ref, scratch = refs
-    rows = near_ref.shape[3] // 2
-    rows_near = place_rows(place_ref, near_ref, 0, rows, scratch)
+    weights_ref, sums_ref, rows_ref, units_ref = refs
+    rows_near = place_rows(place_ref, near_ref, 0)
     rows_ref[...] = rows_near
     live = spread(live_ref[...], chunk)
     protos = own_units_ref.shape[0]
@@ -186,9 +195,8 @@
 
 
 def far_kernel(chunk, place_ref, far_ref, live_ref, near_weights_ref, near_sums_ref, *refs):
-    *unit_refs, weights_ref, rows_ref, sums_ref, scratch, scale_ref, part_ref = refs
-    rows = far_ref.shape[3] // 2
-    rows_far = place_rows(place_ref, far_ref, 0, rows, scratch)
+    *unit_refs, weights_ref, rows_ref, sums_ref, scale_ref, part_ref = refs
+    rows_far = place_rows(place_ref, far_ref, 0)
     rows_ref[...] = rows_far
     live = spread(live_ref[...], chunk)
     protos = unit_refs[0].shape[0]
@@ -205,7 +213,7 @@
 
 def across_kernel(chunk, place_ref, near_ref, far_ref, *refs):
     near_rows_ref, far_rows_ref, near_live_ref, far_live_ref, *refs = refs
-    *proto_refs, weights_ref, student_ref, scratch = refs
+    *proto_refs, weights_ref, student_ref = refs
     protos = proto_refs[0].shape[0]
     rows_all = jnp.concatenate([near_rows_ref[...], far_rows_ref[...]], axis=0)
     live = spread(jnp.concatenate([near_live_ref[...], far_live_ref[...]], axis=0), chunk)
@@ -216,8 +224,7 @@
             weights_ref[:, at], _ = weights_of(rows_all, units, live)
     half = student_ref.shape[0] // 2
     for k, ref in enumerate((near_ref, far_ref)):
-        rows_half = place_rows(place_ref, ref, 1, ref.shape[3] // 2, scratch)
-        student_ref[k * half : (k + 1) * half, :] = rows_half
+        student_ref[k * half : (k + 1) * half, :] = place_rows(place_ref, ref, 1)
 
 
 def scale_columns(sums, near_ref, far_ref, across_ref, row_ref, scale_ref):
@@ -390,7 +397,6 @@
     place = jnp.concatenate([place, live_count])
     tile = f32((8, LANES))
     message = f32((4 * rows + 8, width))
-    row_scratch = pltpu.VMEM((half, width), jnp.float32)
     column = pltpu.VMEM((all_rows, LANES), jnp.float32)
     scale_row = pltpu.VMEM((8, held), jnp.float32)
     sweep_scratch = [column, pltpu.VMEM((8, 2 * held), jnp.float32), column]
@@ -401,7 +407,13 @@
     across_protos = swap(late_protos, "proto", X_CROSS)
     student_protos = (prototypes, swap(prototypes, "proto", CORE))
     teacher_protos = swap(late_protos, "proto", CORE)
-    near = jnp.stack([both, across_x])
+    near = call(
+        pair_kernel,
+        bf16((4 * rows, width)),
+        (place, both, across_x),
+        smem=1,
+        scratch=[pltpu.VMEM((4 * rows, width), jnp.float32)],
+    )
     near = jnp.stack([near] + [swap_dp(near, t) for t in dp_order(n_dp)[1:]])
     near, own_protos = lax.optimization_barrier((near, teacher_prototypes))
     live = f32((half, LANES))
@@ -426,7 +438,6 @@
         ),
         (place, near, near_live, teacher_units, teacher_protos),
         smem=1,
-        scratch=[row_scratch],
         work=held * half,
     )
     far_weights, far_rows, sums = call(
@@ -434,7 +445,7 @@
         (f32((half, held)), bf16((half, width)), tile),
         (place, far, far_live, near_weights, near_sums, teacher_units, other_units),
         smem=1,
-        scratch=[row_scratch, scale_row, column],
+        scratch=[scale_row, column],
         work=held * half,
     )
     sums = sums + swap(sums, "proto", Y_CROSS)
@@ -455,7 +466,6 @@
             swap(across_protos, "proto", CORE),
         ),
         smem=1,
-        scratch=[row_scratch],
         work=held * all_rows,
     )
     weights = (near_weights, far_weights, across_weights)

time: 43.5 us -> 44 us (1.011)
    pallas_call x10 -> x11, Pallas kernels: 12.1 us -> 12.5 us  [call(): pl.pallas_call(kernel, out_shape=out_shape, in_specs=[pl.BlockSpec(memory...]
  transfers between devices with their start and end apart: 15 -> 15, of which waited for: 8 -> 8; matrix products, arithmetic and copies ran while one was open for 2% -> 2% of each run, Pallas kernels for 21% -> 20%
where the time goes in v9:
time: 44 us; the launch traced here: 43.8 us
  starting transfers between devices  18.9 us (43%)
  Pallas kernels  12.5 us (28%)
  waiting for transfers between devices  8.99 us (20%)
  other arithmetic  1.51 us (3%)
  local copies, waits for them, and re-layouts  1.06 us (2%)
  between operations  0.76 us (2%)
    ppermute x12, starting transfers between devices, swap(): return lax.ppermute(values, axis, others)  14 us
    pallas_call x11, Pallas kernels, call(): pl.pallas_call(kernel, out_shape=out_shape, in_specs=[pl.BlockSpec(memory...  12.5 us
    ppermute x12, waiting for transfers between devices, swap(): return lax.ppermute(values, axis, others)  7.12 us
    ppermute x3, starting transfers between devices, swap_dp(): return lax.ppermute(values, ('dp', 'proto'), others)  4.93 us
    ppermute x3, waiting for transfers between devices, swap_dp(): return lax.ppermute(values, ('dp', 'proto'), others)  1.87 us
    unnamed x8, local copies, waits for them, and re-layouts  1.06 us
  transfers between devices with their start and end apart: 15, of which 8 were waited for; matrix products, arithmetic and copies ran while one was open for 2% of the time, Pallas kernels for 20%

profile of v9, /device:TPU:0, one launch (start us, length us, event | category | flops | bytes accessed | tf_op | source)
XLA Modules:
  0.0 43.8 jit_solution(9821698757360027040)
XLA Ops:
  1.4 2.4 %collective-permute-start = (bf16[24,256]{1,0:T(8,128)(2,1)S(1)}, bf16[24,256]{1,0:T(8,128)(2,1)S(1)}, u32[]{:S(2)}, u32[]{:S(2)}) collective-permute-start(bf16[24,256]{1,0:T(8,128)(2,1)S(1)} %pad_maximum_fusion.3.mine_ref), channel_id=1, source_target_pairs={{0,3},{1,2},{2,1},{3,0},{4,7},{5,6},{6,5},{7,4},{8,11},{9,10},{10,... | collective-permute-start | bytes 36872 | tf_op jit(solution)/shard_map/ppermute | solution.py:373
  5.8 4.3 %collective-permute-start.1 = (bf16[48,256]{1,0:T(8,128)(2,1)S(1)}, bf16[48,256]{1,0:T(8,128)(2,1)S(1)}, u32[]{:S(2)}, u32[]{:S(2)}) collective-permute-start(bf16[48,256]{1,0:T(8,128)(2,1)S(1)} %shard_map.68), channel_id=1, source_target_pairs={{0,25},{1,24},{2,27},{3,26},{4,29},{5,28},{6,31},{7,30},{8,17},{9,... | collective-permute-start | bytes 73736 | tf_op jit(solution)/shard_map/ppermute | solution.py:381
  10.8 1.5 %collective-permute-start.8 = (bf16[1024,256]{1,0:T(8,128)(2,1)}, bf16[1024,256]{1,0:T(8,128)(2,1)S(1)}, u32[]{:S(2)}, u32[]{:S(2)}) collective-permute-start(bf16[1024,256]{1,0:T(8,128)(2,1)} %refs_1_.1), channel_id=1, source_target_pairs={{0,3},{1,2},{2,1},{3,0},{4,7},{5,6},{6,5},{7,4},{8,11},{9,10},{10,... | collective-permute-start | bytes 1572872 | tf_op jit(solution)/shard_map/ppermute | solution.py:373
  12.4 1.9 %collective-permute-done.2 = bf16[48,256]{1,0:T(8,128)(2,1)S(1)} collective-permute-done((bf16[48,256]{1,0:T(8,128)(2,1)S(1)}, bf16[48,256]{1,0:T(8,128)(2,1)S(1)}, u32[]{:S(2)}, u32[]{:S(2)}) %collective-permute-start.2) | collective-permute-done | bytes 24608 | tf_op jit(solution)/shard_map/ppermute | solution.py:381
  14.3 1.6 %collective-permute-start.4 = (bf16[4,48,256]{2,1,0:T(8,128)(2,1)S(1)}, bf16[4,48,256]{2,1,0:T(8,128)(2,1)S(1)}, u32[]{:S(2)}, u32[]{:S(2)}) collective-permute-start(bf16[4,48,256]{2,1,0:T(8,128)(2,1)S(1)} %pad_maximum_fusion.1), channel_id=1, source_target_pairs={{0,5},{1,4},{2,7},{3,6},{4,1},{5,0},{6,3},{7,2},{8,13},{9,12},{10,... | collective-permute-start | bytes 294920 | tf_op jit(solution)/shard_map/ppermute | solution.py:373
  15.9 1.0 %copy-done = bf16[1024,256]{1,0:T(8,128)(2,1)S(1)} copy-done((bf16[1024,256]{1,0:T(8,128)(2,1)S(1)}, bf16[1024,256]{1,0:T(8,128)(2,1)}, u32[]{:S(2)}) %copy-start) | copy-done | bytes 524312
  16.9 0.8 %shard_map.69 = (bf16[1024,256]{1,0:T(8,128)(2,1)S(1)}, f32[192,128]{1,0:T(8,128)S(1)}, f32[192,128]{1,0:T(8,128)S(1)}) custom-call(s32[6]{0:T(128)S(1)} %pad_add_fusion.place_ref, bf16[1024,256]{1,0:T(8,128)(2,1)S(1)} %copy-done), custom_call_target="tpu_custom_call" | custom-call | flops 134217728 | bytes 1048576 | tf_op jit(solution)/shard_map/pallas_call | solution.py:358
  17.7 1.1 %collective-permute-done.4 = bf16[4,48,256]{2,1,0:T(8,128)(2,1)S(1)} collective-permute-done((bf16[4,48,256]{2,1,0:T(8,128)(2,1)S(1)}, bf16[4,48,256]{2,1,0:T(8,128)(2,1)S(1)}, u32[]{:S(2)}, u32[]{:S(2)}) %collective-permute-start.4) | collective-permute-done | bytes 98336 | tf_op jit(solution)/shard_map/ppermute | solution.py:373
  19.6 1.1 %shard_map.70 = (f32[192,2048]{1,0:T(8,128)S(1)}, f32[8,2048]{1,0:T(8,128)S(1)}, bf16[192,256]{1,0:T(8,128)(2,1)S(1)}, bf16[1024,256]{1,0:T(8,128)(2,1)S(1)}) custom-call(s32[6]{0:T(128)S(1)} %pad_add_fusion.place_ref, bf16[2,4,48,256]{3,2,1,0:T(8,128)(2,1)S(1)} %pad_maximum_fusion.near_ref, f32[192,128]{1,0:T(8,128)S(1)} %get-tuple-element.47.live_ref.refs_2_, ...), custom_call_target="tpu_custom_call" | custom-call | flops 201326592 | bytes 1572864 | tf_op jit(solution)/shard_map/pallas_call | solution.py:358
  20.8 1.5 %shard_map.71 = (f32[192,2048]{1,0:T(8,128)S(1)}, bf16[192,256]{1,0:T(8,128)(2,1)S(1)}, f32[8,128]{1,0:T(8,128)S(1)}) custom-call(s32[6]{0:T(128)S(1)} %pad_add_fusion.place_ref, bf16[2,4,48,256]{3,2,1,0:T(8,128)(2,1)S(1)} %collective-permute-done.5.far_ref, f32[192,128]{1,0:T(8,128)S(1)} %get-tuple-element.46.live_ref.refs_3_, ...), custom_call_target="tpu_custom_call" | custom-call | flops 201326592 | bytes 1572864 | tf_op jit(solution)/shard_map/pallas_call | solution.py:358
  22.3 1.4 %collective-permute-start.7 = (f32[8,128]{1,0:T(8,128)S(1)}, f32[8,128]{1,0:T(8,128)S(1)}, u32[]{:S(2)}, u32[]{:S(2)}) collective-permute-start(f32[8,128]{1,0:T(8,128)S(1)} %get-tuple-element.53), channel_id=1, source_target_pairs={{0,5},{1,4},{2,7},{3,6},{4,1},{5,0},{6,3},{7,2},{8,13},{9,12},{10,... | collective-permute-start | bytes 12296 | tf_op jit(solution)/shard_map/ppermute | solution.py:373
  23.7 1.7 %collective-permute-done.7 = f32[8,128]{1,0:T(8,128)S(1)} collective-permute-done((f32[8,128]{1,0:T(8,128)S(1)}, f32[8,128]{1,0:T(8,128)S(1)}, u32[]{:S(2)}, u32[]{:S(2)}) %collective-permute-start.7) | collective-permute-done | bytes 4128 | tf_op jit(solution)/shard_map/ppermute | solution.py:373
  25.9 1.4 %collective-permute-start.9 = (f32[8,128]{1,0:T(8,128)S(1)}, f32[8,128]{1,0:T(8,128)S(1)}, u32[]{:S(2)}, u32[]{:S(2)}) collective-permute-start(f32[8,128]{1,0:T(8,128)S(1)} %add.9.mine_ref), channel_id=1, source_target_pairs={{0,3},{1,2},{2,1},{3,0},{4,7},{5,6},{6,5},{7,4},{8,11},{9,10},{10,... | collective-permute-start | bytes 12296 | tf_op jit(solution)/shard_map/ppermute | solution.py:373
  27.3 1.5 %shard_map.72 = (f32[384,2048]{1,0:T(8,128)S(1)}, bf16[384,256]{1,0:T(8,128)(2,1)S(1)}) custom-call(s32[6]{0:T(128)S(1)} %pad_add_fusion.place_ref, bf16[2,4,48,256]{3,2,1,0:T(8,128)(2,1)S(1)} %pad_maximum_fusion.near_ref, bf16[2,4,48,256]{3,2,1,0:T(8,128)(2,1)S(1)} %collective-permute-done.5.far_ref, ...), custom_call_target="tpu_custom_call" | custom-call | flops 402653184 | bytes 3145728 | tf_op jit(solution)/shard_map/pallas_call | solution.py:358
  28.9 1.3 %shard_map.73.mine_ref = f32[8,128]{1,0:T(8,128)S(1)} custom-call(f32[8,128]{1,0:T(8,128)S(1)} %add.9.mine_ref, f32[8,128]{1,0:T(8,128)S(1)} %collective-permute-done.9.other_ref, f32[192,2048]{1,0:T(8,128)S(1)} %get-tuple-element.50.near_weights_ref.near_ref, f32[192,2048]{1,0:T(8,128)S(1)} %get-tuple-element.55.far_ref, ...), custom_call_target="tpu_custom_call" | custom-call | flops 402653184 | bytes 3145728 | tf_op jit(solution)/shard_map/pallas_call | solution.py:358
  30.2 1.4 %collective-permute-start.12 = (f32[8,128]{1,0:T(8,128)S(1)}, f32[8,128]{1,0:T(8,128)S(1)}, u32[]{:S(2)}, u32[]{:S(2)}) collective-permute-start(f32[8,128]{1,0:T(8,128)S(1)} %shard_map.73.mine_ref), channel_id=1, source_target_pairs={{0,5},{1,4},{2,7},{3,6},{4,1},{5,0},{6,3},{7,2},{8,13},{9,12},{10,... | collective-permute-start | bytes 12296 | tf_op jit(solution)/shard_map/ppermute | solution.py:373
  31.7 1.1 %shard_map.74 = (bf16[2048,256]{1,0:T(8,128)(2,1)S(1)}, f32[48,256]{1,0:T(8,128)S(1)}, f32[8,128]{1,0:T(8,128)S(1)}) custom-call(bf16[384,256]{1,0:T(8,128)(2,1)S(1)} %get-tuple-element.62.rows_ref.refs_0_.refs_2_, bf16[1024,256]{1,0:T(8,128)(2,1)S(1)} %copy-done.2, bf16[1024,256]{1,0:T(8,128)(2,1)S(1)} %collective-permute-done.11.refs_1_), custom_call_target="tpu_custom_call" | custom-call | flops 402653184 | bytes 3145728 | tf_op jit(solution)/shard_map/pallas_call | solution.py:358
  33.3 1.5 %shard_map.75 = (f32[8,4096]{1,0:T(8,128)S(1)}, f32[56,256]{1,0:T(8,128)S(1)}, f32[56,256]{1,0:T(8,128)S(1)}) custom-call(s32[6]{0:T(128)S(1)} %pad_add_fusion.place_ref, f32[8,128]{1,0:T(8,128)S(1)} %shard_map.73.mine_ref, f32[8,128]{1,0:T(8,128)S(1)} %collective-permute-done.12.other_ref, f32[192,2048]{1,0:T(8,128)S(1)} %get-tuple-element.50.near_weights_ref.near_ref, ...), custom_call_target="tpu_custom_call" | custom-call | flops 402653184 | bytes 3145728 | tf_op jit(solution)/shard_map/pallas_call | solution.py:358
  34.8 1.5 %collective-permute-start.13 = (f32[56,256]{1,0:T(8,128)S(1)}, f32[56,256]{1,0:T(8,128)S(1)}, u32[]{:S(2)}, u32[]{:S(2)}) collective-permute-start(f32[56,256]{1,0:T(8,128)S(1)} %get-tuple-element.70), channel_id=1, source_target_pairs={{0,3},{1,2},{2,1},{3,0},{4,7},{5,6},{6,5},{7,4},{8,11},{9,10},{10,... | collective-permute-start | bytes 172040 | tf_op jit(solution)/shard_map/ppermute | solution.py:373
  36.9 1.8 %collective-permute-done.13 = f32[56,256]{1,0:T(8,128)S(1)} collective-permute-done((f32[56,256]{1,0:T(8,128)S(1)}, f32[56,256]{1,0:T(8,128)S(1)}, u32[]{:S(2)}, u32[]{:S(2)}) %collective-permute-start.13) | collective-permute-done | bytes 57376 | tf_op jit(solution)/shard_map/ppermute | solution.py:373
  38.8 1.4 %collective-permute-start.14 = (f32[32,256]{1,0:T(8,128)S(1)}, f32[32,256]{1,0:T(8,128)S(1)}, u32[]{:S(2)}, u32[]{:S(2)}) collective-permute-start(f32[32,256]{1,0:T(8,128)S(1)} %pad_maximum_fusion.2), channel_id=1, source_target_pairs={{0,5},{1,4},{2,7},{3,6},{4,1},{5,0},{6,3},{7,2},{8,13},{9,12},{10,... | collective-permute-start | bytes 98312 | tf_op jit(solution)/shard_map/ppermute | solution.py:373
  40.2 1.0 %shard_map.77 = (f32[256,384]{1,0:T(8,128)S(1)}, f32[256,384]{1,0:T(8,128)S(1)}, f32[256,256]{1,0:T(8,128)S(1)}, f32[256,128]{1,0:T(8,128)S(1)}) custom-call(s32[6]{0:T(128)S(1)} %pad_add_fusion.place_ref, f32[8,128]{1,0:T(8,128)S(1)} %shard_map.73.mine_ref, f32[8,128]{1,0:T(8,128)S(1)} %collective-permute-done.12.other_ref, ...), custom_call_target="tpu_custom_call" | custom-call | flops 50331648 | bytes 393216 | tf_op jit(solution)/shard_map/pallas_call | solution.py:358
  41.1 1.1 %collective-permute-done.14.other_ref = f32[32,256]{1,0:T(8,128)S(1)} collective-permute-done((f32[32,256]{1,0:T(8,128)S(1)}, f32[32,256]{1,0:T(8,128)S(1)}, u32[]{:S(2)}, u32[]{:S(2)}) %collective-permute-start.14) | collective-permute-done | bytes 32800 | tf_op jit(solution)/shard_map/ppermute | solution.py:373
  42.2 1.6 %shard_map.78 = (f32[12,256]{1,0:T(8,128)}, f32[1,256,256]{2,1,0:T(8,128)}) custom-call(s32[6]{0:T(128)S(1)} %pad_add_fusion.place_ref, f32[56,256]{1,0:T(8,128)S(1)} %add.10.mine_ref, f32[8,256]{1,0:T(8,128)S(1)} %slice_add_fusion.sums_ref, f32[32,256]{1,0:T(8,128)S(1)} %collective-permute-done.14.other_ref, f32[256,384]{1,0:T(8,128)S(1)} %get-tuple-element.74.targets_ref, ...), custom_call_target="tpu_custom_call" | custom-call | flops 50331648 | bytes 393216 | tf_op jit(solution)/shard_map/pallas_call | solution.py:358
  (34 shorter events, 6.2 us)
Async XLA Ops:
  1.4 3.8 %collective-permute-start = (bf16[24,256]{1,0:T(8,128)(2,1)S(1)}, bf16[24,256]{1,0:T(8,128)(2,1)S(1)}, u32[]{:S(2)}, u32[]{:S(2)}) collective-permute-start(bf16[24,256]{1,0:T(8,128)(2,1)S(1)} %pad_maximum_fusion.3.mine_ref), channel_id=1, source_target_pairs={{0,3},{1,2},{2,1},{3,0},{4,7},{5,6},{6,5},{7,4},{8,11},{9,10},{10,... | collective-permute-start | bytes 36872 | tf_op jit(solution)/shard_map/ppermute | solution.py:373
  5.8 6.5 %collective-permute-start.1 = (bf16[48,256]{1,0:T(8,128)(2,1)S(1)}, bf16[48,256]{1,0:T(8,128)(2,1)S(1)}, u32[]{:S(2)}, u32[]{:S(2)}) collective-permute-start(bf16[48,256]{1,0:T(8,128)(2,1)S(1)} %shard_map.68), channel_id=1, source_target_pairs={{0,25},{1,24},{2,27},{3,26},{4,29},{5,28},{6,31},{7,30},{8,17},{9,... | collective-permute-start | bytes 73736 | tf_op jit(solution)/shard_map/ppermute | solution.py:381
  10.1 4.2 %collective-permute-start.2 = (bf16[48,256]{1,0:T(8,128)(2,1)S(1)}, bf16[48,256]{1,0:T(8,128)(2,1)S(1)}, u32[]{:S(2)}, u32[]{:S(2)}) collective-permute-start(bf16[48,256]{1,0:T(8,128)(2,1)S(1)} %shard_map.68), channel_id=1, source_target_pairs={{0,17},{1,16},{2,19},{3,18},{4,21},{5,20},{6,23},{7,22},{8,25},{9,... | collective-permute-start | bytes 73736 | tf_op jit(solution)/shard_map/ppermute | solution.py:381
  10.1 4.2 %collective-permute-start.3 = (bf16[48,256]{1,0:T(8,128)(2,1)S(1)}, bf16[48,256]{1,0:T(8,128)(2,1)S(1)}, u32[]{:S(2)}, u32[]{:S(2)}) collective-permute-start(bf16[48,256]{1,0:T(8,128)(2,1)S(1)} %shard_map.68), channel_id=1, source_target_pairs={{0,9},{1,8},{2,11},{3,10},{4,13},{5,12},{6,15},{7,14},{8,1},{9,0},... | collective-permute-start | bytes 73736 | tf_op jit(solution)/shard_map/ppermute | solution.py:381
  10.8 8.9 %collective-permute-start.6 = (bf16[1024,256]{1,0:T(8,128)(2,1)}, bf16[1024,256]{1,0:T(8,128)(2,1)S(1)}, u32[]{:S(2)}, u32[]{:S(2)}) collective-permute-start(bf16[1024,256]{1,0:T(8,128)(2,1)} %refs_1_.1), channel_id=1, source_target_pairs={{0,1},{1,0},{2,3},{3,2},{4,5},{5,4},{6,7},{7,6},{8,9},{9,8},{10,11... | collective-permute-start | bytes 1572872 | tf_op jit(solution)/shard_map/ppermute | solution.py:373
  10.8 14.5 %collective-permute-start.8 = (bf16[1024,256]{1,0:T(8,128)(2,1)}, bf16[1024,256]{1,0:T(8,128)(2,1)S(1)}, u32[]{:S(2)}, u32[]{:S(2)}) collective-permute-start(bf16[1024,256]{1,0:T(8,128)(2,1)} %refs_1_.1), channel_id=1, source_target_pairs={{0,3},{1,2},{2,1},{3,0},{4,7},{5,6},{6,5},{7,4},{8,11},{9,10},{10,... | collective-permute-start | bytes 1572872 | tf_op jit(solution)/shard_map/ppermute | solution.py:373
  14.3 4.6 %collective-permute-start.4 = (bf16[4,48,256]{2,1,0:T(8,128)(2,1)S(1)}, bf16[4,48,256]{2,1,0:T(8,128)(2,1)S(1)}, u32[]{:S(2)}, u32[]{:S(2)}) collective-permute-start(bf16[4,48,256]{2,1,0:T(8,128)(2,1)S(1)} %pad_maximum_fusion.1), channel_id=1, source_target_pairs={{0,5},{1,4},{2,7},{3,6},{4,1},{5,0},{6,3},{7,2},{8,13},{9,12},{10,... | collective-permute-start | bytes 294920 | tf_op jit(solution)/shard_map/ppermute | solution.py:373
  15.9 1.0 %copy-start = (bf16[1024,256]{1,0:T(8,128)(2,1)S(1)}, bf16[1024,256]{1,0:T(8,128)(2,1)}, u32[]{:S(2)}) copy-start(bf16[1024,256]{1,0:T(8,128)(2,1)} %refs_1_.1) | copy-start | bytes 1572868
  18.9 1.9 %collective-permute-start.5 = (bf16[2,4,48,256]{3,2,1,0:T(8,128)(2,1)S(1)}, bf16[2,4,48,256]{3,2,1,0:T(8,128)(2,1)S(1)}, u32[]{:S(2)}, u32[]{:S(2)}) collective-permute-start(bf16[2,4,48,256]{3,2,1,0:T(8,128)(2,1)S(1)} %pad_maximum_fusion.near_ref), channel_id=1, source_target_pairs={{0,1},{1,0},{2,3},{3,2},{4,5},{5,4},{6,7},{7,6},{8,9},{9,8},{10,11... | collective-permute-start | bytes 589832 | tf_op jit(solution)/shard_map/ppermute | solution.py:373
  20.8 4.8 %copy-start.2 = (bf16[1024,256]{1,0:T(8,128)(2,1)S(1)}, bf16[1024,256]{1,0:T(8,128)(2,1)}, u32[]{:S(2)}) copy-start(bf16[1024,256]{1,0:T(8,128)(2,1)} %refs_2_.1) | copy-start | bytes 1572868
  22.3 3.1 %collective-permute-start.7 = (f32[8,128]{1,0:T(8,128)S(1)}, f32[8,128]{1,0:T(8,128)S(1)}, u32[]{:S(2)}, u32[]{:S(2)}) collective-permute-start(f32[8,128]{1,0:T(8,128)S(1)} %get-tuple-element.53), channel_id=1, source_target_pairs={{0,5},{1,4},{2,7},{3,6},{4,1},{5,0},{6,3},{7,2},{8,13},{9,12},{10,... | collective-permute-start | bytes 12296 | tf_op jit(solution)/shard_map/ppermute | solution.py:373
  25.4 1.9 %collective-permute-start.10 = (bf16[1024,256]{1,0:T(8,128)(2,1)S(1)}, bf16[1024,256]{1,0:T(8,128)(2,1)S(1)}, u32[]{:S(2)}, u32[]{:S(2)}) collective-permute-start(bf16[1024,256]{1,0:T(8,128)(2,1)S(1)} %collective-permute-done.8.refs_4_), channel_id=1, source_target_pairs={{0,1},{1,0},{2,3},{3,2},{4,5},{5,4},{6,7},{7,6},{8,9},{9,8},{10,11... | collective-permute-start | bytes 1572872 | tf_op jit(solution)/shard_map/ppermute | solution.py:373
  25.6 4.6 %collective-permute-start.11 = (bf16[1024,256]{1,0:T(8,128)(2,1)S(1)}, bf16[1024,256]{1,0:T(8,128)(2,1)S(1)}, u32[]{:S(2)}, u32[]{:S(2)}) collective-permute-start(bf16[1024,256]{1,0:T(8,128)(2,1)S(1)} %copy-done.2), channel_id=1, source_target_pairs={{0,1},{1,0},{2,3},{3,2},{4,5},{5,4},{6,7},{7,6},{8,9},{9,8},{10,11... | collective-permute-start | bytes 1572872 | tf_op jit(solution)/shard_map/ppermute | solution.py:373
  25.9 3.0 %collective-permute-start.9 = (f32[8,128]{1,0:T(8,128)S(1)}, f32[8,128]{1,0:T(8,128)S(1)}, u32[]{:S(2)}, u32[]{:S(2)}) collective-permute-start(f32[8,128]{1,0:T(8,128)S(1)} %add.9.mine_ref), channel_id=1, source_target_pairs={{0,3},{1,2},{2,1},{3,0},{4,7},{5,6},{6,5},{7,4},{8,11},{9,10},{10,... | collective-permute-start | bytes 12296 | tf_op jit(solution)/shard_map/ppermute | solution.py:373
  30.2 3.1 %collective-permute-start.12 = (f32[8,128]{1,0:T(8,128)S(1)}, f32[8,128]{1,0:T(8,128)S(1)}, u32[]{:S(2)}, u32[]{:S(2)}) collective-permute-start(f32[8,128]{1,0:T(8,128)S(1)} %shard_map.73.mine_ref), channel_id=1, source_target_pairs={{0,5},{1,4},{2,7},{3,6},{4,1},{5,0},{6,3},{7,2},{8,13},{9,12},{10,... | collective-permute-start | bytes 12296 | tf_op jit(solution)/shard_map/ppermute | solution.py:373
  34.8 3.9 %collective-permute-start.13 = (f32[56,256]{1,0:T(8,128)S(1)}, f32[56,256]{1,0:T(8,128)S(1)}, u32[]{:S(2)}, u32[]{:S(2)}) collective-permute-start(f32[56,256]{1,0:T(8,128)S(1)} %get-tuple-element.70), channel_id=1, source_target_pairs={{0,3},{1,2},{2,1},{3,0},{4,7},{5,6},{6,5},{7,4},{8,11},{9,10},{10,... | collective-permute-start | bytes 172040 | tf_op jit(solution)/shard_map/ppermute | solution.py:373
  36.3 3.9 %copy-start.1 = (bf16[1024,256]{1,0:T(8,128)(2,1)S(1)}, bf16[1024,256]{1,0:T(8,128)(2,1)}, u32[]{:S(2)}) copy-start(bf16[1024,256]{1,0:T(8,128)(2,1)} %refs_1_.1) | copy-start | bytes 1572868
  36.9 5.3 %copy-start.3 = (bf16[12,256]{1,0:T(8,128)(2,1)S(1)}, bf16[12,256]{1,0:T(8,128)(2,1)}, u32[]{:S(2)}) copy-start(bf16[12,256]{1,0:T(8,128)(2,1)} %refs_3_.1) | copy-start | bytes 18436
  38.8 3.4 %collective-permute-start.14 = (f32[32,256]{1,0:T(8,128)S(1)}, f32[32,256]{1,0:T(8,128)S(1)}, u32[]{:S(2)}, u32[]{:S(2)}) collective-permute-start(f32[32,256]{1,0:T(8,128)S(1)} %pad_maximum_fusion.2), channel_id=1, source_target_pairs={{0,5},{1,4},{2,7},{3,6},{4,1},{5,0},{6,3},{7,2},{8,13},{9,12},{10,... | collective-permute-start | bytes 98312 | tf_op jit(solution)/shard_map/ppermute | solution.py:373

commit v10 on v8

--- a/solution.py
+++ b/solution.py
@@ -29,6 +29,10 @@
 
 def block_of(proto):
     return (proto & X) + ((proto >> 2) & 1)
+
+
+def own_place():
+    return lax.axis_index("dp"), lax.axis_index("proto")
 
 
 def quick_unit(values):
@@ -83,8 +87,8 @@
     return jnp.where(live, 1.0 / jnp.where(live, total, 1.0), 0.0)
 
 
-def place_rows(place_ref, ref, which, rows, scratch):
-    mine_x, mine_y = (place_ref[1] >> 1) & 1, (place_ref[1] >> 2) & 1
+def place_rows(place, ref, which, rows, scratch):
+    mine_x, mine_y = (place[1] >> 1) & 1, (place[1] >> 2) & 1
     start = 0
     for t in range(ref.shape[1]):
         for x in range(2):
@@ -167,10 +171,10 @@
         live_ref[...] = as_column(live_lanes(place_ref, k, live_ref.shape[0], n_dp, rows))
 
 
-def near_kernel(chunk, place_ref, near_ref, live_ref, own_units_ref, proto_ref, *refs):
+def near_kernel(chunk, near_ref, live_ref, own_units_ref, proto_ref, *refs):
     weights_ref, sums_ref, rows_ref, units_ref, scratch = refs
     rows = near_ref.shape[3] // 2
-    rows_near = place_rows(place_ref, near_ref, 0, rows, scratch)
+    rows_near = place_rows(own_place(), near_ref, 0, rows, scratch)
     rows_ref[...] = rows_near
     live = spread(live_ref[...], chunk)
     protos = own_units_ref.shape[0]
@@ -185,10 +189,10 @@
         weights_ref[:, at], sums_ref[:, at] = weights_of(rows_near, units, live)
 
 
-def far_kernel(chunk, place_ref, far_ref, live_ref, near_weights_ref, near_sums_ref, *refs):
+def far_kernel(chunk, far_ref, live_ref, near_weights_ref, near_sums_ref, *refs):
     *unit_refs, weights_ref, rows_ref, sums_ref, scratch, scale_ref, part_ref = refs
     rows = far_ref.shape[3] // 2
-    rows_far = place_rows(place_ref, far_ref, 0, rows, scratch)
+    rows_far = place_rows(own_place(), far_ref, 0, rows, scratch)
     rows_ref[...] = rows_far
     live = spread(live_ref[...], chunk)
     protos = unit_refs[0].shape[0]
@@ -203,7 +207,7 @@
     sums_ref[...] = as_tile(part_ref[...])
 
 
-def across_kernel(chunk, place_ref, near_ref, far_ref, *refs):
+def across_kernel(chunk, near_ref, far_ref, *refs):
     near_rows_ref, far_rows_ref, near_live_ref, far_live_ref, *refs = refs
     *proto_refs, weights_ref, student_ref, scratch = refs
     protos = proto_refs[0].shape[0]
@@ -216,7 +220,7 @@
             weights_ref[:, at], _ = weights_of(rows_all, units, live)
     half = student_ref.shape[0] // 2
     for k, ref in enumerate((near_ref, far_ref)):
-        rows_half = place_rows(place_ref, ref, 1, ref.shape[3] // 2, scratch)
+        rows_half = place_rows(own_place(), ref, 1, ref.shape[3] // 2, scratch)
         student_ref[k * half : (k + 1) * half, :] = rows_half
 
 
@@ -266,7 +270,7 @@
     sums_ref[...] = as_tile(part)
 
 
-def last_kernel(chunk, rows, place_ref, mine_ref, other_ref, near_ref, far_ref, across_ref, *refs):
+def last_kernel(chunk, rows, mine_ref, other_ref, near_ref, far_ref, across_ref, *refs):
     units_ref, exp_pull_ref, exp_sums_ref, scale_ref, keep_ref, send_ref, row_ref, blocks_ref = refs
     first = exp_pull_ref.shape[0]
     sums = mine_ref[...] + other_ref[...]
@@ -280,7 +284,7 @@
     for k, pull in enumerate(pulls):
         for block in range(4):
             blocks_ref[k, block, :rows, :] = pull[block * rows : (block + 1) * rows]
-    mine = place_ref[1]
+    _, mine = own_place()
     for ref, proto in ((keep_ref, mine), (send_ref, mine ^ X)):
         for j, owner in enumerate((proto, proto ^ Y)):
             for k in range(2):
@@ -295,14 +299,14 @@
     sums_ref[:, LANES:] = next_sums(near_ref, far_ref, across_ref, scale_ref, part_ref)
 
 
-def own_kernel(place_ref, mine_ref, other_ref, near_rows_ref, far_rows_ref, *refs):
+def own_kernel(mine_ref, other_ref, near_rows_ref, far_rows_ref, *refs):
     student_rows_ref, teacher_proto_ref, proto_ref, *refs = refs
     targets_ref, exps_ref, unit_ref, scale_ref = refs
     teacher_rows = jnp.concatenate([near_rows_ref[...], far_rows_ref[...]], axis=0)
     own, all_rows = targets_ref.shape
     row_scale = inverse_rows(mine_ref[...] + other_ref[...], all_rows)
     live = jnp.where(row_scale > 0.0, 1.0, 0.0)
-    first = pl.ds(pl.multiple_of(place_ref[0] * own, own), own)
+    first = pl.ds(pl.multiple_of(own_place()[0] * own, own), own)
     units = quick_unit(teacher_proto_ref[first, :])[0].astype(jnp.bfloat16)
     weights = jnp.exp(scores_of(units, teacher_rows) * (1 / teacher_temp)) * live
     inverse = 1.0 / jnp.sum(weights * row_scale, axis=1, keepdims=True)
@@ -315,7 +319,7 @@
     exps_ref[...] = exps * (1 / student_temp)
 
 
-def grads_kernel(place_ref, mine_ref, sums_ref, other_ref, targets_ref, exps_ref, *refs):
+def grads_kernel(mine_ref, sums_ref, other_ref, targets_ref, exps_ref, *refs):
     unit_ref, scale_ref, rows_ref, feat_ref, student_out_ref, proto_out_ref = refs
     all_rows = targets_ref.shape[1]
     rows = feat_ref.shape[0]
@@ -329,7 +333,7 @@
     along = jnp.sum(unit * pushed, axis=1, keepdims=True)
     proto_out_ref[0] = (pushed - unit * along) * twice(scale_ref[...])
 
-    row = lax.broadcasted_iota(jnp.int32, (rows, LANES), 0) + block_of(place_ref[1]) * rows
+    row = lax.broadcasted_iota(jnp.int32, (rows, LANES), 0) + block_of(own_place()[1]) * rows
     here = lax.broadcasted_iota(jnp.int32, (rows, LANES), 1) == row
     target_column, exp_column = [
         jnp.sum(jnp.where(here, scale[:, :LANES], 0.0), axis=1, keepdims=True) * (1 / student_temp)
@@ -424,16 +428,14 @@
             bf16((half, width)),
             bf16((protos, width)),
         ),
-        (place, near, near_live, teacher_units, teacher_protos),
-        smem=1,
+        (near, near_live, teacher_units, teacher_protos),
         scratch=[row_scratch],
         work=held * half,
     )
     far_weights, far_rows, sums = call(
         functools.partial(far_kernel, piece),
         (f32((half, held)), bf16((half, width)), tile),
-        (place, far, far_live, near_weights, near_sums, teacher_units, other_units),
-        smem=1,
+        (far, far_live, near_weights, near_sums, teacher_units, other_units),
         scratch=[row_scratch, scale_row, column],
         work=held * half,
     )
@@ -444,7 +446,6 @@
         functools.partial(across_kernel, piece),
         (f32((all_rows, held)), bf16((all_rows, width))),
         (
-            place,
             near,
             far,
             near_rows,
@@ -454,7 +455,6 @@
             across_protos,
             swap(across_protos, "proto", CORE),
         ),
-        smem=1,
         scratch=[row_scratch],
         work=held * all_rows,
     )
@@ -481,8 +481,7 @@
     scales, keep, send = call(
         functools.partial(last_kernel, own, rows),
         (f32((8, 2 * held)), message, message),
-        (place, *parts, *weights, student_units, exp_pull, exp_sums),
-        smem=1,
+        (*parts, *weights, student_units, exp_pull, exp_sums),
         scratch=[column, pltpu.VMEM((2, 4, 16, width), jnp.float32)],
         work=held * all_rows,
     )
@@ -497,8 +496,7 @@
     targets, exps, own_units, own_scales = call(
         own_kernel,
         (f32((own, all_rows)), f32((own, all_rows)), f32((own, width)), f32((own, LANES))),
-        (place, *parts, near_rows, far_rows, student_rows, teacher_prototypes, prototypes),
-        smem=1,
+        (*parts, near_rows, far_rows, student_rows, teacher_prototypes, prototypes),
         work=own * all_rows,
     )
     total = keep + swap(send, "proto", X_CROSS)
@@ -507,7 +505,6 @@
         grads_kernel,
         (f32((rows, width)), f32((1, own, width))),
         (
-            place,
             total,
             last_sums,
             swap(jnp.concatenate([total[2 * rows : 4 * rows], last_sums]), "proto", Y_CROSS),
@@ -518,7 +515,6 @@
             student_rows,
             student_feat,
         ),
-        smem=1,
         work=own * all_rows,
     )
 

time: 43.5 us -> 41.6 us (0.956)
  Pallas kernels: 12.1 us -> 8.8 us
  starting transfers between devices: 18.6 us -> 20 us
    pallas_call x10, Pallas kernels: 12.1 us -> 8.8 us  [call(): pl.pallas_call(kernel, out_shape=out_shape, in_specs=[pl.BlockSpec(memory...]
    ppermute x12, starting transfers between devices: 13.8 us -> 15.2 us  [swap(): return lax.ppermute(values, axis, others)]
  transfers between devices with their start and end apart: 15 -> 15, of which waited for: 8 -> 9; matrix products, arithmetic and copies ran while one was open for 2% -> 2% of each run, Pallas kernels for 21% -> 16%
where the time goes in v10:
time: 41.6 us; the launch traced here: 41.3 us
  starting transfers between devices  20 us (48%)
  waiting for transfers between devices  9.18 us (22%)
  Pallas kernels  8.8 us (21%)
  other arithmetic  1.52 us (4%)
  local copies, waits for them, and re-layouts  1.06 us (3%)
  between operations  0.75 us (2%)
    ppermute x12, starting transfers between devices, swap(): return lax.ppermute(values, axis, others)  15.2 us
    pallas_call x10, Pallas kernels, call(): pl.pallas_call(kernel, out_shape=out_shape, in_specs=[pl.BlockSpec(memory...  8.8 us
    ppermute x12, waiting for transfers between devices, swap(): return lax.ppermute(values, axis, others)  7.3 us
    ppermute x3, starting transfers between devices, swap_dp(): return lax.ppermute(values, ('dp', 'proto'), others)  4.86 us
    ppermute x3, waiting for transfers between devices, swap_dp(): return lax.ppermute(values, ('dp', 'proto'), others)  1.87 us
    unnamed x8, local copies, waits for them, and re-layouts  1.06 us
  transfers between devices with their start and end apart: 15, of which 9 were waited for; matrix products, arithmetic and copies ran while one was open for 2% of the time, Pallas kernels for 16%

profile of v10, /device:TPU:0, one launch (start us, length us, event | category | flops | bytes accessed | tf_op | source)
XLA Modules:
  0.0 41.3 jit_solution(11429559111654336153)
XLA Ops:
  1.4 2.4 %collective-permute-start = (bf16[24,256]{1,0:T(8,128)(2,1)S(1)}, bf16[24,256]{1,0:T(8,128)(2,1)S(1)}, u32[]{:S(2)}, u32[]{:S(2)}) collective-permute-start(bf16[24,256]{1,0:T(8,128)(2,1)S(1)} %pad_maximum_fusion.4), channel_id=1, source_target_pairs={{0,3},{1,2},{2,1},{3,0},{4,7},{5,6},{6,5},{7,4},{8,11},{9,10},{10,... | collective-permute-start | bytes 36872 | tf_op jit(solution)/shard_map/ppermute | solution.py:370
  3.8 0.7 %pad_add_fusion.place_ref = s32[6]{0:T(128)S(1)} fusion(s32[4]{0:T(128)} %param.9, s32[1]{0:T(128)} %bitcast.2, s32[1]{0:T(128)} %bitcast.1), kind=kLoop, calls=%fused_computation.6 | loop fusion | flops 12 | bytes 48 | tf_op jit(solution)/shard_map/concatenate | solution.py:394
  5.2 4.2 %collective-permute-start.1 = (bf16[2,24,256]{2,1,0:T(8,128)(2,1)S(1)}, bf16[2,24,256]{2,1,0:T(8,128)(2,1)S(1)}, u32[]{:S(2)}, u32[]{:S(2)}) collective-permute-start(bf16[2,24,256]{2,1,0:T(8,128)(2,1)S(1)} %get-tuple-element.79), channel_id=1, source_target_pairs={{0,25},{1,24},{2,27},{3,26},{4,29},{5,28},{6,31},{7,30},{8,17},{9,... | collective-permute-start | bytes 73736 | tf_op jit(solution)/shard_map/ppermute | solution.py:378
  10.1 1.5 %collective-permute-start.8 = (bf16[1024,256]{1,0:T(8,128)(2,1)}, bf16[1024,256]{1,0:T(8,128)(2,1)S(1)}, u32[]{:S(2)}, u32[]{:S(2)}) collective-permute-start(bf16[1024,256]{1,0:T(8,128)(2,1)} %refs_1_.1), channel_id=1, source_target_pairs={{0,3},{1,2},{2,1},{3,0},{4,7},{5,6},{6,5},{7,4},{8,11},{9,10},{10,... | collective-permute-start | bytes 1572872 | tf_op jit(solution)/shard_map/ppermute | solution.py:370
  11.7 1.9 %collective-permute-done.2 = bf16[2,24,256]{2,1,0:T(8,128)(2,1)S(1)} collective-permute-done((bf16[2,24,256]{2,1,0:T(8,128)(2,1)S(1)}, bf16[2,24,256]{2,1,0:T(8,128)(2,1)S(1)}, u32[]{:S(2)}, u32[]{:S(2)}) %collective-permute-start.2) | collective-permute-done | bytes 24608 | tf_op jit(solution)/shard_map/ppermute | solution.py:378
  13.6 1.6 %collective-permute-start.4 = (bf16[4,2,24,256]{3,2,1,0:T(8,128)(2,1)S(1)}, bf16[4,2,24,256]{3,2,1,0:T(8,128)(2,1)S(1)}, u32[]{:S(2)}, u32[]{:S(2)}) collective-permute-start(bf16[4,2,24,256]{3,2,1,0:T(8,128)(2,1)S(1)} %pad_maximum_fusion.1), channel_id=1, source_target_pairs={{0,5},{1,4},{2,7},{3,6},{4,1},{5,0},{6,3},{7,2},{8,13},{9,12},{10,... | collective-permute-start | bytes 294920 | tf_op jit(solution)/shard_map/ppermute | solution.py:370
  15.2 1.0 %copy-done = bf16[1024,256]{1,0:T(8,128)(2,1)S(1)} copy-done((bf16[1024,256]{1,0:T(8,128)(2,1)S(1)}, bf16[1024,256]{1,0:T(8,128)(2,1)}, u32[]{:S(2)}) %copy-start) | copy-done | bytes 524312
  16.2 0.8 %shard_map.68 = (bf16[1024,256]{1,0:T(8,128)(2,1)S(1)}, f32[192,128]{1,0:T(8,128)S(1)}, f32[192,128]{1,0:T(8,128)S(1)}) custom-call(s32[6]{0:T(128)S(1)} %pad_add_fusion.place_ref, bf16[1024,256]{1,0:T(8,128)(2,1)S(1)} %copy-done), custom_call_target="tpu_custom_call" | custom-call | flops 134217728 | bytes 1048576 | tf_op jit(solution)/shard_map/pallas_call | solution.py:355
  17.0 1.1 %collective-permute-done.4 = bf16[4,2,24,256]{3,2,1,0:T(8,128)(2,1)S(1)} collective-permute-done((bf16[4,2,24,256]{3,2,1,0:T(8,128)(2,1)S(1)}, bf16[4,2,24,256]{3,2,1,0:T(8,128)(2,1)S(1)}, u32[]{:S(2)}, u32[]{:S(2)}) %collective-permute-start.4) | collective-permute-done | bytes 98336 | tf_op jit(solution)/shard_map/ppermute | solution.py:370
  18.2 0.8 %collective-permute-start.5 = (bf16[2,4,2,24,256]{4,3,2,1,0:T(8,128)(2,1)S(1)}, bf16[2,4,2,24,256]{4,3,2,1,0:T(8,128)(2,1)S(1)}, u32[]{:S(2)}, u32[]{:S(2)}) collective-permute-start(bf16[2,4,2,24,256]{4,3,2,1,0:T(8,128)(2,1)S(1)} %pad_maximum_fusion.near_ref), channel_id=1, source_target_pairs={{0,1},{1,0},{2,3},{3,2},{4,5},{5,4},{6,7},{7,6},{8,9},{9,8},{10,11... | collective-permute-start | bytes 589832 | tf_op jit(solution)/shard_map/ppermute | solution.py:370
  20.0 1.0 %shard_map.70 = (f32[192,2048]{1,0:T(8,128)S(1)}, bf16[192,256]{1,0:T(8,128)(2,1)S(1)}, f32[8,128]{1,0:T(8,128)S(1)}) custom-call(bf16[2,4,2,24,256]{4,3,2,1,0:T(8,128)(2,1)S(1)} %collective-permute-done.5.far_ref, f32[192,128]{1,0:T(8,128)S(1)} %get-tuple-element.46.live_ref.refs_3_, f32[192,2048]{1,0:T(8,128)S(1)} %get-tuple-element.50.near_weights_ref.near_ref, ...), custom_call_target="tpu_custom_call" | custom-call | flops 201326592 | bytes 1572864 | tf_op jit(solution)/shard_map/pallas_call | solution.py:355
  21.0 1.6 %collective-permute-start.7 = (f32[8,128]{1,0:T(8,128)S(1)}, f32[8,128]{1,0:T(8,128)S(1)}, u32[]{:S(2)}, u32[]{:S(2)}) collective-permute-start(f32[8,128]{1,0:T(8,128)S(1)} %get-tuple-element.53), channel_id=1, source_target_pairs={{0,5},{1,4},{2,7},{3,6},{4,1},{5,0},{6,3},{7,2},{8,13},{9,12},{10,... | collective-permute-start | bytes 12296 | tf_op jit(solution)/shard_map/ppermute | solution.py:370
  22.5 1.6 %collective-permute-done.7 = f32[8,128]{1,0:T(8,128)S(1)} collective-permute-done((f32[8,128]{1,0:T(8,128)S(1)}, f32[8,128]{1,0:T(8,128)S(1)}, u32[]{:S(2)}, u32[]{:S(2)}) %collective-permute-start.7) | collective-permute-done | bytes 4128 | tf_op jit(solution)/shard_map/ppermute | solution.py:370
  24.6 1.6 %collective-permute-start.9 = (f32[8,128]{1,0:T(8,128)S(1)}, f32[8,128]{1,0:T(8,128)S(1)}, u32[]{:S(2)}, u32[]{:S(2)}) collective-permute-start(f32[8,128]{1,0:T(8,128)S(1)} %add.9.mine_ref), channel_id=1, source_target_pairs={{0,3},{1,2},{2,1},{3,0},{4,7},{5,6},{6,5},{7,4},{8,11},{9,10},{10,... | collective-permute-start | bytes 12296 | tf_op jit(solution)/shard_map/ppermute | solution.py:370
  26.2 1.0 %shard_map.71 = (f32[384,2048]{1,0:T(8,128)S(1)}, bf16[384,256]{1,0:T(8,128)(2,1)S(1)}) custom-call(bf16[2,4,2,24,256]{4,3,2,1,0:T(8,128)(2,1)S(1)} %pad_maximum_fusion.near_ref, bf16[2,4,2,24,256]{4,3,2,1,0:T(8,128)(2,1)S(1)} %collective-permute-done.5.far_ref, bf16[192,256]{1,0:T(8,128)(2,1)S(1)} %get-tuple-element.56.refs_0_.near_rows_ref, ...), custom_call_target="tpu_custom_call" | custom-call | flops 402653184 | bytes 3145728 | tf_op jit(solution)/shard_map/pallas_call | solution.py:355
  27.6 1.3 %shard_map.72.mine_ref = f32[8,128]{1,0:T(8,128)S(1)} custom-call(f32[8,128]{1,0:T(8,128)S(1)} %add.9.mine_ref, f32[8,128]{1,0:T(8,128)S(1)} %collective-permute-done.9.other_ref, f32[192,2048]{1,0:T(8,128)S(1)} %get-tuple-element.50.near_weights_ref.near_ref, f32[192,2048]{1,0:T(8,128)S(1)} %get-tuple-element.55.far_ref, ...), custom_call_target="tpu_custom_call" | custom-call | flops 402653184 | bytes 3145728 | tf_op jit(solution)/shard_map/pallas_call | solution.py:355
  28.9 1.6 %collective-permute-start.12 = (f32[8,128]{1,0:T(8,128)S(1)}, f32[8,128]{1,0:T(8,128)S(1)}, u32[]{:S(2)}, u32[]{:S(2)}) collective-permute-start(f32[8,128]{1,0:T(8,128)S(1)} %shard_map.72.mine_ref), channel_id=1, source_target_pairs={{0,5},{1,4},{2,7},{3,6},{4,1},{5,0},{6,3},{7,2},{8,13},{9,12},{10,... | collective-permute-start | bytes 12296 | tf_op jit(solution)/shard_map/ppermute | solution.py:370
  30.6 1.1 %shard_map.73 = (bf16[2048,256]{1,0:T(8,128)(2,1)S(1)}, f32[48,256]{1,0:T(8,128)S(1)}, f32[8,128]{1,0:T(8,128)S(1)}) custom-call(bf16[384,256]{1,0:T(8,128)(2,1)S(1)} %get-tuple-element.62.rows_ref.refs_0_.refs_2_, bf16[1024,256]{1,0:T(8,128)(2,1)S(1)} %copy-done.2, bf16[1024,256]{1,0:T(8,128)(2,1)S(1)} %collective-permute-done.11.refs_1_), custom_call_target="tpu_custom_call" | custom-call | flops 402653184 | bytes 3145728 | tf_op jit(solution)/shard_map/pallas_call | solution.py:355
  32.0 1.0 %shard_map.74 = (f32[8,4096]{1,0:T(8,128)S(1)}, f32[56,256]{1,0:T(8,128)S(1)}, f32[56,256]{1,0:T(8,128)S(1)}) custom-call(f32[8,128]{1,0:T(8,128)S(1)} %shard_map.72.mine_ref, f32[8,128]{1,0:T(8,128)S(1)} %collective-permute-done.12.other_ref, f32[192,2048]{1,0:T(8,128)S(1)} %get-tuple-element.50.near_weights_ref.near_ref, ...), custom_call_target="tpu_custom_call" | custom-call | flops 402653184 | bytes 3145728 | tf_op jit(solution)/shard_map/pallas_call | solution.py:355
  33.0 1.6 %collective-permute-start.13 = (f32[56,256]{1,0:T(8,128)S(1)}, f32[56,256]{1,0:T(8,128)S(1)}, u32[]{:S(2)}, u32[]{:S(2)}) collective-permute-start(f32[56,256]{1,0:T(8,128)S(1)} %get-tuple-element.70), channel_id=1, source_target_pairs={{0,3},{1,2},{2,1},{3,0},{4,7},{5,6},{6,5},{7,4},{8,11},{9,10},{10,... | collective-permute-start | bytes 172040 | tf_op jit(solution)/shard_map/ppermute | solution.py:370
  35.3 1.5 %collective-permute-done.13 = f32[56,256]{1,0:T(8,128)S(1)} collective-permute-done((f32[56,256]{1,0:T(8,128)S(1)}, f32[56,256]{1,0:T(8,128)S(1)}, u32[]{:S(2)}, u32[]{:S(2)}) %collective-permute-start.13) | collective-permute-done | bytes 57376 | tf_op jit(solution)/shard_map/ppermute | solution.py:370
  36.9 1.8 %collective-permute-start.14 = (f32[32,256]{1,0:T(8,128)S(1)}, f32[32,256]{1,0:T(8,128)S(1)}, u32[]{:S(2)}, u32[]{:S(2)}) collective-permute-start(f32[32,256]{1,0:T(8,128)S(1)} %pad_maximum_fusion.2), channel_id=1, source_target_pairs={{0,5},{1,4},{2,7},{3,6},{4,1},{5,0},{6,3},{7,2},{8,13},{9,12},{10,... | collective-permute-start | bytes 98312 | tf_op jit(solution)/shard_map/ppermute | solution.py:370
  39.1 1.2 %collective-permute-done.14.other_ref = f32[32,256]{1,0:T(8,128)S(1)} collective-permute-done((f32[32,256]{1,0:T(8,128)S(1)}, f32[32,256]{1,0:T(8,128)S(1)}, u32[]{:S(2)}, u32[]{:S(2)}) %collective-permute-start.14) | collective-permute-done | bytes 32800 | tf_op jit(solution)/shard_map/ppermute | solution.py:370
  40.3 1.0 %shard_map.77 = (f32[12,256]{1,0:T(8,128)}, f32[1,256,256]{2,1,0:T(8,128)}) custom-call(f32[56,256]{1,0:T(8,128)S(1)} %add.10.mine_ref, f32[8,256]{1,0:T(8,128)S(1)} %slice_add_fusion.sums_ref, f32[32,256]{1,0:T(8,128)S(1)} %collective-permute-done.14.other_ref, f32[256,384]{1,0:T(8,128)S(1)} %get-tuple-element.74.targets_ref, ...), custom_call_target="tpu_custom_call" | custom-call | flops 50331648 | bytes 393216 | tf_op jit(solution)/shard_map/pallas_call | solution.py:355
  (34 shorter events, 5.6 us)
Async XLA Ops:
  1.4 3.8 %collective-permute-start = (bf16[24,256]{1,0:T(8,128)(2,1)S(1)}, bf16[24,256]{1,0:T(8,128)(2,1)S(1)}, u32[]{:S(2)}, u32[]{:S(2)}) collective-permute-start(bf16[24,256]{1,0:T(8,128)(2,1)S(1)} %pad_maximum_fusion.4), channel_id=1, source_target_pairs={{0,3},{1,2},{2,1},{3,0},{4,7},{5,6},{6,5},{7,4},{8,11},{9,10},{10,... | collective-permute-start | bytes 36872 | tf_op jit(solution)/shard_map/ppermute | solution.py:370
  5.2 6.5 %collective-permute-start.1 = (bf16[2,24,256]{2,1,0:T(8,128)(2,1)S(1)}, bf16[2,24,256]{2,1,0:T(8,128)(2,1)S(1)}, u32[]{:S(2)}, u32[]{:S(2)}) collective-permute-start(bf16[2,24,256]{2,1,0:T(8,128)(2,1)S(1)} %get-tuple-element.79), channel_id=1, source_target_pairs={{0,25},{1,24},{2,27},{3,26},{4,29},{5,28},{6,31},{7,30},{8,17},{9,... | collective-permute-start | bytes 73736 | tf_op jit(solution)/shard_map/ppermute | solution.py:378
  9.4 4.2 %collective-permute-start.2 = (bf16[2,24,256]{2,1,0:T(8,128)(2,1)S(1)}, bf16[2,24,256]{2,1,0:T(8,128)(2,1)S(1)}, u32[]{:S(2)}, u32[]{:S(2)}) collective-permute-start(bf16[2,24,256]{2,1,0:T(8,128)(2,1)S(1)} %get-tuple-element.79), channel_id=1, source_target_pairs={{0,17},{1,16},{2,19},{3,18},{4,21},{5,20},{6,23},{7,22},{8,25},{9,... | collective-permute-start | bytes 73736 | tf_op jit(solution)/shard_map/ppermute | solution.py:378
  9.4 4.2 %collective-permute-start.3 = (bf16[2,24,256]{2,1,0:T(8,128)(2,1)S(1)}, bf16[2,24,256]{2,1,0:T(8,128)(2,1)S(1)}, u32[]{:S(2)}, u32[]{:S(2)}) collective-permute-start(bf16[2,24,256]{2,1,0:T(8,128)(2,1)S(1)} %get-tuple-element.79), channel_id=1, source_target_pairs={{0,9},{1,8},{2,11},{3,10},{4,13},{5,12},{6,15},{7,14},{8,1},{9,0},... | collective-permute-start | bytes 73736 | tf_op jit(solution)/shard_map/ppermute | solution.py:378
  10.1 8.9 %collective-permute-start.6 = (bf16[1024,256]{1,0:T(8,128)(2,1)}, bf16[1024,256]{1,0:T(8,128)(2,1)S(1)}, u32[]{:S(2)}, u32[]{:S(2)}) collective-permute-start(bf16[1024,256]{1,0:T(8,128)(2,1)} %refs_1_.1), channel_id=1, source_target_pairs={{0,1},{1,0},{2,3},{3,2},{4,5},{5,4},{6,7},{7,6},{8,9},{9,8},{10,11... | collective-permute-start | bytes 1572872 | tf_op jit(solution)/shard_map/ppermute | solution.py:370
  10.1 13.9 %collective-permute-start.8 = (bf16[1024,256]{1,0:T(8,128)(2,1)}, bf16[1024,256]{1,0:T(8,128)(2,1)S(1)}, u32[]{:S(2)}, u32[]{:S(2)}) collective-permute-start(bf16[1024,256]{1,0:T(8,128)(2,1)} %refs_1_.1), channel_id=1, source_target_pairs={{0,3},{1,2},{2,1},{3,0},{4,7},{5,6},{6,5},{7,4},{8,11},{9,10},{10,... | collective-permute-start | bytes 1572872 | tf_op jit(solution)/shard_map/ppermute | solution.py:370
  13.6 4.6 %collective-permute-start.4 = (bf16[4,2,24,256]{3,2,1,0:T(8,128)(2,1)S(1)}, bf16[4,2,24,256]{3,2,1,0:T(8,128)(2,1)S(1)}, u32[]{:S(2)}, u32[]{:S(2)}) collective-permute-start(bf16[4,2,24,256]{3,2,1,0:T(8,128)(2,1)S(1)} %pad_maximum_fusion.1), channel_id=1, source_target_pairs={{0,5},{1,4},{2,7},{3,6},{4,1},{5,0},{6,3},{7,2},{8,13},{9,12},{10,... | collective-permute-start | bytes 294920 | tf_op jit(solution)/shard_map/ppermute | solution.py:370
  15.2 1.0 %copy-start = (bf16[1024,256]{1,0:T(8,128)(2,1)S(1)}, bf16[1024,256]{1,0:T(8,128)(2,1)}, u32[]{:S(2)}) copy-start(bf16[1024,256]{1,0:T(8,128)(2,1)} %refs_1_.1) | copy-start | bytes 1572868
  18.2 1.8 %collective-permute-start.5 = (bf16[2,4,2,24,256]{4,3,2,1,0:T(8,128)(2,1)S(1)}, bf16[2,4,2,24,256]{4,3,2,1,0:T(8,128)(2,1)S(1)}, u32[]{:S(2)}, u32[]{:S(2)}) collective-permute-start(bf16[2,4,2,24,256]{4,3,2,1,0:T(8,128)(2,1)S(1)} %pad_maximum_fusion.near_ref), channel_id=1, source_target_pairs={{0,1},{1,0},{2,3},{3,2},{4,5},{5,4},{6,7},{7,6},{8,9},{9,8},{10,11... | collective-permute-start | bytes 589832 | tf_op jit(solution)/shard_map/ppermute | solution.py:370
  19.6 4.9 %copy-start.2 = (bf16[1024,256]{1,0:T(8,128)(2,1)S(1)}, bf16[1024,256]{1,0:T(8,128)(2,1)}, u32[]{:S(2)}) copy-start(bf16[1024,256]{1,0:T(8,128)(2,1)} %refs_2_.1) | copy-start | bytes 1572868
  21.0 3.1 %collective-permute-start.7 = (f32[8,128]{1,0:T(8,128)S(1)}, f32[8,128]{1,0:T(8,128)S(1)}, u32[]{:S(2)}, u32[]{:S(2)}) collective-permute-start(f32[8,128]{1,0:T(8,128)S(1)} %get-tuple-element.53), channel_id=1, source_target_pairs={{0,5},{1,4},{2,7},{3,6},{4,1},{5,0},{6,3},{7,2},{8,13},{9,12},{10,... | collective-permute-start | bytes 12296 | tf_op jit(solution)/shard_map/ppermute | solution.py:370
  24.1 2.1 %collective-permute-start.10 = (bf16[1024,256]{1,0:T(8,128)(2,1)S(1)}, bf16[1024,256]{1,0:T(8,128)(2,1)S(1)}, u32[]{:S(2)}, u32[]{:S(2)}) collective-permute-start(bf16[1024,256]{1,0:T(8,128)(2,1)S(1)} %collective-permute-done.8.refs_4_), channel_id=1, source_target_pairs={{0,1},{1,0},{2,3},{3,2},{4,5},{5,4},{6,7},{7,6},{8,9},{9,8},{10,11... | collective-permute-start | bytes 1572872 | tf_op jit(solution)/shard_map/ppermute | solution.py:370
  24.4 4.5 %collective-permute-start.11 = (bf16[1024,256]{1,0:T(8,128)(2,1)S(1)}, bf16[1024,256]{1,0:T(8,128)(2,1)S(1)}, u32[]{:S(2)}, u32[]{:S(2)}) collective-permute-start(bf16[1024,256]{1,0:T(8,128)(2,1)S(1)} %copy-done.2), channel_id=1, source_target_pairs={{0,1},{1,0},{2,3},{3,2},{4,5},{5,4},{6,7},{7,6},{8,9},{9,8},{10,11... | collective-permute-start | bytes 1572872 | tf_op jit(solution)/shard_map/ppermute | solution.py:370
  24.6 3.0 %collective-permute-start.9 = (f32[8,128]{1,0:T(8,128)S(1)}, f32[8,128]{1,0:T(8,128)S(1)}, u32[]{:S(2)}, u32[]{:S(2)}) collective-permute-start(f32[8,128]{1,0:T(8,128)S(1)} %add.9.mine_ref), channel_id=1, source_target_pairs={{0,3},{1,2},{2,1},{3,0},{4,7},{5,6},{6,5},{7,4},{8,11},{9,10},{10,... | collective-permute-start | bytes 12296 | tf_op jit(solution)/shard_map/ppermute | solution.py:370
  28.9 3.1 %collective-permute-start.12 = (f32[8,128]{1,0:T(8,128)S(1)}, f32[8,128]{1,0:T(8,128)S(1)}, u32[]{:S(2)}, u32[]{:S(2)}) collective-permute-start(f32[8,128]{1,0:T(8,128)S(1)} %shard_map.72.mine_ref), channel_id=1, source_target_pairs={{0,5},{1,4},{2,7},{3,6},{4,1},{5,0},{6,3},{7,2},{8,13},{9,12},{10,... | collective-permute-start | bytes 12296 | tf_op jit(solution)/shard_map/ppermute | solution.py:370
  33.0 3.8 %collective-permute-start.13 = (f32[56,256]{1,0:T(8,128)S(1)}, f32[56,256]{1,0:T(8,128)S(1)}, u32[]{:S(2)}, u32[]{:S(2)}) collective-permute-start(f32[56,256]{1,0:T(8,128)S(1)} %get-tuple-element.70), channel_id=1, source_target_pairs={{0,3},{1,2},{2,1},{3,0},{4,7},{5,6},{6,5},{7,4},{8,11},{9,10},{10,... | collective-permute-start | bytes 172040 | tf_op jit(solution)/shard_map/ppermute | solution.py:370
  34.7 4.0 %copy-start.1 = (bf16[1024,256]{1,0:T(8,128)(2,1)S(1)}, bf16[1024,256]{1,0:T(8,128)(2,1)}, u32[]{:S(2)}) copy-start(bf16[1024,256]{1,0:T(8,128)(2,1)} %refs_1_.1) | copy-start | bytes 1572868
  35.3 5.0 %copy-start.3 = (bf16[12,256]{1,0:T(8,128)(2,1)S(1)}, bf16[12,256]{1,0:T(8,128)(2,1)}, u32[]{:S(2)}) copy-start(bf16[12,256]{1,0:T(8,128)(2,1)} %refs_3_.1) | copy-start | bytes 18436
  36.9 3.4 %collective-permute-start.14 = (f32[32,256]{1,0:T(8,128)S(1)}, f32[32,256]{1,0:T(8,128)S(1)}, u32[]{:S(2)}, u32[]{:S(2)}) collective-permute-start(f32[32,256]{1,0:T(8,128)S(1)} %pad_maximum_fusion.2), channel_id=1, source_target_pairs={{0,5},{1,4},{2,7},{3,6},{4,1},{5,0},{6,3},{7,2},{8,13},{9,12},{10,... | collective-permute-start | bytes 98312 | tf_op jit(solution)/shard_map/ppermute | solution.py:370

commit v11 on v10

--- a/solution.py
+++ b/solution.py
@@ -131,7 +131,7 @@
             part_ref[to, :] = part_ref[to, :] + total if add else total
             return 0
 
-        lax.fori_loop(0, ref.shape[0] // 8, body, 0, unroll=8)
+        lax.fori_loop(0, ref.shape[0] // 8, body, 0, unroll=24)
         top += ref.shape[0]
 
 
@@ -148,7 +148,7 @@
                 total + ref[at, k * LANES : (k + 1) * LANES] * row for k, total in enumerate(sums)
             ]
 
-        sums = lax.fori_loop(0, ref.shape[0] // 8, body, sums, unroll=8)
+        sums = lax.fori_loop(0, ref.shape[0] // 8, body, sums, unroll=24)
         top += ref.shape[0]
     for k, total in enumerate(sums):
         inverse = 1.0 / jnp.sum(total, axis=0, keepdims=True)

time: 41.6 us -> 41.4 us (level)
  no operation moved by 1% of the time
where the time goes in v11:
time: 41.4 us; the launch traced here: 41.1 us
  starting transfers between devices  20.2 us (49%)
  waiting for transfers between devices  9.11 us (22%)
  Pallas kernels  8.43 us (20%)
  other arithmetic  1.52 us (4%)
  local copies, waits for them, and re-layouts  1.06 us (3%)
  between operations  0.75 us (2%)
    ppermute x12, starting transfers between devices, swap(): return lax.ppermute(values, axis, others)  15.4 us
    pallas_call x10, Pallas kernels, call(): pl.pallas_call(kernel, out_shape=out_shape, in_specs=[pl.BlockSpec(memory...  8.43 us
    ppermute x12, waiting for transfers between devices, swap(): return lax.ppermute(values, axis, others)  7.23 us
    ppermute x3, starting transfers between devices, swap_dp(): return lax.ppermute(values, ('dp', 'proto'), others)  4.86 us
    ppermute x3, waiting for transfers between devices, swap_dp(): return lax.ppermute(values, ('dp', 'proto'), others)  1.87 us
    unnamed x8, local copies, waits for them, and re-layouts  1.06 us
  transfers between devices with their start and end apart: 15, of which 9 were waited for; matrix products, arithmetic and copies ran while one was open for 2% of the time, Pallas kernels for 16%

profile of v11, /device:TPU:0, one launch (start us, length us, event | category | flops | bytes accessed | tf_op | source)
XLA Modules:
  0.0 41.1 jit_solution(12595593182194898090)
XLA Ops:
  1.4 2.4 %collective-permute-start = (bf16[24,256]{1,0:T(8,128)(2,1)S(1)}, bf16[24,256]{1,0:T(8,128)(2,1)S(1)}, u32[]{:S(2)}, u32[]{:S(2)}) collective-permute-start(bf16[24,256]{1,0:T(8,128)(2,1)S(1)} %pad_maximum_fusion.4), channel_id=1, source_target_pairs={{0,3},{1,2},{2,1},{3,0},{4,7},{5,6},{6,5},{7,4},{8,11},{9,10},{10,... | collective-permute-start | bytes 36872 | tf_op jit(solution)/shard_map/ppermute | solution.py:370
  3.8 0.7 %pad_add_fusion.place_ref = s32[6]{0:T(128)S(1)} fusion(s32[4]{0:T(128)} %param.9, s32[1]{0:T(128)} %bitcast.2, s32[1]{0:T(128)} %bitcast.1), kind=kLoop, calls=%fused_computation.6 | loop fusion | flops 12 | bytes 48 | tf_op jit(solution)/shard_map/concatenate | solution.py:394
  5.2 4.2 %collective-permute-start.1 = (bf16[2,24,256]{2,1,0:T(8,128)(2,1)S(1)}, bf16[2,24,256]{2,1,0:T(8,128)(2,1)S(1)}, u32[]{:S(2)}, u32[]{:S(2)}) collective-permute-start(bf16[2,24,256]{2,1,0:T(8,128)(2,1)S(1)} %get-tuple-element.79), channel_id=1, source_target_pairs={{0,25},{1,24},{2,27},{3,26},{4,29},{5,28},{6,31},{7,30},{8,17},{9,... | collective-permute-start | bytes 73736 | tf_op jit(solution)/shard_map/ppermute | solution.py:378
  10.1 1.5 %collective-permute-start.8 = (bf16[1024,256]{1,0:T(8,128)(2,1)}, bf16[1024,256]{1,0:T(8,128)(2,1)S(1)}, u32[]{:S(2)}, u32[]{:S(2)}) collective-permute-start(bf16[1024,256]{1,0:T(8,128)(2,1)} %refs_1_.1), channel_id=1, source_target_pairs={{0,3},{1,2},{2,1},{3,0},{4,7},{5,6},{6,5},{7,4},{8,11},{9,10},{10,... | collective-permute-start | bytes 1572872 | tf_op jit(solution)/shard_map/ppermute | solution.py:370
  11.7 1.9 %collective-permute-done.2 = bf16[2,24,256]{2,1,0:T(8,128)(2,1)S(1)} collective-permute-done((bf16[2,24,256]{2,1,0:T(8,128)(2,1)S(1)}, bf16[2,24,256]{2,1,0:T(8,128)(2,1)S(1)}, u32[]{:S(2)}, u32[]{:S(2)}) %collective-permute-start.2) | collective-permute-done | bytes 24608 | tf_op jit(solution)/shard_map/ppermute | solution.py:378
  13.6 1.6 %collective-permute-start.4 = (bf16[4,2,24,256]{3,2,1,0:T(8,128)(2,1)S(1)}, bf16[4,2,24,256]{3,2,1,0:T(8,128)(2,1)S(1)}, u32[]{:S(2)}, u32[]{:S(2)}) collective-permute-start(bf16[4,2,24,256]{3,2,1,0:T(8,128)(2,1)S(1)} %pad_maximum_fusion.1), channel_id=1, source_target_pairs={{0,5},{1,4},{2,7},{3,6},{4,1},{5,0},{6,3},{7,2},{8,13},{9,12},{10,... | collective-permute-start | bytes 294920 | tf_op jit(solution)/shard_map/ppermute | solution.py:370
  15.2 1.0 %copy-done = bf16[1024,256]{1,0:T(8,128)(2,1)S(1)} copy-done((bf16[1024,256]{1,0:T(8,128)(2,1)S(1)}, bf16[1024,256]{1,0:T(8,128)(2,1)}, u32[]{:S(2)}) %copy-start) | copy-done | bytes 524312
  16.2 0.8 %shard_map.68 = (bf16[1024,256]{1,0:T(8,128)(2,1)S(1)}, f32[192,128]{1,0:T(8,128)S(1)}, f32[192,128]{1,0:T(8,128)S(1)}) custom-call(s32[6]{0:T(128)S(1)} %pad_add_fusion.place_ref, bf16[1024,256]{1,0:T(8,128)(2,1)S(1)} %copy-done), custom_call_target="tpu_custom_call" | custom-call | flops 134217728 | bytes 1048576 | tf_op jit(solution)/shard_map/pallas_call | solution.py:355
  17.0 1.1 %collective-permute-done.4 = bf16[4,2,24,256]{3,2,1,0:T(8,128)(2,1)S(1)} collective-permute-done((bf16[4,2,24,256]{3,2,1,0:T(8,128)(2,1)S(1)}, bf16[4,2,24,256]{3,2,1,0:T(8,128)(2,1)S(1)}, u32[]{:S(2)}, u32[]{:S(2)}) %collective-permute-start.4) | collective-permute-done | bytes 98336 | tf_op jit(solution)/shard_map/ppermute | solution.py:370
  18.2 0.8 %collective-permute-start.5 = (bf16[2,4,2,24,256]{4,3,2,1,0:T(8,128)(2,1)S(1)}, bf16[2,4,2,24,256]{4,3,2,1,0:T(8,128)(2,1)S(1)}, u32[]{:S(2)}, u32[]{:S(2)}) collective-permute-start(bf16[2,4,2,24,256]{4,3,2,1,0:T(8,128)(2,1)S(1)} %pad_maximum_fusion.near_ref), channel_id=1, source_target_pairs={{0,1},{1,0},{2,3},{3,2},{4,5},{5,4},{6,7},{7,6},{8,9},{9,8},{10,11... | collective-permute-start | bytes 589832 | tf_op jit(solution)/shard_map/ppermute | solution.py:370
  20.0 0.9 %shard_map.70 = (f32[192,2048]{1,0:T(8,128)S(1)}, bf16[192,256]{1,0:T(8,128)(2,1)S(1)}, f32[8,128]{1,0:T(8,128)S(1)}) custom-call(bf16[2,4,2,24,256]{4,3,2,1,0:T(8,128)(2,1)S(1)} %collective-permute-done.5.far_ref, f32[192,128]{1,0:T(8,128)S(1)} %get-tuple-element.46.live_ref.refs_3_, f32[192,2048]{1,0:T(8,128)S(1)} %get-tuple-element.50.near_weights_ref.near_ref, ...), custom_call_target="tpu_custom_call" | custom-call | flops 201326592 | bytes 1572864 | tf_op jit(solution)/shard_map/pallas_call | solution.py:355
  20.8 1.6 %collective-permute-start.7 = (f32[8,128]{1,0:T(8,128)S(1)}, f32[8,128]{1,0:T(8,128)S(1)}, u32[]{:S(2)}, u32[]{:S(2)}) collective-permute-start(f32[8,128]{1,0:T(8,128)S(1)} %get-tuple-element.53), channel_id=1, source_target_pairs={{0,5},{1,4},{2,7},{3,6},{4,1},{5,0},{6,3},{7,2},{8,13},{9,12},{10,... | collective-permute-start | bytes 12296 | tf_op jit(solution)/shard_map/ppermute | solution.py:370
  22.4 1.6 %collective-permute-done.7 = f32[8,128]{1,0:T(8,128)S(1)} collective-permute-done((f32[8,128]{1,0:T(8,128)S(1)}, f32[8,128]{1,0:T(8,128)S(1)}, u32[]{:S(2)}, u32[]{:S(2)}) %collective-permute-start.7) | collective-permute-done | bytes 4128 | tf_op jit(solution)/shard_map/ppermute | solution.py:370
  24.5 1.7 %collective-permute-start.9 = (f32[8,128]{1,0:T(8,128)S(1)}, f32[8,128]{1,0:T(8,128)S(1)}, u32[]{:S(2)}, u32[]{:S(2)}) collective-permute-start(f32[8,128]{1,0:T(8,128)S(1)} %add.9.mine_ref), channel_id=1, source_target_pairs={{0,3},{1,2},{2,1},{3,0},{4,7},{5,6},{6,5},{7,4},{8,11},{9,10},{10,... | collective-permute-start | bytes 12296 | tf_op jit(solution)/shard_map/ppermute | solution.py:370
  26.2 1.0 %shard_map.71 = (f32[384,2048]{1,0:T(8,128)S(1)}, bf16[384,256]{1,0:T(8,128)(2,1)S(1)}) custom-call(bf16[2,4,2,24,256]{4,3,2,1,0:T(8,128)(2,1)S(1)} %pad_maximum_fusion.near_ref, bf16[2,4,2,24,256]{4,3,2,1,0:T(8,128)(2,1)S(1)} %collective-permute-done.5.far_ref, bf16[192,256]{1,0:T(8,128)(2,1)S(1)} %get-tuple-element.56.refs_0_.near_rows_ref, ...), custom_call_target="tpu_custom_call" | custom-call | flops 402653184 | bytes 3145728 | tf_op jit(solution)/shard_map/pallas_call | solution.py:355
  27.6 1.2 %shard_map.72.mine_ref = f32[8,128]{1,0:T(8,128)S(1)} custom-call(f32[8,128]{1,0:T(8,128)S(1)} %add.9.mine_ref, f32[8,128]{1,0:T(8,128)S(1)} %collective-permute-done.9.other_ref, f32[192,2048]{1,0:T(8,128)S(1)} %get-tuple-element.50.near_weights_ref.near_ref, f32[192,2048]{1,0:T(8,128)S(1)} %get-tuple-element.55.far_ref, ...), custom_call_target="tpu_custom_call" | custom-call | flops 402653184 | bytes 3145728 | tf_op jit(solution)/shard_map/pallas_call | solution.py:355
  28.8 1.7 %collective-permute-start.12 = (f32[8,128]{1,0:T(8,128)S(1)}, f32[8,128]{1,0:T(8,128)S(1)}, u32[]{:S(2)}, u32[]{:S(2)}) collective-permute-start(f32[8,128]{1,0:T(8,128)S(1)} %shard_map.72.mine_ref), channel_id=1, source_target_pairs={{0,5},{1,4},{2,7},{3,6},{4,1},{5,0},{6,3},{7,2},{8,13},{9,12},{10,... | collective-permute-start | bytes 12296 | tf_op jit(solution)/shard_map/ppermute | solution.py:370
  30.5 1.1 %shard_map.73 = (bf16[2048,256]{1,0:T(8,128)(2,1)S(1)}, f32[48,256]{1,0:T(8,128)S(1)}, f32[8,128]{1,0:T(8,128)S(1)}) custom-call(bf16[384,256]{1,0:T(8,128)(2,1)S(1)} %get-tuple-element.62.rows_ref.refs_0_.refs_2_, bf16[1024,256]{1,0:T(8,128)(2,1)S(1)} %copy-done.2, bf16[1024,256]{1,0:T(8,128)(2,1)S(1)} %collective-permute-done.11.refs_1_), custom_call_target="tpu_custom_call" | custom-call | flops 402653184 | bytes 3145728 | tf_op jit(solution)/shard_map/pallas_call | solution.py:355
  31.9 0.9 %shard_map.74 = (f32[8,4096]{1,0:T(8,128)S(1)}, f32[56,256]{1,0:T(8,128)S(1)}, f32[56,256]{1,0:T(8,128)S(1)}) custom-call(f32[8,128]{1,0:T(8,128)S(1)} %shard_map.72.mine_ref, f32[8,128]{1,0:T(8,128)S(1)} %collective-permute-done.12.other_ref, f32[192,2048]{1,0:T(8,128)S(1)} %get-tuple-element.50.near_weights_ref.near_ref, ...), custom_call_target="tpu_custom_call" | custom-call | flops 402653184 | bytes 3145728 | tf_op jit(solution)/shard_map/pallas_call | solution.py:355
  32.8 1.7 %collective-permute-start.13 = (f32[56,256]{1,0:T(8,128)S(1)}, f32[56,256]{1,0:T(8,128)S(1)}, u32[]{:S(2)}, u32[]{:S(2)}) collective-permute-start(f32[56,256]{1,0:T(8,128)S(1)} %get-tuple-element.70), channel_id=1, source_target_pairs={{0,3},{1,2},{2,1},{3,0},{4,7},{5,6},{6,5},{7,4},{8,11},{9,10},{10,... | collective-permute-start | bytes 172040 | tf_op jit(solution)/shard_map/ppermute | solution.py:370
  35.0 1.6 %collective-permute-done.13 = f32[56,256]{1,0:T(8,128)S(1)} collective-permute-done((f32[56,256]{1,0:T(8,128)S(1)}, f32[56,256]{1,0:T(8,128)S(1)}, u32[]{:S(2)}, u32[]{:S(2)}) %collective-permute-start.13) | collective-permute-done | bytes 57376 | tf_op jit(solution)/shard_map/ppermute | solution.py:370
  36.6 1.8 %collective-permute-start.14 = (f32[32,256]{1,0:T(8,128)S(1)}, f32[32,256]{1,0:T(8,128)S(1)}, u32[]{:S(2)}, u32[]{:S(2)}) collective-permute-start(f32[32,256]{1,0:T(8,128)S(1)} %pad_maximum_fusion.2), channel_id=1, source_target_pairs={{0,5},{1,4},{2,7},{3,6},{4,1},{5,0},{6,3},{7,2},{8,13},{9,12},{10,... | collective-permute-start | bytes 98312 | tf_op jit(solution)/shard_map/ppermute | solution.py:370
  38.9 1.2 %collective-permute-done.14.other_ref = f32[32,256]{1,0:T(8,128)S(1)} collective-permute-done((f32[32,256]{1,0:T(8,128)S(1)}, f32[32,256]{1,0:T(8,128)S(1)}, u32[]{:S(2)}, u32[]{:S(2)}) %collective-permute-start.14) | collective-permute-done | bytes 32800 | tf_op jit(solution)/shard_map/ppermute | solution.py:370
  40.1 1.0 %shard_map.77 = (f32[12,256]{1,0:T(8,128)}, f32[1,256,256]{2,1,0:T(8,128)}) custom-call(f32[56,256]{1,0:T(8,128)S(1)} %add.10.mine_ref, f32[8,256]{1,0:T(8,128)S(1)} %slice_add_fusion.sums_ref, f32[32,256]{1,0:T(8,128)S(1)} %collective-permute-done.14.other_ref, f32[256,384]{1,0:T(8,128)S(1)} %get-tuple-element.74.targets_ref, ...), custom_call_target="tpu_custom_call" | custom-call | flops 50331648 | bytes 393216 | tf_op jit(solution)/shard_map/pallas_call | solution.py:355
  (34 shorter events, 5.5 us)
Async XLA Ops:
  1.4 3.8 %collective-permute-start = (bf16[24,256]{1,0:T(8,128)(2,1)S(1)}, bf16[24,256]{1,0:T(8,128)(2,1)S(1)}, u32[]{:S(2)}, u32[]{:S(2)}) collective-permute-start(bf16[24,256]{1,0:T(8,128)(2,1)S(1)} %pad_maximum_fusion.4), channel_id=1, source_target_pairs={{0,3},{1,2},{2,1},{3,0},{4,7},{5,6},{6,5},{7,4},{8,11},{9,10},{10,... | collective-permute-start | bytes 36872 | tf_op jit(solution)/shard_map/ppermute | solution.py:370
  5.2 6.5 %collective-permute-start.1 = (bf16[2,24,256]{2,1,0:T(8,128)(2,1)S(1)}, bf16[2,24,256]{2,1,0:T(8,128)(2,1)S(1)}, u32[]{:S(2)}, u32[]{:S(2)}) collective-permute-start(bf16[2,24,256]{2,1,0:T(8,128)(2,1)S(1)} %get-tuple-element.79), channel_id=1, source_target_pairs={{0,25},{1,24},{2,27},{3,26},{4,29},{5,28},{6,31},{7,30},{8,17},{9,... | collective-permute-start | bytes 73736 | tf_op jit(solution)/shard_map/ppermute | solution.py:378
  9.4 4.2 %collective-permute-start.2 = (bf16[2,24,256]{2,1,0:T(8,128)(2,1)S(1)}, bf16[2,24,256]{2,1,0:T(8,128)(2,1)S(1)}, u32[]{:S(2)}, u32[]{:S(2)}) collective-permute-start(bf16[2,24,256]{2,1,0:T(8,128)(2,1)S(1)} %get-tuple-element.79), channel_id=1, source_target_pairs={{0,17},{1,16},{2,19},{3,18},{4,21},{5,20},{6,23},{7,22},{8,25},{9,... | collective-permute-start | bytes 73736 | tf_op jit(solution)/shard_map/ppermute | solution.py:378
  9.4 4.2 %collective-permute-start.3 = (bf16[2,24,256]{2,1,0:T(8,128)(2,1)S(1)}, bf16[2,24,256]{2,1,0:T(8,128)(2,1)S(1)}, u32[]{:S(2)}, u32[]{:S(2)}) collective-permute-start(bf16[2,24,256]{2,1,0:T(8,128)(2,1)S(1)} %get-tuple-element.79), channel_id=1, source_target_pairs={{0,9},{1,8},{2,11},{3,10},{4,13},{5,12},{6,15},{7,14},{8,1},{9,0},... | collective-permute-start | bytes 73736 | tf_op jit(solution)/shard_map/ppermute | solution.py:378
  10.1 8.9 %collective-permute-start.6 = (bf16[1024,256]{1,0:T(8,128)(2,1)}, bf16[1024,256]{1,0:T(8,128)(2,1)S(1)}, u32[]{:S(2)}, u32[]{:S(2)}) collective-permute-start(bf16[1024,256]{1,0:T(8,128)(2,1)} %refs_1_.1), channel_id=1, source_target_pairs={{0,1},{1,0},{2,3},{3,2},{4,5},{5,4},{6,7},{7,6},{8,9},{9,8},{10,11... | collective-permute-start | bytes 1572872 | tf_op jit(solution)/shard_map/ppermute | solution.py:370
  10.1 13.9 %collective-permute-start.8 = (bf16[1024,256]{1,0:T(8,128)(2,1)}, bf16[1024,256]{1,0:T(8,128)(2,1)S(1)}, u32[]{:S(2)}, u32[]{:S(2)}) collective-permute-start(bf16[1024,256]{1,0:T(8,128)(2,1)} %refs_1_.1), channel_id=1, source_target_pairs={{0,3},{1,2},{2,1},{3,0},{4,7},{5,6},{6,5},{7,4},{8,11},{9,10},{10,... | collective-permute-start | bytes 1572872 | tf_op jit(solution)/shard_map/ppermute | solution.py:370
  13.6 4.6 %collective-permute-start.4 = (bf16[4,2,24,256]{3,2,1,0:T(8,128)(2,1)S(1)}, bf16[4,2,24,256]{3,2,1,0:T(8,128)(2,1)S(1)}, u32[]{:S(2)}, u32[]{:S(2)}) collective-permute-start(bf16[4,2,24,256]{3,2,1,0:T(8,128)(2,1)S(1)} %pad_maximum_fusion.1), channel_id=1, source_target_pairs={{0,5},{1,4},{2,7},{3,6},{4,1},{5,0},{6,3},{7,2},{8,13},{9,12},{10,... | collective-permute-start | bytes 294920 | tf_op jit(solution)/shard_map/ppermute | solution.py:370
  15.2 1.0 %copy-start = (bf16[1024,256]{1,0:T(8,128)(2,1)S(1)}, bf16[1024,256]{1,0:T(8,128)(2,1)}, u32[]{:S(2)}) copy-start(bf16[1024,256]{1,0:T(8,128)(2,1)} %refs_1_.1) | copy-start | bytes 1572868
  18.2 1.8 %collective-permute-start.5 = (bf16[2,4,2,24,256]{4,3,2,1,0:T(8,128)(2,1)S(1)}, bf16[2,4,2,24,256]{4,3,2,1,0:T(8,128)(2,1)S(1)}, u32[]{:S(2)}, u32[]{:S(2)}) collective-permute-start(bf16[2,4,2,24,256]{4,3,2,1,0:T(8,128)(2,1)S(1)} %pad_maximum_fusion.near_ref), channel_id=1, source_target_pairs={{0,1},{1,0},{2,3},{3,2},{4,5},{5,4},{6,7},{7,6},{8,9},{9,8},{10,11... | collective-permute-start | bytes 589832 | tf_op jit(solution)/shard_map/ppermute | solution.py:370
  19.6 4.8 %copy-start.2 = (bf16[1024,256]{1,0:T(8,128)(2,1)S(1)}, bf16[1024,256]{1,0:T(8,128)(2,1)}, u32[]{:S(2)}) copy-start(bf16[1024,256]{1,0:T(8,128)(2,1)} %refs_2_.1) | copy-start | bytes 1572868
  20.8 3.1 %collective-permute-start.7 = (f32[8,128]{1,0:T(8,128)S(1)}, f32[8,128]{1,0:T(8,128)S(1)}, u32[]{:S(2)}, u32[]{:S(2)}) collective-permute-start(f32[8,128]{1,0:T(8,128)S(1)} %get-tuple-element.53), channel_id=1, source_target_pairs={{0,5},{1,4},{2,7},{3,6},{4,1},{5,0},{6,3},{7,2},{8,13},{9,12},{10,... | collective-permute-start | bytes 12296 | tf_op jit(solution)/shard_map/ppermute | solution.py:370
  24.0 2.2 %collective-permute-start.10 = (bf16[1024,256]{1,0:T(8,128)(2,1)S(1)}, bf16[1024,256]{1,0:T(8,128)(2,1)S(1)}, u32[]{:S(2)}, u32[]{:S(2)}) collective-permute-start(bf16[1024,256]{1,0:T(8,128)(2,1)S(1)} %collective-permute-done.8.refs_4_), channel_id=1, source_target_pairs={{0,1},{1,0},{2,3},{3,2},{4,5},{5,4},{6,7},{7,6},{8,9},{9,8},{10,11... | collective-permute-start | bytes 1572872 | tf_op jit(solution)/shard_map/ppermute | solution.py:370
  24.4 4.3 %collective-permute-start.11 = (bf16[1024,256]{1,0:T(8,128)(2,1)S(1)}, bf16[1024,256]{1,0:T(8,128)(2,1)S(1)}, u32[]{:S(2)}, u32[]{:S(2)}) collective-permute-start(bf16[1024,256]{1,0:T(8,128)(2,1)S(1)} %copy-done.2), channel_id=1, source_target_pairs={{0,1},{1,0},{2,3},{3,2},{4,5},{5,4},{6,7},{7,6},{8,9},{9,8},{10,11... | collective-permute-start | bytes 1572872 | tf_op jit(solution)/shard_map/ppermute | solution.py:370
  24.5 3.1 %collective-permute-start.9 = (f32[8,128]{1,0:T(8,128)S(1)}, f32[8,128]{1,0:T(8,128)S(1)}, u32[]{:S(2)}, u32[]{:S(2)}) collective-permute-start(f32[8,128]{1,0:T(8,128)S(1)} %add.9.mine_ref), channel_id=1, source_target_pairs={{0,3},{1,2},{2,1},{3,0},{4,7},{5,6},{6,5},{7,4},{8,11},{9,10},{10,... | collective-permute-start | bytes 12296 | tf_op jit(solution)/shard_map/ppermute | solution.py:370
  28.8 3.1 %collective-permute-start.12 = (f32[8,128]{1,0:T(8,128)S(1)}, f32[8,128]{1,0:T(8,128)S(1)}, u32[]{:S(2)}, u32[]{:S(2)}) collective-permute-start(f32[8,128]{1,0:T(8,128)S(1)} %shard_map.72.mine_ref), channel_id=1, source_target_pairs={{0,5},{1,4},{2,7},{3,6},{4,1},{5,0},{6,3},{7,2},{8,13},{9,12},{10,... | collective-permute-start | bytes 12296 | tf_op jit(solution)/shard_map/ppermute | solution.py:370
  32.8 3.8 %collective-permute-start.13 = (f32[56,256]{1,0:T(8,128)S(1)}, f32[56,256]{1,0:T(8,128)S(1)}, u32[]{:S(2)}, u32[]{:S(2)}) collective-permute-start(f32[56,256]{1,0:T(8,128)S(1)} %get-tuple-element.70), channel_id=1, source_target_pairs={{0,3},{1,2},{2,1},{3,0},{4,7},{5,6},{6,5},{7,4},{8,11},{9,10},{10,... | collective-permute-start | bytes 172040 | tf_op jit(solution)/shard_map/ppermute | solution.py:370
  34.5 4.0 %copy-start.1 = (bf16[1024,256]{1,0:T(8,128)(2,1)S(1)}, bf16[1024,256]{1,0:T(8,128)(2,1)}, u32[]{:S(2)}) copy-start(bf16[1024,256]{1,0:T(8,128)(2,1)} %refs_1_.1) | copy-start | bytes 1572868
  35.0 5.0 %copy-start.3 = (bf16[12,256]{1,0:T(8,128)(2,1)S(1)}, bf16[12,256]{1,0:T(8,128)(2,1)}, u32[]{:S(2)}) copy-start(bf16[12,256]{1,0:T(8,128)(2,1)} %refs_3_.1) | copy-start | bytes 18436
  36.6 3.4 %collective-permute-start.14 = (f32[32,256]{1,0:T(8,128)S(1)}, f32[32,256]{1,0:T(8,128)S(1)}, u32[]{:S(2)}, u32[]{:S(2)}) collective-permute-start(f32[32,256]{1,0:T(8,128)S(1)} %pad_maximum_fusion.2), channel_id=1, source_target_pairs={{0,5},{1,4},{2,7},{3,6},{4,1},{5,0},{6,3},{7,2},{8,13},{9,12},{10,... | collective-permute-start | bytes 98312 | tf_op jit(solution)/shard_map/ppermute | solution.py:370

commit v12 on v11

--- a/solution.py
+++ b/solution.py
@@ -300,8 +300,8 @@
 
 
 def own_kernel(mine_ref, other_ref, near_rows_ref, far_rows_ref, *refs):
-    student_rows_ref, teacher_proto_ref, proto_ref, *refs = refs
-    targets_ref, exps_ref, unit_ref, scale_ref = refs
+    student_rows_ref, teacher_proto_ref, proto_ref, feat_ref, *refs = refs
+    targets_ref, exps_ref, unit_ref, scale_ref, row_unit_ref, row_scale_ref = refs
     teacher_rows = jnp.concatenate([near_rows_ref[...], far_rows_ref[...]], axis=0)
     own, all_rows = targets_ref.shape
     row_scale = inverse_rows(mine_ref[...] + other_ref[...], all_rows)
@@ -317,12 +317,16 @@
     units = unit.astype(jnp.bfloat16)
     exps = jnp.exp(scores_of(units, student_rows_ref[...]) * (1 / student_temp))
     exps_ref[...] = exps * (1 / student_temp)
+    unit, scale = quick_unit(feat_ref[...])
+    row_unit_ref[...] = unit
+    row_scale_ref[...] = jnp.broadcast_to(scale, row_scale_ref.shape)
 
 
 def grads_kernel(mine_ref, sums_ref, other_ref, targets_ref, exps_ref, *refs):
-    unit_ref, scale_ref, rows_ref, feat_ref, student_out_ref, proto_out_ref = refs
+    unit_ref, scale_ref, rows_ref, row_unit_ref, row_scale_ref, *refs = refs
+    student_out_ref, proto_out_ref = refs
     all_rows = targets_ref.shape[1]
-    rows = feat_ref.shape[0]
+    rows = row_unit_ref.shape[0]
     sums = sums_ref[...] + other_ref[2 * rows :, :]
     target_scale = inverse_rows(sums[:, LANES:], all_rows)
     exp_scale = jnp.where(target_scale > 0.0, 1.0 / unpack_lanes(sums[:, :LANES], all_rows), 0.0)
@@ -331,7 +335,7 @@
     pushed = jnp.dot(grad.astype(jnp.bfloat16), rows_ref[...], preferred_element_type=jnp.float32)
     unit = unit_ref[...]
     along = jnp.sum(unit * pushed, axis=1, keepdims=True)
-    proto_out_ref[0] = (pushed - unit * along) * twice(scale_ref[...])
+    proto_out_ref[0] = (pushed - unit * along) * scale_ref[...]
 
     row = lax.broadcasted_iota(jnp.int32, (rows, LANES), 0) + block_of(own_place()[1]) * rows
     here = lax.broadcasted_iota(jnp.int32, (rows, LANES), 1) == row
@@ -344,10 +348,10 @@
         for k in range(2)
     ]
     pulled = exp_pull * exp_column - target_pull * target_column
-    unit, scale = quick_unit(feat_ref[...])
+    unit = row_unit_ref[...]
     student_out_ref[...] = (
         pulled - unit * jnp.sum(unit * pulled, axis=1, keepdims=True)
-    ) * scale
+    ) * row_scale_ref[...]
 
 
 def call(kernel, out_shape, operands, smem=0, scratch=(), work=0):
@@ -493,10 +497,10 @@
         work=held * all_rows,
     )
     *parts, send = lax.optimization_barrier((*parts, send))
-    targets, exps, own_units, own_scales = call(
+    targets, exps, own_units, own_scales, row_units, row_scales = call(
         own_kernel,
-        (f32((own, all_rows)), f32((own, all_rows)), f32((own, width)), f32((own, LANES))),
-        (*parts, near_rows, far_rows, student_rows, teacher_prototypes, prototypes),
+        (f32((own, all_rows)), f32((own, all_rows)), *([f32((own, width))] * 2), *([f32((rows, width))] * 2)),
+        (*parts, near_rows, far_rows, student_rows, teacher_prototypes, prototypes, student_feat),
         work=own * all_rows,
     )
     total = keep + swap(send, "proto", X_CROSS)
@@ -513,7 +517,8 @@
             own_units,
             own_scales,
             student_rows,
-            student_feat,
+            row_units,
+            row_scales,
         ),
         work=own * all_rows,
     )

time: 41.4 us -> 41.4 us (level)
  no operation moved by 1% of the time
where the time goes in v12:
time: 41.4 us; the launch traced here: 41.1 us
  starting transfers between devices  20.3 us (49%)
  waiting for transfers between devices  9.09 us (22%)
  Pallas kernels  8.43 us (20%)
  other arithmetic  1.52 us (4%)
  local copies, waits for them, and re-layouts  1.06 us (3%)
  between operations  0.74 us (2%)
    ppermute x12, starting transfers between devices, swap(): return lax.ppermute(values, axis, others)  15.4 us
    pallas_call x10, Pallas kernels, call(): pl.pallas_call(kernel, out_shape=out_shape, in_specs=[pl.BlockSpec(memory...  8.43 us
    ppermute x12, waiting for transfers between devices, swap(): return lax.ppermute(values, axis, others)  7.22 us
    ppermute x3, starting transfers between devices, swap_dp(): return lax.ppermute(values, ('dp', 'proto'), others)  4.86 us
    ppermute x3, waiting for transfers between devices, swap_dp(): return lax.ppermute(values, ('dp', 'proto'), others)  1.87 us
    unnamed x8, local copies, waits for them, and re-layouts  1.05 us
  transfers between devices with their start and end apart: 15, of which 9 were waited for; matrix products, arithmetic and copies ran while one was open for 2% of the time, Pallas kernels for 16%

profile of v12, /device:TPU:0, one launch (start us, length us, event | category | flops | bytes accessed | tf_op | source)
XLA Modules:
  0.0 41.1 jit_solution(18371646141872275228)
XLA Ops:
  1.4 2.4 %collective-permute-start = (bf16[24,256]{1,0:T(8,128)(2,1)S(1)}, bf16[24,256]{1,0:T(8,128)(2,1)S(1)}, u32[]{:S(2)}, u32[]{:S(2)}) collective-permute-start(bf16[24,256]{1,0:T(8,128)(2,1)S(1)} %pad_maximum_fusion.4), channel_id=1, source_target_pairs={{0,3},{1,2},{2,1},{3,0},{4,7},{5,6},{6,5},{7,4},{8,11},{9,10},{10,... | collective-permute-start | bytes 36872 | tf_op jit(solution)/shard_map/ppermute | solution.py:374
  3.8 0.7 %pad_add_fusion.place_ref = s32[6]{0:T(128)S(1)} fusion(s32[4]{0:T(128)} %param.9, s32[1]{0:T(128)} %bitcast.2, s32[1]{0:T(128)} %bitcast.1), kind=kLoop, calls=%fused_computation.6 | loop fusion | flops 12 | bytes 48 | tf_op jit(solution)/shard_map/concatenate | solution.py:398
  5.2 4.2 %collective-permute-start.1 = (bf16[2,24,256]{2,1,0:T(8,128)(2,1)S(1)}, bf16[2,24,256]{2,1,0:T(8,128)(2,1)S(1)}, u32[]{:S(2)}, u32[]{:S(2)}) collective-permute-start(bf16[2,24,256]{2,1,0:T(8,128)(2,1)S(1)} %get-tuple-element.83), channel_id=1, source_target_pairs={{0,25},{1,24},{2,27},{3,26},{4,29},{5,28},{6,31},{7,30},{8,17},{9,... | collective-permute-start | bytes 73736 | tf_op jit(solution)/shard_map/ppermute | solution.py:382
  10.1 1.5 %collective-permute-start.8 = (bf16[1024,256]{1,0:T(8,128)(2,1)}, bf16[1024,256]{1,0:T(8,128)(2,1)S(1)}, u32[]{:S(2)}, u32[]{:S(2)}) collective-permute-start(bf16[1024,256]{1,0:T(8,128)(2,1)} %refs_1_.1), channel_id=1, source_target_pairs={{0,3},{1,2},{2,1},{3,0},{4,7},{5,6},{6,5},{7,4},{8,11},{9,10},{10,... | collective-permute-start | bytes 1572872 | tf_op jit(solution)/shard_map/ppermute | solution.py:374
  11.7 1.9 %collective-permute-done.2 = bf16[2,24,256]{2,1,0:T(8,128)(2,1)S(1)} collective-permute-done((bf16[2,24,256]{2,1,0:T(8,128)(2,1)S(1)}, bf16[2,24,256]{2,1,0:T(8,128)(2,1)S(1)}, u32[]{:S(2)}, u32[]{:S(2)}) %collective-permute-start.2) | collective-permute-done | bytes 24608 | tf_op jit(solution)/shard_map/ppermute | solution.py:382
  13.6 1.6 %collective-permute-start.4 = (bf16[4,2,24,256]{3,2,1,0:T(8,128)(2,1)S(1)}, bf16[4,2,24,256]{3,2,1,0:T(8,128)(2,1)S(1)}, u32[]{:S(2)}, u32[]{:S(2)}) collective-permute-start(bf16[4,2,24,256]{3,2,1,0:T(8,128)(2,1)S(1)} %pad_maximum_fusion.1), channel_id=1, source_target_pairs={{0,5},{1,4},{2,7},{3,6},{4,1},{5,0},{6,3},{7,2},{8,13},{9,12},{10,... | collective-permute-start | bytes 294920 | tf_op jit(solution)/shard_map/ppermute | solution.py:374
  15.2 1.0 %copy-done = bf16[1024,256]{1,0:T(8,128)(2,1)S(1)} copy-done((bf16[1024,256]{1,0:T(8,128)(2,1)S(1)}, bf16[1024,256]{1,0:T(8,128)(2,1)}, u32[]{:S(2)}) %copy-start) | copy-done | bytes 524312
  16.2 0.8 %shard_map.68 = (bf16[1024,256]{1,0:T(8,128)(2,1)S(1)}, f32[192,128]{1,0:T(8,128)S(1)}, f32[192,128]{1,0:T(8,128)S(1)}) custom-call(s32[6]{0:T(128)S(1)} %pad_add_fusion.place_ref, bf16[1024,256]{1,0:T(8,128)(2,1)S(1)} %copy-done), custom_call_target="tpu_custom_call" | custom-call | flops 134217728 | bytes 1048576 | tf_op jit(solution)/shard_map/pallas_call | solution.py:359
  17.0 1.1 %collective-permute-done.4 = bf16[4,2,24,256]{3,2,1,0:T(8,128)(2,1)S(1)} collective-permute-done((bf16[4,2,24,256]{3,2,1,0:T(8,128)(2,1)S(1)}, bf16[4,2,24,256]{3,2,1,0:T(8,128)(2,1)S(1)}, u32[]{:S(2)}, u32[]{:S(2)}) %collective-permute-start.4) | collective-permute-done | bytes 98336 | tf_op jit(solution)/shard_map/ppermute | solution.py:374
  18.2 0.8 %collective-permute-start.5 = (bf16[2,4,2,24,256]{4,3,2,1,0:T(8,128)(2,1)S(1)}, bf16[2,4,2,24,256]{4,3,2,1,0:T(8,128)(2,1)S(1)}, u32[]{:S(2)}, u32[]{:S(2)}) collective-permute-start(bf16[2,4,2,24,256]{4,3,2,1,0:T(8,128)(2,1)S(1)} %pad_maximum_fusion.near_ref), channel_id=1, source_target_pairs={{0,1},{1,0},{2,3},{3,2},{4,5},{5,4},{6,7},{7,6},{8,9},{9,8},{10,11... | collective-permute-start | bytes 589832 | tf_op jit(solution)/shard_map/ppermute | solution.py:374
  20.0 0.9 %shard_map.70 = (f32[192,2048]{1,0:T(8,128)S(1)}, bf16[192,256]{1,0:T(8,128)(2,1)S(1)}, f32[8,128]{1,0:T(8,128)S(1)}) custom-call(bf16[2,4,2,24,256]{4,3,2,1,0:T(8,128)(2,1)S(1)} %collective-permute-done.5.far_ref, f32[192,128]{1,0:T(8,128)S(1)} %get-tuple-element.48.live_ref.refs_3_, f32[192,2048]{1,0:T(8,128)S(1)} %get-tuple-element.52.near_weights_ref.near_ref, ...), custom_call_target="tpu_custom_call" | custom-call | flops 201326592 | bytes 1572864 | tf_op jit(solution)/shard_map/pallas_call | solution.py:359
  20.8 1.6 %collective-permute-start.7 = (f32[8,128]{1,0:T(8,128)S(1)}, f32[8,128]{1,0:T(8,128)S(1)}, u32[]{:S(2)}, u32[]{:S(2)}) collective-permute-start(f32[8,128]{1,0:T(8,128)S(1)} %get-tuple-element.55), channel_id=1, source_target_pairs={{0,5},{1,4},{2,7},{3,6},{4,1},{5,0},{6,3},{7,2},{8,13},{9,12},{10,... | collective-permute-start | bytes 12296 | tf_op jit(solution)/shard_map/ppermute | solution.py:374
  22.4 1.6 %collective-permute-done.7 = f32[8,128]{1,0:T(8,128)S(1)} collective-permute-done((f32[8,128]{1,0:T(8,128)S(1)}, f32[8,128]{1,0:T(8,128)S(1)}, u32[]{:S(2)}, u32[]{:S(2)}) %collective-permute-start.7) | collective-permute-done | bytes 4128 | tf_op jit(solution)/shard_map/ppermute | solution.py:374
  24.5 1.7 %collective-permute-start.9 = (f32[8,128]{1,0:T(8,128)S(1)}, f32[8,128]{1,0:T(8,128)S(1)}, u32[]{:S(2)}, u32[]{:S(2)}) collective-permute-start(f32[8,128]{1,0:T(8,128)S(1)} %add.9.mine_ref), channel_id=1, source_target_pairs={{0,3},{1,2},{2,1},{3,0},{4,7},{5,6},{6,5},{7,4},{8,11},{9,10},{10,... | collective-permute-start | bytes 12296 | tf_op jit(solution)/shard_map/ppermute | solution.py:374
  26.2 1.0 %shard_map.71 = (f32[384,2048]{1,0:T(8,128)S(1)}, bf16[384,256]{1,0:T(8,128)(2,1)S(1)}) custom-call(bf16[2,4,2,24,256]{4,3,2,1,0:T(8,128)(2,1)S(1)} %pad_maximum_fusion.near_ref, bf16[2,4,2,24,256]{4,3,2,1,0:T(8,128)(2,1)S(1)} %collective-permute-done.5.far_ref, bf16[192,256]{1,0:T(8,128)(2,1)S(1)} %get-tuple-element.58.refs_0_.near_rows_ref, ...), custom_call_target="tpu_custom_call" | custom-call | flops 402653184 | bytes 3145728 | tf_op jit(solution)/shard_map/pallas_call | solution.py:359
  27.6 1.2 %shard_map.72.mine_ref = f32[8,128]{1,0:T(8,128)S(1)} custom-call(f32[8,128]{1,0:T(8,128)S(1)} %add.9.mine_ref, f32[8,128]{1,0:T(8,128)S(1)} %collective-permute-done.9.other_ref, f32[192,2048]{1,0:T(8,128)S(1)} %get-tuple-element.52.near_weights_ref.near_ref, f32[192,2048]{1,0:T(8,128)S(1)} %get-tuple-element.57.far_ref, ...), custom_call_target="tpu_custom_call" | custom-call | flops 402653184 | bytes 3145728 | tf_op jit(solution)/shard_map/pallas_call | solution.py:359
  28.8 1.7 %collective-permute-start.12 = (f32[8,128]{1,0:T(8,128)S(1)}, f32[8,128]{1,0:T(8,128)S(1)}, u32[]{:S(2)}, u32[]{:S(2)}) collective-permute-start(f32[8,128]{1,0:T(8,128)S(1)} %shard_map.72.mine_ref), channel_id=1, source_target_pairs={{0,5},{1,4},{2,7},{3,6},{4,1},{5,0},{6,3},{7,2},{8,13},{9,12},{10,... | collective-permute-start | bytes 12296 | tf_op jit(solution)/shard_map/ppermute | solution.py:374
  30.5 1.1 %shard_map.73 = (bf16[2048,256]{1,0:T(8,128)(2,1)S(1)}, f32[48,256]{1,0:T(8,128)S(1)}, f32[8,128]{1,0:T(8,128)S(1)}) custom-call(bf16[384,256]{1,0:T(8,128)(2,1)S(1)} %get-tuple-element.64.rows_ref.refs_0_.refs_2_, bf16[1024,256]{1,0:T(8,128)(2,1)S(1)} %copy-done.2, bf16[1024,256]{1,0:T(8,128)(2,1)S(1)} %collective-permute-done.11.refs_1_), custom_call_target="tpu_custom_call" | custom-call | flops 402653184 | bytes 3145728 | tf_op jit(solution)/shard_map/pallas_call | solution.py:359
  31.9 0.9 %shard_map.74 = (f32[8,4096]{1,0:T(8,128)S(1)}, f32[56,256]{1,0:T(8,128)S(1)}, f32[56,256]{1,0:T(8,128)S(1)}) custom-call(f32[8,128]{1,0:T(8,128)S(1)} %shard_map.72.mine_ref, f32[8,128]{1,0:T(8,128)S(1)} %collective-permute-done.12.other_ref, f32[192,2048]{1,0:T(8,128)S(1)} %get-tuple-element.52.near_weights_ref.near_ref, ...), custom_call_target="tpu_custom_call" | custom-call | flops 402653184 | bytes 3145728 | tf_op jit(solution)/shard_map/pallas_call | solution.py:359
  32.8 1.7 %collective-permute-start.13 = (f32[56,256]{1,0:T(8,128)S(1)}, f32[56,256]{1,0:T(8,128)S(1)}, u32[]{:S(2)}, u32[]{:S(2)}) collective-permute-start(f32[56,256]{1,0:T(8,128)S(1)} %get-tuple-element.72), channel_id=1, source_target_pairs={{0,3},{1,2},{2,1},{3,0},{4,7},{5,6},{6,5},{7,4},{8,11},{9,10},{10,... | collective-permute-start | bytes 172040 | tf_op jit(solution)/shard_map/ppermute | solution.py:374
  35.0 1.6 %collective-permute-done.13 = f32[56,256]{1,0:T(8,128)S(1)} collective-permute-done((f32[56,256]{1,0:T(8,128)S(1)}, f32[56,256]{1,0:T(8,128)S(1)}, u32[]{:S(2)}, u32[]{:S(2)}) %collective-permute-start.13) | collective-permute-done | bytes 57376 | tf_op jit(solution)/shard_map/ppermute | solution.py:374
  36.6 1.8 %collective-permute-start.14 = (f32[32,256]{1,0:T(8,128)S(1)}, f32[32,256]{1,0:T(8,128)S(1)}, u32[]{:S(2)}, u32[]{:S(2)}) collective-permute-start(f32[32,256]{1,0:T(8,128)S(1)} %pad_maximum_fusion.2), channel_id=1, source_target_pairs={{0,5},{1,4},{2,7},{3,6},{4,1},{5,0},{6,3},{7,2},{8,13},{9,12},{10,... | collective-permute-start | bytes 98312 | tf_op jit(solution)/shard_map/ppermute | solution.py:374
  38.9 1.2 %collective-permute-done.14.other_ref = f32[32,256]{1,0:T(8,128)S(1)} collective-permute-done((f32[32,256]{1,0:T(8,128)S(1)}, f32[32,256]{1,0:T(8,128)S(1)}, u32[]{:S(2)}, u32[]{:S(2)}) %collective-permute-start.14) | collective-permute-done | bytes 32800 | tf_op jit(solution)/shard_map/ppermute | solution.py:374
  40.1 1.0 %shard_map.77 = (f32[12,256]{1,0:T(8,128)}, f32[1,256,256]{2,1,0:T(8,128)}) custom-call(f32[56,256]{1,0:T(8,128)S(1)} %add.10.mine_ref, f32[8,256]{1,0:T(8,128)S(1)} %slice_add_fusion.sums_ref, f32[32,256]{1,0:T(8,128)S(1)} %collective-permute-done.14.other_ref, f32[256,384]{1,0:T(8,128)S(1)} %get-tuple-element.76.targets_ref, ...), custom_call_target="tpu_custom_call" | custom-call | flops 50331648 | bytes 393216 | tf_op jit(solution)/shard_map/pallas_call | solution.py:359
  (34 shorter events, 5.5 us)
Async XLA Ops:
  1.4 3.8 %collective-permute-start = (bf16[24,256]{1,0:T(8,128)(2,1)S(1)}, bf16[24,256]{1,0:T(8,128)(2,1)S(1)}, u32[]{:S(2)}, u32[]{:S(2)}) collective-permute-start(bf16[24,256]{1,0:T(8,128)(2,1)S(1)} %pad_maximum_fusion.4), channel_id=1, source_target_pairs={{0,3},{1,2},{2,1},{3,0},{4,7},{5,6},{6,5},{7,4},{8,11},{9,10},{10,... | collective-permute-start | bytes 36872 | tf_op jit(solution)/shard_map/ppermute | solution.py:374
  5.2 6.5 %collective-permute-start.1 = (bf16[2,24,256]{2,1,0:T(8,128)(2,1)S(1)}, bf16[2,24,256]{2,1,0:T(8,128)(2,1)S(1)}, u32[]{:S(2)}, u32[]{:S(2)}) collective-permute-start(bf16[2,24,256]{2,1,0:T(8,128)(2,1)S(1)} %get-tuple-element.83), channel_id=1, source_target_pairs={{0,25},{1,24},{2,27},{3,26},{4,29},{5,28},{6,31},{7,30},{8,17},{9,... | collective-permute-start | bytes 73736 | tf_op jit(solution)/shard_map/ppermute | solution.py:382
  9.4 4.2 %collective-permute-start.2 = (bf16[2,24,256]{2,1,0:T(8,128)(2,1)S(1)}, bf16[2,24,256]{2,1,0:T(8,128)(2,1)S(1)}, u32[]{:S(2)}, u32[]{:S(2)}) collective-permute-start(bf16[2,24,256]{2,1,0:T(8,128)(2,1)S(1)} %get-tuple-element.83), channel_id=1, source_target_pairs={{0,17},{1,16},{2,19},{3,18},{4,21},{5,20},{6,23},{7,22},{8,25},{9,... | collective-permute-start | bytes 73736 | tf_op jit(solution)/shard_map/ppermute | solution.py:382
  9.4 4.2 %collective-permute-start.3 = (bf16[2,24,256]{2,1,0:T(8,128)(2,1)S(1)}, bf16[2,24,256]{2,1,0:T(8,128)(2,1)S(1)}, u32[]{:S(2)}, u32[]{:S(2)}) collective-permute-start(bf16[2,24,256]{2,1,0:T(8,128)(2,1)S(1)} %get-tuple-element.83), channel_id=1, source_target_pairs={{0,9},{1,8},{2,11},{3,10},{4,13},{5,12},{6,15},{7,14},{8,1},{9,0},... | collective-permute-start | bytes 73736 | tf_op jit(solution)/shard_map/ppermute | solution.py:382
  10.1 8.9 %collective-permute-start.6 = (bf16[1024,256]{1,0:T(8,128)(2,1)}, bf16[1024,256]{1,0:T(8,128)(2,1)S(1)}, u32[]{:S(2)}, u32[]{:S(2)}) collective-permute-start(bf16[1024,256]{1,0:T(8,128)(2,1)} %refs_1_.1), channel_id=1, source_target_pairs={{0,1},{1,0},{2,3},{3,2},{4,5},{5,4},{6,7},{7,6},{8,9},{9,8},{10,11... | collective-permute-start | bytes 1572872 | tf_op jit(solution)/shard_map/ppermute | solution.py:374
  10.1 13.9 %collective-permute-start.8 = (bf16[1024,256]{1,0:T(8,128)(2,1)}, bf16[1024,256]{1,0:T(8,128)(2,1)S(1)}, u32[]{:S(2)}, u32[]{:S(2)}) collective-permute-start(bf16[1024,256]{1,0:T(8,128)(2,1)} %refs_1_.1), channel_id=1, source_target_pairs={{0,3},{1,2},{2,1},{3,0},{4,7},{5,6},{6,5},{7,4},{8,11},{9,10},{10,... | collective-permute-start | bytes 1572872 | tf_op jit(solution)/shard_map/ppermute | solution.py:374
  13.6 4.6 %collective-permute-start.4 = (bf16[4,2,24,256]{3,2,1,0:T(8,128)(2,1)S(1)}, bf16[4,2,24,256]{3,2,1,0:T(8,128)(2,1)S(1)}, u32[]{:S(2)}, u32[]{:S(2)}) collective-permute-start(bf16[4,2,24,256]{3,2,1,0:T(8,128)(2,1)S(1)} %pad_maximum_fusion.1), channel_id=1, source_target_pairs={{0,5},{1,4},{2,7},{3,6},{4,1},{5,0},{6,3},{7,2},{8,13},{9,12},{10,... | collective-permute-start | bytes 294920 | tf_op jit(solution)/shard_map/ppermute | solution.py:374
  15.2 1.0 %copy-start = (bf16[1024,256]{1,0:T(8,128)(2,1)S(1)}, bf16[1024,256]{1,0:T(8,128)(2,1)}, u32[]{:S(2)}) copy-start(bf16[1024,256]{1,0:T(8,128)(2,1)} %refs_1_.1) | copy-start | bytes 1572868
  18.2 1.8 %collective-permute-start.5 = (bf16[2,4,2,24,256]{4,3,2,1,0:T(8,128)(2,1)S(1)}, bf16[2,4,2,24,256]{4,3,2,1,0:T(8,128)(2,1)S(1)}, u32[]{:S(2)}, u32[]{:S(2)}) collective-permute-start(bf16[2,4,2,24,256]{4,3,2,1,0:T(8,128)(2,1)S(1)} %pad_maximum_fusion.near_ref), channel_id=1, source_target_pairs={{0,1},{1,0},{2,3},{3,2},{4,5},{5,4},{6,7},{7,6},{8,9},{9,8},{10,11... | collective-permute-start | bytes 589832 | tf_op jit(solution)/shard_map/ppermute | solution.py:374
  19.6 4.8 %copy-start.2 = (bf16[1024,256]{1,0:T(8,128)(2,1)S(1)}, bf16[1024,256]{1,0:T(8,128)(2,1)}, u32[]{:S(2)}) copy-start(bf16[1024,256]{1,0:T(8,128)(2,1)} %refs_2_.1) | copy-start | bytes 1572868
  20.8 3.1 %collective-permute-start.7 = (f32[8,128]{1,0:T(8,128)S(1)}, f32[8,128]{1,0:T(8,128)S(1)}, u32[]{:S(2)}, u32[]{:S(2)}) collective-permute-start(f32[8,128]{1,0:T(8,128)S(1)} %get-tuple-element.55), channel_id=1, source_target_pairs={{0,5},{1,4},{2,7},{3,6},{4,1},{5,0},{6,3},{7,2},{8,13},{9,12},{10,... | collective-permute-start | bytes 12296 | tf_op jit(solution)/shard_map/ppermute | solution.py:374
  24.0 2.2 %collective-permute-start.10 = (bf16[1024,256]{1,0:T(8,128)(2,1)S(1)}, bf16[1024,256]{1,0:T(8,128)(2,1)S(1)}, u32[]{:S(2)}, u32[]{:S(2)}) collective-permute-start(bf16[1024,256]{1,0:T(8,128)(2,1)S(1)} %collective-permute-done.8.refs_4_), channel_id=1, source_target_pairs={{0,1},{1,0},{2,3},{3,2},{4,5},{5,4},{6,7},{7,6},{8,9},{9,8},{10,11... | collective-permute-start | bytes 1572872 | tf_op jit(solution)/shard_map/ppermute | solution.py:374
  24.4 4.3 %collective-permute-start.11 = (bf16[1024,256]{1,0:T(8,128)(2,1)S(1)}, bf16[1024,256]{1,0:T(8,128)(2,1)S(1)}, u32[]{:S(2)}, u32[]{:S(2)}) collective-permute-start(bf16[1024,256]{1,0:T(8,128)(2,1)S(1)} %copy-done.2), channel_id=1, source_target_pairs={{0,1},{1,0},{2,3},{3,2},{4,5},{5,4},{6,7},{7,6},{8,9},{9,8},{10,11... | collective-permute-start | bytes 1572872 | tf_op jit(solution)/shard_map/ppermute | solution.py:374
  24.5 3.1 %collective-permute-start.9 = (f32[8,128]{1,0:T(8,128)S(1)}, f32[8,128]{1,0:T(8,128)S(1)}, u32[]{:S(2)}, u32[]{:S(2)}) collective-permute-start(f32[8,128]{1,0:T(8,128)S(1)} %add.9.mine_ref), channel_id=1, source_target_pairs={{0,3},{1,2},{2,1},{3,0},{4,7},{5,6},{6,5},{7,4},{8,11},{9,10},{10,... | collective-permute-start | bytes 12296 | tf_op jit(solution)/shard_map/ppermute | solution.py:374
  28.8 3.1 %collective-permute-start.12 = (f32[8,128]{1,0:T(8,128)S(1)}, f32[8,128]{1,0:T(8,128)S(1)}, u32[]{:S(2)}, u32[]{:S(2)}) collective-permute-start(f32[8,128]{1,0:T(8,128)S(1)} %shard_map.72.mine_ref), channel_id=1, source_target_pairs={{0,5},{1,4},{2,7},{3,6},{4,1},{5,0},{6,3},{7,2},{8,13},{9,12},{10,... | collective-permute-start | bytes 12296 | tf_op jit(solution)/shard_map/ppermute | solution.py:374
  32.8 3.8 %collective-permute-start.13 = (f32[56,256]{1,0:T(8,128)S(1)}, f32[56,256]{1,0:T(8,128)S(1)}, u32[]{:S(2)}, u32[]{:S(2)}) collective-permute-start(f32[56,256]{1,0:T(8,128)S(1)} %get-tuple-element.72), channel_id=1, source_target_pairs={{0,3},{1,2},{2,1},{3,0},{4,7},{5,6},{6,5},{7,4},{8,11},{9,10},{10,... | collective-permute-start | bytes 172040 | tf_op jit(solution)/shard_map/ppermute | solution.py:374
  34.5 4.0 %copy-start.1 = (bf16[1024,256]{1,0:T(8,128)(2,1)S(1)}, bf16[1024,256]{1,0:T(8,128)(2,1)}, u32[]{:S(2)}) copy-start(bf16[1024,256]{1,0:T(8,128)(2,1)} %refs_1_.1) | copy-start | bytes 1572868
  34.5 4.0 %copy-start.3 = (bf16[12,256]{1,0:T(8,128)(2,1)S(1)}, bf16[12,256]{1,0:T(8,128)(2,1)}, u32[]{:S(2)}) copy-start(bf16[12,256]{1,0:T(8,128)(2,1)} %refs_3_.1) | copy-start | bytes 18436
  36.6 3.4 %collective-permute-start.14 = (f32[32,256]{1,0:T(8,128)S(1)}, f32[32,256]{1,0:T(8,128)S(1)}, u32[]{:S(2)}, u32[]{:S(2)}) collective-permute-start(f32[32,256]{1,0:T(8,128)S(1)} %pad_maximum_fusion.2), channel_id=1, source_target_pairs={{0,5},{1,4},{2,7},{3,6},{4,1},{5,0},{6,3},{7,2},{8,13},{9,12},{10,... | collective-permute-start | bytes 98312 | tf_op jit(solution)/shard_map/ppermute | solution.py:374

commit v13 on v12

--- a/solution.py
+++ b/solution.py
@@ -28,7 +28,7 @@
 
 
 def block_of(proto):
-    return (proto & X) + ((proto >> 2) & 1)
+    return 2 * ((proto >> 2) & 1) + ((proto >> 1) & 1)
 
 
 def own_place():
@@ -54,8 +54,8 @@
     start = 0
     for t in dp_order(n_dp):
         count = place_ref[2 + (place_ref[0] ^ t)]
-        for x in range(2):
-            for y in range(2):
+        for y in range(2):
+            for x in range(2):
                 core = parity ^ x ^ y ^ half ^ (1 if t else 0)
                 proto = core + X * x + Y * y
                 end = start + jnp.clip(count - proto * rows, 0, rows)
@@ -87,17 +87,27 @@
     return jnp.where(live, 1.0 / jnp.where(live, total, 1.0), 0.0)
 
 
-def place_rows(place, ref, which, rows, scratch):
-    mine_x, mine_y = (place[1] >> 1) & 1, (place[1] >> 2) & 1
-    start = 0
-    for t in range(ref.shape[1]):
+def pair_kernel(mine_ref, other_ref, out_ref, scratch):
+    rows = mine_ref.shape[0] // 2
+    swapped = (own_place()[1] & X) > 0
+    mine, other = [quick_unit(ref[...])[0] for ref in (mine_ref, other_ref)]
+    pair = (jnp.where(swapped, other, mine), jnp.where(swapped, mine, other))
+    for which in range(2):
         for x in range(2):
-            for y in range(2):
-                block = ref[mine_y ^ y, t, mine_x ^ x].astype(jnp.float32)
-                scratch[start : start + rows, :] = block[which * rows : (which + 1) * rows]
-                start += rows
-    unit, _ = quick_unit(scratch[...])
-    return unit.astype(jnp.bfloat16)
+            start = (2 * which + x) * rows
+            scratch[start : start + rows, :] = pair[x][which * rows : (which + 1) * rows]
+    out_ref[...] = scratch[...].astype(jnp.bfloat16)
+
+
+def place_rows(place, ref, which):
+    mine_y = (place[1] >> 2) & 1
+    pair = ref.shape[2] // 2
+    blocks = [
+        ref[mine_y ^ y, t].astype(jnp.float32)[which * pair : (which + 1) * pair]
+        for t in range(ref.shape[1])
+        for y in range(2)
+    ]
+    return jnp.concatenate(blocks, axis=0).astype(jnp.bfloat16)
 
 
 def scores_of(rows_all, units):
@@ -172,9 +182,8 @@
 
 
 def near_kernel(chunk, near_ref, live_ref, own_units_ref, proto_ref, *refs):
-    weights_ref, sums_ref, rows_ref, units_ref, scratch = refs
-    rows = near_ref.shape[3] // 2
-    rows_near = place_rows(own_place(), near_ref, 0, rows, scratch)
+    weights_ref, sums_ref, rows_ref, units_ref = refs
+    rows_near = place_rows(own_place(), near_ref, 0)
     rows_ref[...] = rows_near
     live = spread(live_ref[...], chunk)
     protos = own_units_ref.shape[0]
@@ -190,9 +199,8 @@
 
 
 def far_kernel(chunk, far_ref, live_ref, near_weights_ref, near_sums_ref, *refs):
-    *unit_refs, weights_ref, rows_ref, sums_ref, scratch, scale_ref, part_ref = refs
-    rows = far_ref.shape[3] // 2
-    rows_far = place_rows(own_place(), far_ref, 0, rows, scratch)
+    *unit_refs, weights_ref, rows_ref, sums_ref, scale_ref, part_ref = refs
+    rows_far = place_rows(own_place(), far_ref, 0)
     rows_ref[...] = rows_far
     live = spread(live_ref[...], chunk)
     protos = unit_refs[0].shape[0]
@@ -209,7 +217,7 @@
 
 def across_kernel(chunk, near_ref, far_ref, *refs):
     near_rows_ref, far_rows_ref, near_live_ref, far_live_ref, *refs = refs
-    *proto_refs, weights_ref, student_ref, scratch = refs
+    *proto_refs, weights_ref, student_ref = refs
     protos = proto_refs[0].shape[0]
     rows_all = jnp.concatenate([near_rows_ref[...], far_rows_ref[...]], axis=0)
     live = spread(jnp.concatenate([near_live_ref[...], far_live_ref[...]], axis=0), chunk)
@@ -220,8 +228,7 @@
             weights_ref[:, at], _ = weights_of(rows_all, units, live)
     half = student_ref.shape[0] // 2
     for k, ref in enumerate((near_ref, far_ref)):
-        rows_half = place_rows(own_place(), ref, 1, ref.shape[3] // 2, scratch)
-        student_ref[k * half : (k + 1) * half, :] = rows_half
+        student_ref[k * half : (k + 1) * half, :] = place_rows(own_place(), ref, 1)
 
 
 def scale_columns(sums, near_ref, far_ref, across_ref, row_ref, scale_ref):
@@ -398,7 +405,6 @@
     place = jnp.concatenate([place, live_count])
     tile = f32((8, LANES))
     message = f32((4 * rows + 8, width))
-    row_scratch = pltpu.VMEM((half, width), jnp.float32)
     column = pltpu.VMEM((all_rows, LANES), jnp.float32)
     scale_row = pltpu.VMEM((8, held), jnp.float32)
     sweep_scratch = [column, pltpu.VMEM((8, 2 * held), jnp.float32), column]
@@ -409,7 +415,12 @@
     across_protos = swap(late_protos, "proto", X_CROSS)
     student_protos = (prototypes, swap(prototypes, "proto", CORE))
     teacher_protos = swap(late_protos, "proto", CORE)
-    near = jnp.stack([both, across_x])
+    near = call(
+        pair_kernel,
+        bf16((4 * rows, width)),
+        (both, across_x),
+        scratch=[pltpu.VMEM((4 * rows, width), jnp.float32)],
+    )
     near = jnp.stack([near] + [swap_dp(near, t) for t in dp_order(n_dp)[1:]])
     near, own_protos = lax.optimization_barrier((near, teacher_prototypes))
     live = f32((half, LANES))
@@ -433,14 +444,13 @@
             bf16((protos, width)),
         ),
         (near, near_live, teacher_units, teacher_protos),
-        scratch=[row_scratch],
         work=held * half,
     )
     far_weights, far_rows, sums = call(
         functools.partial(far_kernel, piece),
         (f32((half, held)), bf16((half, width)), tile),
         (far, far_live, near_weights, near_sums, teacher_units, other_units),
-        scratch=[row_scratch, scale_row, column],
+        scratch=[scale_row, column],
         work=held * half,
     )
     sums = sums + swap(sums, "proto", Y_CROSS)
@@ -459,7 +469,6 @@
             across_protos,
             swap(across_protos, "proto", CORE),
         ),
-        scratch=[row_scratch],
         work=held * all_rows,
     )
     weights = (near_weights, far_weights, across_weights)

time: 41.4 us -> 41.5 us (level)
    pallas_call x10 -> x11, Pallas kernels: 8.43 us -> 8.33 us  [call(): pl.pallas_call(kernel, out_shape=out_shape, in_specs=[pl.BlockSpec(memory...]
  transfers between devices with their start and end apart: 15 -> 15, of which waited for: 9 -> 10; matrix products, arithmetic and copies ran while one was open for 2% -> 2% of each run, Pallas kernels for 16% -> 15%
where the time goes in v13:
time: 41.5 us; the launch traced here: 41.2 us
  starting transfers between devices  20.3 us (49%)
  waiting for transfers between devices  9.3 us (22%)
  Pallas kernels  8.33 us (20%)
  other arithmetic  1.51 us (4%)
  local copies, waits for them, and re-layouts  1.06 us (3%)
  between operations  0.74 us (2%)
    ppermute x12, starting transfers between devices, swap(): return lax.ppermute(values, axis, others)  15.4 us
    pallas_call x11, Pallas kernels, call(): pl.pallas_call(kernel, out_shape=out_shape, in_specs=[pl.BlockSpec(memory...  8.33 us
    ppermute x12, waiting for transfers between devices, swap(): return lax.ppermute(values, axis, others)  7.43 us
    ppermute x3, starting transfers between devices, swap_dp(): return lax.ppermute(values, ('dp', 'proto'), others)  4.93 us
    ppermute x3, waiting for transfers between devices, swap_dp(): return lax.ppermute(values, ('dp', 'proto'), others)  1.87 us
    unnamed x8, local copies, waits for them, and re-layouts  1.05 us
  transfers between devices with their start and end apart: 15, of which 10 were waited for; matrix products, arithmetic and copies ran while one was open for 2% of the time, Pallas kernels for 15%

profile of v13, /device:TPU:0, one launch (start us, length us, event | category | flops | bytes accessed | tf_op | source)
XLA Modules:
  0.0 41.2 jit_solution(11132349058258487456)
XLA Ops:
  1.4 2.4 %collective-permute-start = (bf16[24,256]{1,0:T(8,128)(2,1)S(1)}, bf16[24,256]{1,0:T(8,128)(2,1)S(1)}, u32[]{:S(2)}, u32[]{:S(2)}) collective-permute-start(bf16[24,256]{1,0:T(8,128)(2,1)S(1)} %pad_maximum_fusion.3.mine_ref), channel_id=1, source_target_pairs={{0,3},{1,2},{2,1},{3,0},{4,7},{5,6},{6,5},{7,4},{8,11},{9,10},{10,... | collective-permute-start | bytes 36872 | tf_op jit(solution)/shard_map/ppermute | solution.py:381
  3.8 0.7 %pad_add_fusion.place_ref = s32[6]{0:T(128)S(1)} fusion(s32[4]{0:T(128)} %param.9, s32[1]{0:T(128)} %bitcast.1, s32[1]{0:T(128)} %bitcast), kind=kLoop, calls=%fused_computation.5 | loop fusion | flops 12 | bytes 48 | tf_op jit(solution)/shard_map/concatenate | solution.py:405
  5.3 4.3 %collective-permute-start.1 = (bf16[48,256]{1,0:T(8,128)(2,1)S(1)}, bf16[48,256]{1,0:T(8,128)(2,1)S(1)}, u32[]{:S(2)}, u32[]{:S(2)}) collective-permute-start(bf16[48,256]{1,0:T(8,128)(2,1)S(1)} %shard_map.68), channel_id=1, source_target_pairs={{0,25},{1,24},{2,27},{3,26},{4,29},{5,28},{6,31},{7,30},{8,17},{9,... | collective-permute-start | bytes 73736 | tf_op jit(solution)/shard_map/ppermute | solution.py:389
  10.3 1.5 %collective-permute-start.8 = (bf16[1024,256]{1,0:T(8,128)(2,1)}, bf16[1024,256]{1,0:T(8,128)(2,1)S(1)}, u32[]{:S(2)}, u32[]{:S(2)}) collective-permute-start(bf16[1024,256]{1,0:T(8,128)(2,1)} %refs_1_.1), channel_id=1, source_target_pairs={{0,3},{1,2},{2,1},{3,0},{4,7},{5,6},{6,5},{7,4},{8,11},{9,10},{10,... | collective-permute-start | bytes 1572872 | tf_op jit(solution)/shard_map/ppermute | solution.py:381
  11.8 1.9 %collective-permute-done.2 = bf16[48,256]{1,0:T(8,128)(2,1)S(1)} collective-permute-done((bf16[48,256]{1,0:T(8,128)(2,1)S(1)}, bf16[48,256]{1,0:T(8,128)(2,1)S(1)}, u32[]{:S(2)}, u32[]{:S(2)}) %collective-permute-start.2) | collective-permute-done | bytes 24608 | tf_op jit(solution)/shard_map/ppermute | solution.py:389
  13.7 1.6 %collective-permute-start.4 = (bf16[4,48,256]{2,1,0:T(8,128)(2,1)S(1)}, bf16[4,48,256]{2,1,0:T(8,128)(2,1)S(1)}, u32[]{:S(2)}, u32[]{:S(2)}) collective-permute-start(bf16[4,48,256]{2,1,0:T(8,128)(2,1)S(1)} %pad_maximum_fusion.1), channel_id=1, source_target_pairs={{0,5},{1,4},{2,7},{3,6},{4,1},{5,0},{6,3},{7,2},{8,13},{9,12},{10,... | collective-permute-start | bytes 294920 | tf_op jit(solution)/shard_map/ppermute | solution.py:381
  15.4 1.0 %copy-done = bf16[1024,256]{1,0:T(8,128)(2,1)S(1)} copy-done((bf16[1024,256]{1,0:T(8,128)(2,1)S(1)}, bf16[1024,256]{1,0:T(8,128)(2,1)}, u32[]{:S(2)}) %copy-start) | copy-done | bytes 524312
  16.4 0.8 %shard_map.69 = (bf16[1024,256]{1,0:T(8,128)(2,1)S(1)}, f32[192,128]{1,0:T(8,128)S(1)}, f32[192,128]{1,0:T(8,128)S(1)}) custom-call(s32[6]{0:T(128)S(1)} %pad_add_fusion.place_ref, bf16[1024,256]{1,0:T(8,128)(2,1)S(1)} %copy-done), custom_call_target="tpu_custom_call" | custom-call | flops 134217728 | bytes 1048576 | tf_op jit(solution)/shard_map/pallas_call | solution.py:366
  17.2 1.1 %collective-permute-done.4 = bf16[4,48,256]{2,1,0:T(8,128)(2,1)S(1)} collective-permute-done((bf16[4,48,256]{2,1,0:T(8,128)(2,1)S(1)}, bf16[4,48,256]{2,1,0:T(8,128)(2,1)S(1)}, u32[]{:S(2)}, u32[]{:S(2)}) %collective-permute-start.4) | collective-permute-done | bytes 98336 | tf_op jit(solution)/shard_map/ppermute | solution.py:381
  18.3 0.8 %collective-permute-start.5 = (bf16[2,4,48,256]{3,2,1,0:T(8,128)(2,1)S(1)}, bf16[2,4,48,256]{3,2,1,0:T(8,128)(2,1)S(1)}, u32[]{:S(2)}, u32[]{:S(2)}) collective-permute-start(bf16[2,4,48,256]{3,2,1,0:T(8,128)(2,1)S(1)} %pad_maximum_fusion.near_ref), channel_id=1, source_target_pairs={{0,1},{1,0},{2,3},{3,2},{4,5},{5,4},{6,7},{7,6},{8,9},{9,8},{10,11... | collective-permute-start | bytes 589832 | tf_op jit(solution)/shard_map/ppermute | solution.py:381
  20.2 0.8 %shard_map.71 = (f32[192,2048]{1,0:T(8,128)S(1)}, bf16[192,256]{1,0:T(8,128)(2,1)S(1)}, f32[8,128]{1,0:T(8,128)S(1)}) custom-call(bf16[2,4,48,256]{3,2,1,0:T(8,128)(2,1)S(1)} %collective-permute-done.5.far_ref, f32[192,128]{1,0:T(8,128)S(1)} %get-tuple-element.48.live_ref.refs_3_, f32[192,2048]{1,0:T(8,128)S(1)} %get-tuple-element.52.near_weights_ref.near_ref, ...), custom_call_target="tpu_custom_call" | custom-call | flops 201326592 | bytes 1572864 | tf_op jit(solution)/shard_map/pallas_call | solution.py:366
  21.0 1.6 %collective-permute-start.7 = (f32[8,128]{1,0:T(8,128)S(1)}, f32[8,128]{1,0:T(8,128)S(1)}, u32[]{:S(2)}, u32[]{:S(2)}) collective-permute-start(f32[8,128]{1,0:T(8,128)S(1)} %get-tuple-element.55), channel_id=1, source_target_pairs={{0,5},{1,4},{2,7},{3,6},{4,1},{5,0},{6,3},{7,2},{8,13},{9,12},{10,... | collective-permute-start | bytes 12296 | tf_op jit(solution)/shard_map/ppermute | solution.py:381
  22.5 1.6 %collective-permute-done.7 = f32[8,128]{1,0:T(8,128)S(1)} collective-permute-done((f32[8,128]{1,0:T(8,128)S(1)}, f32[8,128]{1,0:T(8,128)S(1)}, u32[]{:S(2)}, u32[]{:S(2)}) %collective-permute-start.7) | collective-permute-done | bytes 4128 | tf_op jit(solution)/shard_map/ppermute | solution.py:381
  24.7 1.7 %collective-permute-start.9 = (f32[8,128]{1,0:T(8,128)S(1)}, f32[8,128]{1,0:T(8,128)S(1)}, u32[]{:S(2)}, u32[]{:S(2)}) collective-permute-start(f32[8,128]{1,0:T(8,128)S(1)} %add.9.mine_ref), channel_id=1, source_target_pairs={{0,3},{1,2},{2,1},{3,0},{4,7},{5,6},{6,5},{7,4},{8,11},{9,10},{10,... | collective-permute-start | bytes 12296 | tf_op jit(solution)/shard_map/ppermute | solution.py:381
  26.4 0.9 %shard_map.72 = (f32[384,2048]{1,0:T(8,128)S(1)}, bf16[384,256]{1,0:T(8,128)(2,1)S(1)}) custom-call(bf16[2,4,48,256]{3,2,1,0:T(8,128)(2,1)S(1)} %pad_maximum_fusion.near_ref, bf16[2,4,48,256]{3,2,1,0:T(8,128)(2,1)S(1)} %collective-permute-done.5.far_ref, bf16[192,256]{1,0:T(8,128)(2,1)S(1)} %get-tuple-element.58.refs_0_.near_rows_ref, ...), custom_call_target="tpu_custom_call" | custom-call | flops 402653184 | bytes 3145728 | tf_op jit(solution)/shard_map/pallas_call | solution.py:366
  27.7 1.2 %shard_map.73.mine_ref = f32[8,128]{1,0:T(8,128)S(1)} custom-call(f32[8,128]{1,0:T(8,128)S(1)} %add.9.mine_ref, f32[8,128]{1,0:T(8,128)S(1)} %collective-permute-done.9.other_ref, f32[192,2048]{1,0:T(8,128)S(1)} %get-tuple-element.52.near_weights_ref.near_ref, f32[192,2048]{1,0:T(8,128)S(1)} %get-tuple-element.57.far_ref, ...), custom_call_target="tpu_custom_call" | custom-call | flops 402653184 | bytes 3145728 | tf_op jit(solution)/shard_map/pallas_call | solution.py:366
  28.9 1.7 %collective-permute-start.12 = (f32[8,128]{1,0:T(8,128)S(1)}, f32[8,128]{1,0:T(8,128)S(1)}, u32[]{:S(2)}, u32[]{:S(2)}) collective-permute-start(f32[8,128]{1,0:T(8,128)S(1)} %shard_map.73.mine_ref), channel_id=1, source_target_pairs={{0,5},{1,4},{2,7},{3,6},{4,1},{5,0},{6,3},{7,2},{8,13},{9,12},{10,... | collective-permute-start | bytes 12296 | tf_op jit(solution)/shard_map/ppermute | solution.py:381
  30.6 1.1 %shard_map.74 = (bf16[2048,256]{1,0:T(8,128)(2,1)S(1)}, f32[48,256]{1,0:T(8,128)S(1)}, f32[8,128]{1,0:T(8,128)S(1)}) custom-call(bf16[384,256]{1,0:T(8,128)(2,1)S(1)} %get-tuple-element.64.rows_ref.refs_0_.refs_2_, bf16[1024,256]{1,0:T(8,128)(2,1)S(1)} %copy-done.2, bf16[1024,256]{1,0:T(8,128)(2,1)S(1)} %collective-permute-done.11.refs_1_), custom_call_target="tpu_custom_call" | custom-call | flops 402653184 | bytes 3145728 | tf_op jit(solution)/shard_map/pallas_call | solution.py:366
  32.0 0.9 %shard_map.75 = (f32[8,4096]{1,0:T(8,128)S(1)}, f32[56,256]{1,0:T(8,128)S(1)}, f32[56,256]{1,0:T(8,128)S(1)}) custom-call(f32[8,128]{1,0:T(8,128)S(1)} %shard_map.73.mine_ref, f32[8,128]{1,0:T(8,128)S(1)} %collective-permute-done.12.other_ref, f32[192,2048]{1,0:T(8,128)S(1)} %get-tuple-element.52.near_weights_ref.near_ref, ...), custom_call_target="tpu_custom_call" | custom-call | flops 402653184 | bytes 3145728 | tf_op jit(solution)/shard_map/pallas_call | solution.py:366
  32.9 1.7 %collective-permute-start.13 = (f32[56,256]{1,0:T(8,128)S(1)}, f32[56,256]{1,0:T(8,128)S(1)}, u32[]{:S(2)}, u32[]{:S(2)}) collective-permute-start(f32[56,256]{1,0:T(8,128)S(1)} %get-tuple-element.72), channel_id=1, source_target_pairs={{0,3},{1,2},{2,1},{3,0},{4,7},{5,6},{6,5},{7,4},{8,11},{9,10},{10,... | collective-permute-start | bytes 172040 | tf_op jit(solution)/shard_map/ppermute | solution.py:381
  35.2 1.6 %collective-permute-done.13 = f32[56,256]{1,0:T(8,128)S(1)} collective-permute-done((f32[56,256]{1,0:T(8,128)S(1)}, f32[56,256]{1,0:T(8,128)S(1)}, u32[]{:S(2)}, u32[]{:S(2)}) %collective-permute-start.13) | collective-permute-done | bytes 57376 | tf_op jit(solution)/shard_map/ppermute | solution.py:381
  36.8 1.8 %collective-permute-start.14 = (f32[32,256]{1,0:T(8,128)S(1)}, f32[32,256]{1,0:T(8,128)S(1)}, u32[]{:S(2)}, u32[]{:S(2)}) collective-permute-start(f32[32,256]{1,0:T(8,128)S(1)} %pad_maximum_fusion.2), channel_id=1, source_target_pairs={{0,5},{1,4},{2,7},{3,6},{4,1},{5,0},{6,3},{7,2},{8,13},{9,12},{10,... | collective-permute-start | bytes 98312 | tf_op jit(solution)/shard_map/ppermute | solution.py:381
  39.0 1.2 %collective-permute-done.14.other_ref = f32[32,256]{1,0:T(8,128)S(1)} collective-permute-done((f32[32,256]{1,0:T(8,128)S(1)}, f32[32,256]{1,0:T(8,128)S(1)}, u32[]{:S(2)}, u32[]{:S(2)}) %collective-permute-start.14) | collective-permute-done | bytes 32800 | tf_op jit(solution)/shard_map/ppermute | solution.py:381
  40.2 1.0 %shard_map.78 = (f32[12,256]{1,0:T(8,128)}, f32[1,256,256]{2,1,0:T(8,128)}) custom-call(f32[56,256]{1,0:T(8,128)S(1)} %add.10.mine_ref, f32[8,256]{1,0:T(8,128)S(1)} %slice_add_fusion.sums_ref, f32[32,256]{1,0:T(8,128)S(1)} %collective-permute-done.14.other_ref, f32[256,384]{1,0:T(8,128)S(1)} %get-tuple-element.76.targets_ref, ...), custom_call_target="tpu_custom_call" | custom-call | flops 50331648 | bytes 393216 | tf_op jit(solution)/shard_map/pallas_call | solution.py:366
  (34 shorter events, 5.8 us)
Async XLA Ops:
  1.4 3.8 %collective-permute-start = (bf16[24,256]{1,0:T(8,128)(2,1)S(1)}, bf16[24,256]{1,0:T(8,128)(2,1)S(1)}, u32[]{:S(2)}, u32[]{:S(2)}) collective-permute-start(bf16[24,256]{1,0:T(8,128)(2,1)S(1)} %pad_maximum_fusion.3.mine_ref), channel_id=1, source_target_pairs={{0,3},{1,2},{2,1},{3,0},{4,7},{5,6},{6,5},{7,4},{8,11},{9,10},{10,... | collective-permute-start | bytes 36872 | tf_op jit(solution)/shard_map/ppermute | solution.py:381
  5.3 6.5 %collective-permute-start.1 = (bf16[48,256]{1,0:T(8,128)(2,1)S(1)}, bf16[48,256]{1,0:T(8,128)(2,1)S(1)}, u32[]{:S(2)}, u32[]{:S(2)}) collective-permute-start(bf16[48,256]{1,0:T(8,128)(2,1)S(1)} %shard_map.68), channel_id=1, source_target_pairs={{0,25},{1,24},{2,27},{3,26},{4,29},{5,28},{6,31},{7,30},{8,17},{9,... | collective-permute-start | bytes 73736 | tf_op jit(solution)/shard_map/ppermute | solution.py:389
  9.5 4.2 %collective-permute-start.2 = (bf16[48,256]{1,0:T(8,128)(2,1)S(1)}, bf16[48,256]{1,0:T(8,128)(2,1)S(1)}, u32[]{:S(2)}, u32[]{:S(2)}) collective-permute-start(bf16[48,256]{1,0:T(8,128)(2,1)S(1)} %shard_map.68), channel_id=1, source_target_pairs={{0,17},{1,16},{2,19},{3,18},{4,21},{5,20},{6,23},{7,22},{8,25},{9,... | collective-permute-start | bytes 73736 | tf_op jit(solution)/shard_map/ppermute | solution.py:389
  9.5 4.2 %collective-permute-start.3 = (bf16[48,256]{1,0:T(8,128)(2,1)S(1)}, bf16[48,256]{1,0:T(8,128)(2,1)S(1)}, u32[]{:S(2)}, u32[]{:S(2)}) collective-permute-start(bf16[48,256]{1,0:T(8,128)(2,1)S(1)} %shard_map.68), channel_id=1, source_target_pairs={{0,9},{1,8},{2,11},{3,10},{4,13},{5,12},{6,15},{7,14},{8,1},{9,0},... | collective-permute-start | bytes 73736 | tf_op jit(solution)/shard_map/ppermute | solution.py:389
  10.2 8.9 %collective-permute-start.6 = (bf16[1024,256]{1,0:T(8,128)(2,1)}, bf16[1024,256]{1,0:T(8,128)(2,1)S(1)}, u32[]{:S(2)}, u32[]{:S(2)}) collective-permute-start(bf16[1024,256]{1,0:T(8,128)(2,1)} %refs_1_.1), channel_id=1, source_target_pairs={{0,1},{1,0},{2,3},{3,2},{4,5},{5,4},{6,7},{7,6},{8,9},{9,8},{10,11... | collective-permute-start | bytes 1572872 | tf_op jit(solution)/shard_map/ppermute | solution.py:381
  10.3 13.9 %collective-permute-start.8 = (bf16[1024,256]{1,0:T(8,128)(2,1)}, bf16[1024,256]{1,0:T(8,128)(2,1)S(1)}, u32[]{:S(2)}, u32[]{:S(2)}) collective-permute-start(bf16[1024,256]{1,0:T(8,128)(2,1)} %refs_1_.1), channel_id=1, source_target_pairs={{0,3},{1,2},{2,1},{3,0},{4,7},{5,6},{6,5},{7,4},{8,11},{9,10},{10,... | collective-permute-start | bytes 1572872 | tf_op jit(solution)/shard_map/ppermute | solution.py:381
  13.7 4.6 %collective-permute-start.4 = (bf16[4,48,256]{2,1,0:T(8,128)(2,1)S(1)}, bf16[4,48,256]{2,1,0:T(8,128)(2,1)S(1)}, u32[]{:S(2)}, u32[]{:S(2)}) collective-permute-start(bf16[4,48,256]{2,1,0:T(8,128)(2,1)S(1)} %pad_maximum_fusion.1), channel_id=1, source_target_pairs={{0,5},{1,4},{2,7},{3,6},{4,1},{5,0},{6,3},{7,2},{8,13},{9,12},{10,... | collective-permute-start | bytes 294920 | tf_op jit(solution)/shard_map/ppermute | solution.py:381
  15.4 1.0 %copy-start = (bf16[1024,256]{1,0:T(8,128)(2,1)S(1)}, bf16[1024,256]{1,0:T(8,128)(2,1)}, u32[]{:S(2)}) copy-start(bf16[1024,256]{1,0:T(8,128)(2,1)} %refs_1_.1) | copy-start | bytes 1572868
  18.3 1.8 %collective-permute-start.5 = (bf16[2,4,48,256]{3,2,1,0:T(8,128)(2,1)S(1)}, bf16[2,4,48,256]{3,2,1,0:T(8,128)(2,1)S(1)}, u32[]{:S(2)}, u32[]{:S(2)}) collective-permute-start(bf16[2,4,48,256]{3,2,1,0:T(8,128)(2,1)S(1)} %pad_maximum_fusion.near_ref), channel_id=1, source_target_pairs={{0,1},{1,0},{2,3},{3,2},{4,5},{5,4},{6,7},{7,6},{8,9},{9,8},{10,11... | collective-permute-start | bytes 589832 | tf_op jit(solution)/shard_map/ppermute | solution.py:381
  19.7 4.9 %copy-start.2 = (bf16[1024,256]{1,0:T(8,128)(2,1)S(1)}, bf16[1024,256]{1,0:T(8,128)(2,1)}, u32[]{:S(2)}) copy-start(bf16[1024,256]{1,0:T(8,128)(2,1)} %refs_2_.1) | copy-start | bytes 1572868
  21.0 3.1 %collective-permute-start.7 = (f32[8,128]{1,0:T(8,128)S(1)}, f32[8,128]{1,0:T(8,128)S(1)}, u32[]{:S(2)}, u32[]{:S(2)}) collective-permute-start(f32[8,128]{1,0:T(8,128)S(1)} %get-tuple-element.55), channel_id=1, source_target_pairs={{0,5},{1,4},{2,7},{3,6},{4,1},{5,0},{6,3},{7,2},{8,13},{9,12},{10,... | collective-permute-start | bytes 12296 | tf_op jit(solution)/shard_map/ppermute | solution.py:381
  24.2 2.2 %collective-permute-start.10 = (bf16[1024,256]{1,0:T(8,128)(2,1)S(1)}, bf16[1024,256]{1,0:T(8,128)(2,1)S(1)}, u32[]{:S(2)}, u32[]{:S(2)}) collective-permute-start(bf16[1024,256]{1,0:T(8,128)(2,1)S(1)} %collective-permute-done.8.refs_4_), channel_id=1, source_target_pairs={{0,1},{1,0},{2,3},{3,2},{4,5},{5,4},{6,7},{7,6},{8,9},{9,8},{10,11... | collective-permute-start | bytes 1572872 | tf_op jit(solution)/shard_map/ppermute | solution.py:381
  24.6 4.3 %collective-permute-start.11 = (bf16[1024,256]{1,0:T(8,128)(2,1)S(1)}, bf16[1024,256]{1,0:T(8,128)(2,1)S(1)}, u32[]{:S(2)}, u32[]{:S(2)}) collective-permute-start(bf16[1024,256]{1,0:T(8,128)(2,1)S(1)} %copy-done.2), channel_id=1, source_target_pairs={{0,1},{1,0},{2,3},{3,2},{4,5},{5,4},{6,7},{7,6},{8,9},{9,8},{10,11... | collective-permute-start | bytes 1572872 | tf_op jit(solution)/shard_map/ppermute | solution.py:381
  24.7 3.1 %collective-permute-start.9 = (f32[8,128]{1,0:T(8,128)S(1)}, f32[8,128]{1,0:T(8,128)S(1)}, u32[]{:S(2)}, u32[]{:S(2)}) collective-permute-start(f32[8,128]{1,0:T(8,128)S(1)} %add.9.mine_ref), channel_id=1, source_target_pairs={{0,3},{1,2},{2,1},{3,0},{4,7},{5,6},{6,5},{7,4},{8,11},{9,10},{10,... | collective-permute-start | bytes 12296 | tf_op jit(solution)/shard_map/ppermute | solution.py:381
  28.9 3.1 %collective-permute-start.12 = (f32[8,128]{1,0:T(8,128)S(1)}, f32[8,128]{1,0:T(8,128)S(1)}, u32[]{:S(2)}, u32[]{:S(2)}) collective-permute-start(f32[8,128]{1,0:T(8,128)S(1)} %shard_map.73.mine_ref), channel_id=1, source_target_pairs={{0,5},{1,4},{2,7},{3,6},{4,1},{5,0},{6,3},{7,2},{8,13},{9,12},{10,... | collective-permute-start | bytes 12296 | tf_op jit(solution)/shard_map/ppermute | solution.py:381
  32.9 3.8 %collective-permute-start.13 = (f32[56,256]{1,0:T(8,128)S(1)}, f32[56,256]{1,0:T(8,128)S(1)}, u32[]{:S(2)}, u32[]{:S(2)}) collective-permute-start(f32[56,256]{1,0:T(8,128)S(1)} %get-tuple-element.72), channel_id=1, source_target_pairs={{0,3},{1,2},{2,1},{3,0},{4,7},{5,6},{6,5},{7,4},{8,11},{9,10},{10,... | collective-permute-start | bytes 172040 | tf_op jit(solution)/shard_map/ppermute | solution.py:381
  34.6 4.0 %copy-start.1 = (bf16[1024,256]{1,0:T(8,128)(2,1)S(1)}, bf16[1024,256]{1,0:T(8,128)(2,1)}, u32[]{:S(2)}) copy-start(bf16[1024,256]{1,0:T(8,128)(2,1)} %refs_1_.1) | copy-start | bytes 1572868
  34.6 4.0 %copy-start.3 = (bf16[12,256]{1,0:T(8,128)(2,1)S(1)}, bf16[12,256]{1,0:T(8,128)(2,1)}, u32[]{:S(2)}) copy-start(bf16[12,256]{1,0:T(8,128)(2,1)} %refs_3_.1) | copy-start | bytes 18436
  36.8 3.4 %collective-permute-start.14 = (f32[32,256]{1,0:T(8,128)S(1)}, f32[32,256]{1,0:T(8,128)S(1)}, u32[]{:S(2)}, u32[]{:S(2)}) collective-permute-start(f32[32,256]{1,0:T(8,128)S(1)} %pad_maximum_fusion.2), channel_id=1, source_target_pairs={{0,5},{1,4},{2,7},{3,6},{4,1},{5,0},{6,3},{7,2},{8,13},{9,12},{10,... | collective-permute-start | bytes 98312 | tf_op jit(solution)/shard_map/ppermute | solution.py:381

commit v14 on v12

--- a/solution.py
+++ b/solution.py
@@ -114,9 +114,10 @@
     return jnp.concatenate([column] * (lanes // LANES), axis=1)
 
 
-def weighted_rows(panels, left, scale_ref, part_ref, add=False):
+def weighted_rows(panels, scale_ref, part_ref, across_ref=None):
     tiles = panels[0].shape[1] // LANES
-    scales = [scale_ref[:, left + k * LANES : left + (k + 1) * LANES] for k in range(tiles)]
+    count = tiles if across_ref is None else 2 * tiles
+    scales = [scale_ref[:, k * LANES : (k + 1) * LANES] for k in range(count)]
     top = 0
     for ref in panels:
 
@@ -124,11 +125,13 @@
             at = pl.ds(pl.multiple_of(i * 8, 8), 8)
             to = pl.ds(pl.multiple_of(i * 8 + top, 8), 8)
             sums = [None] * 4
-            for k in range(tiles):
-                term = ref[at, k * LANES : (k + 1) * LANES] * scales[k]
+            for k in range(count):
+                own = k < tiles
+                j = k if own else k - tiles
+                lanes = slice(j * LANES, (j + 1) * LANES)
+                term = (ref[at, lanes] if own else across_ref[to, lanes]) * scales[k]
                 sums[k % 4] = term if sums[k % 4] is None else sums[k % 4] + term
-            total = (sums[0] + sums[1]) + (sums[2] + sums[3])
-            part_ref[to, :] = part_ref[to, :] + total if add else total
+            part_ref[to, :] = (sums[0] + sums[1]) + (sums[2] + sums[3])
             return 0
 
         lax.fori_loop(0, ref.shape[0] // 8, body, 0, unroll=24)
@@ -203,7 +206,7 @@
             weights_ref[:, at] = weights
             inverse = 1.0 / jnp.sum(near_sums_ref[:, at] + sums, axis=0, keepdims=True)
             scale_ref[:, at] = jnp.broadcast_to(inverse, (8, chunk))
-    weighted_rows([near_weights_ref, weights_ref], 0, scale_ref, part_ref)
+    weighted_rows([near_weights_ref, weights_ref], scale_ref, part_ref)
     sums_ref[...] = as_tile(part_ref[...])
 
 
@@ -231,8 +234,7 @@
 
 
 def next_sums(near_ref, far_ref, across_ref, scale_ref, part_ref):
-    weighted_rows([near_ref, far_ref], 0, scale_ref, part_ref)
-    weighted_rows([across_ref], near_ref.shape[1], scale_ref, part_ref, add=True)
+    weighted_rows([near_ref, far_ref], scale_ref, part_ref, across_ref)
     return as_tile(part_ref[...])
 
 

time: 41.4 us -> 41.3 us (level)
  no operation moved by 1% of the time
where the time goes in v14:
time: 41.3 us; the launch traced here: 41 us
  starting transfers between devices  20.2 us (49%)
  waiting for transfers between devices  9.18 us (22%)
  Pallas kernels  8.32 us (20%)
  other arithmetic  1.52 us (4%)
  local copies, waits for them, and re-layouts  1.06 us (3%)
  between operations  0.74 us (2%)
    ppermute x12, starting transfers between devices, swap(): return lax.ppermute(values, axis, others)  15.4 us
    pallas_call x10, Pallas kernels, call(): pl.pallas_call(kernel, out_shape=out_shape, in_specs=[pl.BlockSpec(memory...  8.32 us
    ppermute x12, waiting for transfers between devices, swap(): return lax.ppermute(values, axis, others)  7.3 us
    ppermute x3, starting transfers between devices, swap_dp(): return lax.ppermute(values, ('dp', 'proto'), others)  4.86 us
    ppermute x3, waiting for transfers between devices, swap_dp(): return lax.ppermute(values, ('dp', 'proto'), others)  1.87 us
    unnamed x8, local copies, waits for them, and re-layouts  1.05 us
  transfers between devices with their start and end apart: 15, of which 9 were waited for; matrix products, arithmetic and copies ran while one was open for 2% of the time, Pallas kernels for 16%

profile of v14, /device:TPU:0, one launch (start us, length us, event | category | flops | bytes accessed | tf_op | source)
XLA Modules:
  0.0 41.0 jit_solution(16867540559156502920)
XLA Ops:
  1.4 2.4 %collective-permute-start = (bf16[24,256]{1,0:T(8,128)(2,1)S(1)}, bf16[24,256]{1,0:T(8,128)(2,1)S(1)}, u32[]{:S(2)}, u32[]{:S(2)}) collective-permute-start(bf16[24,256]{1,0:T(8,128)(2,1)S(1)} %pad_maximum_fusion.4), channel_id=1, source_target_pairs={{0,3},{1,2},{2,1},{3,0},{4,7},{5,6},{6,5},{7,4},{8,11},{9,10},{10,... | collective-permute-start | bytes 36872 | tf_op jit(solution)/shard_map/ppermute | solution.py:376
  3.8 0.7 %pad_add_fusion.place_ref = s32[6]{0:T(128)S(1)} fusion(s32[4]{0:T(128)} %param.9, s32[1]{0:T(128)} %bitcast.2, s32[1]{0:T(128)} %bitcast.1), kind=kLoop, calls=%fused_computation.6 | loop fusion | flops 12 | bytes 48 | tf_op jit(solution)/shard_map/concatenate | solution.py:400
  5.2 4.2 %collective-permute-start.1 = (bf16[2,24,256]{2,1,0:T(8,128)(2,1)S(1)}, bf16[2,24,256]{2,1,0:T(8,128)(2,1)S(1)}, u32[]{:S(2)}, u32[]{:S(2)}) collective-permute-start(bf16[2,24,256]{2,1,0:T(8,128)(2,1)S(1)} %get-tuple-element.83), channel_id=1, source_target_pairs={{0,25},{1,24},{2,27},{3,26},{4,29},{5,28},{6,31},{7,30},{8,17},{9,... | collective-permute-start | bytes 73736 | tf_op jit(solution)/shard_map/ppermute | solution.py:384
  10.1 1.5 %collective-permute-start.8 = (bf16[1024,256]{1,0:T(8,128)(2,1)}, bf16[1024,256]{1,0:T(8,128)(2,1)S(1)}, u32[]{:S(2)}, u32[]{:S(2)}) collective-permute-start(bf16[1024,256]{1,0:T(8,128)(2,1)} %refs_1_.1), channel_id=1, source_target_pairs={{0,3},{1,2},{2,1},{3,0},{4,7},{5,6},{6,5},{7,4},{8,11},{9,10},{10,... | collective-permute-start | bytes 1572872 | tf_op jit(solution)/shard_map/ppermute | solution.py:376
  11.7 1.9 %collective-permute-done.2 = bf16[2,24,256]{2,1,0:T(8,128)(2,1)S(1)} collective-permute-done((bf16[2,24,256]{2,1,0:T(8,128)(2,1)S(1)}, bf16[2,24,256]{2,1,0:T(8,128)(2,1)S(1)}, u32[]{:S(2)}, u32[]{:S(2)}) %collective-permute-start.2) | collective-permute-done | bytes 24608 | tf_op jit(solution)/shard_map/ppermute | solution.py:384
  13.6 1.6 %collective-permute-start.4 = (bf16[4,2,24,256]{3,2,1,0:T(8,128)(2,1)S(1)}, bf16[4,2,24,256]{3,2,1,0:T(8,128)(2,1)S(1)}, u32[]{:S(2)}, u32[]{:S(2)}) collective-permute-start(bf16[4,2,24,256]{3,2,1,0:T(8,128)(2,1)S(1)} %pad_maximum_fusion.1), channel_id=1, source_target_pairs={{0,5},{1,4},{2,7},{3,6},{4,1},{5,0},{6,3},{7,2},{8,13},{9,12},{10,... | collective-permute-start | bytes 294920 | tf_op jit(solution)/shard_map/ppermute | solution.py:376
  15.2 1.0 %copy-done = bf16[1024,256]{1,0:T(8,128)(2,1)S(1)} copy-done((bf16[1024,256]{1,0:T(8,128)(2,1)S(1)}, bf16[1024,256]{1,0:T(8,128)(2,1)}, u32[]{:S(2)}) %copy-start) | copy-done | bytes 524312
  16.2 0.8 %shard_map.68 = (bf16[1024,256]{1,0:T(8,128)(2,1)S(1)}, f32[192,128]{1,0:T(8,128)S(1)}, f32[192,128]{1,0:T(8,128)S(1)}) custom-call(s32[6]{0:T(128)S(1)} %pad_add_fusion.place_ref, bf16[1024,256]{1,0:T(8,128)(2,1)S(1)} %copy-done), custom_call_target="tpu_custom_call" | custom-call | flops 134217728 | bytes 1048576 | tf_op jit(solution)/shard_map/pallas_call | solution.py:361
  17.0 1.1 %collective-permute-done.4 = bf16[4,2,24,256]{3,2,1,0:T(8,128)(2,1)S(1)} collective-permute-done((bf16[4,2,24,256]{3,2,1,0:T(8,128)(2,1)S(1)}, bf16[4,2,24,256]{3,2,1,0:T(8,128)(2,1)S(1)}, u32[]{:S(2)}, u32[]{:S(2)}) %collective-permute-start.4) | collective-permute-done | bytes 98336 | tf_op jit(solution)/shard_map/ppermute | solution.py:376
  18.2 0.8 %collective-permute-start.5 = (bf16[2,4,2,24,256]{4,3,2,1,0:T(8,128)(2,1)S(1)}, bf16[2,4,2,24,256]{4,3,2,1,0:T(8,128)(2,1)S(1)}, u32[]{:S(2)}, u32[]{:S(2)}) collective-permute-start(bf16[2,4,2,24,256]{4,3,2,1,0:T(8,128)(2,1)S(1)} %pad_maximum_fusion.near_ref), channel_id=1, source_target_pairs={{0,1},{1,0},{2,3},{3,2},{4,5},{5,4},{6,7},{7,6},{8,9},{9,8},{10,11... | collective-permute-start | bytes 589832 | tf_op jit(solution)/shard_map/ppermute | solution.py:376
  20.0 0.9 %shard_map.70 = (f32[192,2048]{1,0:T(8,128)S(1)}, bf16[192,256]{1,0:T(8,128)(2,1)S(1)}, f32[8,128]{1,0:T(8,128)S(1)}) custom-call(bf16[2,4,2,24,256]{4,3,2,1,0:T(8,128)(2,1)S(1)} %collective-permute-done.5.far_ref, f32[192,128]{1,0:T(8,128)S(1)} %get-tuple-element.48.live_ref.refs_3_, f32[192,2048]{1,0:T(8,128)S(1)} %get-tuple-element.52.near_weights_ref.near_ref, ...), custom_call_target="tpu_custom_call" | custom-call | flops 201326592 | bytes 1572864 | tf_op jit(solution)/shard_map/pallas_call | solution.py:361
  20.8 1.6 %collective-permute-start.7 = (f32[8,128]{1,0:T(8,128)S(1)}, f32[8,128]{1,0:T(8,128)S(1)}, u32[]{:S(2)}, u32[]{:S(2)}) collective-permute-start(f32[8,128]{1,0:T(8,128)S(1)} %get-tuple-element.55), channel_id=1, source_target_pairs={{0,5},{1,4},{2,7},{3,6},{4,1},{5,0},{6,3},{7,2},{8,13},{9,12},{10,... | collective-permute-start | bytes 12296 | tf_op jit(solution)/shard_map/ppermute | solution.py:376
  22.4 1.6 %collective-permute-done.7 = f32[8,128]{1,0:T(8,128)S(1)} collective-permute-done((f32[8,128]{1,0:T(8,128)S(1)}, f32[8,128]{1,0:T(8,128)S(1)}, u32[]{:S(2)}, u32[]{:S(2)}) %collective-permute-start.7) | collective-permute-done | bytes 4128 | tf_op jit(solution)/shard_map/ppermute | solution.py:376
  24.5 1.7 %collective-permute-start.9 = (f32[8,128]{1,0:T(8,128)S(1)}, f32[8,128]{1,0:T(8,128)S(1)}, u32[]{:S(2)}, u32[]{:S(2)}) collective-permute-start(f32[8,128]{1,0:T(8,128)S(1)} %add.9.mine_ref), channel_id=1, source_target_pairs={{0,3},{1,2},{2,1},{3,0},{4,7},{5,6},{6,5},{7,4},{8,11},{9,10},{10,... | collective-permute-start | bytes 12296 | tf_op jit(solution)/shard_map/ppermute | solution.py:376
  26.2 1.0 %shard_map.71 = (f32[384,2048]{1,0:T(8,128)S(1)}, bf16[384,256]{1,0:T(8,128)(2,1)S(1)}) custom-call(bf16[2,4,2,24,256]{4,3,2,1,0:T(8,128)(2,1)S(1)} %pad_maximum_fusion.near_ref, bf16[2,4,2,24,256]{4,3,2,1,0:T(8,128)(2,1)S(1)} %collective-permute-done.5.far_ref, bf16[192,256]{1,0:T(8,128)(2,1)S(1)} %get-tuple-element.58.refs_0_.near_rows_ref, ...), custom_call_target="tpu_custom_call" | custom-call | flops 402653184 | bytes 3145728 | tf_op jit(solution)/shard_map/pallas_call | solution.py:361
  27.6 1.1 %shard_map.72.mine_ref = f32[8,128]{1,0:T(8,128)S(1)} custom-call(f32[8,128]{1,0:T(8,128)S(1)} %add.9.mine_ref, f32[8,128]{1,0:T(8,128)S(1)} %collective-permute-done.9.other_ref, f32[192,2048]{1,0:T(8,128)S(1)} %get-tuple-element.52.near_weights_ref.near_ref, f32[192,2048]{1,0:T(8,128)S(1)} %get-tuple-element.57.far_ref, ...), custom_call_target="tpu_custom_call" | custom-call | flops 402653184 | bytes 3145728 | tf_op jit(solution)/shard_map/pallas_call | solution.py:361
  28.7 1.7 %collective-permute-start.12 = (f32[8,128]{1,0:T(8,128)S(1)}, f32[8,128]{1,0:T(8,128)S(1)}, u32[]{:S(2)}, u32[]{:S(2)}) collective-permute-start(f32[8,128]{1,0:T(8,128)S(1)} %shard_map.72.mine_ref), channel_id=1, source_target_pairs={{0,5},{1,4},{2,7},{3,6},{4,1},{5,0},{6,3},{7,2},{8,13},{9,12},{10,... | collective-permute-start | bytes 12296 | tf_op jit(solution)/shard_map/ppermute | solution.py:376
  30.4 1.1 %shard_map.73 = (bf16[2048,256]{1,0:T(8,128)(2,1)S(1)}, f32[48,256]{1,0:T(8,128)S(1)}, f32[8,128]{1,0:T(8,128)S(1)}) custom-call(bf16[384,256]{1,0:T(8,128)(2,1)S(1)} %get-tuple-element.64.rows_ref.refs_0_.refs_2_, bf16[1024,256]{1,0:T(8,128)(2,1)S(1)} %copy-done.2, bf16[1024,256]{1,0:T(8,128)(2,1)S(1)} %collective-permute-done.11.refs_1_), custom_call_target="tpu_custom_call" | custom-call | flops 402653184 | bytes 3145728 | tf_op jit(solution)/shard_map/pallas_call | solution.py:361
  31.8 0.9 %shard_map.74 = (f32[8,4096]{1,0:T(8,128)S(1)}, f32[56,256]{1,0:T(8,128)S(1)}, f32[56,256]{1,0:T(8,128)S(1)}) custom-call(f32[8,128]{1,0:T(8,128)S(1)} %shard_map.72.mine_ref, f32[8,128]{1,0:T(8,128)S(1)} %collective-permute-done.12.other_ref, f32[192,2048]{1,0:T(8,128)S(1)} %get-tuple-element.52.near_weights_ref.near_ref, ...), custom_call_target="tpu_custom_call" | custom-call | flops 402653184 | bytes 3145728 | tf_op jit(solution)/shard_map/pallas_call | solution.py:361
  32.7 1.7 %collective-permute-start.13 = (f32[56,256]{1,0:T(8,128)S(1)}, f32[56,256]{1,0:T(8,128)S(1)}, u32[]{:S(2)}, u32[]{:S(2)}) collective-permute-start(f32[56,256]{1,0:T(8,128)S(1)} %get-tuple-element.72), channel_id=1, source_target_pairs={{0,3},{1,2},{2,1},{3,0},{4,7},{5,6},{6,5},{7,4},{8,11},{9,10},{10,... | collective-permute-start | bytes 172040 | tf_op jit(solution)/shard_map/ppermute | solution.py:376
  34.9 1.6 %collective-permute-done.13 = f32[56,256]{1,0:T(8,128)S(1)} collective-permute-done((f32[56,256]{1,0:T(8,128)S(1)}, f32[56,256]{1,0:T(8,128)S(1)}, u32[]{:S(2)}, u32[]{:S(2)}) %collective-permute-start.13) | collective-permute-done | bytes 57376 | tf_op jit(solution)/shard_map/ppermute | solution.py:376
  36.6 1.8 %collective-permute-start.14 = (f32[32,256]{1,0:T(8,128)S(1)}, f32[32,256]{1,0:T(8,128)S(1)}, u32[]{:S(2)}, u32[]{:S(2)}) collective-permute-start(f32[32,256]{1,0:T(8,128)S(1)} %pad_maximum_fusion.2), channel_id=1, source_target_pairs={{0,5},{1,4},{2,7},{3,6},{4,1},{5,0},{6,3},{7,2},{8,13},{9,12},{10,... | collective-permute-start | bytes 98312 | tf_op jit(solution)/shard_map/ppermute | solution.py:376
  38.8 1.2 %collective-permute-done.14.other_ref = f32[32,256]{1,0:T(8,128)S(1)} collective-permute-done((f32[32,256]{1,0:T(8,128)S(1)}, f32[32,256]{1,0:T(8,128)S(1)}, u32[]{:S(2)}, u32[]{:S(2)}) %collective-permute-start.14) | collective-permute-done | bytes 32800 | tf_op jit(solution)/shard_map/ppermute | solution.py:376
  40.0 1.0 %shard_map.77 = (f32[12,256]{1,0:T(8,128)}, f32[1,256,256]{2,1,0:T(8,128)}) custom-call(f32[56,256]{1,0:T(8,128)S(1)} %add.10.mine_ref, f32[8,256]{1,0:T(8,128)S(1)} %slice_add_fusion.sums_ref, f32[32,256]{1,0:T(8,128)S(1)} %collective-permute-done.14.other_ref, f32[256,384]{1,0:T(8,128)S(1)} %get-tuple-element.76.targets_ref, ...), custom_call_target="tpu_custom_call" | custom-call | flops 50331648 | bytes 393216 | tf_op jit(solution)/shard_map/pallas_call | solution.py:361
  (34 shorter events, 5.4 us)
Async XLA Ops:
  1.4 3.8 %collective-permute-start = (bf16[24,256]{1,0:T(8,128)(2,1)S(1)}, bf16[24,256]{1,0:T(8,128)(2,1)S(1)}, u32[]{:S(2)}, u32[]{:S(2)}) collective-permute-start(bf16[24,256]{1,0:T(8,128)(2,1)S(1)} %pad_maximum_fusion.4), channel_id=1, source_target_pairs={{0,3},{1,2},{2,1},{3,0},{4,7},{5,6},{6,5},{7,4},{8,11},{9,10},{10,... | collective-permute-start | bytes 36872 | tf_op jit(solution)/shard_map/ppermute | solution.py:376
  5.2 6.5 %collective-permute-start.1 = (bf16[2,24,256]{2,1,0:T(8,128)(2,1)S(1)}, bf16[2,24,256]{2,1,0:T(8,128)(2,1)S(1)}, u32[]{:S(2)}, u32[]{:S(2)}) collective-permute-start(bf16[2,24,256]{2,1,0:T(8,128)(2,1)S(1)} %get-tuple-element.83), channel_id=1, source_target_pairs={{0,25},{1,24},{2,27},{3,26},{4,29},{5,28},{6,31},{7,30},{8,17},{9,... | collective-permute-start | bytes 73736 | tf_op jit(solution)/shard_map/ppermute | solution.py:384
  9.4 4.2 %collective-permute-start.2 = (bf16[2,24,256]{2,1,0:T(8,128)(2,1)S(1)}, bf16[2,24,256]{2,1,0:T(8,128)(2,1)S(1)}, u32[]{:S(2)}, u32[]{:S(2)}) collective-permute-start(bf16[2,24,256]{2,1,0:T(8,128)(2,1)S(1)} %get-tuple-element.83), channel_id=1, source_target_pairs={{0,17},{1,16},{2,19},{3,18},{4,21},{5,20},{6,23},{7,22},{8,25},{9,... | collective-permute-start | bytes 73736 | tf_op jit(solution)/shard_map/ppermute | solution.py:384
  9.4 4.2 %collective-permute-start.3 = (bf16[2,24,256]{2,1,0:T(8,128)(2,1)S(1)}, bf16[2,24,256]{2,1,0:T(8,128)(2,1)S(1)}, u32[]{:S(2)}, u32[]{:S(2)}) collective-permute-start(bf16[2,24,256]{2,1,0:T(8,128)(2,1)S(1)} %get-tuple-element.83), channel_id=1, source_target_pairs={{0,9},{1,8},{2,11},{3,10},{4,13},{5,12},{6,15},{7,14},{8,1},{9,0},... | collective-permute-start | bytes 73736 | tf_op jit(solution)/shard_map/ppermute | solution.py:384
  10.1 8.9 %collective-permute-start.6 = (bf16[1024,256]{1,0:T(8,128)(2,1)}, bf16[1024,256]{1,0:T(8,128)(2,1)S(1)}, u32[]{:S(2)}, u32[]{:S(2)}) collective-permute-start(bf16[1024,256]{1,0:T(8,128)(2,1)} %refs_1_.1), channel_id=1, source_target_pairs={{0,1},{1,0},{2,3},{3,2},{4,5},{5,4},{6,7},{7,6},{8,9},{9,8},{10,11... | collective-permute-start | bytes 1572872 | tf_op jit(solution)/shard_map/ppermute | solution.py:376
  10.1 13.9 %collective-permute-start.8 = (bf16[1024,256]{1,0:T(8,128)(2,1)}, bf16[1024,256]{1,0:T(8,128)(2,1)S(1)}, u32[]{:S(2)}, u32[]{:S(2)}) collective-permute-start(bf16[1024,256]{1,0:T(8,128)(2,1)} %refs_1_.1), channel_id=1, source_target_pairs={{0,3},{1,2},{2,1},{3,0},{4,7},{5,6},{6,5},{7,4},{8,11},{9,10},{10,... | collective-permute-start | bytes 1572872 | tf_op jit(solution)/shard_map/ppermute | solution.py:376
  13.6 4.6 %collective-permute-start.4 = (bf16[4,2,24,256]{3,2,1,0:T(8,128)(2,1)S(1)}, bf16[4,2,24,256]{3,2,1,0:T(8,128)(2,1)S(1)}, u32[]{:S(2)}, u32[]{:S(2)}) collective-permute-start(bf16[4,2,24,256]{3,2,1,0:T(8,128)(2,1)S(1)} %pad_maximum_fusion.1), channel_id=1, source_target_pairs={{0,5},{1,4},{2,7},{3,6},{4,1},{5,0},{6,3},{7,2},{8,13},{9,12},{10,... | collective-permute-start | bytes 294920 | tf_op jit(solution)/shard_map/ppermute | solution.py:376
  15.2 1.0 %copy-start = (bf16[1024,256]{1,0:T(8,128)(2,1)S(1)}, bf16[1024,256]{1,0:T(8,128)(2,1)}, u32[]{:S(2)}) copy-start(bf16[1024,256]{1,0:T(8,128)(2,1)} %refs_1_.1) | copy-start | bytes 1572868
  18.2 1.8 %collective-permute-start.5 = (bf16[2,4,2,24,256]{4,3,2,1,0:T(8,128)(2,1)S(1)}, bf16[2,4,2,24,256]{4,3,2,1,0:T(8,128)(2,1)S(1)}, u32[]{:S(2)}, u32[]{:S(2)}) collective-permute-start(bf16[2,4,2,24,256]{4,3,2,1,0:T(8,128)(2,1)S(1)} %pad_maximum_fusion.near_ref), channel_id=1, source_target_pairs={{0,1},{1,0},{2,3},{3,2},{4,5},{5,4},{6,7},{7,6},{8,9},{9,8},{10,11... | collective-permute-start | bytes 589832 | tf_op jit(solution)/shard_map/ppermute | solution.py:376
  19.6 4.8 %copy-start.2 = (bf16[1024,256]{1,0:T(8,128)(2,1)S(1)}, bf16[1024,256]{1,0:T(8,128)(2,1)}, u32[]{:S(2)}) copy-start(bf16[1024,256]{1,0:T(8,128)(2,1)} %refs_2_.1) | copy-start | bytes 1572868
  20.8 3.1 %collective-permute-start.7 = (f32[8,128]{1,0:T(8,128)S(1)}, f32[8,128]{1,0:T(8,128)S(1)}, u32[]{:S(2)}, u32[]{:S(2)}) collective-permute-start(f32[8,128]{1,0:T(8,128)S(1)} %get-tuple-element.55), channel_id=1, source_target_pairs={{0,5},{1,4},{2,7},{3,6},{4,1},{5,0},{6,3},{7,2},{8,13},{9,12},{10,... | collective-permute-start | bytes 12296 | tf_op jit(solution)/shard_map/ppermute | solution.py:376
  24.0 2.2 %collective-permute-start.10 = (bf16[1024,256]{1,0:T(8,128)(2,1)S(1)}, bf16[1024,256]{1,0:T(8,128)(2,1)S(1)}, u32[]{:S(2)}, u32[]{:S(2)}) collective-permute-start(bf16[1024,256]{1,0:T(8,128)(2,1)S(1)} %collective-permute-done.8.refs_4_), channel_id=1, source_target_pairs={{0,1},{1,0},{2,3},{3,2},{4,5},{5,4},{6,7},{7,6},{8,9},{9,8},{10,11... | collective-permute-start | bytes 1572872 | tf_op jit(solution)/shard_map/ppermute | solution.py:376
  24.4 4.3 %collective-permute-start.11 = (bf16[1024,256]{1,0:T(8,128)(2,1)S(1)}, bf16[1024,256]{1,0:T(8,128)(2,1)S(1)}, u32[]{:S(2)}, u32[]{:S(2)}) collective-permute-start(bf16[1024,256]{1,0:T(8,128)(2,1)S(1)} %copy-done.2), channel_id=1, source_target_pairs={{0,1},{1,0},{2,3},{3,2},{4,5},{5,4},{6,7},{7,6},{8,9},{9,8},{10,11... | collective-permute-start | bytes 1572872 | tf_op jit(solution)/shard_map/ppermute | solution.py:376
  24.5 3.1 %collective-permute-start.9 = (f32[8,128]{1,0:T(8,128)S(1)}, f32[8,128]{1,0:T(8,128)S(1)}, u32[]{:S(2)}, u32[]{:S(2)}) collective-permute-start(f32[8,128]{1,0:T(8,128)S(1)} %add.9.mine_ref), channel_id=1, source_target_pairs={{0,3},{1,2},{2,1},{3,0},{4,7},{5,6},{6,5},{7,4},{8,11},{9,10},{10,... | collective-permute-start | bytes 12296 | tf_op jit(solution)/shard_map/ppermute | solution.py:376
  28.7 3.1 %collective-permute-start.12 = (f32[8,128]{1,0:T(8,128)S(1)}, f32[8,128]{1,0:T(8,128)S(1)}, u32[]{:S(2)}, u32[]{:S(2)}) collective-permute-start(f32[8,128]{1,0:T(8,128)S(1)} %shard_map.72.mine_ref), channel_id=1, source_target_pairs={{0,5},{1,4},{2,7},{3,6},{4,1},{5,0},{6,3},{7,2},{8,13},{9,12},{10,... | collective-permute-start | bytes 12296 | tf_op jit(solution)/shard_map/ppermute | solution.py:376
  32.7 3.8 %collective-permute-start.13 = (f32[56,256]{1,0:T(8,128)S(1)}, f32[56,256]{1,0:T(8,128)S(1)}, u32[]{:S(2)}, u32[]{:S(2)}) collective-permute-start(f32[56,256]{1,0:T(8,128)S(1)} %get-tuple-element.72), channel_id=1, source_target_pairs={{0,3},{1,2},{2,1},{3,0},{4,7},{5,6},{6,5},{7,4},{8,11},{9,10},{10,... | collective-permute-start | bytes 172040 | tf_op jit(solution)/shard_map/ppermute | solution.py:376
  34.4 4.0 %copy-start.1 = (bf16[1024,256]{1,0:T(8,128)(2,1)S(1)}, bf16[1024,256]{1,0:T(8,128)(2,1)}, u32[]{:S(2)}) copy-start(bf16[1024,256]{1,0:T(8,128)(2,1)} %refs_1_.1) | copy-start | bytes 1572868
  34.4 4.0 %copy-start.3 = (bf16[12,256]{1,0:T(8,128)(2,1)S(1)}, bf16[12,256]{1,0:T(8,128)(2,1)}, u32[]{:S(2)}) copy-start(bf16[12,256]{1,0:T(8,128)(2,1)} %refs_3_.1) | copy-start | bytes 18436
  36.6 3.4 %collective-permute-start.14 = (f32[32,256]{1,0:T(8,128)S(1)}, f32[32,256]{1,0:T(8,128)S(1)}, u32[]{:S(2)}, u32[]{:S(2)}) collective-permute-start(f32[32,256]{1,0:T(8,128)S(1)} %pad_maximum_fusion.2), channel_id=1, source_target_pairs={{0,5},{1,4},{2,7},{3,6},{4,1},{5,0},{6,3},{7,2},{8,13},{9,12},{10,... | collective-permute-start | bytes 98312 | tf_op jit(solution)/shard_map/ppermute | solution.py:376

commit v15 on v14

--- a/solution.py
+++ b/solution.py
@@ -138,25 +138,26 @@
         top += ref.shape[0]
 
 
-def column_scales(panels, left, row_ref, scale_ref):
+def column_scales(panels, across_ref, row_ref, scale_ref):
     tiles = panels[0].shape[1] // LANES
-    sums = [jnp.zeros((8, LANES), jnp.float32)] * tiles
+    sums = [jnp.zeros((8, LANES), jnp.float32)] * (2 * tiles)
     top = 0
     for ref in panels:
 
         def body(i, sums, ref=ref, top=top):
             at = pl.ds(pl.multiple_of(i * 8, 8), 8)
-            row = row_ref[pl.ds(pl.multiple_of(i * 8 + top, 8), 8), :]
-            return [
-                total + ref[at, k * LANES : (k + 1) * LANES] * row for k, total in enumerate(sums)
-            ]
-
-        sums = lax.fori_loop(0, ref.shape[0] // 8, body, sums, unroll=24)
+            to = pl.ds(pl.multiple_of(i * 8 + top, 8), 8)
+            row = row_ref[to, :]
+            cut = [slice(k * LANES, (k + 1) * LANES) for k in range(tiles)]
+            terms = [ref[at, lanes] * row for lanes in cut]
+            terms += [across_ref[to, lanes] * row for lanes in cut]
+            return [total + term for total, term in zip(sums, terms)]
+
+        sums = lax.fori_loop(0, ref.shape[0] // 8, body, sums, unroll=8)
         top += ref.shape[0]
     for k, total in enumerate(sums):
         inverse = 1.0 / jnp.sum(total, axis=0, keepdims=True)
-        at = slice(left + k * LANES, left + (k + 1) * LANES)
-        scale_ref[:, at] = jnp.broadcast_to(inverse, (8, LANES))
+        scale_ref[:, k * LANES : (k + 1) * LANES] = jnp.broadcast_to(inverse, (8, LANES))
 
 
 def weights_of(rows, units, live):
@@ -229,8 +230,7 @@
 
 def scale_columns(sums, near_ref, far_ref, across_ref, row_ref, scale_ref):
     row_ref[...] = as_column(inverse_rows(sums, row_ref.shape[0]))
-    column_scales([near_ref, far_ref], 0, row_ref, scale_ref)
-    column_scales([across_ref], near_ref.shape[1], row_ref, scale_ref)
+    column_scales([near_ref, far_ref], across_ref, row_ref, scale_ref)
 
 
 def next_sums(near_ref, far_ref, across_ref, scale_ref, part_ref):

time: 41.3 us -> 41.6 us (level)
  no operation moved by 1% of the time
where the time goes in v15:
time: 41.6 us; the launch traced here: 41.3 us
  starting transfers between devices  20.2 us (49%)
  waiting for transfers between devices  9.17 us (22%)
  Pallas kernels  8.56 us (21%)
  other arithmetic  1.52 us (4%)
  local copies, waits for them, and re-layouts  1.06 us (3%)
  between operations  0.74 us (2%)
    ppermute x12, starting transfers between devices, swap(): return lax.ppermute(values, axis, others)  15.4 us
    pallas_call x10, Pallas kernels, call(): pl.pallas_call(kernel, out_shape=out_shape, in_specs=[pl.BlockSpec(memory...  8.56 us
    ppermute x12, waiting for transfers between devices, swap(): return lax.ppermute(values, axis, others)  7.3 us
    ppermute x3, starting transfers between devices, swap_dp(): return lax.ppermute(values, ('dp', 'proto'), others)  4.86 us
    ppermute x3, waiting for transfers between devices, swap_dp(): return lax.ppermute(values, ('dp', 'proto'), others)  1.87 us
    unnamed x8, local copies, waits for them, and re-layouts  1.05 us
  transfers between devices with their start and end apart: 15, of which 9 were waited for; matrix products, arithmetic and copies ran while one was open for 2% of the time, Pallas kernels for 16%

profile of v15, /device:TPU:0, one launch (start us, length us, event | category | flops | bytes accessed | tf_op | source)
XLA Modules:
  0.0 41.3 jit_solution(7959905452103667447)
XLA Ops:
  1.4 2.4 %collective-permute-start = (bf16[24,256]{1,0:T(8,128)(2,1)S(1)}, bf16[24,256]{1,0:T(8,128)(2,1)S(1)}, u32[]{:S(2)}, u32[]{:S(2)}) collective-permute-start(bf16[24,256]{1,0:T(8,128)(2,1)S(1)} %pad_maximum_fusion.4), channel_id=1, source_target_pairs={{0,3},{1,2},{2,1},{3,0},{4,7},{5,6},{6,5},{7,4},{8,11},{9,10},{10,... | collective-permute-start | bytes 36872 | tf_op jit(solution)/shard_map/ppermute | solution.py:376
  3.8 0.7 %pad_add_fusion.place_ref = s32[6]{0:T(128)S(1)} fusion(s32[4]{0:T(128)} %param.9, s32[1]{0:T(128)} %bitcast.2, s32[1]{0:T(128)} %bitcast.1), kind=kLoop, calls=%fused_computation.6 | loop fusion | flops 12 | bytes 48 | tf_op jit(solution)/shard_map/concatenate | solution.py:400
  5.2 4.2 %collective-permute-start.1 = (bf16[2,24,256]{2,1,0:T(8,128)(2,1)S(1)}, bf16[2,24,256]{2,1,0:T(8,128)(2,1)S(1)}, u32[]{:S(2)}, u32[]{:S(2)}) collective-permute-start(bf16[2,24,256]{2,1,0:T(8,128)(2,1)S(1)} %get-tuple-element.83), channel_id=1, source_target_pairs={{0,25},{1,24},{2,27},{3,26},{4,29},{5,28},{6,31},{7,30},{8,17},{9,... | collective-permute-start | bytes 73736 | tf_op jit(solution)/shard_map/ppermute | solution.py:384
  10.1 1.5 %collective-permute-start.8 = (bf16[1024,256]{1,0:T(8,128)(2,1)}, bf16[1024,256]{1,0:T(8,128)(2,1)S(1)}, u32[]{:S(2)}, u32[]{:S(2)}) collective-permute-start(bf16[1024,256]{1,0:T(8,128)(2,1)} %refs_1_.1), channel_id=1, source_target_pairs={{0,3},{1,2},{2,1},{3,0},{4,7},{5,6},{6,5},{7,4},{8,11},{9,10},{10,... | collective-permute-start | bytes 1572872 | tf_op jit(solution)/shard_map/ppermute | solution.py:376
  11.7 1.9 %collective-permute-done.2 = bf16[2,24,256]{2,1,0:T(8,128)(2,1)S(1)} collective-permute-done((bf16[2,24,256]{2,1,0:T(8,128)(2,1)S(1)}, bf16[2,24,256]{2,1,0:T(8,128)(2,1)S(1)}, u32[]{:S(2)}, u32[]{:S(2)}) %collective-permute-start.2) | collective-permute-done | bytes 24608 | tf_op jit(solution)/shard_map/ppermute | solution.py:384
  13.6 1.6 %collective-permute-start.4 = (bf16[4,2,24,256]{3,2,1,0:T(8,128)(2,1)S(1)}, bf16[4,2,24,256]{3,2,1,0:T(8,128)(2,1)S(1)}, u32[]{:S(2)}, u32[]{:S(2)}) collective-permute-start(bf16[4,2,24,256]{3,2,1,0:T(8,128)(2,1)S(1)} %pad_maximum_fusion.1), channel_id=1, source_target_pairs={{0,5},{1,4},{2,7},{3,6},{4,1},{5,0},{6,3},{7,2},{8,13},{9,12},{10,... | collective-permute-start | bytes 294920 | tf_op jit(solution)/shard_map/ppermute | solution.py:376
  15.2 1.0 %copy-done = bf16[1024,256]{1,0:T(8,128)(2,1)S(1)} copy-done((bf16[1024,256]{1,0:T(8,128)(2,1)S(1)}, bf16[1024,256]{1,0:T(8,128)(2,1)}, u32[]{:S(2)}) %copy-start) | copy-done | bytes 524312
  16.2 0.8 %shard_map.68 = (bf16[1024,256]{1,0:T(8,128)(2,1)S(1)}, f32[192,128]{1,0:T(8,128)S(1)}, f32[192,128]{1,0:T(8,128)S(1)}) custom-call(s32[6]{0:T(128)S(1)} %pad_add_fusion.place_ref, bf16[1024,256]{1,0:T(8,128)(2,1)S(1)} %copy-done), custom_call_target="tpu_custom_call" | custom-call | flops 134217728 | bytes 1048576 | tf_op jit(solution)/shard_map/pallas_call | solution.py:361
  17.0 1.1 %collective-permute-done.4 = bf16[4,2,24,256]{3,2,1,0:T(8,128)(2,1)S(1)} collective-permute-done((bf16[4,2,24,256]{3,2,1,0:T(8,128)(2,1)S(1)}, bf16[4,2,24,256]{3,2,1,0:T(8,128)(2,1)S(1)}, u32[]{:S(2)}, u32[]{:S(2)}) %collective-permute-start.4) | collective-permute-done | bytes 98336 | tf_op jit(solution)/shard_map/ppermute | solution.py:376
  18.2 0.8 %collective-permute-start.5 = (bf16[2,4,2,24,256]{4,3,2,1,0:T(8,128)(2,1)S(1)}, bf16[2,4,2,24,256]{4,3,2,1,0:T(8,128)(2,1)S(1)}, u32[]{:S(2)}, u32[]{:S(2)}) collective-permute-start(bf16[2,4,2,24,256]{4,3,2,1,0:T(8,128)(2,1)S(1)} %pad_maximum_fusion.near_ref), channel_id=1, source_target_pairs={{0,1},{1,0},{2,3},{3,2},{4,5},{5,4},{6,7},{7,6},{8,9},{9,8},{10,11... | collective-permute-start | bytes 589832 | tf_op jit(solution)/shard_map/ppermute | solution.py:376
  20.0 0.9 %shard_map.70 = (f32[192,2048]{1,0:T(8,128)S(1)}, bf16[192,256]{1,0:T(8,128)(2,1)S(1)}, f32[8,128]{1,0:T(8,128)S(1)}) custom-call(bf16[2,4,2,24,256]{4,3,2,1,0:T(8,128)(2,1)S(1)} %collective-permute-done.5.far_ref, f32[192,128]{1,0:T(8,128)S(1)} %get-tuple-element.48.live_ref.refs_3_, f32[192,2048]{1,0:T(8,128)S(1)} %get-tuple-element.52.near_weights_ref.near_ref, ...), custom_call_target="tpu_custom_call" | custom-call | flops 201326592 | bytes 1572864 | tf_op jit(solution)/shard_map/pallas_call | solution.py:361
  20.8 1.6 %collective-permute-start.7 = (f32[8,128]{1,0:T(8,128)S(1)}, f32[8,128]{1,0:T(8,128)S(1)}, u32[]{:S(2)}, u32[]{:S(2)}) collective-permute-start(f32[8,128]{1,0:T(8,128)S(1)} %get-tuple-element.55), channel_id=1, source_target_pairs={{0,5},{1,4},{2,7},{3,6},{4,1},{5,0},{6,3},{7,2},{8,13},{9,12},{10,... | collective-permute-start | bytes 12296 | tf_op jit(solution)/shard_map/ppermute | solution.py:376
  22.4 1.6 %collective-permute-done.7 = f32[8,128]{1,0:T(8,128)S(1)} collective-permute-done((f32[8,128]{1,0:T(8,128)S(1)}, f32[8,128]{1,0:T(8,128)S(1)}, u32[]{:S(2)}, u32[]{:S(2)}) %collective-permute-start.7) | collective-permute-done | bytes 4128 | tf_op jit(solution)/shard_map/ppermute | solution.py:376
  24.5 1.7 %collective-permute-start.9 = (f32[8,128]{1,0:T(8,128)S(1)}, f32[8,128]{1,0:T(8,128)S(1)}, u32[]{:S(2)}, u32[]{:S(2)}) collective-permute-start(f32[8,128]{1,0:T(8,128)S(1)} %add.9.mine_ref), channel_id=1, source_target_pairs={{0,3},{1,2},{2,1},{3,0},{4,7},{5,6},{6,5},{7,4},{8,11},{9,10},{10,... | collective-permute-start | bytes 12296 | tf_op jit(solution)/shard_map/ppermute | solution.py:376
  26.2 1.0 %shard_map.71 = (f32[384,2048]{1,0:T(8,128)S(1)}, bf16[384,256]{1,0:T(8,128)(2,1)S(1)}) custom-call(bf16[2,4,2,24,256]{4,3,2,1,0:T(8,128)(2,1)S(1)} %pad_maximum_fusion.near_ref, bf16[2,4,2,24,256]{4,3,2,1,0:T(8,128)(2,1)S(1)} %collective-permute-done.5.far_ref, bf16[192,256]{1,0:T(8,128)(2,1)S(1)} %get-tuple-element.58.refs_0_.near_rows_ref, ...), custom_call_target="tpu_custom_call" | custom-call | flops 402653184 | bytes 3145728 | tf_op jit(solution)/shard_map/pallas_call | solution.py:361
  27.6 1.2 %shard_map.72.mine_ref = f32[8,128]{1,0:T(8,128)S(1)} custom-call(f32[8,128]{1,0:T(8,128)S(1)} %add.9.mine_ref, f32[8,128]{1,0:T(8,128)S(1)} %collective-permute-done.9.other_ref, f32[192,2048]{1,0:T(8,128)S(1)} %get-tuple-element.52.near_weights_ref.near_ref, f32[192,2048]{1,0:T(8,128)S(1)} %get-tuple-element.57.far_ref, ...), custom_call_target="tpu_custom_call" | custom-call | flops 402653184 | bytes 3145728 | tf_op jit(solution)/shard_map/pallas_call | solution.py:361
  28.8 1.7 %collective-permute-start.12 = (f32[8,128]{1,0:T(8,128)S(1)}, f32[8,128]{1,0:T(8,128)S(1)}, u32[]{:S(2)}, u32[]{:S(2)}) collective-permute-start(f32[8,128]{1,0:T(8,128)S(1)} %shard_map.72.mine_ref), channel_id=1, source_target_pairs={{0,5},{1,4},{2,7},{3,6},{4,1},{5,0},{6,3},{7,2},{8,13},{9,12},{10,... | collective-permute-start | bytes 12296 | tf_op jit(solution)/shard_map/ppermute | solution.py:376
  30.5 1.1 %shard_map.73 = (bf16[2048,256]{1,0:T(8,128)(2,1)S(1)}, f32[48,256]{1,0:T(8,128)S(1)}, f32[8,128]{1,0:T(8,128)S(1)}) custom-call(bf16[384,256]{1,0:T(8,128)(2,1)S(1)} %get-tuple-element.64.rows_ref.refs_0_.refs_2_, bf16[1024,256]{1,0:T(8,128)(2,1)S(1)} %copy-done.2, bf16[1024,256]{1,0:T(8,128)(2,1)S(1)} %collective-permute-done.11.refs_1_), custom_call_target="tpu_custom_call" | custom-call | flops 402653184 | bytes 3145728 | tf_op jit(solution)/shard_map/pallas_call | solution.py:361
  31.9 1.0 %shard_map.74 = (f32[8,4096]{1,0:T(8,128)S(1)}, f32[56,256]{1,0:T(8,128)S(1)}, f32[56,256]{1,0:T(8,128)S(1)}) custom-call(f32[8,128]{1,0:T(8,128)S(1)} %shard_map.72.mine_ref, f32[8,128]{1,0:T(8,128)S(1)} %collective-permute-done.12.other_ref, f32[192,2048]{1,0:T(8,128)S(1)} %get-tuple-element.52.near_weights_ref.near_ref, ...), custom_call_target="tpu_custom_call" | custom-call | flops 402653184 | bytes 3145728 | tf_op jit(solution)/shard_map/pallas_call | solution.py:361
  33.0 1.7 %collective-permute-start.13 = (f32[56,256]{1,0:T(8,128)S(1)}, f32[56,256]{1,0:T(8,128)S(1)}, u32[]{:S(2)}, u32[]{:S(2)}) collective-permute-start(f32[56,256]{1,0:T(8,128)S(1)} %get-tuple-element.72), channel_id=1, source_target_pairs={{0,3},{1,2},{2,1},{3,0},{4,7},{5,6},{6,5},{7,4},{8,11},{9,10},{10,... | collective-permute-start | bytes 172040 | tf_op jit(solution)/shard_map/ppermute | solution.py:376
  35.2 1.6 %collective-permute-done.13 = f32[56,256]{1,0:T(8,128)S(1)} collective-permute-done((f32[56,256]{1,0:T(8,128)S(1)}, f32[56,256]{1,0:T(8,128)S(1)}, u32[]{:S(2)}, u32[]{:S(2)}) %collective-permute-start.13) | collective-permute-done | bytes 57376 | tf_op jit(solution)/shard_map/ppermute | solution.py:376
  36.8 1.8 %collective-permute-start.14 = (f32[32,256]{1,0:T(8,128)S(1)}, f32[32,256]{1,0:T(8,128)S(1)}, u32[]{:S(2)}, u32[]{:S(2)}) collective-permute-start(f32[32,256]{1,0:T(8,128)S(1)} %pad_maximum_fusion.2), channel_id=1, source_target_pairs={{0,5},{1,4},{2,7},{3,6},{4,1},{5,0},{6,3},{7,2},{8,13},{9,12},{10,... | collective-permute-start | bytes 98312 | tf_op jit(solution)/shard_map/ppermute | solution.py:376
  39.1 1.2 %collective-permute-done.14.other_ref = f32[32,256]{1,0:T(8,128)S(1)} collective-permute-done((f32[32,256]{1,0:T(8,128)S(1)}, f32[32,256]{1,0:T(8,128)S(1)}, u32[]{:S(2)}, u32[]{:S(2)}) %collective-permute-start.14) | collective-permute-done | bytes 32800 | tf_op jit(solution)/shard_map/ppermute | solution.py:376
  40.3 1.0 %shard_map.77 = (f32[12,256]{1,0:T(8,128)}, f32[1,256,256]{2,1,0:T(8,128)}) custom-call(f32[56,256]{1,0:T(8,128)S(1)} %add.10.mine_ref, f32[8,256]{1,0:T(8,128)S(1)} %slice_add_fusion.sums_ref, f32[32,256]{1,0:T(8,128)S(1)} %collective-permute-done.14.other_ref, f32[256,384]{1,0:T(8,128)S(1)} %get-tuple-element.76.targets_ref, ...), custom_call_target="tpu_custom_call" | custom-call | flops 50331648 | bytes 393216 | tf_op jit(solution)/shard_map/pallas_call | solution.py:361
  (34 shorter events, 5.4 us)
Async XLA Ops:
  1.4 3.8 %collective-permute-start = (bf16[24,256]{1,0:T(8,128)(2,1)S(1)}, bf16[24,256]{1,0:T(8,128)(2,1)S(1)}, u32[]{:S(2)}, u32[]{:S(2)}) collective-permute-start(bf16[24,256]{1,0:T(8,128)(2,1)S(1)} %pad_maximum_fusion.4), channel_id=1, source_target_pairs={{0,3},{1,2},{2,1},{3,0},{4,7},{5,6},{6,5},{7,4},{8,11},{9,10},{10,... | collective-permute-start | bytes 36872 | tf_op jit(solution)/shard_map/ppermute | solution.py:376
  5.2 6.5 %collective-permute-start.1 = (bf16[2,24,256]{2,1,0:T(8,128)(2,1)S(1)}, bf16[2,24,256]{2,1,0:T(8,128)(2,1)S(1)}, u32[]{:S(2)}, u32[]{:S(2)}) collective-permute-start(bf16[2,24,256]{2,1,0:T(8,128)(2,1)S(1)} %get-tuple-element.83), channel_id=1, source_target_pairs={{0,25},{1,24},{2,27},{3,26},{4,29},{5,28},{6,31},{7,30},{8,17},{9,... | collective-permute-start | bytes 73736 | tf_op jit(solution)/shard_map/ppermute | solution.py:384
  9.4 4.2 %collective-permute-start.2 = (bf16[2,24,256]{2,1,0:T(8,128)(2,1)S(1)}, bf16[2,24,256]{2,1,0:T(8,128)(2,1)S(1)}, u32[]{:S(2)}, u32[]{:S(2)}) collective-permute-start(bf16[2,24,256]{2,1,0:T(8,128)(2,1)S(1)} %get-tuple-element.83), channel_id=1, source_target_pairs={{0,17},{1,16},{2,19},{3,18},{4,21},{5,20},{6,23},{7,22},{8,25},{9,... | collective-permute-start | bytes 73736 | tf_op jit(solution)/shard_map/ppermute | solution.py:384
  9.4 4.2 %collective-permute-start.3 = (bf16[2,24,256]{2,1,0:T(8,128)(2,1)S(1)}, bf16[2,24,256]{2,1,0:T(8,128)(2,1)S(1)}, u32[]{:S(2)}, u32[]{:S(2)}) collective-permute-start(bf16[2,24,256]{2,1,0:T(8,128)(2,1)S(1)} %get-tuple-element.83), channel_id=1, source_target_pairs={{0,9},{1,8},{2,11},{3,10},{4,13},{5,12},{6,15},{7,14},{8,1},{9,0},... | collective-permute-start | bytes 73736 | tf_op jit(solution)/shard_map/ppermute | solution.py:384
  10.1 8.9 %collective-permute-start.6 = (bf16[1024,256]{1,0:T(8,128)(2,1)}, bf16[1024,256]{1,0:T(8,128)(2,1)S(1)}, u32[]{:S(2)}, u32[]{:S(2)}) collective-permute-start(bf16[1024,256]{1,0:T(8,128)(2,1)} %refs_1_.1), channel_id=1, source_target_pairs={{0,1},{1,0},{2,3},{3,2},{4,5},{5,4},{6,7},{7,6},{8,9},{9,8},{10,11... | collective-permute-start | bytes 1572872 | tf_op jit(solution)/shard_map/ppermute | solution.py:376
  10.1 13.9 %collective-permute-start.8 = (bf16[1024,256]{1,0:T(8,128)(2,1)}, bf16[1024,256]{1,0:T(8,128)(2,1)S(1)}, u32[]{:S(2)}, u32[]{:S(2)}) collective-permute-start(bf16[1024,256]{1,0:T(8,128)(2,1)} %refs_1_.1), channel_id=1, source_target_pairs={{0,3},{1,2},{2,1},{3,0},{4,7},{5,6},{6,5},{7,4},{8,11},{9,10},{10,... | collective-permute-start | bytes 1572872 | tf_op jit(solution)/shard_map/ppermute | solution.py:376
  13.6 4.6 %collective-permute-start.4 = (bf16[4,2,24,256]{3,2,1,0:T(8,128)(2,1)S(1)}, bf16[4,2,24,256]{3,2,1,0:T(8,128)(2,1)S(1)}, u32[]{:S(2)}, u32[]{:S(2)}) collective-permute-start(bf16[4,2,24,256]{3,2,1,0:T(8,128)(2,1)S(1)} %pad_maximum_fusion.1), channel_id=1, source_target_pairs={{0,5},{1,4},{2,7},{3,6},{4,1},{5,0},{6,3},{7,2},{8,13},{9,12},{10,... | collective-permute-start | bytes 294920 | tf_op jit(solution)/shard_map/ppermute | solution.py:376
  15.2 1.0 %copy-start = (bf16[1024,256]{1,0:T(8,128)(2,1)S(1)}, bf16[1024,256]{1,0:T(8,128)(2,1)}, u32[]{:S(2)}) copy-start(bf16[1024,256]{1,0:T(8,128)(2,1)} %refs_1_.1) | copy-start | bytes 1572868
  18.2 1.8 %collective-permute-start.5 = (bf16[2,4,2,24,256]{4,3,2,1,0:T(8,128)(2,1)S(1)}, bf16[2,4,2,24,256]{4,3,2,1,0:T(8,128)(2,1)S(1)}, u32[]{:S(2)}, u32[]{:S(2)}) collective-permute-start(bf16[2,4,2,24,256]{4,3,2,1,0:T(8,128)(2,1)S(1)} %pad_maximum_fusion.near_ref), channel_id=1, source_target_pairs={{0,1},{1,0},{2,3},{3,2},{4,5},{5,4},{6,7},{7,6},{8,9},{9,8},{10,11... | collective-permute-start | bytes 589832 | tf_op jit(solution)/shard_map/ppermute | solution.py:376
  19.6 4.8 %copy-start.2 = (bf16[1024,256]{1,0:T(8,128)(2,1)S(1)}, bf16[1024,256]{1,0:T(8,128)(2,1)}, u32[]{:S(2)}) copy-start(bf16[1024,256]{1,0:T(8,128)(2,1)} %refs_2_.1) | copy-start | bytes 1572868
  20.8 3.1 %collective-permute-start.7 = (f32[8,128]{1,0:T(8,128)S(1)}, f32[8,128]{1,0:T(8,128)S(1)}, u32[]{:S(2)}, u32[]{:S(2)}) collective-permute-start(f32[8,128]{1,0:T(8,128)S(1)} %get-tuple-element.55), channel_id=1, source_target_pairs={{0,5},{1,4},{2,7},{3,6},{4,1},{5,0},{6,3},{7,2},{8,13},{9,12},{10,... | collective-permute-start | bytes 12296 | tf_op jit(solution)/shard_map/ppermute | solution.py:376
  24.0 2.2 %collective-permute-start.10 = (bf16[1024,256]{1,0:T(8,128)(2,1)S(1)}, bf16[1024,256]{1,0:T(8,128)(2,1)S(1)}, u32[]{:S(2)}, u32[]{:S(2)}) collective-permute-start(bf16[1024,256]{1,0:T(8,128)(2,1)S(1)} %collective-permute-done.8.refs_4_), channel_id=1, source_target_pairs={{0,1},{1,0},{2,3},{3,2},{4,5},{5,4},{6,7},{7,6},{8,9},{9,8},{10,11... | collective-permute-start | bytes 1572872 | tf_op jit(solution)/shard_map/ppermute | solution.py:376
  24.4 4.4 %collective-permute-start.11 = (bf16[1024,256]{1,0:T(8,128)(2,1)S(1)}, bf16[1024,256]{1,0:T(8,128)(2,1)S(1)}, u32[]{:S(2)}, u32[]{:S(2)}) collective-permute-start(bf16[1024,256]{1,0:T(8,128)(2,1)S(1)} %copy-done.2), channel_id=1, source_target_pairs={{0,1},{1,0},{2,3},{3,2},{4,5},{5,4},{6,7},{7,6},{8,9},{9,8},{10,11... | collective-permute-start | bytes 1572872 | tf_op jit(solution)/shard_map/ppermute | solution.py:376
  24.5 3.1 %collective-permute-start.9 = (f32[8,128]{1,0:T(8,128)S(1)}, f32[8,128]{1,0:T(8,128)S(1)}, u32[]{:S(2)}, u32[]{:S(2)}) collective-permute-start(f32[8,128]{1,0:T(8,128)S(1)} %add.9.mine_ref), channel_id=1, source_target_pairs={{0,3},{1,2},{2,1},{3,0},{4,7},{5,6},{6,5},{7,4},{8,11},{9,10},{10,... | collective-permute-start | bytes 12296 | tf_op jit(solution)/shard_map/ppermute | solution.py:376
  28.8 3.1 %collective-permute-start.12 = (f32[8,128]{1,0:T(8,128)S(1)}, f32[8,128]{1,0:T(8,128)S(1)}, u32[]{:S(2)}, u32[]{:S(2)}) collective-permute-start(f32[8,128]{1,0:T(8,128)S(1)} %shard_map.72.mine_ref), channel_id=1, source_target_pairs={{0,5},{1,4},{2,7},{3,6},{4,1},{5,0},{6,3},{7,2},{8,13},{9,12},{10,... | collective-permute-start | bytes 12296 | tf_op jit(solution)/shard_map/ppermute | solution.py:376
  33.0 3.8 %collective-permute-start.13 = (f32[56,256]{1,0:T(8,128)S(1)}, f32[56,256]{1,0:T(8,128)S(1)}, u32[]{:S(2)}, u32[]{:S(2)}) collective-permute-start(f32[56,256]{1,0:T(8,128)S(1)} %get-tuple-element.72), channel_id=1, source_target_pairs={{0,3},{1,2},{2,1},{3,0},{4,7},{5,6},{6,5},{7,4},{8,11},{9,10},{10,... | collective-permute-start | bytes 172040 | tf_op jit(solution)/shard_map/ppermute | solution.py:376
  34.7 4.0 %copy-start.1 = (bf16[1024,256]{1,0:T(8,128)(2,1)S(1)}, bf16[1024,256]{1,0:T(8,128)(2,1)}, u32[]{:S(2)}) copy-start(bf16[1024,256]{1,0:T(8,128)(2,1)} %refs_1_.1) | copy-start | bytes 1572868
  34.7 4.0 %copy-start.3 = (bf16[12,256]{1,0:T(8,128)(2,1)S(1)}, bf16[12,256]{1,0:T(8,128)(2,1)}, u32[]{:S(2)}) copy-start(bf16[12,256]{1,0:T(8,128)(2,1)} %refs_3_.1) | copy-start | bytes 18436
  36.8 3.4 %collective-permute-start.14 = (f32[32,256]{1,0:T(8,128)S(1)}, f32[32,256]{1,0:T(8,128)S(1)}, u32[]{:S(2)}, u32[]{:S(2)}) collective-permute-start(f32[32,256]{1,0:T(8,128)S(1)} %pad_maximum_fusion.2), channel_id=1, source_target_pairs={{0,5},{1,4},{2,7},{3,6},{4,1},{5,0},{6,3},{7,2},{8,13},{9,12},{10,... | collective-permute-start | bytes 98312 | tf_op jit(solution)/shard_map/ppermute | solution.py:376
